TPU v7x, 32 devices: a whole 2x2x4 slice. The times are simulated.
32 devices in a mesh: blk: 4 (over z), lat: 4 (over y, x), depth: 2 (over core).
Axes of the slice: x: 2, y: 2, z: 4, core: 2. Of those that a mesh axis runs over, the one named last changes fastest.
Arguments:
- face_len: int32 [4, 4, 2, 6], P('blk', 'lat', 'depth'), may hold values from 0 to 128, as said below
- residual: float32 [4, 4, 2, 768, 512], P('blk', 'lat', 'depth'), as said below
- prev_direction: float32 [4, 4, 2, 768, 512], P('blk', 'lat', 'depth'), as said below
- prev_rho: float32 [512], replicated, may hold values from 0.5 to 4
- schur: float32 [4, 4, 2, 768, 768], P('blk', 'lat', 'depth'), as said below
- neumann: float32 [4, 4, 2, 768, 768], P('blk', 'lat', 'depth'), as said below
- coarse_basis: float32 [4, 4, 2, 768, 256], P('blk', 'lat', 'depth'), may hold values from -0.21875 to 0.21875
- coarse_inverse: float32 [4, 4, 2, 256, 256], P('blk', 'lat', 'depth'), as said below
- prim_owner: int32 [4, 4, 2, 256, 1], P('blk', 'lat', 'depth'), may hold values from 0 to 15; in each aligned block of 256 rows (0 to 255, 256 to 511, ..., all dimensions but the last counted through in order) at most 24 rows name the same one
- coarse_row: int32 [4, 4, 2, 256], P('blk', 'lat', 'depth'), may hold values from 0 to 255
Outputs:
- new_residual: float32 [4, 4, 2, 768, 512], P('blk', 'lat', 'depth')
- direction: float32 [4, 4, 2, 768, 512], P('blk', 'lat', 'depth')
- rho_now: float32 [512], replicated
- step_alpha: float32 [512], replicated
- res_norm: float32 [512], replicated
Inputs may be any that keep to these rules, and one draw needn't show every extreme that they name: `face_len`: two subdomains that share a face have equal lengths on it; faces on the outer ends of lat and depth have length 0. `residual`: the two copies of a shared interface row are equal, and rows past a face's length are zero. `prev_direction`: the two copies of a shared interface row are equal, and rows past a face's length are zero. `schur`: each matrix has a positive definite symmetric part. `neumann`: each matrix has a positive definite symmetric part. `coarse_inverse`: each matrix has a positive definite symmetric part. `prim_owner`: at most 24 primal dofs of one subdomain have the same owner.
All inputs are finite; a program needn't handle non-finite values.
Results may differ from a plain program's by a relative error of at most 0.00005.
Values sent between devices are 32-bit elements; how exact they have to be, the bound alone decides.
No kernel may reach another device: no remote copies, remote signals or barrier semaphores. Data moves between devices by JAX's collectives and lax.ppermute only.
A program may use at most 64 MiB of HBM per device.

v0:
```python
import jax
import jax.numpy as jnp
from jax import lax
from jax.sharding import PartitionSpec as P

CAP = 24


exact_mode = lax.Precision.HIGHEST


def from_behind(x, axis, by):
    devices = lax.axis_size(axis)
    return lax.ppermute(x, axis, [(i, (i + by) % devices) for i in range(devices)])


def passed_along(block, axis, distance):
    devices = range(lax.axis_size(axis))
    route = [(i - distance, i) for i in devices if i - distance in devices]
    return lax.ppermute(block, axis, route)


def product(left, right):
    return jnp.dot(left, right, precision=exact_mode, preferred_element_type=jnp.float32)


def product_t(left, right):
    return lax.dot_general(
        left,
        right,
        (((0,), (0,)), ((), ())),
        precision=exact_mode,
        preferred_element_type=jnp.float32,
    )


def assemble(vector, live_mask):
    col_count = vector.shape[1]
    face_rows = vector.shape[0] // 6
    face_list = vector.reshape(6, face_rows, col_count)
    received = [None] * 6
    for facing in range(2):
        shift_by = 1 - 2 * facing
        received[facing] = from_behind(face_list[1 - facing], "blk", shift_by)
        received[2 + facing] = passed_along(face_list[3 - facing], "lat", shift_by)
        received[4 + facing] = passed_along(face_list[5 - facing], "depth", shift_by)
    return live_mask * (vector + jnp.stack(received).reshape(vector.shape))


def coarse_level(coarse_terms, owner_ids, row_ids, inverse):
    primal, col_count = coarse_terms.shape
    owners = lax.axis_size(("blk", "lat"))
    slots = owners * CAP
    owner_hit = (owner_ids[:, None] == lax.broadcasted_iota(jnp.int32, (primal, owners), 1)).astype(
        jnp.int32
    )
    owner_rank = jnp.sum(jnp.cumsum(owner_hit, axis=0) * owner_hit, axis=1) - 1
    slot_index = owner_ids * CAP + owner_rank
    packer = slot_index[None, :] == lax.broadcasted_iota(jnp.int32, (slots, primal), 0)
    pack_table = packer.astype(jnp.float32)
    outgoing = product(pack_table, coarse_terms).reshape(owners, CAP, col_count)
    outgoing_rows = (jnp.sum(jnp.where(packer, row_ids[None, :] + 1, 0), axis=1) - 1).reshape(
        owners, CAP
    )
    incoming, incoming_rows = (
        lax.all_to_all(outgoing, ("blk", "lat"), split_axis=0, concat_axis=0, tiled=True),
        lax.all_to_all(outgoing_rows, ("blk", "lat"), split_axis=0, concat_axis=0, tiled=True),
    )
    owned_rows = inverse.shape[0]
    picker = (
        incoming_rows.reshape(1, slots) == lax.broadcasted_iota(jnp.int32, (owned_rows, slots), 0)
    ).astype(jnp.float32)
    gathered = product(picker, incoming.reshape(slots, col_count))
    solved = product(inverse, gathered)
    answers = product_t(picker, solved)
    returned = lax.all_to_all(
        answers.reshape(owners, CAP, col_count),
        ("blk", "lat"),
        split_axis=0,
        concat_axis=0,
        tiled=True,
    )
    return product_t(pack_table, returned.reshape(slots, col_count))


def shards(
    face_len,
    residual,
    prev_direction,
    prev_rho,
    schur,
    neumann,
    coarse_basis,
    coarse_inverse,
    prim_owner,
    coarse_row,
):
    row_count = residual.shape[3]
    col_count = residual.shape[4]
    face_rows = row_count // 6
    primal = coarse_basis.shape[4]
    owned_rows = coarse_inverse.shape[3]
    lengths = face_len.reshape(6)
    live_mask = (
        (lax.broadcasted_iota(jnp.int32, (6, face_rows), 1) < lengths[:, None])
        .astype(jnp.float32)
        .reshape(row_count, 1)
    )
    residual_live = live_mask * residual.reshape(row_count, col_count)
    weighted = 0.5 * residual_live
    local_part = product(neumann.reshape(row_count, row_count), weighted)
    basis = coarse_basis.reshape(row_count, primal)
    coarse_terms = product_t(basis, weighted)
    correction = coarse_level(
        coarse_terms,
        prim_owner.reshape(primal),
        coarse_row.reshape(primal),
        coarse_inverse.reshape(owned_rows, owned_rows),
    )
    precond_image = local_part + product(basis, correction)
    precond = 0.5 * assemble(precond_image, live_mask)
    devices = lax.axis_size(("blk", "lat", "depth"))
    norm_scale = 0.5 / (devices * row_count)
    rho_now = norm_scale * lax.psum(
        jnp.sum(residual_live * precond, axis=0), ("blk", "lat", "depth")
    )
    direction = precond + rho_now / prev_rho * (
        live_mask * prev_direction.reshape(row_count, col_count)
    )
    schur_image = product(schur.reshape(row_count, row_count), direction)
    applied = assemble(schur_image, live_mask)
    curv_sum, old_square, cross_sum, applied_square = lax.psum(
        (
            jnp.sum(direction * applied, axis=0),
            jnp.sum(residual_live * residual_live, axis=0),
            jnp.sum(residual_live * applied, axis=0),
            jnp.sum(applied * applied, axis=0),
        ),
        ("blk", "lat", "depth"),
    )
    step_alpha = rho_now / (norm_scale * curv_sum)
    new_residual = residual_live - step_alpha * applied
    res_norm = norm_scale * (
        old_square - 2.0 * step_alpha * cross_sum + step_alpha * step_alpha * applied_square
    )
    out_shape = (1, 1, 1, row_count, col_count)
    return (
        new_residual.reshape(out_shape),
        direction.reshape(out_shape),
        rho_now,
        step_alpha,
        res_norm,
    )


def solution(mesh):
    in_specs = (
        P("blk", "lat", "depth", None),
        P("blk", "lat", "depth", None, None),
        P("blk", "lat", "depth", None, None),
        P(),
        P("blk", "lat", "depth", None, None),
        P("blk", "lat", "depth", None, None),
        P("blk", "lat", "depth", None, None),
        P("blk", "lat", "depth", None, None),
        P("blk", "lat", "depth", None, None),
        P("blk", "lat", "depth", None),
    )
    out_specs = (
        P("blk", "lat", "depth", None, None),
        P("blk", "lat", "depth", None, None),
        P(),
        P(),
        P(),
    )
    return jax.shard_map(shards, mesh=mesh, in_specs=in_specs, out_specs=out_specs, check_vma=False)
```

profile of v0, /device:TPU:0, one launch (start us, length us, event | category | flops | bytes accessed | tf_op | source)
XLA Modules:
  0.0 243.4 jit_solution(5289307627829466085)
XLA Ops:
  5.3 8.3 %all-to-all-start = ((s32[16,1,24]{2,1,0:T(1,128)}), s32[16,1,24]{2,1,0:T(1,128)S(1)}, u32[]{:S(2)}, u32[]{:S(2)}) async-start(s32[16,1,24]{2,1,0:T(1,128)} %sub.18), calls=%async_computation | async-start | bytes 16384 | tf_op jit(solution)/shard_map/all_to_all | solution.py:67
  14.3 4.4 %fusion.6 = f32[512,256]{1,0:T(8,128)S(1)} fusion(f32[1,1,1,768,512]{4,3,2,1,0:T(8,128)} %param.11, f32[1,1,1,768,256]{4,3,2,1,0:T(8,128)} %param.16, f32[768]{0:T(1024)S(1)} %convert_bitcast_fusion), kind=kOutput, calls=%fused_computation.7 | convolution fusion | flops 1208745984 | bytes 2886656 | tf_op jit(solution)/shard_map/dot_general | solution.py:28
  20.8 6.4 %all-to-all-start.1 = ((f32[16,24,512]{2,1,0:T(8,128)}), f32[16,24,512]{2,1,0:T(8,128)S(1)}, u32[]{:S(2)}, u32[]{:S(2)}) async-start(f32[16,24,512]{2,1,0:T(8,128)} %bitcast.10), calls=%async_computation.1 | async-start | bytes 1572864 | tf_op jit(solution)/shard_map/all_to_all | solution.py:66
  28.5 17.9 %all-to-all-done.1 = f32[16,24,512]{2,1,0:T(8,128)S(1)} async-done(((f32[16,24,512]{2,1,0:T(8,128)}), f32[16,24,512]{2,1,0:T(8,128)S(1)}, u32[]{:S(2)}, u32[]{:S(2)}) %all-to-all-start.1) | async-done | bytes 786464 | tf_op jit(solution)/shard_map/all_to_all | solution.py:66
  49.6 4.9 %all-to-all-start.2 = ((f32[16,24,512]{2,1,0:T(8,128)}), f32[16,24,512]{2,1,0:T(8,128)S(1)}, u32[]{:S(2)}, u32[]{:S(2)}) async-start(f32[16,24,512]{2,1,0:T(8,128)} %bitcast.107), calls=%async_computation.2 | async-start | bytes 1572864 | tf_op jit(solution)/shard_map/all_to_all | solution.py:76
  54.5 10.2 %fusion.2 = f32[512,768]{1,0:T(8,128)} fusion(f32[1,1,1,768,768]{4,3,2,1,0:T(8,128)S(1)} %copy-done, f32[1,1,1,768,512]{4,3,2,1,0:T(8,128)} %param.11, f32[768]{0:T(1024)S(1)} %convert_bitcast_fusion), kind=kOutput, calls=%fused_computation.2 | convolution fusion | flops 3624665088 | bytes 5508096 | tf_op jit(solution)/shard_map/dot_general | solution.py:24
  64.7 8.4 %all-to-all-done.2 = f32[16,24,512]{2,1,0:T(8,128)S(1)} async-done(((f32[16,24,512]{2,1,0:T(8,128)}), f32[16,24,512]{2,1,0:T(8,128)S(1)}, u32[]{:S(2)}, u32[]{:S(2)}) %all-to-all-start.2) | async-done | bytes 786464 | tf_op jit(solution)/shard_map/all_to_all | solution.py:76
  74.2 4.0 %add_bitcast_fusion = f32[768,512]{0,1:T(8,128)S(1)} fusion(f32[512,768]{1,0:T(8,128)} %fusion.2, f32[256,512]{1,0:T(8,128)S(1)} %fusion.20, f32[1,1,1,768,256]{4,3,2,1,0:T(8,128)S(1)} %copy-done.4), kind=kOutput, calls=%fused_computation.19 | convolution fusion | flops 1208352768 | bytes 4456448 | tf_op jit(solution)/shard_map/dot_general | solution.py:24
  83.5 3.0 %copy.30 = f32[1,1,1,768,512]{3,4,2,1,0:T(8,128)} copy(f32[1,1,1,768,512]{4,3,2,1,0:T(8,128)} %param.11) | data formatting | bytes 3145728 | tf_op args[1]
  86.5 3.0 %copy.34 = f32[1,1,1,768,512]{3,4,2,1,0:T(8,128)} copy(f32[1,1,1,768,512]{4,3,2,1,0:T(8,128)} %param.12) | data formatting | bytes 3145728 | tf_op args[2]
  100.0 3.4 %collective-permute-done.3 = f32[128,512]{0,1:T(8,128)S(1)} collective-permute-done((f32[128,512]{0,1:T(8,128)S(1)}, f32[128,512]{0,1:T(8,128)S(1)}, u32[]{:S(2)}, u32[]{:S(2)}) %collective-permute-start.3) | collective-permute-done | bytes 262176 | tf_op jit(solution)/shard_map/ppermute | solution.py:20
  105.6 3.0 %copy.32 = f32[6,128,512]{2,1,0:T(8,128)} copy(f32[6,128,512]{1,2,0:T(8,128)} %bitcast_dynamic-update-slice_fusion.6) | data formatting | bytes 3145728 | tf_op jit(solution)/shard_map/stack | solution.py:47
  108.6 3.0 %copy.33 = f32[768,512]{0,1:T(8,128)} copy(f32[768,512]{1,0:T(8,128)} %bitcast.103) | data formatting | bytes 3145728 | tf_op jit(solution)/shard_map/reshape | solution.py:47
  114.4 38.6 %psum.35 = f32[512]{0:T(512)S(1)} all-reduce(f32[512]{0:T(512)S(1)} %multiply_reduce_fusion.4), channel_id=1, replica_groups=mesh['blk'=4,'lat'=4,'depth'=2] {'blk','lat','depth'}, use_global_device_ids=true, to_apply=%region_5.6 | all-reduce | flops 512 | bytes 4096 | tf_op jit(solution)/shard_map/psum | solution.py:124
  153.0 2.9 %fusion.5 = f32[768,512]{0,1:T(8,128)S(1)} fusion(f32[1,1,1,768,512]{3,4,2,1,0:T(8,128)} %copy.34, f32[512]{0:T(512)S(1)} %get-tuple-element.31, f32[768]{0:T(1024)S(1)} %convert_bitcast_fusion, f32[768,512]{0,1:T(8,128)} %copy-done.1, f32[768,512]{0,1:T(8,128)} %copy.33), kind=kLoop, calls=%fused_computation.6 | loop fusion | flops 2359296 | bytes 6296576 | tf_op jit(solution)/shard_map/add | solution.py:127
  156.1 4.0 %fusion.9 = f32[768,512]{0,1:T(8,128)S(1)} fusion(f32[768,512]{0,1:T(8,128)S(1)} %fusion.5, f32[1,1,1,768,768]{4,3,2,1,0:T(8,128)S(1)} %copy-done.5), kind=kOutput, calls=%fused_computation.21 | convolution fusion | flops 3623878656 | bytes 5505024 | tf_op jit(solution)/shard_map/dot_general | solution.py:24
  165.3 4.9 %collective-permute-start.8 = (f32[128,512]{0,1:T(8,128)S(1)}, f32[128,512]{0,1:T(8,128)}, u32[]{:S(2)}, u32[]{:S(2)}) collective-permute-start(f32[128,512]{0,1:T(8,128)S(1)} %get-tuple-element.36), channel_id=1, source_target_pairs={{0,2},{2,4},{4,6},{1,3},{3,5},{5,7},{8,10},{10,12},{12,14},{9,11},... | collective-permute-start | bytes 786440 | tf_op jit(solution)/shard_map/ppermute | solution.py:20
  173.5 3.0 %copy.38 = f32[1,1,1,768,512]{4,3,2,1,0:T(8,128)} copy(f32[1,1,1,768,512]{3,4,2,1,0:T(8,128)} %bitcast.102) | data formatting | bytes 3145728
  186.9 3.1 %copy.35 = f32[6,128,512]{2,1,0:T(8,128)} copy(f32[6,128,512]{1,2,0:T(8,128)} %bitcast_dynamic-update-slice_fusion) | data formatting | bytes 3145728 | tf_op jit(solution)/shard_map/stack | solution.py:47
  189.9 3.0 %copy.36 = f32[768,512]{0,1:T(8,128)} copy(f32[768,512]{1,0:T(8,128)} %bitcast.104) | data formatting | bytes 3145728 | tf_op jit(solution)/shard_map/reshape | solution.py:47
  192.9 4.3 %multiply_reduce_fusion.1 = (f32[512]{0:T(512)S(1)}, f32[512]{0:T(512)S(1)}, f32[512]{0:T(512)S(1)}, f32[512]{0:T(512)S(1)}, f32[768,512]{0,1:T(8,128)}) fusion(f32[1,1,1,768,512]{3,4,2,1,0:T(8,128)} %copy.30, f32[768]{0:T(1024)S(1)} %convert_bitcast_fusion, f32[768,512]{0,1:T(8,128)} %copy-done.2, f32[768,512]{0,1:T(8,128)} %copy-done.3, f32[768,512]{0,1:T(8,128)} %copy.36), kind=kLoop, calls=%fused_computation.12 | loop fusion | flops 4323328 | bytes 7875584 | tf_op jit(solution)/shard_map/reduce_sum | solution.py:136
  197.2 39.4 %all-reduce = (f32[512]{0:T(512)S(1)}, f32[512]{0:T(512)S(1)}, f32[512]{0:T(512)S(1)}, f32[512]{0:T(512)S(1)}) all-reduce(f32[512]{0:T(512)S(1)} %get-tuple-element.23, f32[512]{0:T(512)S(1)} %get-tuple-element.22, f32[512]{0:T(512)S(1)} %get-tuple-element.21, ...), channel_id=1, replica_groups=mesh['blk'=4,'lat'=4,'depth'=2] {'blk','lat','depth'}, use_global_device_ids=true, to_apply=%region_7.8 | all-reduce | flops 2048 | bytes 16384 | tf_op jit(solution)/shard_map/psum | solution.py:132
  237.2 3.3 %subtract_bitcast_fusion = f32[1,1,1,768,512]{3,4,2,1,0:T(8,128)} fusion(f32[768,512]{0,1:T(8,128)} %get-tuple-element.30, f32[1,1,1,768,512]{3,4,2,1,0:T(8,128)} %copy.30, f32[512]{0:T(512)S(1)} %get-tuple-element.29, f32[768]{0:T(1024)S(1)} %convert_bitcast_fusion), kind=kLoop, calls=%fused_computation.14 | loop fusion | flops 1179648 | bytes 4723712 | tf_op jit(solution)/shard_map/reshape | solution.py:148
  240.4 3.0 %copy.37 = f32[1,1,1,768,512]{4,3,2,1,0:T(8,128)} copy(f32[1,1,1,768,512]{3,4,2,1,0:T(8,128)} %subtract_bitcast_fusion) | data formatting | bytes 3145728
  (80 shorter events, 53.1 us)
Async XLA Ops:
  0.6 53.8 %copy-start = (f32[1,1,1,768,768]{4,3,2,1,0:T(8,128)S(1)}, f32[1,1,1,768,768]{4,3,2,1,0:T(8,128)}, u32[]{:S(2)}) copy-start(f32[1,1,1,768,768]{4,3,2,1,0:T(8,128)} %param.15) | copy-start | bytes 7077892
  5.3 15.5 %all-to-all-start = ((s32[16,1,24]{2,1,0:T(1,128)}), s32[16,1,24]{2,1,0:T(1,128)S(1)}, u32[]{:S(2)}, u32[]{:S(2)}) async-start(s32[16,1,24]{2,1,0:T(1,128)} %sub.18), calls=%async_computation | async-start | bytes 16384 | tf_op jit(solution)/shard_map/all_to_all | solution.py:67
  20.1 26.9 %copy-start.6 = (f32[1,1,1,256,256]{4,3,2,1,0:T(8,128)S(1)}, f32[1,1,1,256,256]{4,3,2,1,0:T(8,128)}, u32[]{:S(2)}) copy-start(f32[1,1,1,256,256]{4,3,2,1,0:T(8,128)} %param.17) | copy-start | bytes 786436
  20.8 25.6 %all-to-all-start.1 = ((f32[16,24,512]{2,1,0:T(8,128)}), f32[16,24,512]{2,1,0:T(8,128)S(1)}, u32[]{:S(2)}, u32[]{:S(2)}) async-start(f32[16,24,512]{2,1,0:T(8,128)} %bitcast.10), calls=%async_computation.1 | async-start | bytes 1572864 | tf_op jit(solution)/shard_map/all_to_all | solution.py:66
  49.6 23.5 %all-to-all-start.2 = ((f32[16,24,512]{2,1,0:T(8,128)}), f32[16,24,512]{2,1,0:T(8,128)S(1)}, u32[]{:S(2)}, u32[]{:S(2)}) async-start(f32[16,24,512]{2,1,0:T(8,128)} %bitcast.107), calls=%async_computation.2 | async-start | bytes 1572864 | tf_op jit(solution)/shard_map/all_to_all | solution.py:76
  78.3 1.3 copy-start.1
  79.6 15.0 %collective-permute-start = (f32[128,512]{0,1:T(8,128)}, f32[128,512]{0,1:T(8,128)}, u32[]{:S(2)}, u32[]{:S(2)}) collective-permute-start(f32[128,512]{0,1:T(8,128)} %get-tuple-element.44), channel_id=1, source_target_pairs={{0,8},{8,16},{16,24},{24,0},{1,9},{9,17},{17,25},{25,1},{2,10},{10... | collective-permute-start | bytes 786440 | tf_op jit(solution)/shard_map/ppermute | solution.py:14
  81.8 15.8 %collective-permute-start.1 = (f32[128,512]{0,1:T(8,128)}, f32[128,512]{0,1:T(8,128)}, u32[]{:S(2)}, u32[]{:S(2)}) collective-permute-start(f32[128,512]{0,1:T(8,128)} %get-tuple-element.43), channel_id=1, source_target_pairs={{0,24},{8,0},{16,8},{24,16},{1,25},{9,1},{17,9},{25,17},{2,26},{10... | collective-permute-start | bytes 786440 | tf_op jit(solution)/shard_map/ppermute | solution.py:14
  89.5 9.8 %collective-permute-start.2 = (f32[128,512]{0,1:T(8,128)S(1)}, f32[128,512]{0,1:T(8,128)S(1)}, u32[]{:S(2)}, u32[]{:S(2)}) collective-permute-start(f32[128,512]{0,1:T(8,128)S(1)} %get-tuple-element.42), channel_id=1, source_target_pairs={{0,2},{2,4},{4,6},{1,3},{3,5},{5,7},{8,10},{10,12},{12,14},{9,11},... | collective-permute-start | bytes 786440 | tf_op jit(solution)/shard_map/ppermute | solution.py:20
  92.0 11.4 %collective-permute-start.3 = (f32[128,512]{0,1:T(8,128)S(1)}, f32[128,512]{0,1:T(8,128)S(1)}, u32[]{:S(2)}, u32[]{:S(2)}) collective-permute-start(f32[128,512]{0,1:T(8,128)S(1)} %get-tuple-element.41), channel_id=1, source_target_pairs={{2,0},{4,2},{6,4},{3,1},{5,3},{7,5},{10,8},{12,10},{14,12},{11,9},... | collective-permute-start | bytes 786440 | tf_op jit(solution)/shard_map/ppermute | solution.py:20
  93.3 10.8 %collective-permute-start.4 = (f32[128,512]{0,1:T(8,128)S(1)}, f32[128,512]{0,1:T(8,128)S(1)}, u32[]{:S(2)}, u32[]{:S(2)}) collective-permute-start(f32[128,512]{0,1:T(8,128)S(1)} %get-tuple-element.40), channel_id=1, source_target_pairs={{0,1},{2,3},{4,5},{6,7},{8,9},{10,11},{12,13},{14,15},{16,17},{18,... | collective-permute-start | bytes 786440 | tf_op jit(solution)/shard_map/ppermute | solution.py:20
  94.6 10.2 %collective-permute-start.5 = (f32[128,512]{0,1:T(8,128)S(1)}, f32[128,512]{0,1:T(8,128)S(1)}, u32[]{:S(2)}, u32[]{:S(2)}) collective-permute-start(f32[128,512]{0,1:T(8,128)S(1)} %get-tuple-element.39), channel_id=1, source_target_pairs={{1,0},{3,2},{5,4},{7,6},{9,8},{11,10},{13,12},{15,14},{17,16},{19,... | collective-permute-start | bytes 786440 | tf_op jit(solution)/shard_map/ppermute | solution.py:20
  111.6 41.4 %copy-start.9 = (f32[512]{0:T(512)S(1)}, f32[512]{0:T(512)}, u32[]{:S(2)}) copy-start(f32[512]{0:T(512)} %param.13) | copy-start | bytes 6148
  153.0 83.6 %copy-start.8 = (f32[512]{0:T(512)}, f32[512]{0:T(512)S(1)}, u32[]{:S(2)}) copy-start(f32[512]{0:T(512)S(1)} %get-tuple-element.32) | copy-start | bytes 6148
  153.0 3.1 %copy-start.5 = (f32[1,1,1,768,768]{4,3,2,1,0:T(8,128)S(1)}, f32[1,1,1,768,768]{4,3,2,1,0:T(8,128)}, u32[]{:S(2)}) copy-start(f32[1,1,1,768,768]{4,3,2,1,0:T(8,128)} %param.14) | copy-start | bytes 7077892
  156.1 4.1 %copy-start.2 = (f32[768,512]{0,1:T(8,128)}, f32[768,512]{0,1:T(8,128)S(1)}, u32[]{:S(2)}) copy-start(f32[768,512]{0,1:T(8,128)S(1)} %fusion.5) | copy-start | bytes 4718596
  160.1 1.3 copy-start.3
  161.5 15.0 %collective-permute-start.6 = (f32[128,512]{0,1:T(8,128)}, f32[128,512]{0,1:T(8,128)}, u32[]{:S(2)}, u32[]{:S(2)}) collective-permute-start(f32[128,512]{0,1:T(8,128)} %get-tuple-element.38), channel_id=1, source_target_pairs={{0,8},{8,16},{16,24},{24,0},{1,9},{9,17},{17,25},{25,1},{2,10},{10... | collective-permute-start | bytes 786440 | tf_op jit(solution)/shard_map/ppermute | solution.py:14
  162.9 16.5 %collective-permute-start.7 = (f32[128,512]{0,1:T(8,128)}, f32[128,512]{0,1:T(8,128)}, u32[]{:S(2)}, u32[]{:S(2)}) collective-permute-start(f32[128,512]{0,1:T(8,128)} %get-tuple-element.37), channel_id=1, source_target_pairs={{0,24},{8,0},{16,8},{24,16},{1,25},{9,1},{17,9},{25,17},{2,26},{10... | collective-permute-start | bytes 786440 | tf_op jit(solution)/shard_map/ppermute | solution.py:14
  165.3 15.9 %collective-permute-start.8 = (f32[128,512]{0,1:T(8,128)S(1)}, f32[128,512]{0,1:T(8,128)}, u32[]{:S(2)}, u32[]{:S(2)}) collective-permute-start(f32[128,512]{0,1:T(8,128)S(1)} %get-tuple-element.36), channel_id=1, source_target_pairs={{0,2},{2,4},{4,6},{1,3},{3,5},{5,7},{8,10},{10,12},{12,14},{9,11},... | collective-permute-start | bytes 786440 | tf_op jit(solution)/shard_map/ppermute | solution.py:20
  170.2 12.6 %collective-permute-start.9 = (f32[128,512]{0,1:T(8,128)S(1)}, f32[128,512]{0,1:T(8,128)}, u32[]{:S(2)}, u32[]{:S(2)}) collective-permute-start(f32[128,512]{0,1:T(8,128)S(1)} %get-tuple-element.35), channel_id=1, source_target_pairs={{2,0},{4,2},{6,4},{3,1},{5,3},{7,5},{10,8},{12,10},{14,12},{11,9},... | collective-permute-start | bytes 786440 | tf_op jit(solution)/shard_map/ppermute | solution.py:20
  171.4 13.0 %collective-permute-start.10 = (f32[128,512]{0,1:T(8,128)S(1)}, f32[128,512]{0,1:T(8,128)}, u32[]{:S(2)}, u32[]{:S(2)}) collective-permute-start(f32[128,512]{0,1:T(8,128)S(1)} %get-tuple-element.34), channel_id=1, source_target_pairs={{0,1},{2,3},{4,5},{6,7},{8,9},{10,11},{12,13},{14,15},{16,17},{18,... | collective-permute-start | bytes 786440 | tf_op jit(solution)/shard_map/ppermute | solution.py:20
  176.5 9.7 %collective-permute-start.11 = (f32[128,512]{0,1:T(8,128)S(1)}, f32[128,512]{0,1:T(8,128)S(1)}, u32[]{:S(2)}, u32[]{:S(2)}) collective-permute-start(f32[128,512]{0,1:T(8,128)S(1)} %get-tuple-element.33), channel_id=1, source_target_pairs={{1,0},{3,2},{5,4},{7,6},{9,8},{11,10},{13,12},{15,14},{17,16},{19,... | collective-permute-start | bytes 786440 | tf_op jit(solution)/shard_map/ppermute | solution.py:20
  237.2 3.3 %copy-start.7 = (f32[512]{0:T(512)}, f32[512]{0:T(512)S(1)}, u32[]{:S(2)}) copy-start(f32[512]{0:T(512)S(1)} %get-tuple-element.29) | copy-start | bytes 6148
  (1 other events, 1.1 us)
where the time goes:
time: 245 us; the launch traced here: 243 us
  blocking collectives  78 us (32%)
  local copies, waits for them, and re-layouts  44.4 us (18%)
  starting transfers between devices  43.1 us (18%)
  waiting for transfers between devices  30.4 us (12%)
  matrix products  27.9 us (11%)
  other arithmetic  18.9 us (8%)
    psum x1, blocking collectives, shards(): lax.psum((jnp.sum(direction * applied, axis=0), jnp.sum(residual_live * r...  39.4 us
    psum x1, blocking collectives, shards(): lax.psum(jnp.sum(residual_live * precond, axis=0), ('blk', 'lat', 'depth'))  38.6 us
    unnamed x34, local copies, waits for them, and re-layouts  27.3 us
    dot_general x6, matrix products, product(): jnp.dot(left, right, precision=exact_mode, preferred_element_type=jnp.flo...  21.4 us
    all_to_all x1, waiting for transfers between devices, coarse_level(): lax.all_to_all(outgoing, ('blk', 'lat'), split_axis=0, concat_axis=0, til...  17.9 us
    ppermute x8, starting transfers between devices, passed_along(): return lax.ppermute(block, axis, route)  15.8 us
    all_to_all x1, waiting for transfers between devices, coarse_level(): lax.all_to_all(answers.reshape(owners, CAP, col_count), ('blk', 'lat'), s...  8.42 us
    all_to_all x1, starting transfers between devices, coarse_level(): lax.all_to_all(outgoing_rows, ('blk', 'lat'), split_axis=0, concat_axis=0...  8.31 us
  transfers between devices with their start and end apart: 15, of which 4 were waited for; matrix products, arithmetic and copies ran while one was open for 17% of the time, Pallas kernels for 0%

commit v1 on v0

v1 whole, which is shorter than its diff:
```python
import functools

import jax
import jax.numpy as jnp
from jax import lax
from jax.experimental import pallas as pl
from jax.experimental.pallas import tpu as pltpu
from jax.sharding import PartitionSpec as P

CAP = 24
AXES = ("blk", "lat", "depth")
LAYER = ("blk", "lat")
LANES = 128
f32 = jnp.float32
bf16 = jnp.bfloat16

VMEM = pl.BlockSpec(memory_space=pltpu.VMEM)
SMEM = pl.BlockSpec(memory_space=pltpu.SMEM)


def shape_of(*dims, dtype=f32):
    return jax.ShapeDtypeStruct(dims, dtype)


def call(body, out_shape, operands, smem=(), flops=0, moved=0, scratch=()):
    in_specs = [SMEM if i in smem else VMEM for i in range(len(operands))]
    outs = list(out_shape)
    return pl.pallas_call(
        body,
        out_shape=outs,
        in_specs=in_specs,
        out_specs=[VMEM] * len(outs),
        scratch_shapes=list(scratch),
        compiler_params=pltpu.CompilerParams(vmem_limit_bytes=32 << 20),
        cost_estimate=pl.CostEstimate(flops=flops, bytes_accessed=moved, transcendentals=0),
    )(*operands)


def parts(x):
    high = x.astype(bf16)
    low = (x - high.astype(f32)).astype(bf16)
    return high, low


def mul(a, b, dims):
    return lax.dot_general(a, b, (dims, ((), ())), preferred_element_type=f32)


PLAIN = ((1,), (0,))
LEFT_T = ((0,), (0,))


def product(a, b, dims=PLAIN):
    ah, al = parts(a)
    bh, bl = parts(b)
    return mul(ah, bh, dims) + (mul(ah, bl, dims) + mul(al, bh, dims))


def select(table, x, dims=PLAIN):
    high, low = parts(x)
    return mul(table, high, dims) + mul(table, low, dims)


def live_rows(len_ref, face, rows):
    return lax.broadcasted_iota(jnp.int32, (rows, 1), 0) < len_ref[face]


def masked(len_ref, ref, face, rows):
    block = ref[face * rows : (face + 1) * rows, :]
    return jnp.where(live_rows(len_ref, face, rows), block, 0.0)


def spread(out_ref, vector):
    for j in range(out_ref.shape[1]):
        piece = vector[:, j * LANES : (j + 1) * LANES]
        out_ref[:, j, :] = jnp.broadcast_to(piece, (out_ref.shape[0], LANES))


def gathered_sum(ref):
    total = jnp.sum(ref[...], axis=0)
    return jnp.concatenate([total[j : j + 1, :] for j in range(total.shape[0])], axis=1)


def one_hot(hit):
    return jnp.where(hit, 1.0, 0.0).astype(bf16)


def pack_kernel(len_ref, residual_ref, basis_ref, owner_ref, out_ref, table_ref):
    rows = residual_ref.shape[0] // 6
    primal = basis_ref.shape[1]
    slots = out_ref.shape[0]
    weighted = jnp.concatenate(
        [0.5 * masked(len_ref, residual_ref, face, rows) for face in range(6)], axis=0
    )
    terms = product(basis_ref[...], weighted, LEFT_T)
    row_at = lax.broadcasted_iota(jnp.int32, (primal, primal), 0)
    col_at = lax.broadcasted_iota(jnp.int32, (primal, primal), 1)
    own_row = owner_ref[...].astype(f32)
    own_col = jnp.sum(jnp.where(row_at == col_at, own_row, 0.0), axis=1, keepdims=True)
    same = own_row == own_col
    rank_row = jnp.sum(jnp.where(same & (row_at < col_at), 1.0, 0.0), axis=0, keepdims=True)
    rank_col = jnp.sum(jnp.where(same & (col_at < row_at), 1.0, 0.0), axis=1, keepdims=True)
    slot_row = (own_row * CAP + rank_row).astype(jnp.int32)
    slot_col = (own_col * CAP + rank_col).astype(jnp.int32)
    packer = one_hot(lax.broadcasted_iota(jnp.int32, (slots, primal), 0) == slot_row)
    table_ref[...] = one_hot(lax.broadcasted_iota(jnp.int32, (primal, slots), 1) == slot_col)
    out_ref[...] = select(packer, terms)


def neumann_kernel(len_ref, residual_ref, matrix_ref, local_ref, part_ref):
    rows = residual_ref.shape[0] // 6
    live = jnp.concatenate(
        [masked(len_ref, residual_ref, face, rows) for face in range(6)], axis=0
    )
    local = product(matrix_ref[...], 0.5 * live)
    local_ref[...] = local
    part_ref[...] = jnp.sum(live * local, axis=0, keepdims=True)


def table_kernel(owner_ref, row_ref, picker_ref):
    owners, primal = owner_ref.shape
    owned = picker_ref.shape[1]
    me = lax.axis_index(LAYER)
    mine = jnp.where(owner_ref[...] == me, 1.0, 0.0)
    row_at = lax.broadcasted_iota(jnp.int32, (primal, primal), 0)
    col_at = lax.broadcasted_iota(jnp.int32, (primal, primal), 1)
    rank = mul(mine.astype(bf16), one_hot(row_at < col_at), PLAIN)
    rank = jnp.where(mine > 0.0, rank, -1.0).astype(jnp.int32)
    wanted = row_ref[...].astype(f32) + 1.0
    slot_at = lax.broadcasted_iota(jnp.int32, (CAP, primal), 0)
    out_at = lax.broadcasted_iota(jnp.int32, (CAP, owned), 1).astype(f32)
    for source in range(owners):
        hit = slot_at == rank[source : source + 1, :]
        named = jnp.sum(jnp.where(hit, wanted[source : source + 1, :], 0.0), axis=1, keepdims=True)
        picker_ref[source * CAP : (source + 1) * CAP, :] = jnp.where(
            out_at == named - 1.0, 1.0, 0.0
        )


def solve_kernel(incoming_ref, picker_ref, inverse_ref, part_ref, answer_ref, spread_ref):
    picker = picker_ref[...].astype(bf16)
    summed = select(picker, incoming_ref[...], LEFT_T)
    solved = product(inverse_ref[...], summed)
    answer_ref[...] = select(picker, solved)
    spread(spread_ref, part_ref[...] + 2.0 * jnp.sum(summed * solved, axis=0, keepdims=True))


def put_faces(image, rows, pair_depth, face_refs):
    for face in range(4):
        face_refs[face][...] = image[face * rows : (face + 1) * rows, :]
    minus, plus = image[4 * rows : 5 * rows, :], image[5 * rows :, :]
    if pair_depth:
        face_refs[4][...] = jnp.where(lax.axis_index("depth") == 0, plus, minus)
    else:
        face_refs[4][...] = minus
        face_refs[5][...] = plus


def got_face(refs, face, pair_depth):
    if face < 4 or not pair_depth:
        return refs[face][...]
    there = 1 if face == 4 else 0
    return jnp.where(lax.axis_index("depth") == there, refs[4][...], 0.0)


def image_kernel(pair_depth, returned_ref, table_ref, basis_ref, local_ref, image_ref, *face_refs):
    rows = local_ref.shape[0] // 6
    correction = select(table_ref[...], returned_ref[...])
    image = local_ref[...] + product(basis_ref[...], correction)
    image_ref[...] = image
    put_faces(image, rows, pair_depth, face_refs)


def direction_kernel(pair_depth, faces, scale, len_ref, rho_ref, prev_rho_ref, image_ref, prev_ref, schur_ref, *refs):
    got, (direction_ref, spread_ref, rho_out, schur_out), face_refs = (
        refs[:faces],
        refs[faces : faces + 4],
        refs[faces + 4 :],
    )
    rows = image_ref.shape[0] // 6
    rho = scale * gathered_sum(rho_ref)
    rho_out[...] = rho
    beta = rho / prev_rho_ref[...]
    for face in range(6):
        at = slice(face * rows, (face + 1) * rows)
        precond = 0.5 * (image_ref[at, :] + got_face(got, face, pair_depth))
        direction_ref[at, :] = jnp.where(
            live_rows(len_ref, face, rows), precond + beta * prev_ref[at, :], 0.0
        )
    direction = direction_ref[...]
    image = product(schur_ref[...], direction)
    schur_out[...] = image
    put_faces(image, rows, pair_depth, face_refs)
    spread(spread_ref, 2.0 * jnp.sum(direction * image, axis=0, keepdims=True))


def residual_kernel(pair_depth, faces, scale, len_ref, rho_ref, curve_ref, schur_ref, residual_ref, *refs):
    got, (new_ref, spread_ref, alpha_ref) = refs[:faces], refs[faces:]
    rows = schur_ref.shape[0] // 6
    alpha = rho_ref[...] / (scale * gathered_sum(curve_ref))
    alpha_ref[...] = alpha
    total = jnp.zeros(alpha.shape, f32)
    for face in range(6):
        at = slice(face * rows, (face + 1) * rows)
        applied = schur_ref[at, :] + got_face(got, face, pair_depth)
        new = jnp.where(live_rows(len_ref, face, rows), residual_ref[at, :] - alpha * applied, 0.0)
        new_ref[at, :] = new
        total += jnp.sum(new * new, axis=0, keepdims=True)
    spread(spread_ref, total)


def norm_kernel(scale, part_ref, norm_ref):
    norm_ref[...] = scale * gathered_sum(part_ref)


def around(x, axis, by):
    devices = lax.axis_size(axis)
    return lax.ppermute(x, axis, [(i, (i + by) % devices) for i in range(devices)])


def along(x, axis, by):
    devices = range(lax.axis_size(axis))
    return lax.ppermute(x, axis, [(i - by, i) for i in devices if i - by in devices])


def exchange(faces, pair_depth):
    got = [
        around(faces[1], "blk", 1),
        around(faces[0], "blk", -1),
        along(faces[3], "lat", 1),
        along(faces[2], "lat", -1),
    ]
    if pair_depth:
        got.append(lax.ppermute(faces[4], "depth", [(0, 1), (1, 0)]))
    else:
        got += [along(faces[5], "depth", 1), along(faces[4], "depth", -1)]
    return got


def to_all(x):
    return lax.all_to_all(x, AXES, split_axis=0, concat_axis=0, tiled=True)


def shards(
    face_len,
    residual,
    prev_direction,
    prev_rho,
    schur,
    neumann,
    coarse_basis,
    coarse_inverse,
    prim_owner,
    coarse_row,
):
    height, width = residual.shape[3:]
    rows = height // 6
    primal = coarse_basis.shape[4]
    owned = coarse_inverse.shape[3]
    owners = lax.axis_size(LAYER)
    slots = owners * CAP
    devices = lax.axis_size(AXES)
    pair_depth = lax.axis_size("depth") == 2
    faces = 5 if pair_depth else 6
    scale = 0.5 / (devices * height)

    lengths = face_len.reshape(6)
    residual = residual.reshape(height, width)
    prev_direction = prev_direction.reshape(height, width)
    schur = schur.reshape(height, height)
    neumann = neumann.reshape(height, height)
    basis = coarse_basis.reshape(height, primal)
    inverse = coarse_inverse.reshape(owned, owned)
    owner = prim_owner.reshape(1, primal)
    wanted = coarse_row.reshape(1, primal)
    whole = shape_of(height, width)
    row = shape_of(1, width)
    face = shape_of(rows, width)
    copies = shape_of(devices, width // LANES, LANES)

    outgoing, table = call(
        pack_kernel,
        [shape_of(slots, width), shape_of(primal, slots, dtype=bf16)],
        [lengths, residual, basis, owner],
        smem=(0,),
        flops=6 * height * primal * width,
        moved=4 * (height * (width + primal) + slots * width),
    )
    all_owner = lax.all_gather(owner, LAYER, axis=0, tiled=True)
    all_row = lax.all_gather(wanted, LAYER, axis=0, tiled=True)
    incoming = lax.all_to_all(
        outgoing.reshape(owners, CAP, width), LAYER, split_axis=0, concat_axis=0, tiled=True
    )
    local, local_part = call(
        neumann_kernel,
        [whole, row],
        [lengths, residual, neumann],
        smem=(0,),
        flops=6 * height * height * width,
        moved=4 * height * (height + 2 * width),
    )
    (picker,) = call(
        table_kernel,
        [shape_of(slots, owned)],
        [all_owner, all_row],
        flops=2 * owners * primal * primal,
        moved=4 * slots * owned,
    )
    answers, rho_parts = call(
        solve_kernel,
        [shape_of(slots, width), copies],
        [incoming.reshape(slots, width), picker, inverse, local_part],
        flops=(8 * slots + 6 * owned) * owned * width,
        moved=8 * slots * width,
    )
    returned = lax.all_to_all(
        answers.reshape(owners, CAP, width), LAYER, split_axis=0, concat_axis=0, tiled=True
    )
    rho_parts = to_all(rho_parts)
    image, *outward = call(
        functools.partial(image_kernel, pair_depth),
        [whole] + [face] * faces,
        [returned.reshape(slots, width), table, basis, local],
        flops=(6 * height + 4 * slots) * primal * width,
        moved=16 * height * width,
    )
    got = exchange(outward, pair_depth)
    direction, curve_parts, rho, schur_image, *outward = call(
        functools.partial(direction_kernel, pair_depth, faces, scale),
        [whole, copies, row, whole] + [face] * faces,
        [lengths, rho_parts, prev_rho.reshape(1, width), image, prev_direction, schur, *got],
        smem=(0,),
        flops=6 * height * height * width,
        moved=4 * height * (height + 6 * width),
    )
    got = exchange(outward, pair_depth)
    curve_parts = to_all(curve_parts)
    new_residual, norm_parts, alpha = call(
        functools.partial(residual_kernel, pair_depth, faces, scale),
        [whole, copies, row],
        [lengths, rho, curve_parts, schur_image, residual, *got],
        smem=(0,),
        flops=6 * height * width,
        moved=16 * height * width,
    )
    (norm,) = call(
        functools.partial(norm_kernel, scale),
        [row],
        [to_all(norm_parts)],
        moved=4 * devices * width,
    )
    out_shape = (1, 1, 1, height, width)
    return (
        new_residual.reshape(out_shape),
        direction.reshape(out_shape),
        rho.reshape(width),
        alpha.reshape(width),
        norm.reshape(width),
    )


def solution(mesh):
    tall = P("blk", "lat", "depth", None, None)
    flat = P("blk", "lat", "depth", None)
    in_specs = (flat, tall, tall, P(), tall, tall, tall, tall, tall, flat)
    out_specs = (tall, tall, P(), P(), P())
    return jax.shard_map(shards, mesh=mesh, in_specs=in_specs, out_specs=out_specs, check_vma=False)
```

time: 245 us -> 185 us (0.76)
  blocking collectives: 78 us -> 136 us
  local copies, waits for them, and re-layouts: 44.4 us -> 7.87 us
  waiting for transfers between devices: 30.4 us -> 0.03 us
  matrix products: 27.9 us -> 0 us
  other arithmetic: 18.9 us -> 0 us
  starting transfers between devices: 43.1 us -> 24.4 us
  Pallas kernels: 0 us -> 15.7 us
    all_gather x0 -> x2, blocking collectives: none -> 83.8 us  [the longest x1 46.5 us: shards(): all_row = lax.all_gather(wanted, LAYER, axis=0, tiled=True)]
    psum x2 -> x0, blocking collectives: 78 us -> none  [the longest x1 39.4 us: shards(): lax.psum((jnp.sum(direction * applied, axis=0), jnp.sum(residual_live * r...]
    all_to_all x0 -> x4, blocking collectives: none -> 51.9 us  [the longest x3 32.8 us: to_all(): return lax.all_to_all(x, AXES, split_axis=0, concat_axis=0, tiled=True)]
    dot_general x9 -> x0, matrix products: 27.9 us -> none  [the longest x6 21.4 us: product(): jnp.dot(left, right, precision=exact_mode, preferred_element_type=jnp.flo...]
    all_to_all x3 -> x1, waiting for transfers between devices: 27 us -> 0.01 us  [shards(): lax.all_to_all(outgoing.reshape(owners, CAP, width), LAYER, split_axis=0,...]
    unnamed x34 -> x36, local copies, waits for them, and re-layouts: 27.3 us -> 7.87 us
    pallas_call x0 -> x8, Pallas kernels: none -> 15.7 us  [call(): pl.pallas_call(body, out_shape=outs, in_specs=in_specs, out_specs=[VMEM]...]
    all_to_all x3 -> x1, starting transfers between devices: 19.6 us -> 8.49 us  [shards(): lax.all_to_all(outgoing.reshape(owners, CAP, width), LAYER, split_axis=0,...]
  transfers between devices with their start and end apart: 15 -> 11, of which waited for: 4 -> 0; matrix products, arithmetic and copies ran while one was open for 17% -> 0% of each run, Pallas kernels for 0% -> 2%
where the time goes in v1:
time: 185 us
  blocking collectives  136 us (74%)
  starting transfers between devices  24.4 us (13%)
  Pallas kernels  15.7 us (8%)
  local copies, waits for them, and re-layouts  7.87 us (4%)
    all_gather x1, blocking collectives, shards(): all_row = lax.all_gather(wanted, LAYER, axis=0, tiled=True)  46.5 us
    all_gather x1, blocking collectives, shards(): all_owner = lax.all_gather(owner, LAYER, axis=0, tiled=True)  37.3 us
    all_to_all x3, blocking collectives, to_all(): return lax.all_to_all(x, AXES, split_axis=0, concat_axis=0, tiled=True)  32.8 us
    all_to_all x1, blocking collectives, shards(): lax.all_to_all(answers.reshape(owners, CAP, width), LAYER, split_axis=0,...  19.1 us
    pallas_call x8, Pallas kernels, call(): pl.pallas_call(body, out_shape=outs, in_specs=in_specs, out_specs=[VMEM]...  15.7 us
    all_to_all x1, starting transfers between devices, shards(): lax.all_to_all(outgoing.reshape(owners, CAP, width), LAYER, split_axis=0,...  8.49 us
    ppermute x4, starting transfers between devices, along(): lax.ppermute(x, axis, [(i - by, i) for i in devices if i - by in devices])  8.07 us
    unnamed x36, local copies, waits for them, and re-layouts  7.87 us
  transfers between devices with their start and end apart: 11, of which 0 were waited for; matrix products, arithmetic and copies ran while one was open for 0% of the time, Pallas kernels for 2%

profile of v1, /device:TPU:0, one launch (start us, length us, event | category | flops | bytes accessed | tf_op | source)
XLA Modules:
  0.0 184.6 jit_solution(6061119834931748483)
XLA Ops:
  0.6 1.4 copy-done
  2.0 1.1 copy-done.2
  4.5 2.6 %shard_map.137 = (f32[384,512]{1,0:T(8,128)}, bf16[256,384]{1,0:T(8,128)(2,1)S(1)}) custom-call(s32[6]{0:T(128)S(1)} %bitcast.35, f32[768,512]{1,0:T(8,128)S(1)} %bitcast.24, f32[768,256]{1,0:T(8,128)S(1)} %bitcast.28, s32[1,256]{1,0:T(1,128)S(1)} %bitcast.39), custom_call_target="tpu_custom_call" | custom-call | flops 603979776 | bytes 3145728 | tf_op jit(solution)/shard_map/pallas_call | solution.py:28
  7.8 8.5 %all-to-all-start = ((f32[16,24,512]{2,1,0:T(8,128)}), f32[16,24,512]{2,1,0:T(8,128)}, u32[]{:S(2)}, u32[]{:S(2)}) async-start(f32[16,24,512]{2,1,0:T(8,128)} %bitcast.4), calls=%async_computation | async-start | bytes 1572864 | tf_op jit(solution)/shard_map/all_to_all | solution.py:291
  16.3 46.5 %all-gather.1 = s32[16,1,1,256]{3,2,1,0:T(1,128)S(1)} all-gather(s32[1,1,1,256]{3,2,1,0:T(1,128)S(1)} %copy-done.16), channel_id=3, replica_groups=mesh['blk'=4,'lat'=4,'depth'=2] {'blk','lat'}, dimensions={0}, use_global_device_ids=true | all-gather | bytes 17408 | tf_op jit(solution)/shard_map/all_gather | solution.py:290
  62.9 37.3 %all-gather = s32[16,1,1,256,1]{3,4,2,1,0:T(1,128)S(1)} all-gather(s32[1,1,1,256,1]{3,4,2,1,0:T(1,128)S(1)} %copy-done.11), channel_id=2, replica_groups=mesh['blk'=4,'lat'=4,'depth'=2] {'blk','lat'}, dimensions={0}, use_global_device_ids=true | all-gather | bytes 17408 | tf_op jit(solution)/shard_map/all_gather | solution.py:289
  100.5 1.7 copy-done.14
  102.1 2.6 %shard_map.139 = (f32[768,512]{1,0:T(8,128)S(1)}, f32[1,512]{1,0:T(1,128)S(1)}) custom-call(s32[6]{0:T(128)S(1)} %bitcast.36, f32[768,512]{1,0:T(8,128)S(1)} %bitcast.25, f32[768,768]{1,0:T(8,128)S(1)} %bitcast.42), custom_call_target="tpu_custom_call" | custom-call | flops 1811939328 | bytes 5505024 | tf_op jit(solution)/shard_map/pallas_call | solution.py:28
  104.8 0.9 copy-done.15
  105.7 2.4 %shard_map.140 = (f32[384,512]{1,0:T(8,128)S(1)}, f32[32,4,128]{2,1,0:T(4,128)S(1)}) custom-call(f32[384,512]{1,0:T(8,128)} %bitcast.5.incoming_ref, f32[384,256]{1,0:T(8,128)S(1)} %shard_map.138.picker_ref, f32[256,256]{1,0:T(8,128)S(1)} %bitcast.43, f32[1,512]{1,0:T(1,128)S(1)} %get-tuple-element.30.part_ref), custom_call_target="tpu_custom_call" | custom-call | flops 603979776 | bytes 1572864 | tf_op jit(solution)/shard_map/pallas_call | solution.py:28
  108.1 19.1 %all_to_all.25 = f32[16,24,512]{2,1,0:T(8,128)S(1)} all-to-all(f32[16,24,512]{2,1,0:T(8,128)S(1)} %bitcast.32), channel_id=1, replica_groups=mesh['blk'=4,'lat'=4,'depth'=2] {'blk','lat'}, dimensions={0} | all-to-all | bytes 1572864 | tf_op jit(solution)/shard_map/all_to_all | solution.py:316
  127.2 1.2 shard_map.141
  128.5 1.0 collective-permute-start
  129.4 2.9 %collective-permute-start.1 = (f32[128,512]{1,0:T(8,128)S(1)}, f32[128,512]{1,0:T(8,128)S(1)}, u32[]{:S(2)}, u32[]{:S(2)}) collective-permute-start(f32[128,512]{1,0:T(8,128)S(1)} %get-tuple-element.37), channel_id=1, source_target_pairs={{0,24},{8,0},{16,8},{24,16},{1,25},{9,1},{17,9},{25,17},{2,26},{10... | collective-permute-start | bytes 786440 | tf_op jit(solution)/shard_map/ppermute | solution.py:218
  132.3 3.1 %collective-permute-start.2 = (f32[128,512]{1,0:T(8,128)S(1)}, f32[128,512]{1,0:T(8,128)S(1)}, u32[]{:S(2)}, u32[]{:S(2)}) collective-permute-start(f32[128,512]{1,0:T(8,128)S(1)} %get-tuple-element.38), channel_id=1, source_target_pairs={{0,2},{2,4},{4,6},{1,3},{3,5},{5,7},{8,10},{10,12},{12,14},{9,11},... | collective-permute-start | bytes 786440 | tf_op jit(solution)/shard_map/ppermute | solution.py:223
  135.5 1.3 collective-permute-start.3
  136.9 11.6 %all_to_all.26.rho_ref = f32[32,4,128]{2,1,0:T(4,128)S(1)} all-to-all(f32[32,4,128]{2,1,0:T(4,128)S(1)} %get-tuple-element.31), channel_id=1, replica_groups=mesh['blk'=4,'lat'=4,'depth'=2] {'blk','lat','depth'}, dimensions={0} | all-to-all | bytes 131072 | tf_op jit(solution)/shard_map/all_to_all | solution.py:241
  148.5 3.8 %shard_map.142 = (f32[768,512]{1,0:T(8,128)}, f32[32,4,128]{2,1,0:T(4,128)S(1)}, f32[1,512]{1,0:T(1,128)}, f32[768,512]{1,0:T(8,128)S(1)}, f32[128,512]{1,0:T(8,...) custom-call(s32[6]{0:T(128)S(1)} %bitcast.37, ...), custom_call_target="tpu_custom_call" | custom-call | flops 1811939328 | bytes 11796480 | tf_op jit(solution)/shard_map/pallas_call | solution.py:28
  153.0 3.2 %collective-permute-start.6 = (f32[128,512]{1,0:T(8,128)S(1)}, f32[128,512]{1,0:T(8,128)S(1)}, u32[]{:S(2)}, u32[]{:S(2)}) collective-permute-start(f32[128,512]{1,0:T(8,128)S(1)} %get-tuple-element.45), channel_id=1, source_target_pairs={{0,24},{8,0},{16,8},{24,16},{1,25},{9,1},{17,9},{25,17},{2,26},{10... | collective-permute-start | bytes 786440 | tf_op jit(solution)/shard_map/ppermute | solution.py:218
  156.2 2.3 %collective-permute-start.7 = (f32[128,512]{1,0:T(8,128)S(1)}, f32[128,512]{1,0:T(8,128)S(1)}, u32[]{:S(2)}, u32[]{:S(2)}) collective-permute-start(f32[128,512]{1,0:T(8,128)S(1)} %get-tuple-element.46), channel_id=1, source_target_pairs={{0,2},{2,4},{4,6},{1,3},{3,5},{5,7},{8,10},{10,12},{12,14},{9,11},... | collective-permute-start | bytes 786440 | tf_op jit(solution)/shard_map/ppermute | solution.py:223
  158.5 1.3 collective-permute-start.8
  159.9 12.1 %all_to_all.27.curve_ref = f32[32,4,128]{2,1,0:T(4,128)S(1)} all-to-all(f32[32,4,128]{2,1,0:T(4,128)S(1)} %get-tuple-element.42), channel_id=1, replica_groups=mesh['blk'=4,'lat'=4,'depth'=2] {'blk','lat','depth'}, dimensions={0} | all-to-all | bytes 131072 | tf_op jit(solution)/shard_map/all_to_all | solution.py:241
  172.8 2.1 %shard_map.143 = (f32[768,512]{1,0:T(8,128)}, f32[32,4,128]{2,1,0:T(4,128)S(1)}, f32[1,512]{1,0:T(1,128)}) custom-call(s32[6]{0:T(128)S(1)} %bitcast.38, f32[1,512]{1,0:T(1,128)S(1)} %copy-done.13, f32[32,4,128]{2,1,0:T(4,128)S(1)} %all_to_all.27.curve_ref, f32[768,512]{1,0:T(8,128)S(1)} %get-tuple-element.43.schur_ref, f32[768,512]{1,0:T(8,128)S(1)} %bitcast.26, ...), custom_call_target="tpu_custom_call" | custom-call | flops 2359296 | bytes 6291456 | tf_op jit(solution)/shard_map/pallas_call | solution.py:28
  174.9 9.1 %all_to_all.28.part_ref = f32[32,4,128]{2,1,0:T(4,128)S(1)} all-to-all(f32[32,4,128]{2,1,0:T(4,128)S(1)} %get-tuple-element.52), channel_id=1, replica_groups=mesh['blk'=4,'lat'=4,'depth'=2] {'blk','lat','depth'}, dimensions={0} | all-to-all | bytes 131072 | tf_op jit(solution)/shard_map/all_to_all | solution.py:241
  (48 shorter events, 4.4 us)
Async XLA Ops:
  0.6 1.4 copy-start
  2.0 1.1 copy-start.2
  4.5 11.8 %copy-start.16 = (s32[1,1,1,256]{3,2,1,0:T(1,128)S(1)}, s32[1,1,1,256]{3,2,1,0:T(1,128)}, u32[]{:S(2)}) copy-start(s32[1,1,1,256]{3,2,1,0:T(1,128)} %param.19) | copy-start | bytes 3076
  4.5 58.3 %copy-start.11 = (s32[1,1,1,256,1]{3,4,2,1,0:T(1,128)S(1)}, s32[1,1,1,256,1]{3,4,2,1,0:T(1,128)}, u32[]{:S(2)}) copy-start(s32[1,1,1,256,1]{3,4,2,1,0:T(1,128)} %param.18) | copy-start | bytes 3076
  7.8 92.6 %copy-start.1 = (f32[1,1,1,768,512]{4,3,2,1,0:T(8,128)S(1)}, f32[1,1,1,768,512]{4,3,2,1,0:T(8,128)}, u32[]{:S(2)}) copy-start(f32[1,1,1,768,512]{4,3,2,1,0:T(8,128)} %param.11) | copy-start | bytes 4718596
  7.8 92.6 %copy-start.9 = (s32[1,1,1,6]{3,2,1,0:T(1,128)S(1)}, s32[1,1,1,6]{3,2,1,0:T(1,128)}, u32[]{:S(2)}) copy-start(s32[1,1,1,6]{3,2,1,0:T(1,128)} %param.10) | copy-start | bytes 76
  7.8 96.9 %all-to-all-start = ((f32[16,24,512]{2,1,0:T(8,128)}), f32[16,24,512]{2,1,0:T(8,128)}, u32[]{:S(2)}, u32[]{:S(2)}) async-start(f32[16,24,512]{2,1,0:T(8,128)} %bitcast.4), calls=%async_computation | async-start | bytes 1572864 | tf_op jit(solution)/shard_map/all_to_all | solution.py:291
  100.5 1.7 copy-start.14
  104.7 1.0 copy-start.15
  105.7 21.5 %copy-start.3 = (f32[1,1,1,768,256]{4,3,2,1,0:T(8,128)S(1)}, f32[1,1,1,768,256]{4,3,2,1,0:T(8,128)}, u32[]{:S(2)}) copy-start(f32[1,1,1,768,256]{4,3,2,1,0:T(8,128)} %param.16) | copy-start | bytes 2359300
  105.7 21.5 %copy-start.7 = (bf16[256,384]{1,0:T(8,128)(2,1)S(1)}, bf16[256,384]{1,0:T(8,128)(2,1)}, u32[]{:S(2)}) copy-start(bf16[256,384]{1,0:T(8,128)(2,1)} %copy-done.6) | copy-start | bytes 589828
  108.1 40.4 %copy-start.5 = (f32[1,1,1,768,512]{4,3,2,1,0:T(8,128)S(1)}, f32[1,1,1,768,512]{4,3,2,1,0:T(8,128)}, u32[]{:S(2)}) copy-start(f32[1,1,1,768,512]{4,3,2,1,0:T(8,128)} %param.12) | copy-start | bytes 4718596
  127.2 21.3 %copy-start.4 = (f32[1,1,1,768,768]{4,3,2,1,0:T(8,128)S(1)}, f32[1,1,1,768,768]{4,3,2,1,0:T(8,128)}, u32[]{:S(2)}) copy-start(f32[1,1,1,768,768]{4,3,2,1,0:T(8,128)} %param.14) | copy-start | bytes 7077892
  127.2 21.3 %copy-start.12 = (f32[512]{0:T(512)S(1)}, f32[512]{0:T(512)}, u32[]{:S(2)}) copy-start(f32[512]{0:T(512)} %param.13) | copy-start | bytes 6148
  128.5 20.0 %collective-permute-start = (f32[128,512]{1,0:T(8,128)S(1)}, f32[128,512]{1,0:T(8,128)S(1)}, u32[]{:S(2)}, u32[]{:S(2)}) collective-permute-start(f32[128,512]{1,0:T(8,128)S(1)} %get-tuple-element.36), channel_id=1, source_target_pairs={{0,8},{8,16},{16,24},{24,0},{1,9},{9,17},{17,25},{25,1},{2,10},{10... | collective-permute-start | bytes 786440 | tf_op jit(solution)/shard_map/ppermute | solution.py:218
  129.4 19.1 %collective-permute-start.1 = (f32[128,512]{1,0:T(8,128)S(1)}, f32[128,512]{1,0:T(8,128)S(1)}, u32[]{:S(2)}, u32[]{:S(2)}) collective-permute-start(f32[128,512]{1,0:T(8,128)S(1)} %get-tuple-element.37), channel_id=1, source_target_pairs={{0,24},{8,0},{16,8},{24,16},{1,25},{9,1},{17,9},{25,17},{2,26},{10... | collective-permute-start | bytes 786440 | tf_op jit(solution)/shard_map/ppermute | solution.py:218
  132.3 16.2 %collective-permute-start.2 = (f32[128,512]{1,0:T(8,128)S(1)}, f32[128,512]{1,0:T(8,128)S(1)}, u32[]{:S(2)}, u32[]{:S(2)}) collective-permute-start(f32[128,512]{1,0:T(8,128)S(1)} %get-tuple-element.38), channel_id=1, source_target_pairs={{0,2},{2,4},{4,6},{1,3},{3,5},{5,7},{8,10},{10,12},{12,14},{9,11},... | collective-permute-start | bytes 786440 | tf_op jit(solution)/shard_map/ppermute | solution.py:223
  135.5 13.0 %collective-permute-start.3 = (f32[128,512]{1,0:T(8,128)S(1)}, f32[128,512]{1,0:T(8,128)S(1)}, u32[]{:S(2)}, u32[]{:S(2)}) collective-permute-start(f32[128,512]{1,0:T(8,128)S(1)} %get-tuple-element.39), channel_id=1, source_target_pairs={{2,0},{4,2},{6,4},{3,1},{5,3},{7,5},{10,8},{12,10},{14,12},{11,9},... | collective-permute-start | bytes 786440 | tf_op jit(solution)/shard_map/ppermute | solution.py:223
  136.8 11.7 %collective-permute-start.4 = (f32[128,512]{1,0:T(8,128)S(1)}, f32[128,512]{1,0:T(8,128)S(1)}, u32[]{:S(2)}, u32[]{:S(2)}) collective-permute-start(f32[128,512]{1,0:T(8,128)S(1)} %get-tuple-element.40), channel_id=1, source_target_pairs={{0,1},{1,0},{2,3},{3,2},{4,5},{5,4},{6,7},{7,6},{8,9},{9,8},{10,11... | collective-permute-start | bytes 786440 | tf_op jit(solution)/shard_map/ppermute | solution.py:234
  152.4 19.7 %collective-permute-start.5 = (f32[128,512]{1,0:T(8,128)S(1)}, f32[128,512]{1,0:T(8,128)S(1)}, u32[]{:S(2)}, u32[]{:S(2)}) collective-permute-start(f32[128,512]{1,0:T(8,128)S(1)} %get-tuple-element.44), channel_id=1, source_target_pairs={{0,8},{8,16},{16,24},{24,0},{1,9},{9,17},{17,25},{25,1},{2,10},{10... | collective-permute-start | bytes 786440 | tf_op jit(solution)/shard_map/ppermute | solution.py:218
  153.0 19.1 %collective-permute-start.6 = (f32[128,512]{1,0:T(8,128)S(1)}, f32[128,512]{1,0:T(8,128)S(1)}, u32[]{:S(2)}, u32[]{:S(2)}) collective-permute-start(f32[128,512]{1,0:T(8,128)S(1)} %get-tuple-element.45), channel_id=1, source_target_pairs={{0,24},{8,0},{16,8},{24,16},{1,25},{9,1},{17,9},{25,17},{2,26},{10... | collective-permute-start | bytes 786440 | tf_op jit(solution)/shard_map/ppermute | solution.py:218
  156.2 15.9 %collective-permute-start.7 = (f32[128,512]{1,0:T(8,128)S(1)}, f32[128,512]{1,0:T(8,128)S(1)}, u32[]{:S(2)}, u32[]{:S(2)}) collective-permute-start(f32[128,512]{1,0:T(8,128)S(1)} %get-tuple-element.46), channel_id=1, source_target_pairs={{0,2},{2,4},{4,6},{1,3},{3,5},{5,7},{8,10},{10,12},{12,14},{9,11},... | collective-permute-start | bytes 786440 | tf_op jit(solution)/shard_map/ppermute | solution.py:223
  158.5 13.5 %collective-permute-start.8 = (f32[128,512]{1,0:T(8,128)S(1)}, f32[128,512]{1,0:T(8,128)S(1)}, u32[]{:S(2)}, u32[]{:S(2)}) collective-permute-start(f32[128,512]{1,0:T(8,128)S(1)} %get-tuple-element.47), channel_id=1, source_target_pairs={{2,0},{4,2},{6,4},{3,1},{5,3},{7,5},{10,8},{12,10},{14,12},{11,9},... | collective-permute-start | bytes 786440 | tf_op jit(solution)/shard_map/ppermute | solution.py:223
  159.8 12.2 %collective-permute-start.9 = (f32[128,512]{1,0:T(8,128)S(1)}, f32[128,512]{1,0:T(8,128)S(1)}, u32[]{:S(2)}, u32[]{:S(2)}) collective-permute-start(f32[128,512]{1,0:T(8,128)S(1)} %get-tuple-element.48), channel_id=1, source_target_pairs={{0,1},{1,0},{2,3},{3,2},{4,5},{5,4},{6,7},{7,6},{8,9},{9,8},{10,11... | collective-permute-start | bytes 786440 | tf_op jit(solution)/shard_map/ppermute | solution.py:234
  (4 other events, 2.7 us)

commit v2 on v1

v2 whole, which is shorter than its diff:
```python
import functools

import jax
import jax.numpy as jnp
from jax import lax
from jax.experimental import pallas as pl
from jax.experimental.pallas import tpu as pltpu
from jax.sharding import PartitionSpec as P

CAP = 24
PARTS = 2
AXES = ("blk", "lat", "depth")
LAYER = ("blk", "lat")
LANES = 128
TILE = 8
f32 = jnp.float32
bf16 = jnp.bfloat16

VMEM = pl.BlockSpec(memory_space=pltpu.VMEM)
SMEM = pl.BlockSpec(memory_space=pltpu.SMEM)
ANY = pl.BlockSpec(memory_space=pl.ANY)


def shape_of(*dims, dtype=f32):
    return jax.ShapeDtypeStruct(dims, dtype)


def call(body, outs, operands, smem=(), far=(), far_out=(), flops=0, moved=0, scratch=(), room=32):
    in_specs = [SMEM if i in smem else ANY if i in far else VMEM for i in range(len(operands))]
    out_specs = [ANY if i in far_out else VMEM for i in range(len(outs))]
    return pl.pallas_call(
        body,
        out_shape=list(outs),
        in_specs=in_specs,
        out_specs=out_specs,
        scratch_shapes=list(scratch),
        compiler_params=pltpu.CompilerParams(vmem_limit_bytes=room << 20),
        cost_estimate=pl.CostEstimate(flops=flops, bytes_accessed=moved, transcendentals=0),
    )(*operands)


def parts(x):
    high = x.astype(bf16)
    low = (x - high.astype(f32)).astype(bf16)
    return high, low


def mul(a, b, dims):
    return lax.dot_general(a, b, (dims, ((), ())), preferred_element_type=f32)


PLAIN = ((1,), (0,))
LEFT_T = ((0,), (0,))


def product(a, b, dims=PLAIN):
    ah, al = parts(a)
    bh, bl = parts(b)
    return mul(ah, bh, dims) + (mul(ah, bl, dims) + mul(al, bh, dims))


def select(table, x, dims=PLAIN):
    high, low = parts(x)
    return mul(table, high, dims) + mul(table, low, dims)


def one_hot(hit):
    return jnp.where(hit, 1.0, 0.0).astype(bf16)


def live_rows(len_ref, face, rows):
    return lax.broadcasted_iota(jnp.int32, (rows, 1), 0) < len_ref[face]


def masked(len_ref, ref, face, rows):
    block = ref[face * rows : (face + 1) * rows, :]
    return jnp.where(live_rows(len_ref, face, rows), block, 0.0)


def folded(vector):
    pieces = vector.shape[1] // LANES
    return [vector[:, j * LANES : (j + 1) * LANES] for j in range(pieces)]


def unfolded(block, first, pieces):
    return jnp.concatenate([block[first + j : first + j + 1, :] for j in range(pieces)], axis=1)


def tiles(rows):
    return -(-rows // TILE) * TILE


def put_slab(out_ref, block):
    owners = out_ref.shape[0]
    for j in range(block.shape[1] // LANES):
        piece = block[:, j * LANES : (j + 1) * LANES]
        out_ref[:, j * CAP : (j + 1) * CAP, :] = piece.reshape(owners, CAP, LANES)


def get_slab(ref, pieces):
    slots = ref.shape[0] * CAP
    return jnp.concatenate(
        [ref[:, j * CAP : (j + 1) * CAP, :].reshape(slots, LANES) for j in range(pieces)], axis=1
    )


def pack_kernel(count, len_any, owner_any, row_any, residual_any, basis_any, *refs):
    slab_refs, table_ref = refs[:count], refs[count]
    len_ref, owner_ref, row_ref, residual_ref, basis_ref, sems, small_sems = refs[count + 1 :]
    rows = residual_ref.shape[0] // 6
    primal = basis_ref.shape[1]
    owners = slab_refs[0].shape[0]
    slots = owners * CAP
    small = [
        pltpu.make_async_copy(src, dst, small_sems.at[i])
        for i, (src, dst) in enumerate(
            [(owner_any, owner_ref), (row_any, row_ref), (len_any, len_ref)]
        )
    ]
    large = []
    for pair in range(3):
        at = pl.ds(2 * pair * rows, 2 * rows)
        large.append(
            (
                pltpu.make_async_copy(residual_any.at[at], residual_ref.at[at], sems.at[pair, 0]),
                pltpu.make_async_copy(basis_any.at[at], basis_ref.at[at], sems.at[pair, 1]),
            )
        )
    for copy in small:
        copy.start()
    for pair in large:
        for copy in pair:
            copy.start()
    for copy in small:
        copy.wait()
    row_at = lax.broadcasted_iota(jnp.int32, (primal, primal), 0)
    col_at = lax.broadcasted_iota(jnp.int32, (primal, primal), 1)
    own_row = owner_ref[...].astype(f32)
    wanted_row = row_ref[...].astype(f32) + 1.0
    own_col = jnp.sum(jnp.where(row_at == col_at, own_row, 0.0), axis=1, keepdims=True)
    wanted_col = jnp.sum(jnp.where(row_at == col_at, wanted_row, 0.0), axis=1, keepdims=True)
    same = own_row == own_col
    rank_row = jnp.sum(jnp.where(same & (row_at < col_at), 1.0, 0.0), axis=0, keepdims=True)
    rank_col = jnp.sum(jnp.where(same & (col_at < row_at), 1.0, 0.0), axis=1, keepdims=True)
    slot_row = (own_row * CAP + rank_row).astype(jnp.int32)
    slot_col = (own_col * CAP + rank_col).astype(jnp.int32)
    packer = one_hot(lax.broadcasted_iota(jnp.int32, (slots, primal), 0) == slot_row)
    table_ref[...] = one_hot(lax.broadcasted_iota(jnp.int32, (primal, slots), 1) == slot_col)
    to_owner = one_hot(
        lax.broadcasted_iota(jnp.int32, (owners, primal), 0) == owner_ref[...]
    )
    lane_at = lax.broadcasted_iota(jnp.int32, (primal, LANES), 1)
    ranked = jnp.where(lane_at == rank_col.astype(jnp.int32), wanted_col, 0.0)
    names = select(to_owner, ranked)
    terms = None
    for pair in range(3):
        for copy in large[pair]:
            copy.wait()
        weighted = jnp.concatenate(
            [0.5 * masked(len_ref, residual_ref, 2 * pair + side, rows) for side in range(2)],
            axis=0,
        )
        term = product(basis_ref[2 * pair * rows : 2 * (pair + 1) * rows, :], weighted, LEFT_T)
        terms = term if terms is None else terms + term
    packed = select(packer, terms)
    width = packed.shape[1] // count
    for i in range(count):
        put_slab(slab_refs[i], packed[:, i * width : (i + 1) * width])
    tail = slab_refs[0].shape[1] - TILE
    slab_refs[0][:, tail:, :] = jnp.broadcast_to(
        names.reshape(owners, 1, LANES), (owners, TILE, LANES)
    )


def neumann_kernel(len_ref, residual_ref, matrix_ref, local_ref, part_ref, square_ref):
    rows = residual_ref.shape[0] // 6
    live = jnp.concatenate(
        [masked(len_ref, residual_ref, face, rows) for face in range(6)], axis=0
    )
    local = product(matrix_ref[...], 0.5 * live)
    local_ref[...] = local
    part_ref[...] = jnp.sum(live * local, axis=0, keepdims=True)
    square_ref[...] = jnp.sum(live * live, axis=0, keepdims=True)


def picker_table(slab_ref, owned):
    owners, height, _ = slab_ref.shape
    lane_at = lax.broadcasted_iota(jnp.int32, (CAP, LANES), 1)
    rank_at = lax.broadcasted_iota(jnp.int32, (CAP, LANES), 0)
    out_at = lax.broadcasted_iota(jnp.int32, (CAP, owned), 1).astype(f32) + 1.0
    blocks = []
    for source in range(owners):
        names = slab_ref[source, height - TILE : height - TILE + 1, :]
        named = jnp.sum(jnp.where(lane_at == rank_at, names, 0.0), axis=1, keepdims=True)
        blocks.append(jnp.where(out_at == named, 1.0, 0.0))
    return jnp.concatenate(blocks, axis=0)


def solve_kernel(index, count, *refs):
    incoming_ref, inverse_ref, refs = refs[0], refs[1], refs[2:]
    owned = inverse_ref.shape[0]
    if index > 0:
        picker_ref, refs = refs[0], refs[1:]
        picker = picker_ref[...]
    else:
        picker = picker_table(incoming_ref, owned)
    before, refs = refs[:index], refs[index:]
    last = index == count - 1
    if last:
        (local_part_ref, square_ref), refs = refs[:2], refs[2:]
    answer_ref, refs = refs[0], refs[1:]
    if index == 0 and not last:
        refs[-1][...] = picker
    table = picker.astype(bf16)
    pieces = (incoming_ref.shape[1] // CAP) if index else (incoming_ref.shape[1] - TILE) // CAP
    summed = select(table, get_slab(incoming_ref, pieces), LEFT_T)
    solved = product(inverse_ref[...], summed)
    put_slab(answer_ref, select(table, solved))
    mine = 2.0 * jnp.sum(summed * solved, axis=0, keepdims=True)
    if not last:
        refs[0][...] = mine
        return
    total = jnp.concatenate([ref[...] for ref in before] + [mine], axis=1) + local_part_ref[...]
    sums = folded(total) + folded(square_ref[...])
    sums += [jnp.zeros((1, LANES), f32)] * (tiles(len(sums)) - len(sums))
    owners = answer_ref.shape[0]
    start = pieces * CAP
    answer_ref[:, start:, :] = jnp.broadcast_to(
        jnp.concatenate(sums, axis=0)[None], (owners, len(sums), LANES)
    )


def put_faces(image, rows, pair_depth, face_refs):
    for face in range(4):
        face_refs[face][...] = image[face * rows : (face + 1) * rows, :]
    minus, plus = image[4 * rows : 5 * rows, :], image[5 * rows :, :]
    if pair_depth:
        face_refs[4][:rows, :] = jnp.where(lax.axis_index("depth") == 0, plus, minus)
    else:
        face_refs[4][...] = minus
        face_refs[5][...] = plus


def got_face(refs, face, rows, pair_depth):
    if face < 4 or not pair_depth:
        return refs[face][...]
    there = 1 if face == 4 else 0
    return jnp.where(lax.axis_index("depth") == there, refs[4][:rows, :], 0.0)


def image_kernel(pair_depth, count, *refs):
    returned, refs = refs[:count], refs[count:]
    (table_ref, basis_ref, local_ref, image_ref, sums_ref), face_refs = refs[:5], refs[5:]
    rows = local_ref.shape[0] // 6
    width = local_ref.shape[1]
    pieces = width // LANES // count
    terms = jnp.concatenate([get_slab(ref, pieces) for ref in returned], axis=1)
    correction = select(table_ref[...], terms)
    image = local_ref[...] + product(basis_ref[...], correction)
    image_ref[...] = image
    put_faces(image, rows, pair_depth, face_refs)
    tail = jnp.sum(returned[-1][:, pieces * CAP :, :], axis=0)
    if pair_depth:
        folds = width // LANES
        sums = jnp.concatenate(
            [unfolded(tail, 0, folds), unfolded(tail, folds, folds)]
            + [jnp.zeros((TILE - 2, width), f32)],
            axis=0,
        )
        sums_ref[...] = sums
        face_refs[4][rows:, :] = sums
    else:
        sums_ref[...] = jnp.broadcast_to(tail[None], sums_ref.shape)


def direction_kernel(pair_depth, faces, scale, len_ref, sums_ref, prev_rho_ref, image_ref, prev_ref, schur_ref, *refs):
    got, refs = refs[:faces], refs[faces:]
    (direction_out, rho_out, square_out, schur_out), refs = refs[:4], refs[4:]
    face_refs, (direction_ref, sem) = refs[:faces], refs[faces:]
    rows = image_ref.shape[0] // 6
    width = image_ref.shape[1]
    if pair_depth:
        sums = sums_ref[...] + got[4][rows:, :]
        rho, square = sums[0:1, :], sums[1:2, :]
    else:
        folds = width // LANES
        sums = jnp.sum(sums_ref[...], axis=0)
        rho, square = unfolded(sums, 0, folds), unfolded(sums, folds, folds)
    rho = scale * rho
    rho_out[...] = rho
    square_out[...] = square
    beta = rho / prev_rho_ref[...]
    for face in range(6):
        at = slice(face * rows, (face + 1) * rows)
        precond = 0.5 * (image_ref[at, :] + got_face(got, face, rows, pair_depth))
        direction_ref[at, :] = jnp.where(
            live_rows(len_ref, face, rows), precond + beta * prev_ref[at, :], 0.0
        )
    copy = pltpu.make_async_copy(direction_ref, direction_out, sem)
    copy.start()
    image = product(schur_ref[...], direction_ref[...])
    schur_out[...] = image
    put_faces(image, rows, pair_depth, face_refs)
    copy.wait()


def products_kernel(len_ref, direction_ref, schur_ref, residual_ref, curve_ref, cross_ref):
    rows = schur_ref.shape[0] // 6
    image = schur_ref[...]
    live = jnp.concatenate(
        [masked(len_ref, residual_ref, face, rows) for face in range(6)], axis=0
    )
    curve_ref[...] = 2.0 * jnp.sum(direction_ref[...] * image, axis=0, keepdims=True)
    cross_ref[...] = 2.0 * jnp.sum(live * image, axis=0, keepdims=True)


def applied_kernel(pair_depth, faces, len_ref, curve_ref, cross_ref, schur_ref, *refs):
    got, (applied_ref, spread_ref) = refs[:faces], refs[faces:]
    rows = schur_ref.shape[0] // 6
    total = jnp.zeros(curve_ref.shape, f32)
    for face in range(6):
        at = slice(face * rows, (face + 1) * rows)
        applied = schur_ref[at, :] + got_face(got, face, rows, pair_depth)
        applied = jnp.where(live_rows(len_ref, face, rows), applied, 0.0)
        applied_ref[at, :] = applied
        total += jnp.sum(applied * applied, axis=0, keepdims=True)
    for i, vector in enumerate([curve_ref[...], cross_ref[...], total]):
        for j, piece in enumerate(folded(vector)):
            spread_ref[:, i, j, :] = jnp.broadcast_to(piece, (spread_ref.shape[0], LANES))


def finish_kernel(scale, len_ref, sums_ref, rho_ref, square_ref, residual_ref, applied_ref, new_out, alpha_ref, norm_ref, new_ref, sems):
    rows = applied_ref.shape[0] // 6
    folds = sums_ref.shape[2]
    sums = jnp.sum(sums_ref[...], axis=0)
    curve, cross, square = [unfolded(sums[i], 0, folds) for i in range(3)]
    alpha = rho_ref[...] / (scale * curve)
    alpha_ref[...] = alpha
    norm_ref[...] = scale * (square_ref[...] - 2.0 * alpha * cross + alpha * alpha * square)
    copies = []
    for face in range(6):
        at = slice(face * rows, (face + 1) * rows)
        new_ref[at, :] = masked(len_ref, residual_ref, face, rows) - alpha * applied_ref[at, :]
        where = pl.ds(face * rows, rows)
        copies.append(pltpu.make_async_copy(new_ref.at[where], new_out.at[where], sems.at[face]))
        copies[-1].start()
    for copy in copies:
        copy.wait()


def around(x, axis, by):
    devices = lax.axis_size(axis)
    return lax.ppermute(x, axis, [(i, (i + by) % devices) for i in range(devices)])


def along(x, axis, by):
    devices = range(lax.axis_size(axis))
    return lax.ppermute(x, axis, [(i - by, i) for i in devices if i - by in devices])


def exchange(faces, pair_depth):
    got = [
        around(faces[1], "blk", 1),
        around(faces[0], "blk", -1),
        along(faces[3], "lat", 1),
        along(faces[2], "lat", -1),
    ]
    if pair_depth:
        got.append(lax.ppermute(faces[4], "depth", [(0, 1), (1, 0)]))
    else:
        got += [along(faces[5], "depth", 1), along(faces[4], "depth", -1)]
    return got


def to_all(x, axes):
    return lax.all_to_all(x, axes, split_axis=0, concat_axis=0, tiled=True)


def shards(
    face_len,
    residual,
    prev_direction,
    prev_rho,
    schur,
    neumann,
    coarse_basis,
    coarse_inverse,
    prim_owner,
    coarse_row,
):
    height, width = residual.shape[3:]
    rows = height // 6
    primal = coarse_basis.shape[4]
    owned = coarse_inverse.shape[3]
    owners = lax.axis_size(LAYER)
    slots = owners * CAP
    devices = lax.axis_size(AXES)
    layers = lax.axis_size("depth")
    pair_depth = layers == 2
    faces = 5 if pair_depth else 6
    scale = 0.5 / (devices * height)
    count = PARTS
    folds = width // LANES
    pieces = folds // count
    tail = tiles(2 * folds)

    lengths = face_len.reshape(6)
    residual = residual.reshape(height, width)
    prev_direction = prev_direction.reshape(height, width)
    schur = schur.reshape(height, height)
    neumann = neumann.reshape(height, height)
    basis = coarse_basis.reshape(height, primal)
    inverse = coarse_inverse.reshape(owned, owned)
    owner = prim_owner.reshape(1, primal)
    wanted = coarse_row.reshape(1, primal)
    whole = shape_of(height, width)
    row = shape_of(1, width)
    part_row = shape_of(1, width // count)
    face = shape_of(rows, width)

    *outgoing, table = call(
        functools.partial(pack_kernel, count),
        [
            shape_of(owners, pieces * CAP + (0 if i else TILE), LANES) for i in range(count)
        ]
        + [shape_of(primal, slots, dtype=bf16)],
        [lengths, owner, wanted, residual, basis],
        far=range(5),
        flops=6 * height * primal * width,
        moved=4 * (height * (width + primal) + slots * width),
        scratch=[
            pltpu.SMEM((6,), jnp.int32),
            pltpu.VMEM((1, primal), jnp.int32),
            pltpu.VMEM((1, primal), jnp.int32),
            pltpu.VMEM((height, width), f32),
            pltpu.VMEM((height, primal), f32),
            pltpu.SemaphoreType.DMA((3, 2)),
            pltpu.SemaphoreType.DMA((3,)),
        ],
        room=60,
    )
    incoming = [to_all(x, LAYER) for x in outgoing]
    local, local_part, square = call(
        neumann_kernel,
        [whole, row, row],
        [lengths, residual, neumann],
        smem=(0,),
        flops=6 * height * height * width,
        moved=4 * height * (height + 2 * width),
    )
    picker, before, returned = None, [], []
    for i in range(count):
        last = i == count - 1
        operands = [incoming[i], inverse] + ([picker] if i else []) + before
        outs = [shape_of(owners, pieces * CAP + (tail if last else 0), LANES)]
        if last:
            operands += [local_part, square]
        else:
            outs.append(part_row)
            if i == 0:
                outs.append(shape_of(slots, owned))
        got = call(
            functools.partial(solve_kernel, i, count),
            outs,
            operands,
            flops=(8 * slots + 6 * owned) * owned * width // count,
            moved=8 * slots * width // count,
        )
        returned.append(to_all(got[0], LAYER))
        if not last:
            before.append(got[1])
            if i == 0:
                picker = got[2]
    extra = TILE if pair_depth else 0
    image, sums, *outward = call(
        functools.partial(image_kernel, pair_depth, count),
        [whole, shape_of(TILE, width) if pair_depth else shape_of(layers, tail, LANES)]
        + [face] * 4
        + ([shape_of(rows + extra, width)] if pair_depth else [face] * 2),
        [*returned, table, basis, local],
        flops=(6 * height + 4 * slots) * primal * width,
        moved=16 * height * width,
    )
    if not pair_depth:
        sums = to_all(sums, "depth")
    got = exchange(outward, pair_depth)
    direction, rho, square, schur_image, *outward = call(
        functools.partial(direction_kernel, pair_depth, faces, scale),
        [whole, row, row, whole] + [face] * faces,
        [lengths, sums, prev_rho.reshape(1, width), image, prev_direction, schur, *got],
        smem=(0,),
        far_out=(0,),
        flops=6 * height * height * width,
        moved=4 * height * (height + 6 * width),
        scratch=[pltpu.VMEM((height, width), f32), pltpu.SemaphoreType.DMA],
    )
    got = exchange(outward, pair_depth)
    curve, cross = call(
        products_kernel,
        [row, row],
        [lengths, direction, schur_image, residual],
        smem=(0,),
        flops=4 * height * width,
        moved=12 * height * width,
    )
    applied, spread = call(
        functools.partial(applied_kernel, pair_depth, faces),
        [whole, shape_of(devices, 3, folds, LANES)],
        [lengths, curve, cross, schur_image, *got],
        smem=(0,),
        flops=4 * height * width,
        moved=12 * height * width,
    )
    new_residual, alpha, norm = call(
        functools.partial(finish_kernel, scale),
        [whole, row, row],
        [lengths, to_all(spread, AXES), rho, square, residual, applied],
        smem=(0,),
        far_out=(0,),
        flops=4 * height * width,
        moved=12 * height * width,
        scratch=[pltpu.VMEM((height, width), f32), pltpu.SemaphoreType.DMA((6,))],
    )
    out_shape = (1, 1, 1, height, width)
    return (
        new_residual.reshape(out_shape),
        direction.reshape(out_shape),
        rho.reshape(width),
        alpha.reshape(width),
        norm.reshape(width),
    )


def solution(mesh):
    tall = P("blk", "lat", "depth", None, None)
    flat = P("blk", "lat", "depth", None)
    in_specs = (flat, tall, tall, P(), tall, tall, tall, tall, tall, flat)
    out_specs = (tall, tall, P(), P(), P())
    return jax.shard_map(shards, mesh=mesh, in_specs=in_specs, out_specs=out_specs, check_vma=False)
```

time: 185 us -> 134 us (0.72)
  blocking collectives: 136 us -> 49.2 us
  waiting for transfers between devices: 0.03 us -> 32.5 us
  Pallas kernels: 15.7 us -> 19.7 us
    all_gather x2 -> x0, blocking collectives: 83.8 us -> none  [the longest x1 46.5 us: shards(): all_row = lax.all_gather(wanted, LAYER, axis=0, tiled=True)]
    all_to_all x1 -> x2, waiting for transfers between devices: 0.01 us -> 13.7 us  [to_all(): return lax.all_to_all(x, axes, split_axis=0, concat_axis=0, tiled=True)]
    ppermute x4, waiting for transfers between devices: 0.01 us -> 10.3 us  [around(): lax.ppermute(x, axis, [(i, (i + by) % devices) for i in range(devices)])]
    ppermute x4, waiting for transfers between devices: 0.01 us -> 8.46 us  [along(): lax.ppermute(x, axis, [(i - by, i) for i in devices if i - by in devices])]
    pallas_call x8 -> x9, Pallas kernels: 15.7 us -> 19.7 us  [call(): pl.pallas_call(body, out_shape=list(outs), in_specs=in_specs, out_specs=o...]
    all_to_all x4 -> x3, blocking collectives: 51.9 us -> 49.2 us  [to_all(): return lax.all_to_all(x, axes, split_axis=0, concat_axis=0, tiled=True)]
    unnamed x36 -> x30, local copies, waits for them, and re-layouts: 7.87 us -> 7.34 us
    all_to_all x1 -> x2, starting transfers between devices: 8.49 us -> 8.1 us  [to_all(): return lax.all_to_all(x, axes, split_axis=0, concat_axis=0, tiled=True)]
  transfers between devices with their start and end apart: 11 -> 12, of which waited for: 0 -> 8; matrix products, arithmetic and copies ran while one was open for 0% -> 0% of each run, Pallas kernels for 2% -> 5%
where the time goes in v2:
time: 134 us; the launch traced here: 133 us
  blocking collectives  49.2 us (37%)
  waiting for transfers between devices  32.5 us (24%)
  starting transfers between devices  23.5 us (18%)
  Pallas kernels  19.7 us (15%)
  local copies, waits for them, and re-layouts  7.34 us (5%)
    all_to_all x3, blocking collectives, to_all(): return lax.all_to_all(x, axes, split_axis=0, concat_axis=0, tiled=True)  49.2 us
    pallas_call x9, Pallas kernels, call(): pl.pallas_call(body, out_shape=list(outs), in_specs=in_specs, out_specs=o...  19.7 us
    all_to_all x2, waiting for transfers between devices, to_all(): return lax.all_to_all(x, axes, split_axis=0, concat_axis=0, tiled=True)  13.7 us
    ppermute x4, waiting for transfers between devices, around(): lax.ppermute(x, axis, [(i, (i + by) % devices) for i in range(devices)])  10.3 us
    ppermute x4, waiting for transfers between devices, along(): lax.ppermute(x, axis, [(i - by, i) for i in devices if i - by in devices])  8.46 us
    all_to_all x2, starting transfers between devices, to_all(): return lax.all_to_all(x, axes, split_axis=0, concat_axis=0, tiled=True)  8.1 us
    ppermute x4, starting transfers between devices, around(): lax.ppermute(x, axis, [(i, (i + by) % devices) for i in range(devices)])  7.75 us
    ppermute x4, starting transfers between devices, along(): lax.ppermute(x, axis, [(i - by, i) for i in devices if i - by in devices])  7.52 us
  transfers between devices with their start and end apart: 12, of which 8 were waited for; matrix products, arithmetic and copies ran while one was open for 0% of the time, Pallas kernels for 5%

profile of v2, /device:TPU:0, one launch (start us, length us, event | category | flops | bytes accessed | tf_op | source)
XLA Modules:
  0.0 133.1 jit_solution(12203991430388140569)
XLA Ops:
  0.6 4.1 %shard_map.137 = (f32[16,56,128]{2,1,0:T(8,128)}, f32[16,48,128]{2,1,0:T(8,128)}, bf16[256,384]{1,0:T(8,128)(2,1)}) custom-call(s32[6]{0:T(128)} %bitcast.26, s32[1,256]{1,0:T(1,128)} %bitcast.35, s32[1,256]{1,0:T(1,128)} %bitcast.36, f32[768,512]{1,0:T(8,128)} %bitcast.15, f32[768,256]{1,0:T(8,128)} %bitcast.19), custom_call_target="tpu_custom_call" | custom-call | flops 603979776 | bytes 3145728 | tf_op jit(solution)/shard_map/pallas_call | solution.py:31
  4.8 22.2 %all_to_all.25.refs_0_ = f32[16,56,128]{2,1,0:T(8,128)S(1)} all-to-all(f32[16,56,128]{2,1,0:T(8,128)} %get-tuple-element.37), channel_id=1, replica_groups=mesh['blk'=4,'lat'=4,'depth'=2] {'blk','lat'}, dimensions={0} | all-to-all | bytes 917504 | tf_op jit(solution)/shard_map/all_to_all | solution.py:376
  27.0 3.9 %all-to-all-start.2 = ((f32[16,48,128]{2,1,0:T(8,128)}), f32[16,48,128]{2,1,0:T(8,128)S(1)}, u32[]{:S(2)}, u32[]{:S(2)}) async-start(f32[16,48,128]{2,1,0:T(8,128)} %get-tuple-element.39), calls=%async_computation.2 | async-start | bytes 786432 | tf_op jit(solution)/shard_map/all_to_all | solution.py:376
  30.9 1.9 %shard_map.138 = (f32[16,48,128]{2,1,0:T(8,128)}, f32[1,256]{1,0:T(1,128)S(1)}, f32[384,256]{1,0:T(8,128)S(1)}) custom-call(f32[16,56,128]{2,1,0:T(8,128)S(1)} %all_to_all.25.refs_0_, f32[256,256]{1,0:T(8,128)S(1)} %bitcast.24), custom_call_target="tpu_custom_call" | custom-call | flops 301989888 | bytes 786432 | tf_op jit(solution)/shard_map/pallas_call | solution.py:31
  33.6 9.2 %all-to-all-done.2.refs_0_ = f32[16,48,128]{2,1,0:T(8,128)S(1)} async-done(((f32[16,48,128]{2,1,0:T(8,128)}), f32[16,48,128]{2,1,0:T(8,128)S(1)}, u32[]{:S(2)}, u32[]{:S(2)}) %all-to-all-start.2) | async-done | bytes 393248 | tf_op jit(solution)/shard_map/all_to_all | solution.py:376
  42.8 4.2 %all-to-all-start.1 = ((f32[16,48,128]{2,1,0:T(8,128)}), f32[16,48,128]{2,1,0:T(8,128)}, u32[]{:S(2)}, u32[]{:S(2)}) async-start(f32[16,48,128]{2,1,0:T(8,128)} %get-tuple-element.38), calls=%async_computation.1 | async-start | bytes 786432 | tf_op jit(solution)/shard_map/all_to_all | solution.py:376
  47.0 1.7 %copy-done.14 = f32[1,1,1,768,768]{4,3,2,1,0:T(8,128)S(1)} copy-done((f32[1,1,1,768,768]{4,3,2,1,0:T(8,128)S(1)}, f32[1,1,1,768,768]{4,3,2,1,0:T(8,128)}, u32[]{:S(2)}) %copy-start.14) | copy-done | bytes 2359320
  48.7 2.6 %shard_map.139 = (f32[768,512]{1,0:T(8,128)S(1)}, f32[1,512]{1,0:T(1,128)S(1)}, f32[1,512]{1,0:T(1,128)S(1)}) custom-call(s32[6]{0:T(128)S(1)} %bitcast.27, f32[768,512]{1,0:T(8,128)S(1)} %bitcast.16, f32[768,768]{1,0:T(8,128)S(1)} %bitcast.34), custom_call_target="tpu_custom_call" | custom-call | flops 1811939328 | bytes 5505024 | tf_op jit(solution)/shard_map/pallas_call | solution.py:31
  53.5 4.5 %all-to-all-done.1.refs_0_ = f32[16,48,128]{2,1,0:T(8,128)} async-done(((f32[16,48,128]{2,1,0:T(8,128)}), f32[16,48,128]{2,1,0:T(8,128)}, u32[]{:S(2)}, u32[]{:S(2)}) %all-to-all-start.1) | async-done | bytes 393248 | tf_op jit(solution)/shard_map/all_to_all | solution.py:376
  58.0 16.4 %all_to_all.26.refs_1_ = f32[16,56,128]{2,1,0:T(8,128)S(1)} all-to-all(f32[16,56,128]{2,1,0:T(8,128)S(1)} %shard_map.140), channel_id=1, replica_groups=mesh['blk'=4,'lat'=4,'depth'=2] {'blk','lat'}, dimensions={0} | all-to-all | bytes 917504 | tf_op jit(solution)/shard_map/all_to_all | solution.py:376
  74.4 1.4 %copy-done.6 = f32[768,512]{1,0:T(8,128)S(1)} copy-done((f32[768,512]{1,0:T(8,128)S(1)}, f32[768,512]{1,0:T(8,128)}, u32[]{:S(2)}) %copy-start.6) | copy-done | bytes 1572888
  76.8 2.4 %shard_map.141 = (f32[768,512]{1,0:T(8,128)S(1)}, f32[8,512]{1,0:T(8,128)S(1)}, f32[128,512]{1,0:T(8,128)S(1)}, f32[128,512]{1,0:T(8,128)S(1)}, f32[128,512]{1,0...) custom-call(f32[16,48,128]{2,1,0:T(8,128)} %all-to-all-done.1.refs_0_, ...), custom_call_target="tpu_custom_call" | custom-call | flops 805306368 | bytes 6291456 | tf_op jit(solution)/shard_map/pallas_call | solution.py:31
  80.5 2.6 %collective-permute-start.1 = (f32[128,512]{1,0:T(8,128)S(1)}, f32[128,512]{1,0:T(8,128)S(1)}, u32[]{:S(2)}, u32[]{:S(2)}) collective-permute-start(f32[128,512]{1,0:T(8,128)S(1)} %get-tuple-element.49), channel_id=1, source_target_pairs={{0,24},{8,0},{16,8},{24,16},{1,25},{9,1},{17,9},{25,17},{2,26},{10... | collective-permute-start | bytes 786440 | tf_op jit(solution)/shard_map/ppermute | solution.py:353
  83.1 2.5 %collective-permute-start.2 = (f32[128,512]{1,0:T(8,128)S(1)}, f32[128,512]{1,0:T(8,128)S(1)}, u32[]{:S(2)}, u32[]{:S(2)}) collective-permute-start(f32[128,512]{1,0:T(8,128)S(1)} %get-tuple-element.50), channel_id=1, source_target_pairs={{0,2},{2,4},{4,6},{1,3},{3,5},{5,7},{8,10},{10,12},{12,14},{9,11},... | collective-permute-start | bytes 786440 | tf_op jit(solution)/shard_map/ppermute | solution.py:358
  86.9 3.4 %collective-permute-done.refs_0_ = f32[128,512]{1,0:T(8,128)S(1)} collective-permute-done((f32[128,512]{1,0:T(8,128)S(1)}, f32[128,512]{1,0:T(8,128)S(1)}, u32[]{:S(2)}, u32[]{:S(2)}) %collective-permute-start) | collective-permute-done | bytes 262176 | tf_op jit(solution)/shard_map/ppermute | solution.py:353
  90.2 4.2 %collective-permute-done.1.refs_1_ = f32[128,512]{1,0:T(8,128)S(1)} collective-permute-done((f32[128,512]{1,0:T(8,128)S(1)}, f32[128,512]{1,0:T(8,128)S(1)}, u32[]{:S(2)}, u32[]{:S(2)}) %collective-permute-start.1) | collective-permute-done | bytes 262176 | tf_op jit(solution)/shard_map/ppermute | solution.py:353
  94.5 4.5 %collective-permute-done.3.refs_3_ = f32[128,512]{1,0:T(8,128)S(1)} collective-permute-done((f32[128,512]{1,0:T(8,128)S(1)}, f32[128,512]{1,0:T(8,128)S(1)}, u32[]{:S(2)}, u32[]{:S(2)}) %collective-permute-start.3) | collective-permute-done | bytes 262176 | tf_op jit(solution)/shard_map/ppermute | solution.py:358
  99.0 3.3 %shard_map.142 = (f32[768,512]{1,0:T(8,128)}, f32[1,512]{1,0:T(1,128)}, f32[1,512]{1,0:T(1,128)S(1)}, f32[768,512]{1,0:T(8,128)S(1)}, f32[128,512]{1,0:T(8,128)S...) custom-call(s32[6]{0:T(128)S(1)} %bitcast.28, ...), custom_call_target="tpu_custom_call" | custom-call | flops 1811939328 | bytes 11796480 | tf_op jit(solution)/shard_map/pallas_call | solution.py:31
  102.4 3.8 %collective-permute-start.6 = (f32[128,512]{1,0:T(8,128)S(1)}, f32[128,512]{1,0:T(8,128)S(1)}, u32[]{:S(2)}, u32[]{:S(2)}) collective-permute-start(f32[128,512]{1,0:T(8,128)S(1)} %get-tuple-element.58), channel_id=1, source_target_pairs={{0,24},{8,0},{16,8},{24,16},{1,25},{9,1},{17,9},{25,17},{2,26},{10... | collective-permute-start | bytes 786440 | tf_op jit(solution)/shard_map/ppermute | solution.py:353
  106.2 2.5 %collective-permute-start.7 = (f32[128,512]{1,0:T(8,128)S(1)}, f32[128,512]{1,0:T(8,128)S(1)}, u32[]{:S(2)}, u32[]{:S(2)}) collective-permute-start(f32[128,512]{1,0:T(8,128)S(1)} %get-tuple-element.59), channel_id=1, source_target_pairs={{0,2},{2,4},{4,6},{1,3},{3,5},{5,7},{8,10},{10,12},{12,14},{9,11},... | collective-permute-start | bytes 786440 | tf_op jit(solution)/shard_map/ppermute | solution.py:358
  113.4 1.9 %collective-permute-done.6.refs_1_ = f32[128,512]{1,0:T(8,128)S(1)} collective-permute-done((f32[128,512]{1,0:T(8,128)S(1)}, f32[128,512]{1,0:T(8,128)S(1)}, u32[]{:S(2)}, u32[]{:S(2)}) %collective-permute-start.6) | collective-permute-done | bytes 262176 | tf_op jit(solution)/shard_map/ppermute | solution.py:353
  115.3 3.9 %collective-permute-done.8.refs_3_ = f32[128,512]{1,0:T(8,128)S(1)} collective-permute-done((f32[128,512]{1,0:T(8,128)S(1)}, f32[128,512]{1,0:T(8,128)S(1)}, u32[]{:S(2)}, u32[]{:S(2)}) %collective-permute-start.8) | collective-permute-done | bytes 262176 | tf_op jit(solution)/shard_map/ppermute | solution.py:358
  120.1 10.6 %all_to_all.27.sums_ref = f32[32,3,4,128]{3,2,1,0:T(4,128)S(1)} all-to-all(f32[32,3,4,128]{3,2,1,0:T(4,128)S(1)} %get-tuple-element.62), channel_id=1, replica_groups=mesh['blk'=4,'lat'=4,'depth'=2] {'blk','lat','depth'}, dimensions={0} | all-to-all | bytes 393216 | tf_op jit(solution)/shard_map/all_to_all | solution.py:376
  130.7 2.4 %shard_map.145 = (f32[768,512]{1,0:T(8,128)}, f32[1,512]{1,0:T(1,128)}, f32[1,512]{1,0:T(1,128)}) custom-call(s32[6]{0:T(128)S(1)} %bitcast.31, f32[32,3,4,128]{3,2,1,0:T(4,128)S(1)} %all_to_all.27.sums_ref, f32[1,512]{1,0:T(1,128)S(1)} %copy-done.13, f32[1,512]{1,0:T(1,128)S(1)} %get-tuple-element.64.square_ref, f32[768,512]{1,0:T(8,128)S(1)} %bitcast.18, ...), custom_call_target="tpu_custom_call" | custom-call | flops 1572864 | bytes 4718592 | tf_op jit(solution)/shard_map/pallas_call | solution.py:31
  (42 shorter events, 12.2 us)
Async XLA Ops:
  0.6 30.2 %copy-start.9 = (f32[1,1,1,256,256]{4,3,2,1,0:T(8,128)S(1)}, f32[1,1,1,256,256]{4,3,2,1,0:T(8,128)}, u32[]{:S(2)}) copy-start(f32[1,1,1,256,256]{4,3,2,1,0:T(8,128)} %param.17) | copy-start | bytes 786436
  27.0 20.0 %copy-start = (f32[1,1,1,768,512]{4,3,2,1,0:T(8,128)S(1)}, f32[1,1,1,768,512]{4,3,2,1,0:T(8,128)}, u32[]{:S(2)}) copy-start(f32[1,1,1,768,512]{4,3,2,1,0:T(8,128)} %param.11) | copy-start | bytes 4718596
  27.0 20.0 %copy-start.11 = (s32[1,1,1,6]{3,2,1,0:T(1,128)S(1)}, s32[1,1,1,6]{3,2,1,0:T(1,128)}, u32[]{:S(2)}) copy-start(s32[1,1,1,6]{3,2,1,0:T(1,128)} %param.10) | copy-start | bytes 76
  27.0 15.8 %all-to-all-start.2 = ((f32[16,48,128]{2,1,0:T(8,128)}), f32[16,48,128]{2,1,0:T(8,128)S(1)}, u32[]{:S(2)}, u32[]{:S(2)}) async-start(f32[16,48,128]{2,1,0:T(8,128)} %get-tuple-element.39), calls=%async_computation.2 | async-start | bytes 786432 | tf_op jit(solution)/shard_map/all_to_all | solution.py:376
  42.8 15.2 %all-to-all-start.1 = ((f32[16,48,128]{2,1,0:T(8,128)}), f32[16,48,128]{2,1,0:T(8,128)}, u32[]{:S(2)}, u32[]{:S(2)}) async-start(f32[16,48,128]{2,1,0:T(8,128)} %get-tuple-element.38), calls=%async_computation.1 | async-start | bytes 786432 | tf_op jit(solution)/shard_map/all_to_all | solution.py:376
  47.0 1.7 %copy-start.14 = (f32[1,1,1,768,768]{4,3,2,1,0:T(8,128)S(1)}, f32[1,1,1,768,768]{4,3,2,1,0:T(8,128)}, u32[]{:S(2)}) copy-start(f32[1,1,1,768,768]{4,3,2,1,0:T(8,128)} %param.15) | copy-start | bytes 7077892
  48.7 3.8 %copy-start.8 = (f32[384,256]{1,0:T(8,128)S(1)}, f32[384,256]{1,0:T(8,128)}, u32[]{:S(2)}) copy-start(f32[384,256]{1,0:T(8,128)} %copy-done.7) | copy-start | bytes 1179652
  52.5 22.0 %copy-start.1 = (f32[1,1,1,768,256]{4,3,2,1,0:T(8,128)S(1)}, f32[1,1,1,768,256]{4,3,2,1,0:T(8,128)}, u32[]{:S(2)}) copy-start(f32[1,1,1,768,256]{4,3,2,1,0:T(8,128)} %param.16) | copy-start | bytes 2359300
  58.0 41.0 %copy-start.4 = (f32[1,1,1,768,512]{4,3,2,1,0:T(8,128)S(1)}, f32[1,1,1,768,512]{4,3,2,1,0:T(8,128)}, u32[]{:S(2)}) copy-start(f32[1,1,1,768,512]{4,3,2,1,0:T(8,128)} %param.12) | copy-start | bytes 4718596
  74.4 1.4 %copy-start.6 = (f32[768,512]{1,0:T(8,128)S(1)}, f32[768,512]{1,0:T(8,128)}, u32[]{:S(2)}) copy-start(f32[768,512]{1,0:T(8,128)} %copy-done.5) | copy-start | bytes 4718596
  76.8 22.2 %copy-start.2 = (f32[1,1,1,768,768]{4,3,2,1,0:T(8,128)S(1)}, f32[1,1,1,768,768]{4,3,2,1,0:T(8,128)}, u32[]{:S(2)}) copy-start(f32[1,1,1,768,768]{4,3,2,1,0:T(8,128)} %param.14) | copy-start | bytes 7077892
  76.8 22.3 %copy-start.12 = (f32[512]{0:T(512)S(1)}, f32[512]{0:T(512)}, u32[]{:S(2)}) copy-start(f32[512]{0:T(512)} %param.13) | copy-start | bytes 6148
  79.2 19.9 %collective-permute-start.4 = (f32[136,512]{1,0:T(8,128)S(1)}, f32[136,512]{1,0:T(8,128)S(1)}, u32[]{:S(2)}, u32[]{:S(2)}) collective-permute-start(f32[136,512]{1,0:T(8,128)S(1)} %get-tuple-element.52), channel_id=1, source_target_pairs={{0,1},{1,0},{2,3},{3,2},{4,5},{5,4},{6,7},{7,6},{8,9},{9,8},{10,11... | collective-permute-start | bytes 835592 | tf_op jit(solution)/shard_map/ppermute | solution.py:369
  79.2 11.0 %collective-permute-start = (f32[128,512]{1,0:T(8,128)S(1)}, f32[128,512]{1,0:T(8,128)S(1)}, u32[]{:S(2)}, u32[]{:S(2)}) collective-permute-start(f32[128,512]{1,0:T(8,128)S(1)} %get-tuple-element.48), channel_id=1, source_target_pairs={{0,8},{8,16},{16,24},{24,0},{1,9},{9,17},{17,25},{25,1},{2,10},{10... | collective-permute-start | bytes 786440 | tf_op jit(solution)/shard_map/ppermute | solution.py:353
  80.5 14.0 %collective-permute-start.1 = (f32[128,512]{1,0:T(8,128)S(1)}, f32[128,512]{1,0:T(8,128)S(1)}, u32[]{:S(2)}, u32[]{:S(2)}) collective-permute-start(f32[128,512]{1,0:T(8,128)S(1)} %get-tuple-element.49), channel_id=1, source_target_pairs={{0,24},{8,0},{16,8},{24,16},{1,25},{9,1},{17,9},{25,17},{2,26},{10... | collective-permute-start | bytes 786440 | tf_op jit(solution)/shard_map/ppermute | solution.py:353
  83.1 11.3 %collective-permute-start.2 = (f32[128,512]{1,0:T(8,128)S(1)}, f32[128,512]{1,0:T(8,128)S(1)}, u32[]{:S(2)}, u32[]{:S(2)}) collective-permute-start(f32[128,512]{1,0:T(8,128)S(1)} %get-tuple-element.50), channel_id=1, source_target_pairs={{0,2},{2,4},{4,6},{1,3},{3,5},{5,7},{8,10},{10,12},{12,14},{9,11},... | collective-permute-start | bytes 786440 | tf_op jit(solution)/shard_map/ppermute | solution.py:358
  85.6 13.4 %collective-permute-start.3 = (f32[128,512]{1,0:T(8,128)S(1)}, f32[128,512]{1,0:T(8,128)S(1)}, u32[]{:S(2)}, u32[]{:S(2)}) collective-permute-start(f32[128,512]{1,0:T(8,128)S(1)} %get-tuple-element.51), channel_id=1, source_target_pairs={{2,0},{4,2},{6,4},{3,1},{5,3},{7,5},{10,8},{12,10},{14,12},{11,9},... | collective-permute-start | bytes 786440 | tf_op jit(solution)/shard_map/ppermute | solution.py:358
  102.3 11.1 %collective-permute-start.5 = (f32[128,512]{1,0:T(8,128)S(1)}, f32[128,512]{1,0:T(8,128)S(1)}, u32[]{:S(2)}, u32[]{:S(2)}) collective-permute-start(f32[128,512]{1,0:T(8,128)S(1)} %get-tuple-element.57), channel_id=1, source_target_pairs={{0,8},{8,16},{16,24},{24,0},{1,9},{9,17},{17,25},{25,1},{2,10},{10... | collective-permute-start | bytes 786440 | tf_op jit(solution)/shard_map/ppermute | solution.py:353
  102.4 12.9 %collective-permute-start.6 = (f32[128,512]{1,0:T(8,128)S(1)}, f32[128,512]{1,0:T(8,128)S(1)}, u32[]{:S(2)}, u32[]{:S(2)}) collective-permute-start(f32[128,512]{1,0:T(8,128)S(1)} %get-tuple-element.58), channel_id=1, source_target_pairs={{0,24},{8,0},{16,8},{24,16},{1,25},{9,1},{17,9},{25,17},{2,26},{10... | collective-permute-start | bytes 786440 | tf_op jit(solution)/shard_map/ppermute | solution.py:353
  106.2 9.1 %collective-permute-start.7 = (f32[128,512]{1,0:T(8,128)S(1)}, f32[128,512]{1,0:T(8,128)S(1)}, u32[]{:S(2)}, u32[]{:S(2)}) collective-permute-start(f32[128,512]{1,0:T(8,128)S(1)} %get-tuple-element.59), channel_id=1, source_target_pairs={{0,2},{2,4},{4,6},{1,3},{3,5},{5,7},{8,10},{10,12},{12,14},{9,11},... | collective-permute-start | bytes 786440 | tf_op jit(solution)/shard_map/ppermute | solution.py:358
  108.7 10.5 %collective-permute-start.8 = (f32[128,512]{1,0:T(8,128)S(1)}, f32[128,512]{1,0:T(8,128)S(1)}, u32[]{:S(2)}, u32[]{:S(2)}) collective-permute-start(f32[128,512]{1,0:T(8,128)S(1)} %get-tuple-element.60), channel_id=1, source_target_pairs={{2,0},{4,2},{6,4},{3,1},{5,3},{7,5},{10,8},{12,10},{14,12},{11,9},... | collective-permute-start | bytes 786440 | tf_op jit(solution)/shard_map/ppermute | solution.py:358
  110.0 9.2 %collective-permute-start.9 = (f32[128,512]{1,0:T(8,128)S(1)}, f32[128,512]{1,0:T(8,128)S(1)}, u32[]{:S(2)}, u32[]{:S(2)}) collective-permute-start(f32[128,512]{1,0:T(8,128)S(1)} %get-tuple-element.61), channel_id=1, source_target_pairs={{0,1},{1,0},{2,3},{3,2},{4,5},{5,4},{6,7},{7,6},{8,9},{9,8},{10,11... | collective-permute-start | bytes 786440 | tf_op jit(solution)/shard_map/ppermute | solution.py:369
  110.1 1.4 %copy-start.3 = (f32[768,512]{1,0:T(8,128)S(1)}, f32[768,512]{1,0:T(8,128)}, u32[]{:S(2)}) copy-start(f32[768,512]{1,0:T(8,128)} %get-tuple-element.53.direction_ref) | copy-start | bytes 4718596
  119.2 11.5 %copy-start.13 = (f32[1,512]{1,0:T(1,128)S(1)}, f32[1,512]{1,0:T(1,128)}, u32[]{:S(2)}) copy-start(f32[1,512]{1,0:T(1,128)} %get-tuple-element.63.rho_ref) | copy-start | bytes 6148
  (3 other events, 2.8 us)

commit v3 on v2

--- a/solution.py
+++ b/solution.py
@@ -8,7 +8,6 @@
 from jax.sharding import PartitionSpec as P
 
 CAP = 24
-PARTS = 2
 AXES = ("blk", "lat", "depth")
 LAYER = ("blk", "lat")
 LANES = 128
@@ -54,8 +53,7 @@
 
 
 def product(a, b, dims=PLAIN):
-    ah, al = parts(a)
-    bh, bl = parts(b)
+    (ah, al), (bh, bl) = a, b
     return mul(ah, bh, dims) + (mul(ah, bl, dims) + mul(al, bh, dims))
 
 
@@ -104,12 +102,11 @@
     )
 
 
-def pack_kernel(count, len_any, owner_any, row_any, residual_any, basis_any, *refs):
-    slab_refs, table_ref = refs[:count], refs[count]
-    len_ref, owner_ref, row_ref, residual_ref, basis_ref, sems, small_sems = refs[count + 1 :]
+def pack_kernel(len_any, owner_any, row_any, residual_any, basis_any, slab_ref, *refs):
+    len_ref, owner_ref, row_ref, residual_ref, basis_ref, sems, small_sems = refs
     rows = residual_ref.shape[0] // 6
     primal = basis_ref.shape[1]
-    owners = slab_refs[0].shape[0]
+    owners = slab_ref.shape[0]
     slots = owners * CAP
     small = [
         pltpu.make_async_copy(src, dst, small_sems.at[i])
@@ -143,12 +140,8 @@
     rank_row = jnp.sum(jnp.where(same & (row_at < col_at), 1.0, 0.0), axis=0, keepdims=True)
     rank_col = jnp.sum(jnp.where(same & (col_at < row_at), 1.0, 0.0), axis=1, keepdims=True)
     slot_row = (own_row * CAP + rank_row).astype(jnp.int32)
-    slot_col = (own_col * CAP + rank_col).astype(jnp.int32)
     packer = one_hot(lax.broadcasted_iota(jnp.int32, (slots, primal), 0) == slot_row)
-    table_ref[...] = one_hot(lax.broadcasted_iota(jnp.int32, (primal, slots), 1) == slot_col)
-    to_owner = one_hot(
-        lax.broadcasted_iota(jnp.int32, (owners, primal), 0) == owner_ref[...]
-    )
+    to_owner = one_hot(lax.broadcasted_iota(jnp.int32, (owners, primal), 0) == owner_ref[...])
     lane_at = lax.broadcasted_iota(jnp.int32, (primal, LANES), 1)
     ranked = jnp.where(lane_at == rank_col.astype(jnp.int32), wanted_col, 0.0)
     names = select(to_owner, ranked)
@@ -160,27 +153,38 @@
             [0.5 * masked(len_ref, residual_ref, 2 * pair + side, rows) for side in range(2)],
             axis=0,
         )
-        term = product(basis_ref[2 * pair * rows : 2 * (pair + 1) * rows, :], weighted, LEFT_T)
+        basis = basis_ref[2 * pair * rows : 2 * (pair + 1) * rows, :]
+        term = product(parts(basis), parts(weighted), LEFT_T)
         terms = term if terms is None else terms + term
-    packed = select(packer, terms)
-    width = packed.shape[1] // count
-    for i in range(count):
-        put_slab(slab_refs[i], packed[:, i * width : (i + 1) * width])
-    tail = slab_refs[0].shape[1] - TILE
-    slab_refs[0][:, tail:, :] = jnp.broadcast_to(
+    put_slab(slab_ref, select(packer, terms))
+    tail = slab_ref.shape[1] - TILE
+    slab_ref[:, tail:, :] = jnp.broadcast_to(
         names.reshape(owners, 1, LANES), (owners, TILE, LANES)
     )
 
 
-def neumann_kernel(len_ref, residual_ref, matrix_ref, local_ref, part_ref, square_ref):
+def local_kernel(len_ref, residual_ref, matrix_ref, owner_ref, *refs):
+    whole, refs = refs[:3], refs[3:]
+    local_ref, part_ref, square_ref, table_ref, refs = *refs[:4], refs[4:]
     rows = residual_ref.shape[0] // 6
     live = jnp.concatenate(
         [masked(len_ref, residual_ref, face, rows) for face in range(6)], axis=0
     )
-    local = product(matrix_ref[...], 0.5 * live)
+    local = product(parts(matrix_ref[...]), parts(0.5 * live))
     local_ref[...] = local
     part_ref[...] = jnp.sum(live * local, axis=0, keepdims=True)
     square_ref[...] = jnp.sum(live * live, axis=0, keepdims=True)
+    for i in range(3):
+        refs[2 * i][...], refs[2 * i + 1][...] = parts(whole[i][...])
+    primal, slots = table_ref.shape
+    row_at = lax.broadcasted_iota(jnp.int32, (primal, primal), 0)
+    col_at = lax.broadcasted_iota(jnp.int32, (primal, primal), 1)
+    own_row = owner_ref[...].astype(f32)
+    own_col = jnp.sum(jnp.where(row_at == col_at, own_row, 0.0), axis=1, keepdims=True)
+    before = (own_row == own_col) & (col_at < row_at)
+    rank_col = jnp.sum(jnp.where(before, 1.0, 0.0), axis=1, keepdims=True)
+    slot_col = (own_col * CAP + rank_col).astype(jnp.int32)
+    table_ref[...] = one_hot(lax.broadcasted_iota(jnp.int32, (primal, slots), 1) == slot_col)
 
 
 def picker_table(slab_ref, owned):
@@ -196,91 +200,96 @@
     return jnp.concatenate(blocks, axis=0)
 
 
-def solve_kernel(index, count, *refs):
-    incoming_ref, inverse_ref, refs = refs[0], refs[1], refs[2:]
-    owned = inverse_ref.shape[0]
-    if index > 0:
-        picker_ref, refs = refs[0], refs[1:]
-        picker = picker_ref[...]
-    else:
-        picker = picker_table(incoming_ref, owned)
-    before, refs = refs[:index], refs[index:]
-    last = index == count - 1
-    if last:
-        (local_part_ref, square_ref), refs = refs[:2], refs[2:]
-    answer_ref, refs = refs[0], refs[1:]
-    if index == 0 and not last:
-        refs[-1][...] = picker
-    table = picker.astype(bf16)
-    pieces = (incoming_ref.shape[1] // CAP) if index else (incoming_ref.shape[1] - TILE) // CAP
+def solve_kernel(incoming_ref, high_ref, low_ref, local_part_ref, square_ref, answer_ref):
+    owners, height, _ = incoming_ref.shape
+    pieces = (height - TILE) // CAP
+    table = picker_table(incoming_ref, high_ref.shape[0]).astype(bf16)
     summed = select(table, get_slab(incoming_ref, pieces), LEFT_T)
-    solved = product(inverse_ref[...], summed)
+    solved = product((high_ref[...], low_ref[...]), parts(summed))
     put_slab(answer_ref, select(table, solved))
-    mine = 2.0 * jnp.sum(summed * solved, axis=0, keepdims=True)
-    if not last:
-        refs[0][...] = mine
-        return
-    total = jnp.concatenate([ref[...] for ref in before] + [mine], axis=1) + local_part_ref[...]
+    total = local_part_ref[...] + 2.0 * jnp.sum(summed * solved, axis=0, keepdims=True)
     sums = folded(total) + folded(square_ref[...])
     sums += [jnp.zeros((1, LANES), f32)] * (tiles(len(sums)) - len(sums))
-    owners = answer_ref.shape[0]
-    start = pieces * CAP
-    answer_ref[:, start:, :] = jnp.broadcast_to(
+    answer_ref[:, pieces * CAP :, :] = jnp.broadcast_to(
         jnp.concatenate(sums, axis=0)[None], (owners, len(sums), LANES)
     )
 
 
-def put_faces(image, rows, pair_depth, face_refs):
-    for face in range(4):
-        face_refs[face][...] = image[face * rows : (face + 1) * rows, :]
-    minus, plus = image[4 * rows : 5 * rows, :], image[5 * rows :, :]
-    if pair_depth:
-        face_refs[4][:rows, :] = jnp.where(lax.axis_index("depth") == 0, plus, minus)
-    else:
-        face_refs[4][...] = minus
-        face_refs[5][...] = plus
-
-
-def got_face(refs, face, rows, pair_depth):
-    if face < 4 or not pair_depth:
-        return refs[face][...]
-    there = 1 if face == 4 else 0
-    return jnp.where(lax.axis_index("depth") == there, refs[4][:rows, :], 0.0)
-
-
-def image_kernel(pair_depth, count, *refs):
-    returned, refs = refs[:count], refs[count:]
-    (table_ref, basis_ref, local_ref, image_ref, sums_ref), face_refs = refs[:5], refs[5:]
+AXIS_AT = {"blk": 0, "lat": 2, "depth": 4}
+
+
+def swaps():
+    order = [("blk", 0), ("lat", 1), ("blk", 1), ("lat", 0), ("depth", 0), ("depth", 1)]
+    return [(axis, odd) for axis, odd in order if pairs(axis, odd)]
+
+
+def pairs(axis, odd):
+    devices = lax.axis_size(axis)
+    ends = [(i, i + 1) for i in range(odd, devices - 1, 2)]
+    if axis == "blk" and odd:
+        ends.append((devices - 1, 0))
+    return [pair for i, j in ends for pair in ((i, j), (j, i))]
+
+
+def sends_plus(axis, odd):
+    return lax.rem(lax.axis_index(axis), 2) == odd
+
+
+def put_faces(image, rows, face_refs):
+    for ref, (axis, odd) in zip(face_refs, swaps(), strict=True):
+        at = AXIS_AT[axis] * rows
+        minus, plus = image[at : at + rows, :], image[at + rows : at + 2 * rows, :]
+        ref[:rows, :] = jnp.where(sends_plus(axis, odd), plus, minus)
+
+
+def got_face(refs, face, rows):
+    axis = ("blk", "lat", "depth")[face // 2]
+    total = None
+    for ref, (axis_of, odd) in zip(refs, swaps(), strict=True):
+        if axis_of == axis:
+            mine = sends_plus(axis, odd) == (face % 2 == 1)
+            piece = jnp.where(mine, ref[:rows, :], 0.0)
+            total = piece if total is None else total + piece
+    return total
+
+
+def exchange(faces):
+    return [
+        lax.ppermute(block, axis, pairs(axis, odd))
+        for block, (axis, odd) in zip(faces, swaps(), strict=True)
+    ]
+
+
+def image_kernel(pair_depth, returned_ref, table_ref, high_ref, low_ref, local_ref, image_ref, sums_ref, *face_refs):
     rows = local_ref.shape[0] // 6
     width = local_ref.shape[1]
-    pieces = width // LANES // count
-    terms = jnp.concatenate([get_slab(ref, pieces) for ref in returned], axis=1)
-    correction = select(table_ref[...], terms)
-    image = local_ref[...] + product(basis_ref[...], correction)
+    folds = width // LANES
+    correction = select(table_ref[...], get_slab(returned_ref, folds))
+    image = local_ref[...] + product((high_ref[...], low_ref[...]), parts(correction))
     image_ref[...] = image
-    put_faces(image, rows, pair_depth, face_refs)
-    tail = jnp.sum(returned[-1][:, pieces * CAP :, :], axis=0)
+    put_faces(image, rows, face_refs)
+    tail = jnp.sum(returned_ref[:, folds * CAP :, :], axis=0)
     if pair_depth:
-        folds = width // LANES
         sums = jnp.concatenate(
             [unfolded(tail, 0, folds), unfolded(tail, folds, folds)]
             + [jnp.zeros((TILE - 2, width), f32)],
             axis=0,
         )
         sums_ref[...] = sums
-        face_refs[4][rows:, :] = sums
+        face_refs[-1][rows:, :] = sums
     else:
         sums_ref[...] = jnp.broadcast_to(tail[None], sums_ref.shape)
 
 
-def direction_kernel(pair_depth, faces, scale, len_ref, sums_ref, prev_rho_ref, image_ref, prev_ref, schur_ref, *refs):
+def direction_kernel(pair_depth, scale, len_ref, sums_ref, prev_rho_ref, image_ref, prev_ref, high_ref, low_ref, *refs):
+    faces = len(swaps())
     got, refs = refs[:faces], refs[faces:]
     (direction_out, rho_out, square_out, schur_out), refs = refs[:4], refs[4:]
     face_refs, (direction_ref, sem) = refs[:faces], refs[faces:]
     rows = image_ref.shape[0] // 6
     width = image_ref.shape[1]
     if pair_depth:
-        sums = sums_ref[...] + got[4][rows:, :]
+        sums = sums_ref[...] + got[-1][rows:, :]
         rho, square = sums[0:1, :], sums[1:2, :]
     else:
         folds = width // LANES
@@ -292,15 +301,15 @@
     beta = rho / prev_rho_ref[...]
     for face in range(6):
         at = slice(face * rows, (face + 1) * rows)
-        precond = 0.5 * (image_ref[at, :] + got_face(got, face, rows, pair_depth))
+        precond = 0.5 * (image_ref[at, :] + got_face(got, face, rows))
         direction_ref[at, :] = jnp.where(
             live_rows(len_ref, face, rows), precond + beta * prev_ref[at, :], 0.0
         )
     copy = pltpu.make_async_copy(direction_ref, direction_out, sem)
     copy.start()
-    image = product(schur_ref[...], direction_ref[...])
+    image = product((high_ref[...], low_ref[...]), parts(direction_ref[...]))
     schur_out[...] = image
-    put_faces(image, rows, pair_depth, face_refs)
+    put_faces(image, rows, face_refs)
     copy.wait()
 
 
@@ -314,13 +323,13 @@
     cross_ref[...] = 2.0 * jnp.sum(live * image, axis=0, keepdims=True)
 
 
-def applied_kernel(pair_depth, faces, len_ref, curve_ref, cross_ref, schur_ref, *refs):
-    got, (applied_ref, spread_ref) = refs[:faces], refs[faces:]
+def applied_kernel(len_ref, curve_ref, cross_ref, schur_ref, *refs):
+    got, (applied_ref, spread_ref) = refs[:-2], refs[-2:]
     rows = schur_ref.shape[0] // 6
     total = jnp.zeros(curve_ref.shape, f32)
     for face in range(6):
         at = slice(face * rows, (face + 1) * rows)
-        applied = schur_ref[at, :] + got_face(got, face, rows, pair_depth)
+        applied = schur_ref[at, :] + got_face(got, face, rows)
         applied = jnp.where(live_rows(len_ref, face, rows), applied, 0.0)
         applied_ref[at, :] = applied
         total += jnp.sum(applied * applied, axis=0, keepdims=True)
@@ -346,30 +355,6 @@
         copies[-1].start()
     for copy in copies:
         copy.wait()
-
-
-def around(x, axis, by):
-    devices = lax.axis_size(axis)
-    return lax.ppermute(x, axis, [(i, (i + by) % devices) for i in range(devices)])
-
-
-def along(x, axis, by):
-    devices = range(lax.axis_size(axis))
-    return lax.ppermute(x, axis, [(i - by, i) for i in devices if i - by in devices])
-
-
-def exchange(faces, pair_depth):
-    got = [
-        around(faces[1], "blk", 1),
-        around(faces[0], "blk", -1),
-        along(faces[3], "lat", 1),
-        along(faces[2], "lat", -1),
-    ]
-    if pair_depth:
-        got.append(lax.ppermute(faces[4], "depth", [(0, 1), (1, 0)]))
-    else:
-        got += [along(faces[5], "depth", 1), along(faces[4], "depth", -1)]
-    return got
 
 
 def to_all(x, axes):
@@ -397,11 +382,8 @@
     devices = lax.axis_size(AXES)
     layers = lax.axis_size("depth")
     pair_depth = layers == 2
-    faces = 5 if pair_depth else 6
     scale = 0.5 / (devices * height)
-    count = PARTS
     folds = width // LANES
-    pieces = folds // count
     tail = tiles(2 * folds)
 
     lengths = face_len.reshape(6)
@@ -415,15 +397,11 @@
     wanted = coarse_row.reshape(1, primal)
     whole = shape_of(height, width)
     row = shape_of(1, width)
-    part_row = shape_of(1, width // count)
     face = shape_of(rows, width)
 
-    *outgoing, table = call(
-        functools.partial(pack_kernel, count),
-        [
-            shape_of(owners, pieces * CAP + (0 if i else TILE), LANES) for i in range(count)
-        ]
-        + [shape_of(primal, slots, dtype=bf16)],
+    (outgoing,) = call(
+        pack_kernel,
+        [shape_of(owners, folds * CAP + TILE, LANES)],
         [lengths, owner, wanted, residual, basis],
         far=range(5),
         flops=6 * height * primal * width,
@@ -439,62 +417,52 @@
         ],
         room=60,
     )
-    incoming = [to_all(x, LAYER) for x in outgoing]
-    local, local_part, square = call(
-        neumann_kernel,
-        [whole, row, row],
-        [lengths, residual, neumann],
+    incoming = to_all(outgoing, LAYER)
+    local, local_part, square, table, *halves = call(
+        local_kernel,
+        [whole, row, row, shape_of(primal, slots, dtype=bf16)]
+        + [shape_of(height, primal, dtype=bf16)] * 2
+        + [shape_of(owned, owned, dtype=bf16)] * 2
+        + [shape_of(height, height, dtype=bf16)] * 2,
+        [lengths, residual, neumann, owner, basis, inverse, schur],
         smem=(0,),
         flops=6 * height * height * width,
-        moved=4 * height * (height + 2 * width),
-    )
-    picker, before, returned = None, [], []
-    for i in range(count):
-        last = i == count - 1
-        operands = [incoming[i], inverse] + ([picker] if i else []) + before
-        outs = [shape_of(owners, pieces * CAP + (tail if last else 0), LANES)]
-        if last:
-            operands += [local_part, square]
-        else:
-            outs.append(part_row)
-            if i == 0:
-                outs.append(shape_of(slots, owned))
-        got = call(
-            functools.partial(solve_kernel, i, count),
-            outs,
-            operands,
-            flops=(8 * slots + 6 * owned) * owned * width // count,
-            moved=8 * slots * width // count,
-        )
-        returned.append(to_all(got[0], LAYER))
-        if not last:
-            before.append(got[1])
-            if i == 0:
-                picker = got[2]
-    extra = TILE if pair_depth else 0
+        moved=4 * height * (3 * height + 2 * width),
+    )
+    basis_halves, inverse_halves, schur_halves = halves[:2], halves[2:4], halves[4:]
+    (answers,) = call(
+        solve_kernel,
+        [shape_of(owners, folds * CAP + tail, LANES)],
+        [incoming, *inverse_halves, local_part, square],
+        flops=(8 * slots + 6 * owned) * owned * width,
+        moved=8 * slots * width,
+    )
+    returned = to_all(answers, LAYER)
+    faces = len(swaps())
+    last = shape_of(rows + TILE, width) if pair_depth else face
     image, sums, *outward = call(
-        functools.partial(image_kernel, pair_depth, count),
+        functools.partial(image_kernel, pair_depth),
         [whole, shape_of(TILE, width) if pair_depth else shape_of(layers, tail, LANES)]
-        + [face] * 4
-        + ([shape_of(rows + extra, width)] if pair_depth else [face] * 2),
-        [*returned, table, basis, local],
+        + [face] * (faces - 1)
+        + [last],
+        [returned, table, *basis_halves, local],
         flops=(6 * height + 4 * slots) * primal * width,
         moved=16 * height * width,
     )
     if not pair_depth:
         sums = to_all(sums, "depth")
-    got = exchange(outward, pair_depth)
+    got = exchange(outward)
     direction, rho, square, schur_image, *outward = call(
-        functools.partial(direction_kernel, pair_depth, faces, scale),
+        functools.partial(direction_kernel, pair_depth, scale),
         [whole, row, row, whole] + [face] * faces,
-        [lengths, sums, prev_rho.reshape(1, width), image, prev_direction, schur, *got],
+        [lengths, sums, prev_rho.reshape(1, width), image, prev_direction, *schur_halves, *got],
         smem=(0,),
         far_out=(0,),
         flops=6 * height * height * width,
         moved=4 * height * (height + 6 * width),
         scratch=[pltpu.VMEM((height, width), f32), pltpu.SemaphoreType.DMA],
     )
-    got = exchange(outward, pair_depth)
+    got = exchange(outward)
     curve, cross = call(
         products_kernel,
         [row, row],
@@ -504,7 +472,7 @@
         moved=12 * height * width,
     )
     applied, spread = call(
-        functools.partial(applied_kernel, pair_depth, faces),
+        applied_kernel,
         [whole, shape_of(devices, 3, folds, LANES)],
         [lengths, curve, cross, schur_image, *got],
         smem=(0,),

time: 134 us -> 120 us (0.90)
  blocking collectives: 49.2 us -> 38.4 us
  waiting for transfers between devices: 32.5 us -> 24.6 us
  local copies, waits for them, and re-layouts: 7.34 us -> 13.2 us
    all_to_all x3 -> x2, blocking collectives: 49.2 us -> 38.4 us  [to_all(): return lax.all_to_all(x, axes, split_axis=0, concat_axis=0, tiled=True)]
    all_to_all x2 -> x1, waiting for transfers between devices: 13.7 us -> 7.47 us  [to_all(): return lax.all_to_all(x, axes, split_axis=0, concat_axis=0, tiled=True)]
    unnamed x30 -> x50, local copies, waits for them, and re-layouts: 7.34 us -> 13.2 us
    ppermute x10, waiting for transfers between devices: 18.8 us -> 17.1 us  [exchange(): lax.ppermute(block, axis, pairs(axis, odd))]
    pallas_call x9 -> x8, Pallas kernels: 19.7 us -> 19.2 us  [call(): pl.pallas_call(body, out_shape=list(outs), in_specs=in_specs, out_specs=o...]
    all_to_all x2 -> x1, starting transfers between devices: 8.1 us -> 8.5 us  [to_all(): return lax.all_to_all(x, axes, split_axis=0, concat_axis=0, tiled=True)]
  transfers between devices with their start and end apart: 12 -> 11, of which waited for: 8 -> 6; matrix products, arithmetic and copies ran while one was open for 0% -> 0% of each run, Pallas kernels for 5% -> 4%
where the time goes in v3:
time: 120 us; the launch traced here: 119 us
  blocking collectives  38.4 us (32%)
  waiting for transfers between devices  24.6 us (20%)
  starting transfers between devices  22.7 us (19%)
  Pallas kernels  19.2 us (16%)
  local copies, waits for them, and re-layouts  13.2 us (11%)
    all_to_all x2, blocking collectives, to_all(): return lax.all_to_all(x, axes, split_axis=0, concat_axis=0, tiled=True)  38.4 us
    pallas_call x8, Pallas kernels, call(): pl.pallas_call(body, out_shape=list(outs), in_specs=in_specs, out_specs=o...  19.2 us
    ppermute x10, waiting for transfers between devices, exchange(): lax.ppermute(block, axis, pairs(axis, odd))  17.1 us
    ppermute x10, starting transfers between devices, exchange(): lax.ppermute(block, axis, pairs(axis, odd))  14.2 us
    unnamed x50, local copies, waits for them, and re-layouts  13.2 us
    all_to_all x1, starting transfers between devices, to_all(): return lax.all_to_all(x, axes, split_axis=0, concat_axis=0, tiled=True)  8.5 us
    all_to_all x1, waiting for transfers between devices, to_all(): return lax.all_to_all(x, axes, split_axis=0, concat_axis=0, tiled=True)  7.47 us
  transfers between devices with their start and end apart: 11, of which 6 were waited for; matrix products, arithmetic and copies ran while one was open for 0% of the time, Pallas kernels for 4%

profile of v3, /device:TPU:0, one launch (start us, length us, event | category | flops | bytes accessed | tf_op | source)
XLA Modules:
  0.0 119.0 jit_solution(18079733450221247293)
XLA Ops:
  0.6 4.1 %shard_map.137 = f32[16,104,128]{2,1,0:T(8,128)} custom-call(s32[6]{0:T(128)} %bitcast.26, s32[1,256]{1,0:T(1,128)} %bitcast.32, s32[1,256]{1,0:T(1,128)} %bitcast.36, f32[768,512]{1,0:T(8,128)} %bitcast.15, f32[768,256]{1,0:T(8,128)} %bitcast.19), custom_call_target="tpu_custom_call" | custom-call | flops 603979776 | bytes 3145728 | tf_op jit(solution)/shard_map/pallas_call | solution.py:30
  4.8 8.5 %all-to-all-start = ((f32[16,104,128]{2,1,0:T(8,128)}), f32[16,104,128]{2,1,0:T(8,128)}, u32[]{:S(2)}, u32[]{:S(2)}) async-start(f32[16,104,128]{2,1,0:T(8,128)} %shard_map.137), calls=%async_computation | async-start | bytes 1703936 | tf_op jit(solution)/shard_map/all_to_all | solution.py:361
  13.3 1.7 %copy-done.2 = f32[1,1,1,768,768]{4,3,2,1,0:T(8,128)S(1)} copy-done((f32[1,1,1,768,768]{4,3,2,1,0:T(8,128)S(1)}, f32[1,1,1,768,768]{4,3,2,1,0:T(8,128)}, u32[]{:S(2)}) %copy-start.2) | copy-done | bytes 2359320
  15.0 1.7 %copy-done.3 = f32[1,1,1,768,768]{4,3,2,1,0:T(8,128)S(1)} copy-done((f32[1,1,1,768,768]{4,3,2,1,0:T(8,128)S(1)}, f32[1,1,1,768,768]{4,3,2,1,0:T(8,128)}, u32[]{:S(2)}) %copy-start.3) | copy-done | bytes 2359320
  17.6 3.5 %shard_map.138 = (f32[768,512]{1,0:T(8,128)S(1)}, f32[1,512]{1,0:T(1,128)S(1)}, f32[1,512]{1,0:T(1,128)S(1)}, bf16[256,384]{1,0:T(8,128)(2,1)S(1)}, bf16[768,256...) custom-call(s32[6]{0:T(128)S(1)} %bitcast.27, ...), custom_call_target="tpu_custom_call" | custom-call | flops 1811939328 | bytes 10223616 | tf_op jit(solution)/shard_map/pallas_call | solution.py:30
  21.1 1.1 copy-done.6
  26.8 7.5 %all-to-all-done.incoming_ref = f32[16,104,128]{2,1,0:T(8,128)} async-done(((f32[16,104,128]{2,1,0:T(8,128)}), f32[16,104,128]{2,1,0:T(8,128)}, u32[]{:S(2)}, u32[]{:S(2)}) %all-to-all-start) | async-done | bytes 852000 | tf_op jit(solution)/shard_map/all_to_all | solution.py:361
  36.1 2.6 %shard_map.139 = f32[16,104,128]{2,1,0:T(8,128)S(1)} custom-call(f32[16,104,128]{2,1,0:T(8,128)} %all-to-all-done.incoming_ref, bf16[256,256]{1,0:T(8,128)(2,1)S(1)} %copy-done.22, bf16[256,256]{1,0:T(8,128)(2,1)S(1)} %copy-done.24, f32[1,512]{1,0:T(1,128)S(1)} %get-tuple-element.40.local_part_ref, f32[1,512]{1,0:T(1,128)S(1)} %get-tuple-element.41.square_ref), custom_call_target="tpu_custom_call" | custom-call | flops 603979776 | bytes 1572864 | tf_op jit(solution)/shard_map/pallas_call | solution.py:30
  38.6 26.4 %all_to_all.15.returned_ref = f32[16,104,128]{2,1,0:T(8,128)S(1)} all-to-all(f32[16,104,128]{2,1,0:T(8,128)S(1)} %shard_map.139), channel_id=1, replica_groups=mesh['blk'=4,'lat'=4,'depth'=2] {'blk','lat'}, dimensions={0} | all-to-all | bytes 1703936 | tf_op jit(solution)/shard_map/all_to_all | solution.py:361
  65.1 1.2 %shard_map.140 = (f32[768,512]{1,0:T(8,128)S(1)}, f32[8,512]{1,0:T(8,128)S(1)}, f32[128,512]{1,0:T(8,128)S(1)}, f32[128,512]{1,0:T(8,128)S(1)}, f32[128,512]{1,0...) custom-call(f32[16,104,128]{2,1,0:T(8,128)S(1)} %all_to_all.15.returned_ref, ...), custom_call_target="tpu_custom_call" | custom-call | flops 805306368 | bytes 6291456 | tf_op jit(solution)/shard_map/pallas_call | solution.py:30
  69.2 3.5 %collective-permute-start.3 = (f32[128,512]{1,0:T(8,128)S(1)}, f32[128,512]{1,0:T(8,128)S(1)}, u32[]{:S(2)}, u32[]{:S(2)}) collective-permute-start(f32[128,512]{1,0:T(8,128)S(1)} %get-tuple-element.53), channel_id=1, source_target_pairs={{0,2},{2,0},{4,6},{6,4},{1,3},{3,1},{5,7},{7,5},{8,10},{10,8},{12,... | collective-permute-start | bytes 786440 | tf_op jit(solution)/shard_map/ppermute | solution.py:258
  72.7 2.9 %collective-permute-done.refs_0_ = f32[128,512]{1,0:T(8,128)S(1)} collective-permute-done((f32[128,512]{1,0:T(8,128)S(1)}, f32[128,512]{1,0:T(8,128)S(1)}, u32[]{:S(2)}, u32[]{:S(2)}) %collective-permute-start) | collective-permute-done | bytes 262176 | tf_op jit(solution)/shard_map/ppermute | solution.py:258
  75.6 5.2 %collective-permute-done.2.refs_2_ = f32[128,512]{1,0:T(8,128)S(1)} collective-permute-done((f32[128,512]{1,0:T(8,128)S(1)}, f32[128,512]{1,0:T(8,128)S(1)}, u32[]{:S(2)}, u32[]{:S(2)}) %collective-permute-start.2) | collective-permute-done | bytes 262176 | tf_op jit(solution)/shard_map/ppermute | solution.py:258
  80.8 2.7 %collective-permute-done.3.refs_3_ = f32[128,512]{1,0:T(8,128)S(1)} collective-permute-done((f32[128,512]{1,0:T(8,128)S(1)}, f32[128,512]{1,0:T(8,128)S(1)}, u32[]{:S(2)}, u32[]{:S(2)}) %collective-permute-start.3) | collective-permute-done | bytes 262176 | tf_op jit(solution)/shard_map/ppermute | solution.py:258
  83.6 3.4 %shard_map.141 = (f32[768,512]{1,0:T(8,128)}, f32[1,512]{1,0:T(1,128)}, f32[1,512]{1,0:T(1,128)S(1)}, f32[768,512]{1,0:T(8,128)S(1)}, f32[128,512]{1,0:T(8,128)S...) custom-call(s32[6]{0:T(128)S(1)} %bitcast.28, ...), custom_call_target="tpu_custom_call" | custom-call | flops 1811939328 | bytes 11796480 | tf_op jit(solution)/shard_map/pallas_call | solution.py:30
  87.0 1.1 collective-permute-start.5
  88.7 2.0 %collective-permute-start.7 = (f32[128,512]{1,0:T(8,128)S(1)}, f32[128,512]{1,0:T(8,128)S(1)}, u32[]{:S(2)}, u32[]{:S(2)}) collective-permute-start(f32[128,512]{1,0:T(8,128)S(1)} %get-tuple-element.61), channel_id=1, source_target_pairs={{8,16},{16,8},{24,0},{0,24},{9,17},{17,9},{25,1},{1,25},{10,18},{1... | collective-permute-start | bytes 786440 | tf_op jit(solution)/shard_map/ppermute | solution.py:258
  90.7 4.1 %collective-permute-start.8 = (f32[128,512]{1,0:T(8,128)S(1)}, f32[128,512]{1,0:T(8,128)S(1)}, u32[]{:S(2)}, u32[]{:S(2)}) collective-permute-start(f32[128,512]{1,0:T(8,128)S(1)} %get-tuple-element.62), channel_id=1, source_target_pairs={{0,2},{2,0},{4,6},{6,4},{1,3},{3,1},{5,7},{7,5},{8,10},{10,8},{12,... | collective-permute-start | bytes 786440 | tf_op jit(solution)/shard_map/ppermute | solution.py:258
  94.8 1.4 %copy-done.4 = f32[768,512]{1,0:T(8,128)S(1)} copy-done((f32[768,512]{1,0:T(8,128)S(1)}, f32[768,512]{1,0:T(8,128)}, u32[]{:S(2)}) %copy-start.4) | copy-done | bytes 1572888
  96.2 1.1 shard_map.142
  97.3 3.9 %collective-permute-done.7.refs_2_ = f32[128,512]{1,0:T(8,128)S(1)} collective-permute-done((f32[128,512]{1,0:T(8,128)S(1)}, f32[128,512]{1,0:T(8,128)S(1)}, u32[]{:S(2)}, u32[]{:S(2)}) %collective-permute-start.7) | collective-permute-done | bytes 262176 | tf_op jit(solution)/shard_map/ppermute | solution.py:258
  101.2 2.4 %collective-permute-done.8.refs_3_ = f32[128,512]{1,0:T(8,128)S(1)} collective-permute-done((f32[128,512]{1,0:T(8,128)S(1)}, f32[128,512]{1,0:T(8,128)S(1)}, u32[]{:S(2)}, u32[]{:S(2)}) %collective-permute-start.8) | collective-permute-done | bytes 262176 | tf_op jit(solution)/shard_map/ppermute | solution.py:258
  104.6 12.1 %all_to_all.16.sums_ref = f32[32,3,4,128]{3,2,1,0:T(4,128)S(1)} all-to-all(f32[32,3,4,128]{3,2,1,0:T(4,128)S(1)} %get-tuple-element.64), channel_id=1, replica_groups=mesh['blk'=4,'lat'=4,'depth'=2] {'blk','lat','depth'}, dimensions={0} | all-to-all | bytes 393216 | tf_op jit(solution)/shard_map/all_to_all | solution.py:361
  116.6 2.4 %shard_map.144 = (f32[768,512]{1,0:T(8,128)}, f32[1,512]{1,0:T(1,128)}, f32[1,512]{1,0:T(1,128)}) custom-call(s32[6]{0:T(128)S(1)} %bitcast.31, f32[32,3,4,128]{3,2,1,0:T(4,128)S(1)} %all_to_all.16.sums_ref, f32[1,512]{1,0:T(1,128)S(1)} %copy-done.20, f32[1,512]{1,0:T(1,128)S(1)} %get-tuple-element.66.square_ref, f32[768,512]{1,0:T(8,128)S(1)} %bitcast.18, ...), custom_call_target="tpu_custom_call" | custom-call | flops 1572864 | bytes 4718592 | tf_op jit(solution)/shard_map/pallas_call | solution.py:30
  (58 shorter events, 11.9 us)
Async XLA Ops:
  0.6 12.6 %copy-start.1 = (f32[1,1,1,768,256]{4,3,2,1,0:T(8,128)S(1)}, f32[1,1,1,768,256]{4,3,2,1,0:T(8,128)}, u32[]{:S(2)}) copy-start(f32[1,1,1,768,256]{4,3,2,1,0:T(8,128)} %param.16) | copy-start | bytes 2359300
  4.7 8.6 %copy-start = (f32[1,1,1,768,512]{4,3,2,1,0:T(8,128)S(1)}, f32[1,1,1,768,512]{4,3,2,1,0:T(8,128)}, u32[]{:S(2)}) copy-start(f32[1,1,1,768,512]{4,3,2,1,0:T(8,128)} %param.11) | copy-start | bytes 4718596
  4.7 8.6 %copy-start.17 = (s32[1,1,1,6]{3,2,1,0:T(1,128)S(1)}, s32[1,1,1,6]{3,2,1,0:T(1,128)}, u32[]{:S(2)}) copy-start(s32[1,1,1,6]{3,2,1,0:T(1,128)} %param.10) | copy-start | bytes 76
  4.7 8.6 %copy-start.18 = (s32[1,1,1,256,1]{3,4,2,1,0:T(1,128)S(1)}, s32[1,1,1,256,1]{3,4,2,1,0:T(1,128)}, u32[]{:S(2)}) copy-start(s32[1,1,1,256,1]{3,4,2,1,0:T(1,128)} %param.18) | copy-start | bytes 3076
  4.8 29.5 %all-to-all-start = ((f32[16,104,128]{2,1,0:T(8,128)}), f32[16,104,128]{2,1,0:T(8,128)}, u32[]{:S(2)}, u32[]{:S(2)}) async-start(f32[16,104,128]{2,1,0:T(8,128)} %shard_map.137), calls=%async_computation | async-start | bytes 1703936 | tf_op jit(solution)/shard_map/all_to_all | solution.py:361
  13.3 1.7 %copy-start.2 = (f32[1,1,1,768,768]{4,3,2,1,0:T(8,128)S(1)}, f32[1,1,1,768,768]{4,3,2,1,0:T(8,128)}, u32[]{:S(2)}) copy-start(f32[1,1,1,768,768]{4,3,2,1,0:T(8,128)} %param.15) | copy-start | bytes 7077892
  36.0 29.0 %copy-start.7 = (f32[768,512]{1,0:T(8,128)S(1)}, f32[768,512]{1,0:T(8,128)}, u32[]{:S(2)}) copy-start(f32[768,512]{1,0:T(8,128)} %copy-done.6) | copy-start | bytes 4718596
  36.1 29.0 %copy-start.11 = (bf16[768,256]{1,0:T(8,128)(2,1)S(1)}, bf16[768,256]{1,0:T(8,128)(2,1)}, u32[]{:S(2)}) copy-start(bf16[768,256]{1,0:T(8,128)(2,1)} %copy-done.10) | copy-start | bytes 1179652
  36.1 29.0 %copy-start.13 = (bf16[768,256]{1,0:T(8,128)(2,1)S(1)}, bf16[768,256]{1,0:T(8,128)(2,1)}, u32[]{:S(2)}) copy-start(bf16[768,256]{1,0:T(8,128)(2,1)} %copy-done.12) | copy-start | bytes 1179652
  36.1 29.0 %copy-start.16 = (bf16[256,384]{1,0:T(8,128)(2,1)S(1)}, bf16[256,384]{1,0:T(8,128)(2,1)}, u32[]{:S(2)}) copy-start(bf16[256,384]{1,0:T(8,128)(2,1)} %copy-done.15) | copy-start | bytes 589828
  65.0 18.5 %copy-start.5 = (f32[1,1,1,768,512]{4,3,2,1,0:T(8,128)S(1)}, f32[1,1,1,768,512]{4,3,2,1,0:T(8,128)}, u32[]{:S(2)}) copy-start(f32[1,1,1,768,512]{4,3,2,1,0:T(8,128)} %param.12) | copy-start | bytes 4718596
  65.0 18.5 %copy-start.9 = (bf16[768,768]{1,0:T(8,128)(2,1)S(1)}, bf16[768,768]{1,0:T(8,128)(2,1)}, u32[]{:S(2)}) copy-start(bf16[768,768]{1,0:T(8,128)(2,1)} %copy-done.8) | copy-start | bytes 3538948
  65.1 18.5 %copy-start.19 = (f32[512]{0:T(512)S(1)}, f32[512]{0:T(512)}, u32[]{:S(2)}) copy-start(f32[512]{0:T(512)} %param.13) | copy-start | bytes 6148
  66.3 17.2 %collective-permute-start.4 = (f32[136,512]{1,0:T(8,128)S(1)}, f32[136,512]{1,0:T(8,128)S(1)}, u32[]{:S(2)}, u32[]{:S(2)}) collective-permute-start(f32[136,512]{1,0:T(8,128)S(1)} %get-tuple-element.54), channel_id=1, source_target_pairs={{0,1},{1,0},{2,3},{3,2},{4,5},{5,4},{6,7},{7,6},{8,9},{9,8},{10,11... | collective-permute-start | bytes 835592 | tf_op jit(solution)/shard_map/ppermute | solution.py:258
  66.4 9.2 %collective-permute-start = (f32[128,512]{1,0:T(8,128)S(1)}, f32[128,512]{1,0:T(8,128)S(1)}, u32[]{:S(2)}, u32[]{:S(2)}) collective-permute-start(f32[128,512]{1,0:T(8,128)S(1)} %get-tuple-element.50), channel_id=1, source_target_pairs={{0,8},{8,0},{16,24},{24,16},{1,9},{9,1},{17,25},{25,17},{2,10},{10... | collective-permute-start | bytes 786440 | tf_op jit(solution)/shard_map/ppermute | solution.py:258
  67.5 8.1 %collective-permute-start.1 = (f32[128,512]{1,0:T(8,128)S(1)}, f32[128,512]{1,0:T(8,128)S(1)}, u32[]{:S(2)}, u32[]{:S(2)}) collective-permute-start(f32[128,512]{1,0:T(8,128)S(1)} %get-tuple-element.51), channel_id=1, source_target_pairs={{2,4},{4,2},{3,5},{5,3},{10,12},{12,10},{11,13},{13,11},{18,20},{2... | collective-permute-start | bytes 786440 | tf_op jit(solution)/shard_map/ppermute | solution.py:258
  68.1 12.7 %collective-permute-start.2 = (f32[128,512]{1,0:T(8,128)S(1)}, f32[128,512]{1,0:T(8,128)S(1)}, u32[]{:S(2)}, u32[]{:S(2)}) collective-permute-start(f32[128,512]{1,0:T(8,128)S(1)} %get-tuple-element.52), channel_id=1, source_target_pairs={{8,16},{16,8},{24,0},{0,24},{9,17},{17,9},{25,1},{1,25},{10,18},{1... | collective-permute-start | bytes 786440 | tf_op jit(solution)/shard_map/ppermute | solution.py:258
  69.2 14.4 %collective-permute-start.3 = (f32[128,512]{1,0:T(8,128)S(1)}, f32[128,512]{1,0:T(8,128)S(1)}, u32[]{:S(2)}, u32[]{:S(2)}) collective-permute-start(f32[128,512]{1,0:T(8,128)S(1)} %get-tuple-element.53), channel_id=1, source_target_pairs={{0,2},{2,0},{4,6},{6,4},{1,3},{3,1},{5,7},{7,5},{8,10},{10,8},{12,... | collective-permute-start | bytes 786440 | tf_op jit(solution)/shard_map/ppermute | solution.py:258
  87.0 10.3 %collective-permute-start.5 = (f32[128,512]{1,0:T(8,128)S(1)}, f32[128,512]{1,0:T(8,128)S(1)}, u32[]{:S(2)}, u32[]{:S(2)}) collective-permute-start(f32[128,512]{1,0:T(8,128)S(1)} %get-tuple-element.59), channel_id=1, source_target_pairs={{0,8},{8,0},{16,24},{24,16},{1,9},{9,1},{17,25},{25,17},{2,10},{10... | collective-permute-start | bytes 786440 | tf_op jit(solution)/shard_map/ppermute | solution.py:258
  88.1 9.2 %collective-permute-start.6 = (f32[128,512]{1,0:T(8,128)S(1)}, f32[128,512]{1,0:T(8,128)S(1)}, u32[]{:S(2)}, u32[]{:S(2)}) collective-permute-start(f32[128,512]{1,0:T(8,128)S(1)} %get-tuple-element.60), channel_id=1, source_target_pairs={{2,4},{4,2},{3,5},{5,3},{10,12},{12,10},{11,13},{13,11},{18,20},{2... | collective-permute-start | bytes 786440 | tf_op jit(solution)/shard_map/ppermute | solution.py:258
  88.7 12.5 %collective-permute-start.7 = (f32[128,512]{1,0:T(8,128)S(1)}, f32[128,512]{1,0:T(8,128)S(1)}, u32[]{:S(2)}, u32[]{:S(2)}) collective-permute-start(f32[128,512]{1,0:T(8,128)S(1)} %get-tuple-element.61), channel_id=1, source_target_pairs={{8,16},{16,8},{24,0},{0,24},{9,17},{17,9},{25,1},{1,25},{10,18},{1... | collective-permute-start | bytes 786440 | tf_op jit(solution)/shard_map/ppermute | solution.py:258
  90.7 12.9 %collective-permute-start.8 = (f32[128,512]{1,0:T(8,128)S(1)}, f32[128,512]{1,0:T(8,128)S(1)}, u32[]{:S(2)}, u32[]{:S(2)}) collective-permute-start(f32[128,512]{1,0:T(8,128)S(1)} %get-tuple-element.62), channel_id=1, source_target_pairs={{0,2},{2,0},{4,6},{6,4},{1,3},{3,1},{5,7},{7,5},{8,10},{10,8},{12,... | collective-permute-start | bytes 786440 | tf_op jit(solution)/shard_map/ppermute | solution.py:258
  94.8 8.8 %collective-permute-start.9 = (f32[128,512]{1,0:T(8,128)S(1)}, f32[128,512]{1,0:T(8,128)S(1)}, u32[]{:S(2)}, u32[]{:S(2)}) collective-permute-start(f32[128,512]{1,0:T(8,128)S(1)} %get-tuple-element.63), channel_id=1, source_target_pairs={{0,1},{1,0},{2,3},{3,2},{4,5},{5,4},{6,7},{7,6},{8,9},{9,8},{10,11... | collective-permute-start | bytes 786440 | tf_op jit(solution)/shard_map/ppermute | solution.py:258
  103.6 13.1 %copy-start.20 = (f32[1,512]{1,0:T(1,128)S(1)}, f32[1,512]{1,0:T(1,128)}, u32[]{:S(2)}) copy-start(f32[1,512]{1,0:T(1,128)} %get-tuple-element.65.rho_ref) | copy-start | bytes 6148
  (12 other events, 11.5 us)

commit v4 on v3

--- a/solution.py
+++ b/solution.py
@@ -54,12 +54,16 @@
 
 def product(a, b, dims=PLAIN):
     (ah, al), (bh, bl) = a, b
-    return mul(ah, bh, dims) + (mul(ah, bl, dims) + mul(al, bh, dims))
+    (along_a,), (along_b,) = dims
+    left = jnp.concatenate([ah, ah, al], axis=along_a)
+    right = jnp.concatenate([bh, bl, bh], axis=along_b)
+    return mul(left, right, dims)
 
 
 def select(table, x, dims=PLAIN):
-    high, low = parts(x)
-    return mul(table, high, dims) + mul(table, low, dims)
+    (along_a,), (along_b,) = dims
+    left = jnp.concatenate([table, table], axis=along_a)
+    return mul(left, jnp.concatenate(parts(x), axis=along_b), dims)
 
 
 def one_hot(hit):
@@ -164,7 +168,7 @@
 
 
 def local_kernel(len_ref, residual_ref, matrix_ref, owner_ref, *refs):
-    whole, refs = refs[:3], refs[3:]
+    whole, refs = refs[:2], refs[2:]
     local_ref, part_ref, square_ref, table_ref, refs = *refs[:4], refs[4:]
     rows = residual_ref.shape[0] // 6
     live = jnp.concatenate(
@@ -174,7 +178,7 @@
     local_ref[...] = local
     part_ref[...] = jnp.sum(live * local, axis=0, keepdims=True)
     square_ref[...] = jnp.sum(live * live, axis=0, keepdims=True)
-    for i in range(3):
+    for i in range(2):
         refs[2 * i][...], refs[2 * i + 1][...] = parts(whole[i][...])
     primal, slots = table_ref.shape
     row_at = lax.broadcasted_iota(jnp.int32, (primal, primal), 0)
@@ -187,25 +191,44 @@
     table_ref[...] = one_hot(lax.broadcasted_iota(jnp.int32, (primal, slots), 1) == slot_col)
 
 
-def picker_table(slab_ref, owned):
-    owners, height, _ = slab_ref.shape
+def picker_table(names_ref, owned):
+    owners = names_ref.shape[0]
     lane_at = lax.broadcasted_iota(jnp.int32, (CAP, LANES), 1)
     rank_at = lax.broadcasted_iota(jnp.int32, (CAP, LANES), 0)
     out_at = lax.broadcasted_iota(jnp.int32, (CAP, owned), 1).astype(f32) + 1.0
     blocks = []
     for source in range(owners):
-        names = slab_ref[source, height - TILE : height - TILE + 1, :]
+        names = names_ref[source, 0:1, :]
         named = jnp.sum(jnp.where(lane_at == rank_at, names, 0.0), axis=1, keepdims=True)
         blocks.append(jnp.where(out_at == named, 1.0, 0.0))
     return jnp.concatenate(blocks, axis=0)
 
 
-def solve_kernel(incoming_ref, high_ref, low_ref, local_part_ref, square_ref, answer_ref):
-    owners, height, _ = incoming_ref.shape
-    pieces = (height - TILE) // CAP
-    table = picker_table(incoming_ref, high_ref.shape[0]).astype(bf16)
-    summed = select(table, get_slab(incoming_ref, pieces), LEFT_T)
-    solved = product((high_ref[...], low_ref[...]), parts(summed))
+def solve_kernel(incoming_any, inverse_any, local_part_ref, square_ref, answer_ref, *refs):
+    names_ref, slab_ref, inverse_ref, sems = refs
+    owners, height, _ = slab_ref.shape
+    pieces = height // CAP
+    half = pieces // 2 * CAP
+    copies = [
+        pltpu.make_async_copy(incoming_any.at[:, pl.ds(height, TILE)], names_ref, sems.at[0]),
+        pltpu.make_async_copy(
+            incoming_any.at[:, pl.ds(0, half)], slab_ref.at[:, pl.ds(0, half)], sems.at[1]
+        ),
+        pltpu.make_async_copy(
+            incoming_any.at[:, pl.ds(half, height - half)],
+            slab_ref.at[:, pl.ds(half, height - half)],
+            sems.at[2],
+        ),
+        pltpu.make_async_copy(inverse_any, inverse_ref, sems.at[3]),
+    ]
+    for copy in copies:
+        copy.start()
+    copies[0].wait()
+    table = picker_table(names_ref, inverse_ref.shape[0]).astype(bf16)
+    for copy in copies[1:]:
+        copy.wait()
+    summed = select(table, get_slab(slab_ref, pieces), LEFT_T)
+    solved = product(parts(inverse_ref[...]), parts(summed))
     put_slab(answer_ref, select(table, solved))
     total = local_part_ref[...] + 2.0 * jnp.sum(summed * solved, axis=0, keepdims=True)
     sums = folded(total) + folded(square_ref[...])
@@ -219,7 +242,7 @@
 
 
 def swaps():
-    order = [("blk", 0), ("lat", 1), ("blk", 1), ("lat", 0), ("depth", 0), ("depth", 1)]
+    order = [("blk", 1), ("lat", 1), ("blk", 0), ("lat", 0), ("depth", 1), ("depth", 0)]
     return [(axis, odd) for axis, odd in order if pairs(axis, odd)]
 
 
@@ -422,20 +445,26 @@
         local_kernel,
         [whole, row, row, shape_of(primal, slots, dtype=bf16)]
         + [shape_of(height, primal, dtype=bf16)] * 2
-        + [shape_of(owned, owned, dtype=bf16)] * 2
         + [shape_of(height, height, dtype=bf16)] * 2,
-        [lengths, residual, neumann, owner, basis, inverse, schur],
+        [lengths, residual, neumann, owner, basis, schur],
         smem=(0,),
         flops=6 * height * height * width,
         moved=4 * height * (3 * height + 2 * width),
     )
-    basis_halves, inverse_halves, schur_halves = halves[:2], halves[2:4], halves[4:]
+    basis_halves, schur_halves = halves[:2], halves[2:]
     (answers,) = call(
         solve_kernel,
         [shape_of(owners, folds * CAP + tail, LANES)],
-        [incoming, *inverse_halves, local_part, square],
+        [incoming, inverse, local_part, square],
+        far=range(2),
         flops=(8 * slots + 6 * owned) * owned * width,
         moved=8 * slots * width,
+        scratch=[
+            pltpu.VMEM((owners, TILE, LANES), f32),
+            pltpu.VMEM((owners, folds * CAP, LANES), f32),
+            pltpu.VMEM((owned, owned), f32),
+            pltpu.SemaphoreType.DMA((4,)),
+        ],
     )
     returned = to_all(answers, LAYER)
     faces = len(swaps())

time: 120 us -> 119 us (level)
  waiting for transfers between devices: 24.6 us -> 30.1 us
  local copies, waits for them, and re-layouts: 13.2 us -> 10.1 us
  starting transfers between devices: 22.7 us -> 19.6 us
    ppermute x10, waiting for transfers between devices: 17.1 us -> 20.3 us  [exchange(): lax.ppermute(block, axis, pairs(axis, odd))]
    unnamed x50 -> x42, local copies, waits for them, and re-layouts: 13.2 us -> 10.1 us
    ppermute x10, starting transfers between devices: 14.2 us -> 11.1 us  [exchange(): lax.ppermute(block, axis, pairs(axis, odd))]
    all_to_all x1, waiting for transfers between devices: 7.47 us -> 9.75 us  [to_all(): return lax.all_to_all(x, axes, split_axis=0, concat_axis=0, tiled=True)]
  transfers between devices with their start and end apart: 11 -> 11, of which waited for: 6 -> 7; matrix products, arithmetic and copies ran while one was open for 0% -> 0% of each run, Pallas kernels for 4% -> 4%
where the time goes in v4:
time: 119 us
  blocking collectives  38.1 us (32%)
  waiting for transfers between devices  30.1 us (25%)
  Pallas kernels  20 us (17%)
  starting transfers between devices  19.6 us (16%)
  local copies, waits for them, and re-layouts  10.1 us (8%)
    all_to_all x2, blocking collectives, to_all(): return lax.all_to_all(x, axes, split_axis=0, concat_axis=0, tiled=True)  38.1 us
    ppermute x10, waiting for transfers between devices, exchange(): lax.ppermute(block, axis, pairs(axis, odd))  20.3 us
    pallas_call x8, Pallas kernels, call(): pl.pallas_call(body, out_shape=list(outs), in_specs=in_specs, out_specs=o...  20 us
    ppermute x10, starting transfers between devices, exchange(): lax.ppermute(block, axis, pairs(axis, odd))  11.1 us
    unnamed x42, local copies, waits for them, and re-layouts  10.1 us
    all_to_all x1, waiting for transfers between devices, to_all(): return lax.all_to_all(x, axes, split_axis=0, concat_axis=0, tiled=True)  9.75 us
    all_to_all x1, starting transfers between devices, to_all(): return lax.all_to_all(x, axes, split_axis=0, concat_axis=0, tiled=True)  8.5 us
  transfers between devices with their start and end apart: 11, of which 7 were waited for; matrix products, arithmetic and copies ran while one was open for 0% of the time, Pallas kernels for 4%

profile of v4, /device:TPU:0, one launch (start us, length us, event | category | flops | bytes accessed | tf_op | source)
XLA Modules:
  0.0 118.8 jit_solution(10327271977909602518)
XLA Ops:
  0.6 4.1 %shard_map.137 = f32[16,104,128]{2,1,0:T(8,128)} custom-call(s32[6]{0:T(128)} %bitcast.25, s32[1,256]{1,0:T(1,128)} %bitcast.31, s32[1,256]{1,0:T(1,128)} %bitcast.36, f32[768,512]{1,0:T(8,128)} %bitcast.15, f32[768,256]{1,0:T(8,128)} %bitcast.19), custom_call_target="tpu_custom_call" | custom-call | flops 603979776 | bytes 3145728 | tf_op jit(solution)/shard_map/pallas_call | solution.py:30
  4.8 8.5 %all-to-all-start = ((f32[16,104,128]{2,1,0:T(8,128)}), f32[16,104,128]{2,1,0:T(8,128)}, u32[]{:S(2)}, u32[]{:S(2)}) async-start(f32[16,104,128]{2,1,0:T(8,128)} %shard_map.137), calls=%async_computation | async-start | bytes 1703936 | tf_op jit(solution)/shard_map/all_to_all | solution.py:384
  13.3 1.7 %copy-done.2 = f32[1,1,1,768,768]{4,3,2,1,0:T(8,128)S(1)} copy-done((f32[1,1,1,768,768]{4,3,2,1,0:T(8,128)S(1)}, f32[1,1,1,768,768]{4,3,2,1,0:T(8,128)}, u32[]{:S(2)}) %copy-start.2) | copy-done | bytes 2359320
  15.0 1.7 %copy-done.3 = f32[1,1,1,768,768]{4,3,2,1,0:T(8,128)S(1)} copy-done((f32[1,1,1,768,768]{4,3,2,1,0:T(8,128)S(1)}, f32[1,1,1,768,768]{4,3,2,1,0:T(8,128)}, u32[]{:S(2)}) %copy-start.3) | copy-done | bytes 2359320
  16.6 3.5 %shard_map.138 = (f32[768,512]{1,0:T(8,128)S(1)}, f32[1,512]{1,0:T(1,128)S(1)}, f32[1,512]{1,0:T(1,128)S(1)}, bf16[256,384]{1,0:T(8,128)(2,1)S(1)}, bf16[768,256...) custom-call(s32[6]{0:T(128)S(1)} %bitcast.26, ...), custom_call_target="tpu_custom_call" | custom-call | flops 1811939328 | bytes 10223616 | tf_op jit(solution)/shard_map/pallas_call | solution.py:30
  20.1 1.1 copy-done.6
  24.5 9.8 %all-to-all-done.incoming_any = f32[16,104,128]{2,1,0:T(8,128)} async-done(((f32[16,104,128]{2,1,0:T(8,128)}), f32[16,104,128]{2,1,0:T(8,128)}, u32[]{:S(2)}, u32[]{:S(2)}) %all-to-all-start) | async-done | bytes 852000 | tf_op jit(solution)/shard_map/all_to_all | solution.py:384
  35.2 2.4 %shard_map.139 = f32[16,104,128]{2,1,0:T(8,128)S(1)} custom-call(f32[16,104,128]{2,1,0:T(8,128)} %all-to-all-done.incoming_any, f32[256,256]{1,0:T(8,128)S(1)} %bitcast.35, f32[1,512]{1,0:T(1,128)S(1)} %get-tuple-element.36.local_part_ref, f32[1,512]{1,0:T(1,128)S(1)} %get-tuple-element.37.square_ref), custom_call_target="tpu_custom_call" | custom-call | flops 603979776 | bytes 1572864 | tf_op jit(solution)/shard_map/pallas_call | solution.py:30
  37.6 26.4 %all_to_all.15.returned_ref = f32[16,104,128]{2,1,0:T(8,128)S(1)} all-to-all(f32[16,104,128]{2,1,0:T(8,128)S(1)} %shard_map.139), channel_id=1, replica_groups=mesh['blk'=4,'lat'=4,'depth'=2] {'blk','lat'}, dimensions={0} | all-to-all | bytes 1703936 | tf_op jit(solution)/shard_map/all_to_all | solution.py:384
  64.0 1.2 shard_map.140
  65.3 1.7 %collective-permute-start = (f32[128,512]{1,0:T(8,128)S(1)}, f32[128,512]{1,0:T(8,128)S(1)}, u32[]{:S(2)}, u32[]{:S(2)}) collective-permute-start(f32[128,512]{1,0:T(8,128)S(1)} %get-tuple-element.46), channel_id=1, source_target_pairs={{8,16},{16,8},{24,0},{0,24},{9,17},{17,9},{25,1},{1,25},{10,18},{1... | collective-permute-start | bytes 786440 | tf_op jit(solution)/shard_map/ppermute | solution.py:281
  67.8 3.8 %collective-permute-start.3 = (f32[128,512]{1,0:T(8,128)S(1)}, f32[128,512]{1,0:T(8,128)S(1)}, u32[]{:S(2)}, u32[]{:S(2)}) collective-permute-start(f32[128,512]{1,0:T(8,128)S(1)} %get-tuple-element.49), channel_id=1, source_target_pairs={{0,2},{2,0},{4,6},{6,4},{1,3},{3,1},{5,7},{7,5},{8,10},{10,8},{12,... | collective-permute-start | bytes 786440 | tf_op jit(solution)/shard_map/ppermute | solution.py:281
  71.5 4.8 %collective-permute-done.refs_0_ = f32[128,512]{1,0:T(8,128)S(1)} collective-permute-done((f32[128,512]{1,0:T(8,128)S(1)}, f32[128,512]{1,0:T(8,128)S(1)}, u32[]{:S(2)}, u32[]{:S(2)}) %collective-permute-start) | collective-permute-done | bytes 262176 | tf_op jit(solution)/shard_map/ppermute | solution.py:281
  76.3 5.2 %collective-permute-done.2.refs_2_ = f32[128,512]{1,0:T(8,128)S(1)} collective-permute-done((f32[128,512]{1,0:T(8,128)S(1)}, f32[128,512]{1,0:T(8,128)S(1)}, u32[]{:S(2)}, u32[]{:S(2)}) %collective-permute-start.2) | collective-permute-done | bytes 262176 | tf_op jit(solution)/shard_map/ppermute | solution.py:281
  81.5 1.8 %collective-permute-done.3.refs_3_ = f32[128,512]{1,0:T(8,128)S(1)} collective-permute-done((f32[128,512]{1,0:T(8,128)S(1)}, f32[128,512]{1,0:T(8,128)S(1)}, u32[]{:S(2)}, u32[]{:S(2)}) %collective-permute-start.3) | collective-permute-done | bytes 262176 | tf_op jit(solution)/shard_map/ppermute | solution.py:281
  83.4 4.4 %shard_map.141 = (f32[768,512]{1,0:T(8,128)}, f32[1,512]{1,0:T(1,128)}, f32[1,512]{1,0:T(1,128)S(1)}, f32[768,512]{1,0:T(8,128)S(1)}, f32[128,512]{1,0:T(8,128)S...) custom-call(s32[6]{0:T(128)S(1)} %bitcast.27, ...), custom_call_target="tpu_custom_call" | custom-call | flops 1811939328 | bytes 11796480 | tf_op jit(solution)/shard_map/pallas_call | solution.py:30
  87.8 2.0 %collective-permute-start.5 = (f32[128,512]{1,0:T(8,128)S(1)}, f32[128,512]{1,0:T(8,128)S(1)}, u32[]{:S(2)}, u32[]{:S(2)}) collective-permute-start(f32[128,512]{1,0:T(8,128)S(1)} %get-tuple-element.55), channel_id=1, source_target_pairs={{8,16},{16,8},{24,0},{0,24},{9,17},{17,9},{25,1},{1,25},{10,18},{1... | collective-permute-start | bytes 786440 | tf_op jit(solution)/shard_map/ppermute | solution.py:281
  90.5 2.1 %collective-permute-start.8 = (f32[128,512]{1,0:T(8,128)S(1)}, f32[128,512]{1,0:T(8,128)S(1)}, u32[]{:S(2)}, u32[]{:S(2)}) collective-permute-start(f32[128,512]{1,0:T(8,128)S(1)} %get-tuple-element.58), channel_id=1, source_target_pairs={{0,2},{2,0},{4,6},{6,4},{1,3},{3,1},{5,7},{7,5},{8,10},{10,8},{12,... | collective-permute-start | bytes 786440 | tf_op jit(solution)/shard_map/ppermute | solution.py:281
  92.6 1.4 %copy-done.4 = f32[768,512]{1,0:T(8,128)S(1)} copy-done((f32[768,512]{1,0:T(8,128)S(1)}, f32[768,512]{1,0:T(8,128)}, u32[]{:S(2)}) %copy-start.4) | copy-done | bytes 1572888
  94.0 1.1 shard_map.142
  95.1 3.8 %collective-permute-done.5.refs_0_ = f32[128,512]{1,0:T(8,128)S(1)} collective-permute-done((f32[128,512]{1,0:T(8,128)S(1)}, f32[128,512]{1,0:T(8,128)S(1)}, u32[]{:S(2)}, u32[]{:S(2)}) %collective-permute-start.5) | collective-permute-done | bytes 262176 | tf_op jit(solution)/shard_map/ppermute | solution.py:281
  98.9 4.0 %collective-permute-done.7.refs_2_ = f32[128,512]{1,0:T(8,128)S(1)} collective-permute-done((f32[128,512]{1,0:T(8,128)S(1)}, f32[128,512]{1,0:T(8,128)S(1)}, u32[]{:S(2)}, u32[]{:S(2)}) %collective-permute-start.7) | collective-permute-done | bytes 262176 | tf_op jit(solution)/shard_map/ppermute | solution.py:281
  104.6 11.8 %all_to_all.16.sums_ref = f32[32,3,4,128]{3,2,1,0:T(4,128)S(1)} all-to-all(f32[32,3,4,128]{3,2,1,0:T(4,128)S(1)} %get-tuple-element.60), channel_id=1, replica_groups=mesh['blk'=4,'lat'=4,'depth'=2] {'blk','lat','depth'}, dimensions={0} | all-to-all | bytes 393216 | tf_op jit(solution)/shard_map/all_to_all | solution.py:384
  116.4 2.4 %shard_map.144 = (f32[768,512]{1,0:T(8,128)}, f32[1,512]{1,0:T(1,128)}, f32[1,512]{1,0:T(1,128)}) custom-call(s32[6]{0:T(128)S(1)} %bitcast.30, f32[32,3,4,128]{3,2,1,0:T(4,128)S(1)} %all_to_all.16.sums_ref, f32[1,512]{1,0:T(1,128)S(1)} %copy-done.19, f32[1,512]{1,0:T(1,128)S(1)} %get-tuple-element.62.square_ref, f32[768,512]{1,0:T(8,128)S(1)} %bitcast.18, ...), custom_call_target="tpu_custom_call" | custom-call | flops 1572864 | bytes 4718592 | tf_op jit(solution)/shard_map/pallas_call | solution.py:30
  (50 shorter events, 7.5 us)
Async XLA Ops:
  0.6 12.6 %copy-start.1 = (f32[1,1,1,768,256]{4,3,2,1,0:T(8,128)S(1)}, f32[1,1,1,768,256]{4,3,2,1,0:T(8,128)}, u32[]{:S(2)}) copy-start(f32[1,1,1,768,256]{4,3,2,1,0:T(8,128)} %param.16) | copy-start | bytes 2359300
  4.7 8.6 %copy-start = (f32[1,1,1,768,512]{4,3,2,1,0:T(8,128)S(1)}, f32[1,1,1,768,512]{4,3,2,1,0:T(8,128)}, u32[]{:S(2)}) copy-start(f32[1,1,1,768,512]{4,3,2,1,0:T(8,128)} %param.11) | copy-start | bytes 4718596
  4.7 8.6 %copy-start.16 = (s32[1,1,1,6]{3,2,1,0:T(1,128)S(1)}, s32[1,1,1,6]{3,2,1,0:T(1,128)}, u32[]{:S(2)}) copy-start(s32[1,1,1,6]{3,2,1,0:T(1,128)} %param.10) | copy-start | bytes 76
  4.7 8.6 %copy-start.17 = (s32[1,1,1,256,1]{3,4,2,1,0:T(1,128)S(1)}, s32[1,1,1,256,1]{3,4,2,1,0:T(1,128)}, u32[]{:S(2)}) copy-start(s32[1,1,1,256,1]{3,4,2,1,0:T(1,128)} %param.18) | copy-start | bytes 3076
  4.8 29.5 %all-to-all-start = ((f32[16,104,128]{2,1,0:T(8,128)}), f32[16,104,128]{2,1,0:T(8,128)}, u32[]{:S(2)}, u32[]{:S(2)}) async-start(f32[16,104,128]{2,1,0:T(8,128)} %shard_map.137), calls=%async_computation | async-start | bytes 1703936 | tf_op jit(solution)/shard_map/all_to_all | solution.py:384
  13.3 1.7 %copy-start.2 = (f32[1,1,1,768,768]{4,3,2,1,0:T(8,128)S(1)}, f32[1,1,1,768,768]{4,3,2,1,0:T(8,128)}, u32[]{:S(2)}) copy-start(f32[1,1,1,768,768]{4,3,2,1,0:T(8,128)} %param.15) | copy-start | bytes 7077892
  35.2 28.8 %copy-start.7 = (f32[768,512]{1,0:T(8,128)S(1)}, f32[768,512]{1,0:T(8,128)}, u32[]{:S(2)}) copy-start(f32[768,512]{1,0:T(8,128)} %copy-done.6) | copy-start | bytes 4718596
  35.2 28.8 %copy-start.11 = (bf16[768,256]{1,0:T(8,128)(2,1)S(1)}, bf16[768,256]{1,0:T(8,128)(2,1)}, u32[]{:S(2)}) copy-start(bf16[768,256]{1,0:T(8,128)(2,1)} %copy-done.10) | copy-start | bytes 1179652
  35.2 28.8 %copy-start.13 = (bf16[768,256]{1,0:T(8,128)(2,1)S(1)}, bf16[768,256]{1,0:T(8,128)(2,1)}, u32[]{:S(2)}) copy-start(bf16[768,256]{1,0:T(8,128)(2,1)} %copy-done.12) | copy-start | bytes 1179652
  35.2 28.8 %copy-start.15 = (bf16[256,384]{1,0:T(8,128)(2,1)S(1)}, bf16[256,384]{1,0:T(8,128)(2,1)}, u32[]{:S(2)}) copy-start(bf16[256,384]{1,0:T(8,128)(2,1)} %copy-done.14) | copy-start | bytes 589828
  64.0 19.3 %copy-start.5 = (f32[1,1,1,768,512]{4,3,2,1,0:T(8,128)S(1)}, f32[1,1,1,768,512]{4,3,2,1,0:T(8,128)}, u32[]{:S(2)}) copy-start(f32[1,1,1,768,512]{4,3,2,1,0:T(8,128)} %param.12) | copy-start | bytes 4718596
  64.0 19.3 %copy-start.9 = (bf16[768,768]{1,0:T(8,128)(2,1)S(1)}, bf16[768,768]{1,0:T(8,128)(2,1)}, u32[]{:S(2)}) copy-start(bf16[768,768]{1,0:T(8,128)(2,1)} %copy-done.8) | copy-start | bytes 3538948
  64.0 19.3 %copy-start.18 = (f32[512]{0:T(512)S(1)}, f32[512]{0:T(512)}, u32[]{:S(2)}) copy-start(f32[512]{0:T(512)} %param.13) | copy-start | bytes 6148
  65.2 18.1 %collective-permute-start.4 = (f32[136,512]{1,0:T(8,128)S(1)}, f32[136,512]{1,0:T(8,128)S(1)}, u32[]{:S(2)}, u32[]{:S(2)}) collective-permute-start(f32[136,512]{1,0:T(8,128)S(1)} %get-tuple-element.50), channel_id=1, source_target_pairs={{0,1},{1,0},{2,3},{3,2},{4,5},{5,4},{6,7},{7,6},{8,9},{9,8},{10,11... | collective-permute-start | bytes 835592 | tf_op jit(solution)/shard_map/ppermute | solution.py:281
  65.3 11.1 %collective-permute-start = (f32[128,512]{1,0:T(8,128)S(1)}, f32[128,512]{1,0:T(8,128)S(1)}, u32[]{:S(2)}, u32[]{:S(2)}) collective-permute-start(f32[128,512]{1,0:T(8,128)S(1)} %get-tuple-element.46), channel_id=1, source_target_pairs={{8,16},{16,8},{24,0},{0,24},{9,17},{17,9},{25,1},{1,25},{10,18},{1... | collective-permute-start | bytes 786440 | tf_op jit(solution)/shard_map/ppermute | solution.py:281
  67.0 9.3 %collective-permute-start.1 = (f32[128,512]{1,0:T(8,128)S(1)}, f32[128,512]{1,0:T(8,128)S(1)}, u32[]{:S(2)}, u32[]{:S(2)}) collective-permute-start(f32[128,512]{1,0:T(8,128)S(1)} %get-tuple-element.47), channel_id=1, source_target_pairs={{2,4},{4,2},{3,5},{5,3},{10,12},{12,10},{11,13},{13,11},{18,20},{2... | collective-permute-start | bytes 786440 | tf_op jit(solution)/shard_map/ppermute | solution.py:281
  67.7 13.8 %collective-permute-start.2 = (f32[128,512]{1,0:T(8,128)S(1)}, f32[128,512]{1,0:T(8,128)S(1)}, u32[]{:S(2)}, u32[]{:S(2)}) collective-permute-start(f32[128,512]{1,0:T(8,128)S(1)} %get-tuple-element.48), channel_id=1, source_target_pairs={{0,8},{8,0},{16,24},{24,16},{1,9},{9,1},{17,25},{25,17},{2,10},{10... | collective-permute-start | bytes 786440 | tf_op jit(solution)/shard_map/ppermute | solution.py:281
  67.8 15.6 %collective-permute-start.3 = (f32[128,512]{1,0:T(8,128)S(1)}, f32[128,512]{1,0:T(8,128)S(1)}, u32[]{:S(2)}, u32[]{:S(2)}) collective-permute-start(f32[128,512]{1,0:T(8,128)S(1)} %get-tuple-element.49), channel_id=1, source_target_pairs={{0,2},{2,0},{4,6},{6,4},{1,3},{3,1},{5,7},{7,5},{8,10},{10,8},{12,... | collective-permute-start | bytes 786440 | tf_op jit(solution)/shard_map/ppermute | solution.py:281
  87.8 11.2 %collective-permute-start.5 = (f32[128,512]{1,0:T(8,128)S(1)}, f32[128,512]{1,0:T(8,128)S(1)}, u32[]{:S(2)}, u32[]{:S(2)}) collective-permute-start(f32[128,512]{1,0:T(8,128)S(1)} %get-tuple-element.55), channel_id=1, source_target_pairs={{8,16},{16,8},{24,0},{0,24},{9,17},{17,9},{25,1},{1,25},{10,18},{1... | collective-permute-start | bytes 786440 | tf_op jit(solution)/shard_map/ppermute | solution.py:281
  89.8 9.2 %collective-permute-start.6 = (f32[128,512]{1,0:T(8,128)S(1)}, f32[128,512]{1,0:T(8,128)S(1)}, u32[]{:S(2)}, u32[]{:S(2)}) collective-permute-start(f32[128,512]{1,0:T(8,128)S(1)} %get-tuple-element.56), channel_id=1, source_target_pairs={{2,4},{4,2},{3,5},{5,3},{10,12},{12,10},{11,13},{13,11},{18,20},{2... | collective-permute-start | bytes 786440 | tf_op jit(solution)/shard_map/ppermute | solution.py:281
  90.5 12.4 %collective-permute-start.7 = (f32[128,512]{1,0:T(8,128)S(1)}, f32[128,512]{1,0:T(8,128)S(1)}, u32[]{:S(2)}, u32[]{:S(2)}) collective-permute-start(f32[128,512]{1,0:T(8,128)S(1)} %get-tuple-element.57), channel_id=1, source_target_pairs={{0,8},{8,0},{16,24},{24,16},{1,9},{9,1},{17,25},{25,17},{2,10},{10... | collective-permute-start | bytes 786440 | tf_op jit(solution)/shard_map/ppermute | solution.py:281
  90.5 13.1 %collective-permute-start.8 = (f32[128,512]{1,0:T(8,128)S(1)}, f32[128,512]{1,0:T(8,128)S(1)}, u32[]{:S(2)}, u32[]{:S(2)}) collective-permute-start(f32[128,512]{1,0:T(8,128)S(1)} %get-tuple-element.58), channel_id=1, source_target_pairs={{0,2},{2,0},{4,6},{6,4},{1,3},{3,1},{5,7},{7,5},{8,10},{10,8},{12,... | collective-permute-start | bytes 786440 | tf_op jit(solution)/shard_map/ppermute | solution.py:281
  92.6 11.0 %collective-permute-start.9 = (f32[128,512]{1,0:T(8,128)S(1)}, f32[128,512]{1,0:T(8,128)S(1)}, u32[]{:S(2)}, u32[]{:S(2)}) collective-permute-start(f32[128,512]{1,0:T(8,128)S(1)} %get-tuple-element.59), channel_id=1, source_target_pairs={{0,1},{1,0},{2,3},{3,2},{4,5},{5,4},{6,7},{7,6},{8,9},{9,8},{10,11... | collective-permute-start | bytes 786440 | tf_op jit(solution)/shard_map/ppermute | solution.py:281
  103.6 12.8 %copy-start.19 = (f32[1,512]{1,0:T(1,128)S(1)}, f32[1,512]{1,0:T(1,128)}, u32[]{:S(2)}) copy-start(f32[1,512]{1,0:T(1,128)} %get-tuple-element.61.rho_ref) | copy-start | bytes 6148
  (8 other events, 8.4 us)

commit v5 on v4

--- a/solution.py
+++ b/solution.py
@@ -26,6 +26,10 @@
 
 def call(body, outs, operands, smem=(), far=(), far_out=(), flops=0, moved=0, scratch=(), room=32):
     in_specs = [SMEM if i in smem else ANY if i in far else VMEM for i in range(len(operands))]
+    operands = [
+        pltpu.with_memory_space_constraint(x, pltpu.HBM) if i in far else x
+        for i, x in enumerate(operands)
+    ]
     out_specs = [ANY if i in far_out else VMEM for i in range(len(outs))]
     return pl.pallas_call(
         body,
@@ -54,16 +58,12 @@
 
 def product(a, b, dims=PLAIN):
     (ah, al), (bh, bl) = a, b
-    (along_a,), (along_b,) = dims
-    left = jnp.concatenate([ah, ah, al], axis=along_a)
-    right = jnp.concatenate([bh, bl, bh], axis=along_b)
-    return mul(left, right, dims)
+    return mul(ah, bh, dims) + (mul(ah, bl, dims) + mul(al, bh, dims))
 
 
 def select(table, x, dims=PLAIN):
-    (along_a,), (along_b,) = dims
-    left = jnp.concatenate([table, table], axis=along_a)
-    return mul(left, jnp.concatenate(parts(x), axis=along_b), dims)
+    high, low = parts(x)
+    return mul(table, high, dims) + mul(table, low, dims)
 
 
 def one_hot(hit):
@@ -104,6 +104,21 @@
     return jnp.concatenate(
         [ref[:, j * CAP : (j + 1) * CAP, :].reshape(slots, LANES) for j in range(pieces)], axis=1
     )
+
+
+def columns(*rows):
+    spare = [jnp.zeros_like(rows[0])] * (TILE - len(rows))
+    turned = jnp.transpose(jnp.concatenate([*rows, *spare], axis=0))
+    return [turned[:, i : i + 1] for i in range(len(rows))]
+
+
+def ranks(own_row):
+    primal = own_row.shape[1]
+    (own_col,) = columns(own_row)
+    row_at = lax.broadcasted_iota(jnp.int32, (primal, primal), 0)
+    col_at = lax.broadcasted_iota(jnp.int32, (primal, primal), 1)
+    before = (own_row == own_col) & (row_at < col_at)
+    return jnp.sum(jnp.where(before, 1.0, 0.0), axis=0, keepdims=True), own_col
 
 
 def pack_kernel(len_any, owner_any, row_any, residual_any, basis_any, slab_ref, *refs):
@@ -134,16 +149,11 @@
             copy.start()
     for copy in small:
         copy.wait()
-    row_at = lax.broadcasted_iota(jnp.int32, (primal, primal), 0)
-    col_at = lax.broadcasted_iota(jnp.int32, (primal, primal), 1)
     own_row = owner_ref[...].astype(f32)
     wanted_row = row_ref[...].astype(f32) + 1.0
-    own_col = jnp.sum(jnp.where(row_at == col_at, own_row, 0.0), axis=1, keepdims=True)
-    wanted_col = jnp.sum(jnp.where(row_at == col_at, wanted_row, 0.0), axis=1, keepdims=True)
-    same = own_row == own_col
-    rank_row = jnp.sum(jnp.where(same & (row_at < col_at), 1.0, 0.0), axis=0, keepdims=True)
-    rank_col = jnp.sum(jnp.where(same & (col_at < row_at), 1.0, 0.0), axis=1, keepdims=True)
+    rank_row, _ = ranks(own_row)
     slot_row = (own_row * CAP + rank_row).astype(jnp.int32)
+    rank_col, wanted_col = columns(rank_row, wanted_row)
     packer = one_hot(lax.broadcasted_iota(jnp.int32, (slots, primal), 0) == slot_row)
     to_owner = one_hot(lax.broadcasted_iota(jnp.int32, (owners, primal), 0) == owner_ref[...])
     lane_at = lax.broadcasted_iota(jnp.int32, (primal, LANES), 1)
@@ -181,12 +191,8 @@
     for i in range(2):
         refs[2 * i][...], refs[2 * i + 1][...] = parts(whole[i][...])
     primal, slots = table_ref.shape
-    row_at = lax.broadcasted_iota(jnp.int32, (primal, primal), 0)
-    col_at = lax.broadcasted_iota(jnp.int32, (primal, primal), 1)
-    own_row = owner_ref[...].astype(f32)
-    own_col = jnp.sum(jnp.where(row_at == col_at, own_row, 0.0), axis=1, keepdims=True)
-    before = (own_row == own_col) & (col_at < row_at)
-    rank_col = jnp.sum(jnp.where(before, 1.0, 0.0), axis=1, keepdims=True)
+    rank_row, own_col = ranks(owner_ref[...].astype(f32))
+    (rank_col,) = columns(rank_row)
     slot_col = (own_col * CAP + rank_col).astype(jnp.int32)
     table_ref[...] = one_hot(lax.broadcasted_iota(jnp.int32, (primal, slots), 1) == slot_col)
 
@@ -241,45 +247,50 @@
 AXIS_AT = {"blk": 0, "lat": 2, "depth": 4}
 
 
-def swaps():
-    order = [("blk", 1), ("lat", 1), ("blk", 0), ("lat", 0), ("depth", 1), ("depth", 0)]
-    return [(axis, odd) for axis, odd in order if pairs(axis, odd)]
-
-
-def pairs(axis, odd):
+def moves():
+    order = [("blk", "up"), ("lat", 1), ("blk", "down"), ("lat", 0), ("depth", 1), ("depth", 0)]
+    return [(axis, way) for axis, way in order if route(axis, way)]
+
+
+def route(axis, way):
     devices = lax.axis_size(axis)
-    ends = [(i, i + 1) for i in range(odd, devices - 1, 2)]
-    if axis == "blk" and odd:
-        ends.append((devices - 1, 0))
-    return [pair for i, j in ends for pair in ((i, j), (j, i))]
-
-
-def sends_plus(axis, odd):
-    return lax.rem(lax.axis_index(axis), 2) == odd
+    if way in ("up", "down"):
+        by = 1 if way == "up" else -1
+        return [(i, (i + by) % devices) for i in range(devices)]
+    return [pair for i in range(way, devices - 1, 2) for pair in ((i, i + 1), (i + 1, i))]
+
+
+def sends_plus(axis, way):
+    return lax.rem(lax.axis_index(axis), 2) == way
 
 
 def put_faces(image, rows, face_refs):
-    for ref, (axis, odd) in zip(face_refs, swaps(), strict=True):
+    for ref, (axis, way) in zip(face_refs, moves(), strict=True):
         at = AXIS_AT[axis] * rows
         minus, plus = image[at : at + rows, :], image[at + rows : at + 2 * rows, :]
-        ref[:rows, :] = jnp.where(sends_plus(axis, odd), plus, minus)
-
-
-def got_face(refs, face, rows):
-    axis = ("blk", "lat", "depth")[face // 2]
+        if way in ("up", "down"):
+            ref[...] = plus if way == "up" else minus
+        else:
+            ref[...] = jnp.where(sends_plus(axis, way), plus, minus)
+
+
+def got_face(got, face):
+    axis, side = ("blk", "lat", "depth")[face // 2], face % 2
+    if axis == "blk":
+        return got["blk", "down" if side else "up"][...]
     total = None
-    for ref, (axis_of, odd) in zip(refs, swaps(), strict=True):
+    for (axis_of, way), ref in got.items():
         if axis_of == axis:
-            mine = sends_plus(axis, odd) == (face % 2 == 1)
-            piece = jnp.where(mine, ref[:rows, :], 0.0)
+            mine = sends_plus(axis, way) == (side == 1)
+            piece = jnp.where(mine, ref[...], 0.0)
             total = piece if total is None else total + piece
     return total
 
 
 def exchange(faces):
     return [
-        lax.ppermute(block, axis, pairs(axis, odd))
-        for block, (axis, odd) in zip(faces, swaps(), strict=True)
+        lax.ppermute(block, axis, route(axis, way))
+        for block, (axis, way) in zip(faces, moves(), strict=True)
     ]
 
 
@@ -293,47 +304,70 @@
     put_faces(image, rows, face_refs)
     tail = jnp.sum(returned_ref[:, folds * CAP :, :], axis=0)
     if pair_depth:
-        sums = jnp.concatenate(
-            [unfolded(tail, 0, folds), unfolded(tail, folds, folds)]
-            + [jnp.zeros((TILE - 2, width), f32)],
-            axis=0,
-        )
-        sums_ref[...] = sums
-        face_refs[-1][rows:, :] = sums
+        sums_ref[...] = tail
     else:
         sums_ref[...] = jnp.broadcast_to(tail[None], sums_ref.shape)
 
 
-def direction_kernel(pair_depth, scale, len_ref, sums_ref, prev_rho_ref, image_ref, prev_ref, high_ref, low_ref, *refs):
-    faces = len(swaps())
-    got, refs = refs[:faces], refs[faces:]
-    (direction_out, rho_out, square_out, schur_out), refs = refs[:4], refs[4:]
-    face_refs, (direction_ref, sem) = refs[:faces], refs[faces:]
+def new_direction(len_ref, beta, image_ref, prev_ref, got, face, rows):
+    at = slice(face * rows, (face + 1) * rows)
+    precond = 0.5 * (image_ref[at, :] + got_face(got, face))
+    return jnp.where(live_rows(len_ref, face, rows), precond + beta * prev_ref[at, :], 0.0)
+
+
+def near_kernel(pair_depth, scale, keys, len_ref, sums_ref, prev_rho_ref, image_ref, prev_ref, high_ref, low_ref, *refs):
+    got, refs = dict(zip(keys, refs)), refs[len(keys) :]
+    if pair_depth:
+        sums, refs = sums_ref[...] + refs[0][...], refs[1:]
+    else:
+        sums = jnp.sum(sums_ref[...], axis=0)
+    rho_out, beta_out, square_out, near_ref, image_out = refs
     rows = image_ref.shape[0] // 6
-    width = image_ref.shape[1]
-    if pair_depth:
-        sums = sums_ref[...] + got[-1][rows:, :]
-        rho, square = sums[0:1, :], sums[1:2, :]
-    else:
-        folds = width // LANES
-        sums = jnp.sum(sums_ref[...], axis=0)
-        rho, square = unfolded(sums, 0, folds), unfolded(sums, folds, folds)
-    rho = scale * rho
+    folds = image_ref.shape[1] // LANES
+    rho = scale * unfolded(sums, 0, folds)
+    beta = rho / prev_rho_ref[...]
     rho_out[...] = rho
-    square_out[...] = square
-    beta = rho / prev_rho_ref[...]
-    for face in range(6):
-        at = slice(face * rows, (face + 1) * rows)
-        precond = 0.5 * (image_ref[at, :] + got_face(got, face, rows))
-        direction_ref[at, :] = jnp.where(
-            live_rows(len_ref, face, rows), precond + beta * prev_ref[at, :], 0.0
+    beta_out[...] = beta
+    square_out[...] = unfolded(sums, folds, folds)
+    for i, face in enumerate((0, 1, 4, 5)):
+        near_ref[i * rows : (i + 1) * rows, :] = new_direction(
+            len_ref, beta, image_ref, prev_ref, got, face, rows
         )
-    copy = pltpu.make_async_copy(direction_ref, direction_out, sem)
-    copy.start()
-    image = product((high_ref[...], low_ref[...]), parts(direction_ref[...]))
+    high, low = parts(near_ref[...])
+    first, last = 2 * rows, 4 * rows
+    image_out[...] = product(
+        (high_ref[:, :first], low_ref[:, :first]), (high[:first], low[:first])
+    ) + product((high_ref[:, last:], low_ref[:, last:]), (high[first:], low[first:]))
+
+
+def far_kernel(keys, len_ref, beta_ref, image_ref, prev_ref, high_ref, low_ref, near_ref, near_image_ref, *refs):
+    got, refs = dict(zip(keys, refs)), refs[len(keys) :]
+    (direction_out, schur_out), face_refs, (far_ref, sems) = refs[:2], refs[2:-2], refs[-2:]
+    rows = image_ref.shape[0] // 6
+    first, last = 2 * rows, 4 * rows
+    pair = pl.ds(0, first)
+    copies = [
+        pltpu.make_async_copy(near_ref.at[pair], direction_out.at[pair], sems.at[0]),
+        pltpu.make_async_copy(
+            near_ref.at[pl.ds(first, first)], direction_out.at[pl.ds(last, first)], sems.at[1]
+        ),
+        pltpu.make_async_copy(far_ref, direction_out.at[pl.ds(first, first)], sems.at[2]),
+    ]
+    copies[0].start()
+    copies[1].start()
+    beta = beta_ref[...]
+    for face in (2, 3):
+        far_ref[(face - 2) * rows : (face - 1) * rows, :] = new_direction(
+            len_ref, beta, image_ref, prev_ref, got, face, rows
+        )
+    copies[2].start()
+    image = near_image_ref[...] + product(
+        (high_ref[:, first:last], low_ref[:, first:last]), parts(far_ref[...])
+    )
     schur_out[...] = image
     put_faces(image, rows, face_refs)
-    copy.wait()
+    for copy in copies:
+        copy.wait()
 
 
 def products_kernel(len_ref, direction_ref, schur_ref, residual_ref, curve_ref, cross_ref):
@@ -347,12 +381,12 @@
 
 
 def applied_kernel(len_ref, curve_ref, cross_ref, schur_ref, *refs):
-    got, (applied_ref, spread_ref) = refs[:-2], refs[-2:]
+    got, (applied_ref, spread_ref) = dict(zip(moves(), refs)), refs[-2:]
     rows = schur_ref.shape[0] // 6
     total = jnp.zeros(curve_ref.shape, f32)
     for face in range(6):
         at = slice(face * rows, (face + 1) * rows)
-        applied = schur_ref[at, :] + got_face(got, face, rows)
+        applied = schur_ref[at, :] + got_face(got, face)
         applied = jnp.where(live_rows(len_ref, face, rows), applied, 0.0)
         applied_ref[at, :] = applied
         total += jnp.sum(applied * applied, axis=0, keepdims=True)
@@ -438,7 +472,6 @@
             pltpu.SemaphoreType.DMA((3, 2)),
             pltpu.SemaphoreType.DMA((3,)),
         ],
-        room=60,
     )
     incoming = to_all(outgoing, LAYER)
     local, local_part, square, table, *halves = call(
@@ -467,29 +500,42 @@
         ],
     )
     returned = to_all(answers, LAYER)
-    faces = len(swaps())
-    last = shape_of(rows + TILE, width) if pair_depth else face
+    keys = moves()
+    faces = [face] * len(keys)
     image, sums, *outward = call(
         functools.partial(image_kernel, pair_depth),
-        [whole, shape_of(TILE, width) if pair_depth else shape_of(layers, tail, LANES)]
-        + [face] * (faces - 1)
-        + [last],
+        [whole, shape_of(tail, LANES) if pair_depth else shape_of(layers, tail, LANES), *faces],
         [returned, table, *basis_halves, local],
         flops=(6 * height + 4 * slots) * primal * width,
         moved=16 * height * width,
     )
-    if not pair_depth:
-        sums = to_all(sums, "depth")
-    got = exchange(outward)
-    direction, rho, square, schur_image, *outward = call(
-        functools.partial(direction_kernel, pair_depth, scale),
-        [whole, row, row, whole] + [face] * faces,
-        [lengths, sums, prev_rho.reshape(1, width), image, prev_direction, *schur_halves, *got],
+    got = dict(zip(keys, exchange(outward)))
+    if pair_depth:
+        sums = [sums, lax.ppermute(sums, "depth", route("depth", 0))]
+    else:
+        sums = [to_all(sums, "depth")]
+    near_keys = [key for key in keys if key[0] != "lat"]
+    far_keys = [key for key in keys if key[0] == "lat"]
+    rho, beta, square, near, near_image = call(
+        functools.partial(near_kernel, pair_depth, scale, near_keys),
+        [row, row, row, shape_of(4 * rows, width), whole],
+        [lengths, sums[0], prev_rho.reshape(1, width), image, prev_direction, *schur_halves]
+        + [got[key] for key in near_keys]
+        + sums[1:],
+        smem=(0,),
+        flops=4 * height * height * width,
+        moved=4 * height * (height + 4 * width),
+    )
+    direction, schur_image, *outward = call(
+        functools.partial(far_kernel, far_keys),
+        [whole, whole, *faces],
+        [lengths, beta, image, prev_direction, *schur_halves, near, near_image]
+        + [got[key] for key in far_keys],
         smem=(0,),
         far_out=(0,),
-        flops=6 * height * height * width,
-        moved=4 * height * (height + 6 * width),
-        scratch=[pltpu.VMEM((height, width), f32), pltpu.SemaphoreType.DMA],
+        flops=2 * height * height * width,
+        moved=4 * height * (height + 4 * width),
+        scratch=[pltpu.VMEM((2 * rows, width), f32), pltpu.SemaphoreType.DMA((3,))],
     )
     got = exchange(outward)
     curve, cross = call(

time: 119 us -> 118 us (level)
  waiting for transfers between devices: 30.1 us -> 23.9 us
  starting transfers between devices: 19.6 us -> 23.3 us
  blocking collectives: 38.1 us -> 40 us
    ppermute x10 -> x11, waiting for transfers between devices: 20.3 us -> 14.1 us  [the longest x10 13.8 us: exchange(): lax.ppermute(block, axis, route(axis, way))]
    ppermute x10 -> x11, starting transfers between devices: 11.1 us -> 14.9 us  [the longest x10 14.3 us: exchange(): lax.ppermute(block, axis, route(axis, way))]
    all_to_all x2, blocking collectives: 38.1 us -> 40 us  [to_all(): return lax.all_to_all(x, axes, split_axis=0, concat_axis=0, tiled=True)]
    unnamed x42 -> x40, local copies, waits for them, and re-layouts: 10.1 us -> 9.12 us
    pallas_call x8 -> x9, Pallas kernels: 20 us -> 20.5 us  [call(): pl.pallas_call(body, out_shape=list(outs), in_specs=in_specs, out_specs=o...]
  transfers between devices with their start and end apart: 11 -> 12, of which waited for: 7 -> 7; matrix products, arithmetic and copies ran while one was open for 0% -> 0% of each run, Pallas kernels for 4% -> 6%
where the time goes in v5:
time: 118 us
  blocking collectives  40 us (34%)
  waiting for transfers between devices  23.9 us (20%)
  starting transfers between devices  23.3 us (20%)
  Pallas kernels  20.5 us (17%)
  local copies, waits for them, and re-layouts  9.12 us (8%)
    all_to_all x2, blocking collectives, to_all(): return lax.all_to_all(x, axes, split_axis=0, concat_axis=0, tiled=True)  40 us
    pallas_call x9, Pallas kernels, call(): pl.pallas_call(body, out_shape=list(outs), in_specs=in_specs, out_specs=o...  20.5 us
    ppermute x10, starting transfers between devices, exchange(): lax.ppermute(block, axis, route(axis, way))  14.3 us
    ppermute x10, waiting for transfers between devices, exchange(): lax.ppermute(block, axis, route(axis, way))  13.8 us
    all_to_all x1, waiting for transfers between devices, to_all(): return lax.all_to_all(x, axes, split_axis=0, concat_axis=0, tiled=True)  9.81 us
    unnamed x40, local copies, waits for them, and re-layouts  9.12 us
    all_to_all x1, starting transfers between devices, to_all(): return lax.all_to_all(x, axes, split_axis=0, concat_axis=0, tiled=True)  8.49 us
  transfers between devices with their start and end apart: 12, of which 7 were waited for; matrix products, arithmetic and copies ran while one was open for 0% of the time, Pallas kernels for 6%

profile of v5, /device:TPU:0, one launch (start us, length us, event | category | flops | bytes accessed | tf_op | source)
XLA Modules:
  0.0 117.7 jit_solution(7993005464307125783)
XLA Ops:
  0.6 4.4 %shard_map.137 = f32[16,104,128]{2,1,0:T(8,128)} custom-call(s32[6]{0:T(128)} %bitcast.26, s32[1,256]{1,0:T(1,128)} %bitcast.33, s32[1,256]{1,0:T(1,128)} %bitcast.37, f32[768,512]{1,0:T(8,128)} %bitcast.15, f32[768,256]{1,0:T(8,128)} %bitcast.21), custom_call_target="tpu_custom_call" | custom-call | flops 603979776 | bytes 3145728 | tf_op jit(solution)/shard_map/pallas_call | solution.py:34
  5.1 8.5 %all-to-all-start = ((f32[16,104,128]{2,1,0:T(8,128)}), f32[16,104,128]{2,1,0:T(8,128)}, u32[]{:S(2)}, u32[]{:S(2)}) async-start(f32[16,104,128]{2,1,0:T(8,128)} %shard_map.137), calls=%async_computation | async-start | bytes 1703936 | tf_op jit(solution)/shard_map/all_to_all | solution.py:418
  13.6 1.7 %copy-done.5 = f32[1,1,1,768,768]{4,3,2,1,0:T(8,128)S(1)} copy-done((f32[1,1,1,768,768]{4,3,2,1,0:T(8,128)S(1)}, f32[1,1,1,768,768]{4,3,2,1,0:T(8,128)}, u32[]{:S(2)}) %copy-start.5) | copy-done | bytes 2359320
  15.3 1.7 %copy-done.6 = f32[1,1,1,768,768]{4,3,2,1,0:T(8,128)S(1)} copy-done((f32[1,1,1,768,768]{4,3,2,1,0:T(8,128)S(1)}, f32[1,1,1,768,768]{4,3,2,1,0:T(8,128)}, u32[]{:S(2)}) %copy-start.6) | copy-done | bytes 2359320
  16.9 3.4 %shard_map.138 = (f32[768,512]{1,0:T(8,128)S(1)}, f32[1,512]{1,0:T(1,128)S(1)}, f32[1,512]{1,0:T(1,128)S(1)}, bf16[256,384]{1,0:T(8,128)(2,1)S(1)}, bf16[768,256...) custom-call(s32[6]{0:T(128)S(1)} %bitcast.27, ...), custom_call_target="tpu_custom_call" | custom-call | flops 1811939328 | bytes 10223616 | tf_op jit(solution)/shard_map/pallas_call | solution.py:34
  21.4 1.1 copy-done.8
  24.7 9.8 %all-to-all-done.incoming_any = f32[16,104,128]{2,1,0:T(8,128)} async-done(((f32[16,104,128]{2,1,0:T(8,128)}), f32[16,104,128]{2,1,0:T(8,128)}, u32[]{:S(2)}, u32[]{:S(2)}) %all-to-all-start) | async-done | bytes 852000 | tf_op jit(solution)/shard_map/all_to_all | solution.py:418
  34.5 2.6 %shard_map.139 = f32[16,104,128]{2,1,0:T(8,128)S(1)} custom-call(f32[16,104,128]{2,1,0:T(8,128)} %all-to-all-done.incoming_any, f32[256,256]{1,0:T(8,128)} %bitcast.39, f32[1,512]{1,0:T(1,128)S(1)} %get-tuple-element.39.local_part_ref, f32[1,512]{1,0:T(1,128)S(1)} %get-tuple-element.40.square_ref), custom_call_target="tpu_custom_call" | custom-call | flops 603979776 | bytes 1572864 | tf_op jit(solution)/shard_map/pallas_call | solution.py:34
  37.1 26.4 %all_to_all.15.returned_ref = f32[16,104,128]{2,1,0:T(8,128)S(1)} all-to-all(f32[16,104,128]{2,1,0:T(8,128)S(1)} %shard_map.139), channel_id=1, replica_groups=mesh['blk'=4,'lat'=4,'depth'=2] {'blk','lat'}, dimensions={0} | all-to-all | bytes 1703936 | tf_op jit(solution)/shard_map/all_to_all | solution.py:418
  63.5 1.2 %shard_map.140 = (f32[768,512]{1,0:T(8,128)S(1)}, f32[8,128]{1,0:T(8,128)S(1)}, f32[128,512]{1,0:T(8,128)S(1)}, f32[128,512]{1,0:T(8,128)S(1)}, f32[128,512]{1,0...) custom-call(f32[16,104,128]{2,1,0:T(8,128)S(1)} %all_to_all.15.returned_ref, ...), custom_call_target="tpu_custom_call" | custom-call | flops 805306368 | bytes 6291456 | tf_op jit(solution)/shard_map/pallas_call | solution.py:34
  65.8 2.8 %collective-permute-start.1 = (f32[128,512]{1,0:T(8,128)S(1)}, f32[128,512]{1,0:T(8,128)S(1)}, u32[]{:S(2)}, u32[]{:S(2)}) collective-permute-start(f32[128,512]{1,0:T(8,128)S(1)} %get-tuple-element.50), channel_id=1, source_target_pairs={{0,24},{8,0},{16,8},{24,16},{1,25},{9,1},{17,9},{25,17},{2,26},{10... | collective-permute-start | bytes 786440 | tf_op jit(solution)/shard_map/ppermute | solution.py:292
  70.2 3.2 %collective-permute-start.5 = (f32[128,512]{1,0:T(8,128)S(1)}, f32[128,512]{1,0:T(8,128)S(1)}, u32[]{:S(2)}, u32[]{:S(2)}) collective-permute-start(f32[128,512]{1,0:T(8,128)S(1)} %get-tuple-element.56), channel_id=1, source_target_pairs={{0,2},{2,0},{4,6},{6,4},{1,3},{3,1},{5,7},{7,5},{8,10},{10,8},{12,... | collective-permute-start | bytes 786440 | tf_op jit(solution)/shard_map/ppermute | solution.py:292
  73.4 2.0 %collective-permute-done.refs_0_ = f32[128,512]{1,0:T(8,128)S(1)} collective-permute-done((f32[128,512]{1,0:T(8,128)S(1)}, f32[128,512]{1,0:T(8,128)S(1)}, u32[]{:S(2)}, u32[]{:S(2)}) %collective-permute-start) | collective-permute-done | bytes 262176 | tf_op jit(solution)/shard_map/ppermute | solution.py:292
  75.4 2.0 %collective-permute-done.1.refs_1_ = f32[128,512]{1,0:T(8,128)S(1)} collective-permute-done((f32[128,512]{1,0:T(8,128)S(1)}, f32[128,512]{1,0:T(8,128)S(1)}, u32[]{:S(2)}, u32[]{:S(2)}) %collective-permute-start.1) | collective-permute-done | bytes 262176 | tf_op jit(solution)/shard_map/ppermute | solution.py:292
  77.4 2.6 %shard_map.141 = (f32[1,512]{1,0:T(1,128)}, f32[1,512]{1,0:T(1,128)S(1)}, f32[1,512]{1,0:T(1,128)S(1)}, f32[512,512]{1,0:T(8,128)S(1)}, f32[768,512]{1,0:T(8,128)S(1)}) custom-call(s32[6]{0:T(128)S(1)} %bitcast.28, f32[8,128]{1,0:T(8,128)S(1)} %get-tuple-element.45.sums_ref, f32[1,512]{1,0:T(1,128)S(1)} %bitcast.35, ...), custom_call_target="tpu_custom_call" | custom-call | flops 1207959552 | bytes 8650752 | tf_op jit(solution)/shard_map/pallas_call | solution.py:34
  80.0 5.1 %collective-permute-done.5.refs_1_ = f32[128,512]{1,0:T(8,128)S(1)} collective-permute-done((f32[128,512]{1,0:T(8,128)S(1)}, f32[128,512]{1,0:T(8,128)S(1)}, u32[]{:S(2)}, u32[]{:S(2)}) %collective-permute-start.5) | collective-permute-done | bytes 262176 | tf_op jit(solution)/shard_map/ppermute | solution.py:292
  85.1 1.9 %shard_map.142 = (f32[768,512]{1,0:T(8,128)}, f32[768,512]{1,0:T(8,128)S(1)}, f32[128,512]{1,0:T(8,128)S(1)}, f32[128,512]{1,0:T(8,128)S(1)}, f32[128,512]{1,0:T...) custom-call(s32[6]{0:T(128)S(1)} %bitcast.29, f32[1,512]{1,0:T(1,128)S(1)} %get-tuple-element.52.beta_ref, ...), custom_call_target="tpu_custom_call" | custom-call | flops 603979776 | bytes 8650752 | tf_op jit(solution)/shard_map/pallas_call | solution.py:34
  87.7 3.9 %collective-permute-start.8 = (f32[128,512]{1,0:T(8,128)S(1)}, f32[128,512]{1,0:T(8,128)S(1)}, u32[]{:S(2)}, u32[]{:S(2)}) collective-permute-start(f32[128,512]{1,0:T(8,128)S(1)} %get-tuple-element.63), channel_id=1, source_target_pairs={{0,24},{8,0},{16,8},{24,16},{1,25},{9,1},{17,9},{25,17},{2,26},{10... | collective-permute-start | bytes 786440 | tf_op jit(solution)/shard_map/ppermute | solution.py:292
  91.6 2.0 %collective-permute-start.9 = (f32[128,512]{1,0:T(8,128)S(1)}, f32[128,512]{1,0:T(8,128)S(1)}, u32[]{:S(2)}, u32[]{:S(2)}) collective-permute-start(f32[128,512]{1,0:T(8,128)S(1)} %get-tuple-element.64), channel_id=1, source_target_pairs={{0,2},{2,0},{4,6},{6,4},{1,3},{3,1},{5,7},{7,5},{8,10},{10,8},{12,... | collective-permute-start | bytes 786440 | tf_op jit(solution)/shard_map/ppermute | solution.py:292
  93.6 1.4 %copy-done.7 = f32[768,512]{1,0:T(8,128)S(1)} copy-done((f32[768,512]{1,0:T(8,128)S(1)}, f32[768,512]{1,0:T(8,128)}, u32[]{:S(2)}) %copy-start.7) | copy-done | bytes 1572888
  96.1 2.0 %collective-permute-done.6.refs_0_ = f32[128,512]{1,0:T(8,128)S(1)} collective-permute-done((f32[128,512]{1,0:T(8,128)S(1)}, f32[128,512]{1,0:T(8,128)S(1)}, u32[]{:S(2)}, u32[]{:S(2)}) %collective-permute-start.6) | collective-permute-done | bytes 262176 | tf_op jit(solution)/shard_map/ppermute | solution.py:292
  98.1 2.7 %collective-permute-done.8.refs_2_ = f32[128,512]{1,0:T(8,128)S(1)} collective-permute-done((f32[128,512]{1,0:T(8,128)S(1)}, f32[128,512]{1,0:T(8,128)S(1)}, u32[]{:S(2)}, u32[]{:S(2)}) %collective-permute-start.8) | collective-permute-done | bytes 262176 | tf_op jit(solution)/shard_map/ppermute | solution.py:292
  101.7 13.6 %all_to_all.16.sums_ref = f32[32,3,4,128]{3,2,1,0:T(4,128)S(1)} all-to-all(f32[32,3,4,128]{3,2,1,0:T(4,128)S(1)} %get-tuple-element.66), channel_id=1, replica_groups=mesh['blk'=4,'lat'=4,'depth'=2] {'blk','lat','depth'}, dimensions={0} | all-to-all | bytes 393216 | tf_op jit(solution)/shard_map/all_to_all | solution.py:418
  115.3 2.4 %shard_map.145 = (f32[768,512]{1,0:T(8,128)}, f32[1,512]{1,0:T(1,128)}, f32[1,512]{1,0:T(1,128)}) custom-call(s32[6]{0:T(128)S(1)} %bitcast.32, f32[32,3,4,128]{3,2,1,0:T(4,128)S(1)} %all_to_all.16.sums_ref, f32[1,512]{1,0:T(1,128)S(1)} %copy-done.19, f32[1,512]{1,0:T(1,128)S(1)} %get-tuple-element.68.square_ref, f32[768,512]{1,0:T(8,128)S(1)} %bitcast.18, ...), custom_call_target="tpu_custom_call" | custom-call | flops 1572864 | bytes 4718592 | tf_op jit(solution)/shard_map/pallas_call | solution.py:34
  (51 shorter events, 8.6 us)
Async XLA Ops:
  0.6 12.9 %copy-start.4 = (f32[1,1,1,768,256]{4,3,2,1,0:T(8,128)S(1)}, f32[1,1,1,768,256]{4,3,2,1,0:T(8,128)}, u32[]{:S(2)}) copy-start(f32[1,1,1,768,256]{4,3,2,1,0:T(8,128)} %param.16) | copy-start | bytes 2359300
  5.0 8.5 %copy-start = (f32[1,1,1,768,512]{4,3,2,1,0:T(8,128)S(1)}, f32[1,1,1,768,512]{4,3,2,1,0:T(8,128)}, u32[]{:S(2)}) copy-start(f32[1,1,1,768,512]{4,3,2,1,0:T(8,128)} %param.11) | copy-start | bytes 4718596
  5.0 8.5 %copy-start.16 = (s32[1,1,1,6]{3,2,1,0:T(1,128)S(1)}, s32[1,1,1,6]{3,2,1,0:T(1,128)}, u32[]{:S(2)}) copy-start(s32[1,1,1,6]{3,2,1,0:T(1,128)} %param.10) | copy-start | bytes 76
  5.0 8.5 %copy-start.17 = (s32[1,1,1,256,1]{3,4,2,1,0:T(1,128)S(1)}, s32[1,1,1,256,1]{3,4,2,1,0:T(1,128)}, u32[]{:S(2)}) copy-start(s32[1,1,1,256,1]{3,4,2,1,0:T(1,128)} %param.18) | copy-start | bytes 3076
  5.1 29.5 %all-to-all-start = ((f32[16,104,128]{2,1,0:T(8,128)}), f32[16,104,128]{2,1,0:T(8,128)}, u32[]{:S(2)}, u32[]{:S(2)}) async-start(f32[16,104,128]{2,1,0:T(8,128)} %shard_map.137), calls=%async_computation | async-start | bytes 1703936 | tf_op jit(solution)/shard_map/all_to_all | solution.py:418
  34.5 29.0 %copy-start.9 = (f32[768,512]{1,0:T(8,128)S(1)}, f32[768,512]{1,0:T(8,128)}, u32[]{:S(2)}) copy-start(f32[768,512]{1,0:T(8,128)} %copy-done.8) | copy-start | bytes 4718596
  34.5 29.0 %copy-start.11 = (bf16[768,256]{1,0:T(8,128)(2,1)S(1)}, bf16[768,256]{1,0:T(8,128)(2,1)}, u32[]{:S(2)}) copy-start(bf16[768,256]{1,0:T(8,128)(2,1)} %copy-done.10) | copy-start | bytes 1179652
  34.5 29.0 %copy-start.13 = (bf16[768,256]{1,0:T(8,128)(2,1)S(1)}, bf16[768,256]{1,0:T(8,128)(2,1)}, u32[]{:S(2)}) copy-start(bf16[768,256]{1,0:T(8,128)(2,1)} %copy-done.12) | copy-start | bytes 1179652
  34.5 29.0 %copy-start.15 = (bf16[256,384]{1,0:T(8,128)(2,1)S(1)}, bf16[256,384]{1,0:T(8,128)(2,1)}, u32[]{:S(2)}) copy-start(bf16[256,384]{1,0:T(8,128)(2,1)} %copy-done.14) | copy-start | bytes 589828
  63.5 13.9 %copy-start.1 = (f32[1,1,1,768,512]{4,3,2,1,0:T(8,128)S(1)}, f32[1,1,1,768,512]{4,3,2,1,0:T(8,128)}, u32[]{:S(2)}) copy-start(f32[1,1,1,768,512]{4,3,2,1,0:T(8,128)} %param.12) | copy-start | bytes 4718596
  63.5 13.9 %copy-start.3 = (bf16[768,768]{1,0:T(8,128)(2,1)S(1)}, bf16[768,768]{1,0:T(8,128)(2,1)}, u32[]{:S(2)}) copy-start(bf16[768,768]{1,0:T(8,128)(2,1)} %copy-done.2) | copy-start | bytes 3538948
  63.5 13.9 %copy-start.18 = (f32[512]{0:T(512)S(1)}, f32[512]{0:T(512)}, u32[]{:S(2)}) copy-start(f32[512]{0:T(512)} %param.13) | copy-start | bytes 6148
  64.8 10.6 %collective-permute-start = (f32[128,512]{1,0:T(8,128)S(1)}, f32[128,512]{1,0:T(8,128)S(1)}, u32[]{:S(2)}, u32[]{:S(2)}) collective-permute-start(f32[128,512]{1,0:T(8,128)S(1)} %get-tuple-element.49), channel_id=1, source_target_pairs={{0,8},{8,16},{16,24},{24,0},{1,9},{9,17},{17,25},{25,1},{2,10},{10... | collective-permute-start | bytes 786440 | tf_op jit(solution)/shard_map/ppermute | solution.py:292
  65.8 11.6 %collective-permute-start.1 = (f32[128,512]{1,0:T(8,128)S(1)}, f32[128,512]{1,0:T(8,128)S(1)}, u32[]{:S(2)}, u32[]{:S(2)}) collective-permute-start(f32[128,512]{1,0:T(8,128)S(1)} %get-tuple-element.50), channel_id=1, source_target_pairs={{0,24},{8,0},{16,8},{24,16},{1,25},{9,1},{17,9},{25,17},{2,26},{10... | collective-permute-start | bytes 786440 | tf_op jit(solution)/shard_map/ppermute | solution.py:292
  68.6 8.8 %collective-permute-start.2 = (f32[128,512]{1,0:T(8,128)S(1)}, f32[128,512]{1,0:T(8,128)S(1)}, u32[]{:S(2)}, u32[]{:S(2)}) collective-permute-start(f32[128,512]{1,0:T(8,128)S(1)} %get-tuple-element.51), channel_id=1, source_target_pairs={{0,1},{1,0},{2,3},{3,2},{4,5},{5,4},{6,7},{7,6},{8,9},{9,8},{10,11... | collective-permute-start | bytes 786440 | tf_op jit(solution)/shard_map/ppermute | solution.py:292
  68.6 1.5 %collective-permute-start.3 = (f32[8,128]{1,0:T(8,128)S(1)}, f32[8,128]{1,0:T(8,128)S(1)}, u32[]{:S(2)}, u32[]{:S(2)}) collective-permute-start(f32[8,128]{1,0:T(8,128)S(1)} %get-tuple-element.45.sums_ref), channel_id=1, source_target_pairs={{0,1},{1,0},{2,3},{3,2},{4,5},{5,4},{6,7},{7,6},{8,9},{9,8},{10,11... | collective-permute-start | bytes 12296 | tf_op jit(solution)/shard_map/ppermute | solution.py:514
  69.2 10.8 %collective-permute-start.4 = (f32[128,512]{1,0:T(8,128)S(1)}, f32[128,512]{1,0:T(8,128)S(1)}, u32[]{:S(2)}, u32[]{:S(2)}) collective-permute-start(f32[128,512]{1,0:T(8,128)S(1)} %get-tuple-element.55), channel_id=1, source_target_pairs={{2,4},{4,2},{3,5},{5,3},{10,12},{12,10},{11,13},{13,11},{18,20},{2... | collective-permute-start | bytes 786440 | tf_op jit(solution)/shard_map/ppermute | solution.py:292
  70.2 14.9 %collective-permute-start.5 = (f32[128,512]{1,0:T(8,128)S(1)}, f32[128,512]{1,0:T(8,128)S(1)}, u32[]{:S(2)}, u32[]{:S(2)}) collective-permute-start(f32[128,512]{1,0:T(8,128)S(1)} %get-tuple-element.56), channel_id=1, source_target_pairs={{0,2},{2,0},{4,6},{6,4},{1,3},{3,1},{5,7},{7,5},{8,10},{10,8},{12,... | collective-permute-start | bytes 786440 | tf_op jit(solution)/shard_map/ppermute | solution.py:292
  87.0 11.1 %collective-permute-start.6 = (f32[128,512]{1,0:T(8,128)S(1)}, f32[128,512]{1,0:T(8,128)S(1)}, u32[]{:S(2)}, u32[]{:S(2)}) collective-permute-start(f32[128,512]{1,0:T(8,128)S(1)} %get-tuple-element.61), channel_id=1, source_target_pairs={{0,8},{8,16},{16,24},{24,0},{1,9},{9,17},{17,25},{25,1},{2,10},{10... | collective-permute-start | bytes 786440 | tf_op jit(solution)/shard_map/ppermute | solution.py:292
  87.0 11.0 %collective-permute-start.7 = (f32[128,512]{1,0:T(8,128)S(1)}, f32[128,512]{1,0:T(8,128)S(1)}, u32[]{:S(2)}, u32[]{:S(2)}) collective-permute-start(f32[128,512]{1,0:T(8,128)S(1)} %get-tuple-element.62), channel_id=1, source_target_pairs={{2,4},{4,2},{3,5},{5,3},{10,12},{12,10},{11,13},{13,11},{18,20},{2... | collective-permute-start | bytes 786440 | tf_op jit(solution)/shard_map/ppermute | solution.py:292
  87.7 13.0 %collective-permute-start.8 = (f32[128,512]{1,0:T(8,128)S(1)}, f32[128,512]{1,0:T(8,128)S(1)}, u32[]{:S(2)}, u32[]{:S(2)}) collective-permute-start(f32[128,512]{1,0:T(8,128)S(1)} %get-tuple-element.63), channel_id=1, source_target_pairs={{0,24},{8,0},{16,8},{24,16},{1,25},{9,1},{17,9},{25,17},{2,26},{10... | collective-permute-start | bytes 786440 | tf_op jit(solution)/shard_map/ppermute | solution.py:292
  91.6 9.2 %collective-permute-start.9 = (f32[128,512]{1,0:T(8,128)S(1)}, f32[128,512]{1,0:T(8,128)S(1)}, u32[]{:S(2)}, u32[]{:S(2)}) collective-permute-start(f32[128,512]{1,0:T(8,128)S(1)} %get-tuple-element.64), channel_id=1, source_target_pairs={{0,2},{2,0},{4,6},{6,4},{1,3},{3,1},{5,7},{7,5},{8,10},{10,8},{12,... | collective-permute-start | bytes 786440 | tf_op jit(solution)/shard_map/ppermute | solution.py:292
  93.6 7.2 %collective-permute-start.10 = (f32[128,512]{1,0:T(8,128)S(1)}, f32[128,512]{1,0:T(8,128)S(1)}, u32[]{:S(2)}, u32[]{:S(2)}) collective-permute-start(f32[128,512]{1,0:T(8,128)S(1)} %get-tuple-element.65), channel_id=1, source_target_pairs={{0,1},{1,0},{2,3},{3,2},{4,5},{5,4},{6,7},{7,6},{8,9},{9,8},{10,11... | collective-permute-start | bytes 786440 | tf_op jit(solution)/shard_map/ppermute | solution.py:292
  100.8 14.6 %copy-start.19 = (f32[1,512]{1,0:T(1,128)S(1)}, f32[1,512]{1,0:T(1,128)}, u32[]{:S(2)}) copy-start(f32[1,512]{1,0:T(1,128)} %get-tuple-element.67.rho_ref) | copy-start | bytes 6148
  (8 other events, 9.1 us)

commit v6 on v5

--- a/solution.py
+++ b/solution.py
@@ -77,6 +77,16 @@
 def masked(len_ref, ref, face, rows):
     block = ref[face * rows : (face + 1) * rows, :]
     return jnp.where(live_rows(len_ref, face, rows), block, 0.0)
+
+
+def spread(out_ref, vector):
+    for j, piece in enumerate(folded(vector)):
+        out_ref[:, j, :] = jnp.broadcast_to(piece, (out_ref.shape[0], LANES))
+
+
+def gathered_sum(ref):
+    total = jnp.sum(ref[...], axis=0)
+    return unfolded(total, 0, total.shape[0])
 
 
 def folded(vector):
@@ -179,7 +189,7 @@
 
 def local_kernel(len_ref, residual_ref, matrix_ref, owner_ref, *refs):
     whole, refs = refs[:2], refs[2:]
-    local_ref, part_ref, square_ref, table_ref, refs = *refs[:4], refs[4:]
+    local_ref, part_ref, table_ref, refs = *refs[:3], refs[3:]
     rows = residual_ref.shape[0] // 6
     live = jnp.concatenate(
         [masked(len_ref, residual_ref, face, rows) for face in range(6)], axis=0
@@ -187,7 +197,6 @@
     local = product(parts(matrix_ref[...]), parts(0.5 * live))
     local_ref[...] = local
     part_ref[...] = jnp.sum(live * local, axis=0, keepdims=True)
-    square_ref[...] = jnp.sum(live * live, axis=0, keepdims=True)
     for i in range(2):
         refs[2 * i][...], refs[2 * i + 1][...] = parts(whole[i][...])
     primal, slots = table_ref.shape
@@ -210,7 +219,7 @@
     return jnp.concatenate(blocks, axis=0)
 
 
-def solve_kernel(incoming_any, inverse_any, local_part_ref, square_ref, answer_ref, *refs):
+def solve_kernel(incoming_any, inverse_any, local_part_ref, answer_ref, *refs):
     names_ref, slab_ref, inverse_ref, sems = refs
     owners, height, _ = slab_ref.shape
     pieces = height // CAP
@@ -237,7 +246,7 @@
     solved = product(parts(inverse_ref[...]), parts(summed))
     put_slab(answer_ref, select(table, solved))
     total = local_part_ref[...] + 2.0 * jnp.sum(summed * solved, axis=0, keepdims=True)
-    sums = folded(total) + folded(square_ref[...])
+    sums = folded(total)
     sums += [jnp.zeros((1, LANES), f32)] * (tiles(len(sums)) - len(sums))
     answer_ref[:, pieces * CAP :, :] = jnp.broadcast_to(
         jnp.concatenate(sums, axis=0)[None], (owners, len(sums), LANES)
@@ -248,7 +257,7 @@
 
 
 def moves():
-    order = [("blk", "up"), ("lat", 1), ("blk", "down"), ("lat", 0), ("depth", 1), ("depth", 0)]
+    order = [("lat", 1), ("blk", "up"), ("lat", 0), ("depth", 1), ("depth", 0), ("blk", "down")]
     return [(axis, way) for axis, way in order if route(axis, way)]
 
 
@@ -321,97 +330,97 @@
         sums, refs = sums_ref[...] + refs[0][...], refs[1:]
     else:
         sums = jnp.sum(sums_ref[...], axis=0)
-    rho_out, beta_out, square_out, near_ref, image_out = refs
+    rho_out, beta_out, near_ref, image_out = refs
     rows = image_ref.shape[0] // 6
     folds = image_ref.shape[1] // LANES
     rho = scale * unfolded(sums, 0, folds)
     beta = rho / prev_rho_ref[...]
     rho_out[...] = rho
     beta_out[...] = beta
-    square_out[...] = unfolded(sums, folds, folds)
-    for i, face in enumerate((0, 1, 4, 5)):
+    for i, face in enumerate((0, 2, 3, 4, 5)):
         near_ref[i * rows : (i + 1) * rows, :] = new_direction(
             len_ref, beta, image_ref, prev_ref, got, face, rows
         )
     high, low = parts(near_ref[...])
-    first, last = 2 * rows, 4 * rows
+    last = 2 * rows
     image_out[...] = product(
-        (high_ref[:, :first], low_ref[:, :first]), (high[:first], low[:first])
-    ) + product((high_ref[:, last:], low_ref[:, last:]), (high[first:], low[first:]))
+        (high_ref[:, last:], low_ref[:, last:]), (high[rows:], low[rows:])
+    ) + product((high_ref[:, :rows], low_ref[:, :rows]), (high[:rows], low[:rows]))
 
 
 def far_kernel(keys, len_ref, beta_ref, image_ref, prev_ref, high_ref, low_ref, near_ref, near_image_ref, *refs):
     got, refs = dict(zip(keys, refs)), refs[len(keys) :]
-    (direction_out, schur_out), face_refs, (far_ref, sems) = refs[:2], refs[2:-2], refs[-2:]
+    far_ref, schur_out, spread_ref, *face_refs = refs
     rows = image_ref.shape[0] // 6
-    first, last = 2 * rows, 4 * rows
-    pair = pl.ds(0, first)
-    copies = [
-        pltpu.make_async_copy(near_ref.at[pair], direction_out.at[pair], sems.at[0]),
-        pltpu.make_async_copy(
-            near_ref.at[pl.ds(first, first)], direction_out.at[pl.ds(last, first)], sems.at[1]
-        ),
-        pltpu.make_async_copy(far_ref, direction_out.at[pl.ds(first, first)], sems.at[2]),
-    ]
-    copies[0].start()
-    copies[1].start()
-    beta = beta_ref[...]
-    for face in (2, 3):
-        far_ref[(face - 2) * rows : (face - 1) * rows, :] = new_direction(
-            len_ref, beta, image_ref, prev_ref, got, face, rows
-        )
-    copies[2].start()
-    image = near_image_ref[...] + product(
-        (high_ref[:, first:last], low_ref[:, first:last]), parts(far_ref[...])
-    )
+    far = new_direction(len_ref, beta_ref[...], image_ref, prev_ref, got, 1, rows)
+    far_ref[...] = far
+    at = slice(rows, 2 * rows)
+    image = near_image_ref[...] + product((high_ref[:, at], low_ref[:, at]), parts(far))
     schur_out[...] = image
     put_faces(image, rows, face_refs)
+    near = near_ref[...]
+    curve = (
+        jnp.sum(near[:rows] * image[:rows], axis=0, keepdims=True)
+        + jnp.sum(far * image[at], axis=0, keepdims=True)
+        + jnp.sum(near[rows:] * image[2 * rows :], axis=0, keepdims=True)
+    )
+    spread(spread_ref, 2.0 * curve)
+
+
+def store_kernel(near_ref, far_ref, direction_out, sems):
+    rows = far_ref.shape[0]
+    copies = [
+        pltpu.make_async_copy(
+            near_ref.at[pl.ds(0, rows)], direction_out.at[pl.ds(0, rows)], sems.at[0]
+        ),
+        pltpu.make_async_copy(far_ref, direction_out.at[pl.ds(rows, rows)], sems.at[1]),
+        pltpu.make_async_copy(
+            near_ref.at[pl.ds(rows, 4 * rows)],
+            direction_out.at[pl.ds(2 * rows, 4 * rows)],
+            sems.at[2],
+        ),
+    ]
+    for copy in copies:
+        copy.start()
     for copy in copies:
         copy.wait()
 
 
-def products_kernel(len_ref, direction_ref, schur_ref, residual_ref, curve_ref, cross_ref):
+def applied_kernel(scale, len_ref, curve_ref, rho_ref, schur_ref, residual_ref, *refs):
+    got, (applied_ref, alpha_ref, spread_ref) = dict(zip(moves(), refs)), refs[-3:]
     rows = schur_ref.shape[0] // 6
-    image = schur_ref[...]
-    live = jnp.concatenate(
-        [masked(len_ref, residual_ref, face, rows) for face in range(6)], axis=0
-    )
-    curve_ref[...] = 2.0 * jnp.sum(direction_ref[...] * image, axis=0, keepdims=True)
-    cross_ref[...] = 2.0 * jnp.sum(live * image, axis=0, keepdims=True)
-
-
-def applied_kernel(len_ref, curve_ref, cross_ref, schur_ref, *refs):
-    got, (applied_ref, spread_ref) = dict(zip(moves(), refs)), refs[-2:]
-    rows = schur_ref.shape[0] // 6
-    total = jnp.zeros(curve_ref.shape, f32)
+    alpha = rho_ref[...] / (scale * gathered_sum(curve_ref))
+    alpha_ref[...] = alpha
+    total = jnp.zeros(alpha.shape, f32)
     for face in range(6):
         at = slice(face * rows, (face + 1) * rows)
         applied = schur_ref[at, :] + got_face(got, face)
-        applied = jnp.where(live_rows(len_ref, face, rows), applied, 0.0)
         applied_ref[at, :] = applied
-        total += jnp.sum(applied * applied, axis=0, keepdims=True)
-    for i, vector in enumerate([curve_ref[...], cross_ref[...], total]):
-        for j, piece in enumerate(folded(vector)):
-            spread_ref[:, i, j, :] = jnp.broadcast_to(piece, (spread_ref.shape[0], LANES))
-
-
-def finish_kernel(scale, len_ref, sums_ref, rho_ref, square_ref, residual_ref, applied_ref, new_out, alpha_ref, norm_ref, new_ref, sems):
+        new = jnp.where(
+            live_rows(len_ref, face, rows), residual_ref[at, :] - alpha * applied, 0.0
+        )
+        total += jnp.sum(new * new, axis=0, keepdims=True)
+    spread(spread_ref, total)
+
+
+def residual_kernel(len_ref, alpha_ref, residual_ref, applied_ref, new_out, new_ref, sems):
     rows = applied_ref.shape[0] // 6
-    folds = sums_ref.shape[2]
-    sums = jnp.sum(sums_ref[...], axis=0)
-    curve, cross, square = [unfolded(sums[i], 0, folds) for i in range(3)]
-    alpha = rho_ref[...] / (scale * curve)
-    alpha_ref[...] = alpha
-    norm_ref[...] = scale * (square_ref[...] - 2.0 * alpha * cross + alpha * alpha * square)
+    alpha = alpha_ref[...]
     copies = []
     for face in range(6):
         at = slice(face * rows, (face + 1) * rows)
-        new_ref[at, :] = masked(len_ref, residual_ref, face, rows) - alpha * applied_ref[at, :]
+        new_ref[at, :] = jnp.where(
+            live_rows(len_ref, face, rows), residual_ref[at, :] - alpha * applied_ref[at, :], 0.0
+        )
         where = pl.ds(face * rows, rows)
         copies.append(pltpu.make_async_copy(new_ref.at[where], new_out.at[where], sems.at[face]))
         copies[-1].start()
     for copy in copies:
         copy.wait()
+
+
+def norm_kernel(scale, part_ref, norm_ref):
+    norm_ref[...] = scale * gathered_sum(part_ref)
 
 
 def to_all(x, axes):
@@ -441,7 +450,7 @@
     pair_depth = layers == 2
     scale = 0.5 / (devices * height)
     folds = width // LANES
-    tail = tiles(2 * folds)
+    tail = tiles(folds)
 
     lengths = face_len.reshape(6)
     residual = residual.reshape(height, width)
@@ -455,6 +464,7 @@
     whole = shape_of(height, width)
     row = shape_of(1, width)
     face = shape_of(rows, width)
+    copies = shape_of(devices, folds, LANES)
 
     (outgoing,) = call(
         pack_kernel,
@@ -474,9 +484,9 @@
         ],
     )
     incoming = to_all(outgoing, LAYER)
-    local, local_part, square, table, *halves = call(
+    local, local_part, table, *halves = call(
         local_kernel,
-        [whole, row, row, shape_of(primal, slots, dtype=bf16)]
+        [whole, row, shape_of(primal, slots, dtype=bf16)]
         + [shape_of(height, primal, dtype=bf16)] * 2
         + [shape_of(height, height, dtype=bf16)] * 2,
         [lengths, residual, neumann, owner, basis, schur],
@@ -488,7 +498,7 @@
     (answers,) = call(
         solve_kernel,
         [shape_of(owners, folds * CAP + tail, LANES)],
-        [incoming, inverse, local_part, square],
+        [incoming, inverse, local_part],
         far=range(2),
         flops=(8 * slots + 6 * owned) * owned * width,
         moved=8 * slots * width,
@@ -514,11 +524,11 @@
         sums = [sums, lax.ppermute(sums, "depth", route("depth", 0))]
     else:
         sums = [to_all(sums, "depth")]
-    near_keys = [key for key in keys if key[0] != "lat"]
-    far_keys = [key for key in keys if key[0] == "lat"]
-    rho, beta, square, near, near_image = call(
+    near_keys = [key for key in keys if key != ("blk", "down")]
+    far_keys = [("blk", "down")]
+    rho, beta, near, near_image = call(
         functools.partial(near_kernel, pair_depth, scale, near_keys),
-        [row, row, row, shape_of(4 * rows, width), whole],
+        [row, row, shape_of(5 * rows, width), whole],
         [lengths, sums[0], prev_rho.reshape(1, width), image, prev_direction, *schur_halves]
         + [got[key] for key in near_keys]
         + sums[1:],
@@ -526,43 +536,46 @@
         flops=4 * height * height * width,
         moved=4 * height * (height + 4 * width),
     )
-    direction, schur_image, *outward = call(
+    far, schur_image, curve, *outward = call(
         functools.partial(far_kernel, far_keys),
-        [whole, whole, *faces],
+        [face, whole, copies, *faces],
         [lengths, beta, image, prev_direction, *schur_halves, near, near_image]
         + [got[key] for key in far_keys],
         smem=(0,),
+        flops=height * height * width,
+        moved=4 * height * (height + 4 * width),
+    )
+    got = exchange(outward)
+    curve = to_all(curve, AXES)
+    (direction,) = call(
+        store_kernel,
+        [whole],
+        [near, far],
         far_out=(0,),
-        flops=2 * height * height * width,
-        moved=4 * height * (height + 4 * width),
-        scratch=[pltpu.VMEM((2 * rows, width), f32), pltpu.SemaphoreType.DMA((3,))],
-    )
-    got = exchange(outward)
-    curve, cross = call(
-        products_kernel,
-        [row, row],
-        [lengths, direction, schur_image, residual],
+        moved=8 * height * width,
+        scratch=[pltpu.SemaphoreType.DMA((3,))],
+    )
+    applied, alpha, norm_parts = call(
+        functools.partial(applied_kernel, scale),
+        [whole, row, copies],
+        [lengths, curve, rho, schur_image, residual, *got],
         smem=(0,),
         flops=4 * height * width,
         moved=12 * height * width,
     )
-    applied, spread = call(
-        applied_kernel,
-        [whole, shape_of(devices, 3, folds, LANES)],
-        [lengths, curve, cross, schur_image, *got],
-        smem=(0,),
-        flops=4 * height * width,
-        moved=12 * height * width,
-    )
-    new_residual, alpha, norm = call(
-        functools.partial(finish_kernel, scale),
-        [whole, row, row],
-        [lengths, to_all(spread, AXES), rho, square, residual, applied],
+    norm_parts = to_all(norm_parts, AXES)
+    (new_residual,) = call(
+        residual_kernel,
+        [whole],
+        [lengths, alpha, residual, applied],
         smem=(0,),
         far_out=(0,),
         flops=4 * height * width,
         moved=12 * height * width,
         scratch=[pltpu.VMEM((height, width), f32), pltpu.SemaphoreType.DMA((6,))],
+    )
+    (norm,) = call(
+        functools.partial(norm_kernel, scale), [row], [norm_parts], moved=4 * devices * width
     )
     out_shape = (1, 1, 1, height, width)
     return (

time: 118 us -> 118 us (level)
  starting transfers between devices: 23.3 us -> 27.2 us
  waiting for transfers between devices: 23.9 us -> 20.1 us
  blocking collectives: 40 us -> 38.6 us
  Pallas kernels: 20.5 us -> 21.7 us
    ppermute x10, waiting for transfers between devices: 13.8 us -> 4.48 us  [exchange(): lax.ppermute(block, axis, route(axis, way))]
    all_to_all x1 -> x2, waiting for transfers between devices: 9.81 us -> 14.6 us  [to_all(): return lax.all_to_all(x, axes, split_axis=0, concat_axis=0, tiled=True)]
    all_to_all x1 -> x2, starting transfers between devices: 8.49 us -> 11 us  [to_all(): return lax.all_to_all(x, axes, split_axis=0, concat_axis=0, tiled=True)]
    all_to_all x2, blocking collectives: 40 us -> 38.6 us  [to_all(): return lax.all_to_all(x, axes, split_axis=0, concat_axis=0, tiled=True)]
    ppermute x10, starting transfers between devices: 14.3 us -> 15.7 us  [exchange(): lax.ppermute(block, axis, route(axis, way))]
    pallas_call x9 -> x10, Pallas kernels: 20.5 us -> 21.7 us  [call(): pl.pallas_call(body, out_shape=list(outs), in_specs=in_specs, out_specs=o...]
    unnamed x40 -> x36, local copies, waits for them, and re-layouts: 9.12 us -> 8.48 us
  transfers between devices with their start and end apart: 12 -> 13, of which waited for: 7 -> 4; matrix products, arithmetic and copies ran while one was open for 0% -> 0% of each run, Pallas kernels for 6% -> 8%
where the time goes in v6:
time: 118 us; the launch traced here: 117 us
  blocking collectives  38.6 us (33%)
  starting transfers between devices  27.2 us (23%)
  Pallas kernels  21.7 us (18%)
  waiting for transfers between devices  20.1 us (17%)
  local copies, waits for them, and re-layouts  8.48 us (7%)
    all_to_all x2, blocking collectives, to_all(): return lax.all_to_all(x, axes, split_axis=0, concat_axis=0, tiled=True)  38.6 us
    pallas_call x10, Pallas kernels, call(): pl.pallas_call(body, out_shape=list(outs), in_specs=in_specs, out_specs=o...  21.7 us
    ppermute x10, starting transfers between devices, exchange(): lax.ppermute(block, axis, route(axis, way))  15.7 us
    all_to_all x2, waiting for transfers between devices, to_all(): return lax.all_to_all(x, axes, split_axis=0, concat_axis=0, tiled=True)  14.6 us
    all_to_all x2, starting transfers between devices, to_all(): return lax.all_to_all(x, axes, split_axis=0, concat_axis=0, tiled=True)  11 us
    unnamed x36, local copies, waits for them, and re-layouts  8.48 us
    ppermute x10, waiting for transfers between devices, exchange(): lax.ppermute(block, axis, route(axis, way))  4.48 us
  transfers between devices with their start and end apart: 13, of which 4 were waited for; matrix products, arithmetic and copies ran while one was open for 0% of the time, Pallas kernels for 8%

profile of v6, /device:TPU:0, one launch (start us, length us, event | category | flops | bytes accessed | tf_op | source)
XLA Modules:
  0.0 117.1 jit_solution(14242424252127594543)
XLA Ops:
  0.6 4.4 %shard_map.137 = f32[16,104,128]{2,1,0:T(8,128)} custom-call(s32[6]{0:T(128)} %bitcast.25, s32[1,256]{1,0:T(1,128)} %bitcast.31, s32[1,256]{1,0:T(1,128)} %bitcast.39, f32[768,512]{1,0:T(8,128)} %bitcast.15, f32[768,256]{1,0:T(8,128)} %bitcast.21), custom_call_target="tpu_custom_call" | custom-call | flops 603979776 | bytes 3145728 | tf_op jit(solution)/shard_map/pallas_call | solution.py:34
  5.1 8.5 %all-to-all-start = ((f32[16,104,128]{2,1,0:T(8,128)}), f32[16,104,128]{2,1,0:T(8,128)}, u32[]{:S(2)}, u32[]{:S(2)}) async-start(f32[16,104,128]{2,1,0:T(8,128)} %shard_map.137), calls=%async_computation | async-start | bytes 1703936 | tf_op jit(solution)/shard_map/all_to_all | solution.py:427
  13.6 1.7 %copy-done.7 = f32[1,1,1,768,768]{4,3,2,1,0:T(8,128)S(1)} copy-done((f32[1,1,1,768,768]{4,3,2,1,0:T(8,128)S(1)}, f32[1,1,1,768,768]{4,3,2,1,0:T(8,128)}, u32[]{:S(2)}) %copy-start.7) | copy-done | bytes 2359320
  15.3 1.7 %copy-done.8 = f32[1,1,1,768,768]{4,3,2,1,0:T(8,128)S(1)} copy-done((f32[1,1,1,768,768]{4,3,2,1,0:T(8,128)S(1)}, f32[1,1,1,768,768]{4,3,2,1,0:T(8,128)}, u32[]{:S(2)}) %copy-start.8) | copy-done | bytes 2359320
  16.9 3.4 %shard_map.138 = (f32[768,512]{1,0:T(8,128)S(1)}, f32[1,512]{1,0:T(1,128)S(1)}, bf16[256,384]{1,0:T(8,128)(2,1)S(1)}, bf16[768,256]{1,0:T(8,128)(2,1)S(1)}, bf16...) custom-call(s32[6]{0:T(128)S(1)} %bitcast.26, f32[768,512]{1,0:T(8,128)S(1)} %bitcast.16, ...), custom_call_target="tpu_custom_call" | custom-call | flops 1811939328 | bytes 10223616 | tf_op jit(solution)/shard_map/pallas_call | solution.py:34
  22.4 1.1 copy-done.9
  23.6 11.0 %all-to-all-done.incoming_any = f32[16,104,128]{2,1,0:T(8,128)} async-done(((f32[16,104,128]{2,1,0:T(8,128)}), f32[16,104,128]{2,1,0:T(8,128)}, u32[]{:S(2)}, u32[]{:S(2)}) %all-to-all-start) | async-done | bytes 852000 | tf_op jit(solution)/shard_map/all_to_all | solution.py:427
  34.5 2.5 %shard_map.139 = f32[16,104,128]{2,1,0:T(8,128)S(1)} custom-call(f32[16,104,128]{2,1,0:T(8,128)} %all-to-all-done.incoming_any, f32[256,256]{1,0:T(8,128)} %bitcast.40, f32[1,512]{1,0:T(1,128)S(1)} %get-tuple-element.34.local_part_ref), custom_call_target="tpu_custom_call" | custom-call | flops 603979776 | bytes 1572864 | tf_op jit(solution)/shard_map/pallas_call | solution.py:34
  37.1 26.5 %all_to_all.20.returned_ref = f32[16,104,128]{2,1,0:T(8,128)S(1)} all-to-all(f32[16,104,128]{2,1,0:T(8,128)S(1)} %shard_map.139), channel_id=1, replica_groups=mesh['blk'=4,'lat'=4,'depth'=2] {'blk','lat'}, dimensions={0} | all-to-all | bytes 1703936 | tf_op jit(solution)/shard_map/all_to_all | solution.py:427
  63.6 1.2 %shard_map.140 = (f32[768,512]{1,0:T(8,128)S(1)}, f32[8,128]{1,0:T(8,128)S(1)}, f32[128,512]{1,0:T(8,128)S(1)}, f32[128,512]{1,0:T(8,128)S(1)}, f32[128,512]{1,0...) custom-call(f32[16,104,128]{2,1,0:T(8,128)S(1)} %all_to_all.20.returned_ref, ...), custom_call_target="tpu_custom_call" | custom-call | flops 805306368 | bytes 6291456 | tf_op jit(solution)/shard_map/pallas_call | solution.py:34
  66.6 3.5 %collective-permute-start.2 = (f32[128,512]{1,0:T(8,128)S(1)}, f32[128,512]{1,0:T(8,128)S(1)}, u32[]{:S(2)}, u32[]{:S(2)}) collective-permute-start(f32[128,512]{1,0:T(8,128)S(1)} %get-tuple-element.45), channel_id=1, source_target_pairs={{0,2},{2,0},{4,6},{6,4},{1,3},{3,1},{5,7},{7,5},{8,10},{10,8},{12,... | collective-permute-start | bytes 786440 | tf_op jit(solution)/shard_map/ppermute | solution.py:301
  71.6 2.8 %collective-permute-start.5 = (f32[128,512]{1,0:T(8,128)S(1)}, f32[128,512]{1,0:T(8,128)S(1)}, u32[]{:S(2)}, u32[]{:S(2)}) collective-permute-start(f32[128,512]{1,0:T(8,128)S(1)} %get-tuple-element.50), channel_id=1, source_target_pairs={{0,24},{8,0},{16,8},{24,16},{1,25},{9,1},{17,9},{25,17},{2,26},{10... | collective-permute-start | bytes 786440 | tf_op jit(solution)/shard_map/ppermute | solution.py:301
  74.4 4.5 %collective-permute-done.2.refs_2_ = f32[128,512]{1,0:T(8,128)S(1)} collective-permute-done((f32[128,512]{1,0:T(8,128)S(1)}, f32[128,512]{1,0:T(8,128)S(1)}, u32[]{:S(2)}, u32[]{:S(2)}) %collective-permute-start.2) | collective-permute-done | bytes 262176 | tf_op jit(solution)/shard_map/ppermute | solution.py:301
  78.9 3.2 %shard_map.141 = (f32[1,512]{1,0:T(1,128)}, f32[1,512]{1,0:T(1,128)S(1)}, f32[640,512]{1,0:T(8,128)S(1)}, f32[768,512]{1,0:T(8,128)S(1)}) custom-call(s32[6]{0:T(128)S(1)} %bitcast.27, f32[8,128]{1,0:T(8,128)S(1)} %get-tuple-element.39.sums_ref, f32[1,512]{1,0:T(1,128)S(1)} %bitcast.33, f32[768,512]{1,0:T(8,128)S(1)} %get-tuple-element.40.image_ref, ...), custom_call_target="tpu_custom_call" | custom-call | flops 1207959552 | bytes 8650752 | tf_op jit(solution)/shard_map/pallas_call | solution.py:34
  82.2 1.5 %shard_map.142 = (f32[128,512]{1,0:T(8,128)S(1)}, f32[768,512]{1,0:T(8,128)S(1)}, f32[32,4,128]{2,1,0:T(4,128)S(1)}, f32[128,512]{1,0:T(8,128)S(1)}, f32[128,512...) custom-call(s32[6]{0:T(128)S(1)} %bitcast.28, ...), custom_call_target="tpu_custom_call" | custom-call | flops 301989888 | bytes 8650752 | tf_op jit(solution)/shard_map/pallas_call | solution.py:34
  84.3 1.5 %collective-permute-start.7 = (f32[128,512]{1,0:T(8,128)S(1)}, f32[128,512]{1,0:T(8,128)S(1)}, u32[]{:S(2)}, u32[]{:S(2)}) collective-permute-start(f32[128,512]{1,0:T(8,128)S(1)} %get-tuple-element.55), channel_id=1, source_target_pairs={{0,8},{8,16},{16,24},{24,0},{1,9},{9,17},{17,25},{25,1},{2,10},{10... | collective-permute-start | bytes 786440 | tf_op jit(solution)/shard_map/ppermute | solution.py:301
  85.8 2.3 %collective-permute-start.8 = (f32[128,512]{1,0:T(8,128)S(1)}, f32[128,512]{1,0:T(8,128)S(1)}, u32[]{:S(2)}, u32[]{:S(2)}) collective-permute-start(f32[128,512]{1,0:T(8,128)S(1)} %get-tuple-element.56), channel_id=1, source_target_pairs={{0,2},{2,0},{4,6},{6,4},{1,3},{3,1},{5,7},{7,5},{8,10},{10,8},{12,... | collective-permute-start | bytes 786440 | tf_op jit(solution)/shard_map/ppermute | solution.py:301
  88.1 3.2 %collective-permute-start.10 = (f32[128,512]{1,0:T(8,128)S(1)}, f32[128,512]{1,0:T(8,128)S(1)}, u32[]{:S(2)}, u32[]{:S(2)}) collective-permute-start(f32[128,512]{1,0:T(8,128)S(1)} %get-tuple-element.58), channel_id=1, source_target_pairs={{0,24},{8,0},{16,8},{24,16},{1,25},{9,1},{17,9},{25,17},{2,26},{10... | collective-permute-start | bytes 786440 | tf_op jit(solution)/shard_map/ppermute | solution.py:301
  91.3 12.1 %all_to_all.21.curve_ref = f32[32,4,128]{2,1,0:T(4,128)S(1)} all-to-all(f32[32,4,128]{2,1,0:T(4,128)S(1)} %get-tuple-element.51), channel_id=1, replica_groups=mesh['blk'=4,'lat'=4,'depth'=2] {'blk','lat','depth'}, dimensions={0} | all-to-all | bytes 131072 | tf_op jit(solution)/shard_map/all_to_all | solution.py:427
  103.4 1.9 %shard_map.143 = (f32[768,512]{1,0:T(8,128)S(1)}, f32[1,512]{1,0:T(1,128)}, f32[32,4,128]{2,1,0:T(4,128)}) custom-call(s32[6]{0:T(128)S(1)} %bitcast.29, f32[32,4,128]{2,1,0:T(4,128)S(1)} %all_to_all.21.curve_ref, f32[1,512]{1,0:T(1,128)S(1)} %copy-done.16, f32[768,512]{1,0:T(8,128)S(1)} %get-tuple-element.53.schur_ref, f32[768,512]{1,0:T(8,128)S(1)} %bitcast.17, ...), custom_call_target="tpu_custom_call" | custom-call | flops 1572864 | bytes 4718592 | tf_op jit(solution)/shard_map/pallas_call | solution.py:34
  106.5 2.6 %all-to-all-start.3 = ((f32[32,4,128]{2,1,0:T(4,128)}), f32[32,4,128]{2,1,0:T(4,128)S(1)}, u32[]{:S(2)}, u32[]{:S(2)}) async-start(f32[32,4,128]{2,1,0:T(4,128)} %get-tuple-element.62), calls=%async_computation.3 | async-start | bytes 131072 | tf_op jit(solution)/shard_map/all_to_all | solution.py:427
  109.1 1.2 %shard_map.145 = f32[768,512]{1,0:T(8,128)} custom-call(f32[640,512]{1,0:T(8,128)S(1)} %get-tuple-element.48.near_ref, f32[128,512]{1,0:T(8,128)S(1)} %get-tuple-element.61.far_ref), custom_call_target="tpu_custom_call" | custom-call | bytes 3145728 | tf_op jit(solution)/shard_map/pallas_call | solution.py:34
  111.0 1.8 %shard_map.144 = f32[768,512]{1,0:T(8,128)} custom-call(s32[6]{0:T(128)S(1)} %bitcast.30, f32[1,512]{1,0:T(1,128)S(1)} %copy-done.17, f32[768,512]{1,0:T(8,128)S(1)} %bitcast.18, f32[768,512]{1,0:T(8,128)S(1)} %copy-done.12), custom_call_target="tpu_custom_call" | custom-call | flops 1572864 | bytes 4718592 | tf_op jit(solution)/shard_map/pallas_call | solution.py:34
  112.8 3.7 %all-to-all-done.3.part_ref = f32[32,4,128]{2,1,0:T(4,128)S(1)} async-done(((f32[32,4,128]{2,1,0:T(4,128)}), f32[32,4,128]{2,1,0:T(4,128)S(1)}, u32[]{:S(2)}, u32[]{:S(2)}) %all-to-all-start.3) | async-done | bytes 65568 | tf_op jit(solution)/shard_map/all_to_all | solution.py:427
  (50 shorter events, 8.6 us)
Async XLA Ops:
  0.6 12.9 %copy-start.6 = (f32[1,1,1,768,256]{4,3,2,1,0:T(8,128)S(1)}, f32[1,1,1,768,256]{4,3,2,1,0:T(8,128)}, u32[]{:S(2)}) copy-start(f32[1,1,1,768,256]{4,3,2,1,0:T(8,128)} %param.16) | copy-start | bytes 2359300
  5.0 8.5 %copy-start = (f32[1,1,1,768,512]{4,3,2,1,0:T(8,128)S(1)}, f32[1,1,1,768,512]{4,3,2,1,0:T(8,128)}, u32[]{:S(2)}) copy-start(f32[1,1,1,768,512]{4,3,2,1,0:T(8,128)} %param.11) | copy-start | bytes 4718596
  5.0 8.5 %copy-start.13 = (s32[1,1,1,6]{3,2,1,0:T(1,128)S(1)}, s32[1,1,1,6]{3,2,1,0:T(1,128)}, u32[]{:S(2)}) copy-start(s32[1,1,1,6]{3,2,1,0:T(1,128)} %param.10) | copy-start | bytes 76
  5.0 8.5 %copy-start.14 = (s32[1,1,1,256,1]{3,4,2,1,0:T(1,128)S(1)}, s32[1,1,1,256,1]{3,4,2,1,0:T(1,128)}, u32[]{:S(2)}) copy-start(s32[1,1,1,256,1]{3,4,2,1,0:T(1,128)} %param.18) | copy-start | bytes 3076
  5.1 29.5 %all-to-all-start = ((f32[16,104,128]{2,1,0:T(8,128)}), f32[16,104,128]{2,1,0:T(8,128)}, u32[]{:S(2)}, u32[]{:S(2)}) async-start(f32[16,104,128]{2,1,0:T(8,128)} %shard_map.137), calls=%async_computation | async-start | bytes 1703936 | tf_op jit(solution)/shard_map/all_to_all | solution.py:427
  34.5 29.1 %copy-start.10 = (f32[768,512]{1,0:T(8,128)S(1)}, f32[768,512]{1,0:T(8,128)}, u32[]{:S(2)}) copy-start(f32[768,512]{1,0:T(8,128)} %copy-done.9) | copy-start | bytes 4718596
  37.1 41.8 %copy-start.5 = (bf16[768,768]{1,0:T(8,128)(2,1)S(1)}, bf16[768,768]{1,0:T(8,128)(2,1)}, u32[]{:S(2)}) copy-start(bf16[768,768]{1,0:T(8,128)(2,1)} %copy-done.4) | copy-start | bytes 3538948
  63.6 15.3 %copy-start.1 = (f32[1,1,1,768,512]{4,3,2,1,0:T(8,128)S(1)}, f32[1,1,1,768,512]{4,3,2,1,0:T(8,128)}, u32[]{:S(2)}) copy-start(f32[1,1,1,768,512]{4,3,2,1,0:T(8,128)} %param.12) | copy-start | bytes 4718596
  63.6 15.3 %copy-start.3 = (bf16[768,768]{1,0:T(8,128)(2,1)S(1)}, bf16[768,768]{1,0:T(8,128)(2,1)}, u32[]{:S(2)}) copy-start(bf16[768,768]{1,0:T(8,128)(2,1)} %copy-done.2) | copy-start | bytes 3538948
  63.6 15.3 %copy-start.15 = (f32[512]{0:T(512)S(1)}, f32[512]{0:T(512)}, u32[]{:S(2)}) copy-start(f32[512]{0:T(512)} %param.13) | copy-start | bytes 6148
  64.8 9.6 %collective-permute-start = (f32[128,512]{1,0:T(8,128)S(1)}, f32[128,512]{1,0:T(8,128)S(1)}, u32[]{:S(2)}, u32[]{:S(2)}) collective-permute-start(f32[128,512]{1,0:T(8,128)S(1)} %get-tuple-element.43), channel_id=1, source_target_pairs={{2,4},{4,2},{3,5},{5,3},{10,12},{12,10},{11,13},{13,11},{18,20},{2... | collective-permute-start | bytes 786440 | tf_op jit(solution)/shard_map/ppermute | solution.py:301
  65.5 8.9 %collective-permute-start.1 = (f32[128,512]{1,0:T(8,128)S(1)}, f32[128,512]{1,0:T(8,128)S(1)}, u32[]{:S(2)}, u32[]{:S(2)}) collective-permute-start(f32[128,512]{1,0:T(8,128)S(1)} %get-tuple-element.44), channel_id=1, source_target_pairs={{0,8},{8,16},{16,24},{24,0},{1,9},{9,17},{17,25},{25,1},{2,10},{10... | collective-permute-start | bytes 786440 | tf_op jit(solution)/shard_map/ppermute | solution.py:301
  66.6 12.3 %collective-permute-start.2 = (f32[128,512]{1,0:T(8,128)S(1)}, f32[128,512]{1,0:T(8,128)S(1)}, u32[]{:S(2)}, u32[]{:S(2)}) collective-permute-start(f32[128,512]{1,0:T(8,128)S(1)} %get-tuple-element.45), channel_id=1, source_target_pairs={{0,2},{2,0},{4,6},{6,4},{1,3},{3,1},{5,7},{7,5},{8,10},{10,8},{12,... | collective-permute-start | bytes 786440 | tf_op jit(solution)/shard_map/ppermute | solution.py:301
  70.0 8.8 %collective-permute-start.3 = (f32[128,512]{1,0:T(8,128)S(1)}, f32[128,512]{1,0:T(8,128)S(1)}, u32[]{:S(2)}, u32[]{:S(2)}) collective-permute-start(f32[128,512]{1,0:T(8,128)S(1)} %get-tuple-element.46), channel_id=1, source_target_pairs={{0,1},{1,0},{2,3},{3,2},{4,5},{5,4},{6,7},{7,6},{8,9},{9,8},{10,11... | collective-permute-start | bytes 786440 | tf_op jit(solution)/shard_map/ppermute | solution.py:301
  70.0 1.5 %collective-permute-start.4 = (f32[8,128]{1,0:T(8,128)S(1)}, f32[8,128]{1,0:T(8,128)S(1)}, u32[]{:S(2)}, u32[]{:S(2)}) collective-permute-start(f32[8,128]{1,0:T(8,128)S(1)} %get-tuple-element.39.sums_ref), channel_id=1, source_target_pairs={{0,1},{1,0},{2,3},{3,2},{4,5},{5,4},{6,7},{7,6},{8,9},{9,8},{10,11... | collective-permute-start | bytes 12296 | tf_op jit(solution)/shard_map/ppermute | solution.py:524
  71.6 10.6 %collective-permute-start.5 = (f32[128,512]{1,0:T(8,128)S(1)}, f32[128,512]{1,0:T(8,128)S(1)}, u32[]{:S(2)}, u32[]{:S(2)}) collective-permute-start(f32[128,512]{1,0:T(8,128)S(1)} %get-tuple-element.50), channel_id=1, source_target_pairs={{0,24},{8,0},{16,8},{24,16},{1,25},{9,1},{17,9},{25,17},{2,26},{10... | collective-permute-start | bytes 786440 | tf_op jit(solution)/shard_map/ppermute | solution.py:301
  82.2 21.3 %copy-start.16 = (f32[1,512]{1,0:T(1,128)S(1)}, f32[1,512]{1,0:T(1,128)}, u32[]{:S(2)}) copy-start(f32[1,512]{1,0:T(1,128)} %get-tuple-element.52.rho_ref) | copy-start | bytes 6148
  83.6 19.7 %collective-permute-start.6 = (f32[128,512]{1,0:T(8,128)S(1)}, f32[128,512]{1,0:T(8,128)S(1)}, u32[]{:S(2)}, u32[]{:S(2)}) collective-permute-start(f32[128,512]{1,0:T(8,128)S(1)} %get-tuple-element.54), channel_id=1, source_target_pairs={{2,4},{4,2},{3,5},{5,3},{10,12},{12,10},{11,13},{13,11},{18,20},{2... | collective-permute-start | bytes 786440 | tf_op jit(solution)/shard_map/ppermute | solution.py:301
  84.3 19.1 %collective-permute-start.7 = (f32[128,512]{1,0:T(8,128)S(1)}, f32[128,512]{1,0:T(8,128)S(1)}, u32[]{:S(2)}, u32[]{:S(2)}) collective-permute-start(f32[128,512]{1,0:T(8,128)S(1)} %get-tuple-element.55), channel_id=1, source_target_pairs={{0,8},{8,16},{16,24},{24,0},{1,9},{9,17},{17,25},{25,1},{2,10},{10... | collective-permute-start | bytes 786440 | tf_op jit(solution)/shard_map/ppermute | solution.py:301
  85.8 17.6 %collective-permute-start.8 = (f32[128,512]{1,0:T(8,128)S(1)}, f32[128,512]{1,0:T(8,128)S(1)}, u32[]{:S(2)}, u32[]{:S(2)}) collective-permute-start(f32[128,512]{1,0:T(8,128)S(1)} %get-tuple-element.56), channel_id=1, source_target_pairs={{0,2},{2,0},{4,6},{6,4},{1,3},{3,1},{5,7},{7,5},{8,10},{10,8},{12,... | collective-permute-start | bytes 786440 | tf_op jit(solution)/shard_map/ppermute | solution.py:301
  88.1 15.3 %collective-permute-start.9 = (f32[128,512]{1,0:T(8,128)S(1)}, f32[128,512]{1,0:T(8,128)S(1)}, u32[]{:S(2)}, u32[]{:S(2)}) collective-permute-start(f32[128,512]{1,0:T(8,128)S(1)} %get-tuple-element.57), channel_id=1, source_target_pairs={{0,1},{1,0},{2,3},{3,2},{4,5},{5,4},{6,7},{7,6},{8,9},{9,8},{10,11... | collective-permute-start | bytes 786440 | tf_op jit(solution)/shard_map/ppermute | solution.py:301
  88.1 15.3 %collective-permute-start.10 = (f32[128,512]{1,0:T(8,128)S(1)}, f32[128,512]{1,0:T(8,128)S(1)}, u32[]{:S(2)}, u32[]{:S(2)}) collective-permute-start(f32[128,512]{1,0:T(8,128)S(1)} %get-tuple-element.58), channel_id=1, source_target_pairs={{0,24},{8,0},{16,8},{24,16},{1,25},{9,1},{17,9},{25,17},{2,26},{10... | collective-permute-start | bytes 786440 | tf_op jit(solution)/shard_map/ppermute | solution.py:301
  106.5 10.0 %all-to-all-start.3 = ((f32[32,4,128]{2,1,0:T(4,128)}), f32[32,4,128]{2,1,0:T(4,128)S(1)}, u32[]{:S(2)}, u32[]{:S(2)}) async-start(f32[32,4,128]{2,1,0:T(4,128)} %get-tuple-element.62), calls=%async_computation.3 | async-start | bytes 131072 | tf_op jit(solution)/shard_map/all_to_all | solution.py:427
  109.0 2.0 %copy-start.12 = (f32[768,512]{1,0:T(8,128)S(1)}, f32[768,512]{1,0:T(8,128)}, u32[]{:S(2)}) copy-start(f32[768,512]{1,0:T(8,128)} %copy-done.11) | copy-start | bytes 4718596
  (7 other events, 9.6 us)

commit v7 on v6

--- a/solution.py
+++ b/solution.py
@@ -24,8 +24,11 @@
     return jax.ShapeDtypeStruct(dims, dtype)
 
 
-def call(body, outs, operands, smem=(), far=(), far_out=(), flops=0, moved=0, scratch=(), room=32):
-    in_specs = [SMEM if i in smem else ANY if i in far else VMEM for i in range(len(operands))]
+def call(body, outs, operands, smem=(), far=(), loose=(), far_out=(), flops=0, moved=0, scratch=(), room=32):
+    in_specs = [
+        SMEM if i in smem else ANY if i in far or i in loose else VMEM
+        for i in range(len(operands))
+    ]
     operands = [
         pltpu.with_memory_space_constraint(x, pltpu.HBM) if i in far else x
         for i, x in enumerate(operands)
@@ -77,16 +80,6 @@
 def masked(len_ref, ref, face, rows):
     block = ref[face * rows : (face + 1) * rows, :]
     return jnp.where(live_rows(len_ref, face, rows), block, 0.0)
-
-
-def spread(out_ref, vector):
-    for j, piece in enumerate(folded(vector)):
-        out_ref[:, j, :] = jnp.broadcast_to(piece, (out_ref.shape[0], LANES))
-
-
-def gathered_sum(ref):
-    total = jnp.sum(ref[...], axis=0)
-    return unfolded(total, 0, total.shape[0])
 
 
 def folded(vector):
@@ -189,7 +182,7 @@
 
 def local_kernel(len_ref, residual_ref, matrix_ref, owner_ref, *refs):
     whole, refs = refs[:2], refs[2:]
-    local_ref, part_ref, table_ref, refs = *refs[:3], refs[3:]
+    local_ref, part_ref, square_ref, table_ref, refs = *refs[:4], refs[4:]
     rows = residual_ref.shape[0] // 6
     live = jnp.concatenate(
         [masked(len_ref, residual_ref, face, rows) for face in range(6)], axis=0
@@ -197,6 +190,7 @@
     local = product(parts(matrix_ref[...]), parts(0.5 * live))
     local_ref[...] = local
     part_ref[...] = jnp.sum(live * local, axis=0, keepdims=True)
+    square_ref[...] = jnp.sum(live * live, axis=0, keepdims=True)
     for i in range(2):
         refs[2 * i][...], refs[2 * i + 1][...] = parts(whole[i][...])
     primal, slots = table_ref.shape
@@ -219,7 +213,7 @@
     return jnp.concatenate(blocks, axis=0)
 
 
-def solve_kernel(incoming_any, inverse_any, local_part_ref, answer_ref, *refs):
+def solve_kernel(incoming_any, inverse_any, local_part_ref, square_ref, answer_ref, *refs):
     names_ref, slab_ref, inverse_ref, sems = refs
     owners, height, _ = slab_ref.shape
     pieces = height // CAP
@@ -246,7 +240,7 @@
     solved = product(parts(inverse_ref[...]), parts(summed))
     put_slab(answer_ref, select(table, solved))
     total = local_part_ref[...] + 2.0 * jnp.sum(summed * solved, axis=0, keepdims=True)
-    sums = folded(total)
+    sums = folded(total) + folded(square_ref[...])
     sums += [jnp.zeros((1, LANES), f32)] * (tiles(len(sums)) - len(sums))
     answer_ref[:, pieces * CAP :, :] = jnp.broadcast_to(
         jnp.concatenate(sums, axis=0)[None], (owners, len(sums), LANES)
@@ -256,8 +250,11 @@
 AXIS_AT = {"blk": 0, "lat": 2, "depth": 4}
 
 
-def moves():
-    order = [("lat", 1), ("blk", "up"), ("lat", 0), ("depth", 1), ("depth", 0), ("blk", "down")]
+FIRST = [("lat", 1), ("blk", "up"), ("lat", 0), ("depth", 1), ("depth", 0), ("blk", "down")]
+SECOND = [("blk", "up"), ("lat", 1), ("blk", "down"), ("lat", 0), ("depth", 1), ("depth", 0)]
+
+
+def moves(order):
     return [(axis, way) for axis, way in order if route(axis, way)]
 
 
@@ -273,8 +270,8 @@
     return lax.rem(lax.axis_index(axis), 2) == way
 
 
-def put_faces(image, rows, face_refs):
-    for ref, (axis, way) in zip(face_refs, moves(), strict=True):
+def put_faces(image, rows, order, face_refs):
+    for ref, (axis, way) in zip(face_refs, moves(order), strict=True):
         at = AXIS_AT[axis] * rows
         minus, plus = image[at : at + rows, :], image[at + rows : at + 2 * rows, :]
         if way in ("up", "down"):
@@ -296,10 +293,10 @@
     return total
 
 
-def exchange(faces):
+def exchange(faces, order):
     return [
         lax.ppermute(block, axis, route(axis, way))
-        for block, (axis, way) in zip(faces, moves(), strict=True)
+        for block, (axis, way) in zip(faces, moves(order), strict=True)
     ]
 
 
@@ -310,7 +307,7 @@
     correction = select(table_ref[...], get_slab(returned_ref, folds))
     image = local_ref[...] + product((high_ref[...], low_ref[...]), parts(correction))
     image_ref[...] = image
-    put_faces(image, rows, face_refs)
+    put_faces(image, rows, FIRST, face_refs)
     tail = jnp.sum(returned_ref[:, folds * CAP :, :], axis=0)
     if pair_depth:
         sums_ref[...] = tail
@@ -330,13 +327,14 @@
         sums, refs = sums_ref[...] + refs[0][...], refs[1:]
     else:
         sums = jnp.sum(sums_ref[...], axis=0)
-    rho_out, beta_out, near_ref, image_out = refs
+    rho_out, beta_out, square_out, near_ref, image_out = refs
     rows = image_ref.shape[0] // 6
     folds = image_ref.shape[1] // LANES
     rho = scale * unfolded(sums, 0, folds)
     beta = rho / prev_rho_ref[...]
     rho_out[...] = rho
     beta_out[...] = beta
+    square_out[...] = unfolded(sums, folds, folds)
     for i, face in enumerate((0, 2, 3, 4, 5)):
         near_ref[i * rows : (i + 1) * rows, :] = new_direction(
             len_ref, beta, image_ref, prev_ref, got, face, rows
@@ -350,21 +348,14 @@
 
 def far_kernel(keys, len_ref, beta_ref, image_ref, prev_ref, high_ref, low_ref, near_ref, near_image_ref, *refs):
     got, refs = dict(zip(keys, refs)), refs[len(keys) :]
-    far_ref, schur_out, spread_ref, *face_refs = refs
+    far_ref, schur_out, *face_refs = refs
     rows = image_ref.shape[0] // 6
     far = new_direction(len_ref, beta_ref[...], image_ref, prev_ref, got, 1, rows)
     far_ref[...] = far
     at = slice(rows, 2 * rows)
     image = near_image_ref[...] + product((high_ref[:, at], low_ref[:, at]), parts(far))
     schur_out[...] = image
-    put_faces(image, rows, face_refs)
-    near = near_ref[...]
-    curve = (
-        jnp.sum(near[:rows] * image[:rows], axis=0, keepdims=True)
-        + jnp.sum(far * image[at], axis=0, keepdims=True)
-        + jnp.sum(near[rows:] * image[2 * rows :], axis=0, keepdims=True)
-    )
-    spread(spread_ref, 2.0 * curve)
+    put_faces(image, rows, SECOND, face_refs)
 
 
 def store_kernel(near_ref, far_ref, direction_out, sems):
@@ -386,41 +377,66 @@
         copy.wait()
 
 
-def applied_kernel(scale, len_ref, curve_ref, rho_ref, schur_ref, residual_ref, *refs):
-    got, (applied_ref, alpha_ref, spread_ref) = dict(zip(moves(), refs)), refs[-3:]
+def products_kernel(len_ref, near_ref, far_ref, schur_ref, residual_ref, arrived, out_ref):
+    rows = far_ref.shape[0]
+    image = schur_ref[...]
+    near = near_ref[...]
+    direction = jnp.concatenate([near[:rows], far_ref[...], near[rows:]], axis=0)
+    live = jnp.concatenate(
+        [masked(len_ref, residual_ref, face, rows) for face in range(6)], axis=0
+    )
+    curve = 2.0 * jnp.sum(direction * image, axis=0, keepdims=True)
+    cross = 2.0 * jnp.sum(live * image, axis=0, keepdims=True)
+    for j, piece in enumerate(folded(curve) + folded(cross)):
+        out_ref[j : j + 1, :] = piece
+
+
+def applied_kernel(pair_depth, len_ref, schur_ref, *refs):
+    keys = moves(SECOND)
+    got, refs = dict(zip(keys, refs)), refs[len(keys) :]
+    products, (applied_ref, spread_ref) = refs[:-2], refs[-2:]
     rows = schur_ref.shape[0] // 6
-    alpha = rho_ref[...] / (scale * gathered_sum(curve_ref))
-    alpha_ref[...] = alpha
-    total = jnp.zeros(alpha.shape, f32)
+    folds = schur_ref.shape[1] // LANES
+    total = jnp.zeros((1, schur_ref.shape[1]), f32)
     for face in range(6):
         at = slice(face * rows, (face + 1) * rows)
         applied = schur_ref[at, :] + got_face(got, face)
+        applied = jnp.where(live_rows(len_ref, face, rows), applied, 0.0)
         applied_ref[at, :] = applied
-        new = jnp.where(
-            live_rows(len_ref, face, rows), residual_ref[at, :] - alpha * applied, 0.0
-        )
-        total += jnp.sum(new * new, axis=0, keepdims=True)
-    spread(spread_ref, total)
-
-
-def residual_kernel(len_ref, alpha_ref, residual_ref, applied_ref, new_out, new_ref, sems):
+        total += jnp.sum(applied * applied, axis=0, keepdims=True)
+    products = sum(ref[...] for ref in products)
+    halves = [products[:folds], products[folds : 2 * folds]]
+    if pair_depth:
+        halves = [jnp.where(lax.axis_index("depth") == 0, *halves)]
+    for i, half in enumerate([*halves, jnp.concatenate(folded(total), axis=0)]):
+        spread_ref[:, i, :, :] = jnp.broadcast_to(half[None], (spread_ref.shape[0], folds, LANES))
+
+
+def finish_kernel(pair_depth, scale, len_ref, sums_ref, rho_ref, square_ref, residual_ref, applied_ref, new_out, alpha_ref, norm_ref, new_ref, sems):
     rows = applied_ref.shape[0] // 6
-    alpha = alpha_ref[...]
+    devices, _, folds, _ = sums_ref.shape
+    if pair_depth:
+        pairs = sums_ref[...].reshape(devices // 2, 2, 2, folds, LANES)
+        pairs = jnp.sum(pairs, axis=0)
+        sums = [pairs[0, 0], pairs[1, 0], pairs[0, 1] + pairs[1, 1]]
+    else:
+        total = jnp.sum(sums_ref[...], axis=0)
+        sums = [total[i] for i in range(3)]
+    curve, cross, applied_square = [unfolded(x, 0, folds) for x in sums]
+    alpha = rho_ref[...] / (scale * curve)
+    alpha_ref[...] = alpha
+    norm_ref[...] = scale * (
+        square_ref[...] - 2.0 * alpha * cross + alpha * alpha * applied_square
+    )
     copies = []
     for face in range(6):
         at = slice(face * rows, (face + 1) * rows)
-        new_ref[at, :] = jnp.where(
-            live_rows(len_ref, face, rows), residual_ref[at, :] - alpha * applied_ref[at, :], 0.0
-        )
+        new_ref[at, :] = masked(len_ref, residual_ref, face, rows) - alpha * applied_ref[at, :]
         where = pl.ds(face * rows, rows)
         copies.append(pltpu.make_async_copy(new_ref.at[where], new_out.at[where], sems.at[face]))
         copies[-1].start()
     for copy in copies:
         copy.wait()
-
-
-def norm_kernel(scale, part_ref, norm_ref):
-    norm_ref[...] = scale * gathered_sum(part_ref)
 
 
 def to_all(x, axes):
@@ -450,7 +466,7 @@
     pair_depth = layers == 2
     scale = 0.5 / (devices * height)
     folds = width // LANES
-    tail = tiles(folds)
+    tail = tiles(2 * folds)
 
     lengths = face_len.reshape(6)
     residual = residual.reshape(height, width)
@@ -464,7 +480,6 @@
     whole = shape_of(height, width)
     row = shape_of(1, width)
     face = shape_of(rows, width)
-    copies = shape_of(devices, folds, LANES)
 
     (outgoing,) = call(
         pack_kernel,
@@ -484,9 +499,9 @@
         ],
     )
     incoming = to_all(outgoing, LAYER)
-    local, local_part, table, *halves = call(
+    local, local_part, square, table, *halves = call(
         local_kernel,
-        [whole, row, shape_of(primal, slots, dtype=bf16)]
+        [whole, row, row, shape_of(primal, slots, dtype=bf16)]
         + [shape_of(height, primal, dtype=bf16)] * 2
         + [shape_of(height, height, dtype=bf16)] * 2,
         [lengths, residual, neumann, owner, basis, schur],
@@ -498,7 +513,7 @@
     (answers,) = call(
         solve_kernel,
         [shape_of(owners, folds * CAP + tail, LANES)],
-        [incoming, inverse, local_part],
+        [incoming, inverse, local_part, square],
         far=range(2),
         flops=(8 * slots + 6 * owned) * owned * width,
         moved=8 * slots * width,
@@ -510,7 +525,7 @@
         ],
     )
     returned = to_all(answers, LAYER)
-    keys = moves()
+    keys = moves(FIRST)
     faces = [face] * len(keys)
     image, sums, *outward = call(
         functools.partial(image_kernel, pair_depth),
@@ -519,16 +534,16 @@
         flops=(6 * height + 4 * slots) * primal * width,
         moved=16 * height * width,
     )
-    got = dict(zip(keys, exchange(outward)))
+    got = dict(zip(keys, exchange(outward, FIRST)))
     if pair_depth:
         sums = [sums, lax.ppermute(sums, "depth", route("depth", 0))]
     else:
         sums = [to_all(sums, "depth")]
     near_keys = [key for key in keys if key != ("blk", "down")]
     far_keys = [("blk", "down")]
-    rho, beta, near, near_image = call(
+    rho, beta, square, near, near_image = call(
         functools.partial(near_kernel, pair_depth, scale, near_keys),
-        [row, row, shape_of(5 * rows, width), whole],
+        [row, row, row, shape_of(5 * rows, width), whole],
         [lengths, sums[0], prev_rho.reshape(1, width), image, prev_direction, *schur_halves]
         + [got[key] for key in near_keys]
         + sums[1:],
@@ -536,17 +551,28 @@
         flops=4 * height * height * width,
         moved=4 * height * (height + 4 * width),
     )
-    far, schur_image, curve, *outward = call(
+    far, schur_image, *outward = call(
         functools.partial(far_kernel, far_keys),
-        [face, whole, copies, *faces],
+        [face, whole, *faces],
         [lengths, beta, image, prev_direction, *schur_halves, near, near_image]
         + [got[key] for key in far_keys],
         smem=(0,),
         flops=height * height * width,
         moved=4 * height * (height + 4 * width),
     )
-    got = exchange(outward)
-    curve = to_all(curve, AXES)
+    got = exchange(outward, SECOND)
+    (products,) = call(
+        products_kernel,
+        [shape_of(2 * folds, LANES)],
+        [lengths, near, far, schur_image, residual, got[0]],
+        smem=(0,),
+        loose=(5,),
+        flops=4 * height * width,
+        moved=12 * height * width,
+    )
+    products = [products]
+    if pair_depth:
+        products.append(lax.ppermute(products[0], "depth", route("depth", 0)))
     (direction,) = call(
         store_kernel,
         [whole],
@@ -555,27 +581,23 @@
         moved=8 * height * width,
         scratch=[pltpu.SemaphoreType.DMA((3,))],
     )
-    applied, alpha, norm_parts = call(
-        functools.partial(applied_kernel, scale),
-        [whole, row, copies],
-        [lengths, curve, rho, schur_image, residual, *got],
+    applied, spread_sums = call(
+        functools.partial(applied_kernel, pair_depth),
+        [whole, shape_of(devices, 2 if pair_depth else 3, folds, LANES)],
+        [lengths, schur_image, *got, *products],
         smem=(0,),
         flops=4 * height * width,
         moved=12 * height * width,
     )
-    norm_parts = to_all(norm_parts, AXES)
-    (new_residual,) = call(
-        residual_kernel,
-        [whole],
-        [lengths, alpha, residual, applied],
+    new_residual, alpha, norm = call(
+        functools.partial(finish_kernel, pair_depth, scale),
+        [whole, row, row],
+        [lengths, to_all(spread_sums, AXES), rho, square, residual, applied],
         smem=(0,),
         far_out=(0,),
         flops=4 * height * width,
         moved=12 * height * width,
         scratch=[pltpu.VMEM((height, width), f32), pltpu.SemaphoreType.DMA((6,))],
-    )
-    (norm,) = call(
-        functools.partial(norm_kernel, scale), [row], [norm_parts], moved=4 * devices * width
     )
     out_shape = (1, 1, 1, height, width)
     return (

time: 118 us -> 119 us (level)
  blocking collectives: 38.6 us -> 26.5 us
  waiting for transfers between devices: 20.1 us -> 30.5 us
  starting transfers between devices: 27.2 us -> 29.3 us
    all_to_all x2 -> x1, blocking collectives: 38.6 us -> 26.5 us  [to_all(): return lax.all_to_all(x, axes, split_axis=0, concat_axis=0, tiled=True)]
    ppermute x10, waiting for transfers between devices: 4.48 us -> 11.5 us  [exchange(): lax.ppermute(block, axis, route(axis, way))]
    all_to_all x2, waiting for transfers between devices: 14.6 us -> 18 us  [to_all(): return lax.all_to_all(x, axes, split_axis=0, concat_axis=0, tiled=True)]
    all_to_all x2, starting transfers between devices: 11 us -> 13.1 us  [to_all(): return lax.all_to_all(x, axes, split_axis=0, concat_axis=0, tiled=True)]
    unnamed x36 -> x34, local copies, waits for them, and re-layouts: 8.48 us -> 9.12 us
  transfers between devices with their start and end apart: 13 -> 14, of which waited for: 4 -> 7; matrix products, arithmetic and copies ran while one was open for 0% -> 0% of each run, Pallas kernels for 8% -> 8%
where the time goes in v7:
time: 119 us
  waiting for transfers between devices  30.5 us (26%)
  starting transfers between devices  29.3 us (25%)
  blocking collectives  26.5 us (22%)
  Pallas kernels  22.6 us (19%)
  local copies, waits for them, and re-layouts  9.12 us (8%)
    all_to_all x1, blocking collectives, to_all(): return lax.all_to_all(x, axes, split_axis=0, concat_axis=0, tiled=True)  26.5 us
    pallas_call x10, Pallas kernels, call(): pl.pallas_call(body, out_shape=list(outs), in_specs=in_specs, out_specs=o...  22.6 us
    all_to_all x2, waiting for transfers between devices, to_all(): return lax.all_to_all(x, axes, split_axis=0, concat_axis=0, tiled=True)  18 us
    ppermute x10, starting transfers between devices, exchange(): lax.ppermute(block, axis, route(axis, way))  15.7 us
    all_to_all x2, starting transfers between devices, to_all(): return lax.all_to_all(x, axes, split_axis=0, concat_axis=0, tiled=True)  13.1 us
    ppermute x10, waiting for transfers between devices, exchange(): lax.ppermute(block, axis, route(axis, way))  11.5 us
    unnamed x34, local copies, waits for them, and re-layouts  9.12 us
  transfers between devices with their start and end apart: 14, of which 7 were waited for; matrix products, arithmetic and copies ran while one was open for 0% of the time, Pallas kernels for 8%

profile of v7, /device:TPU:0, one launch (start us, length us, event | category | flops | bytes accessed | tf_op | source)
XLA Modules:
  0.0 118.9 jit_solution(8778453519326521544)
XLA Ops:
  0.6 4.4 %shard_map.137 = f32[16,104,128]{2,1,0:T(8,128)} custom-call(s32[6]{0:T(128)} %bitcast.25, s32[1,256]{1,0:T(1,128)} %bitcast.32, s32[1,256]{1,0:T(1,128)} %bitcast.37, f32[768,512]{1,0:T(8,128)} %bitcast.15, f32[768,256]{1,0:T(8,128)} %bitcast.21), custom_call_target="tpu_custom_call" | custom-call | flops 603979776 | bytes 3145728 | tf_op jit(solution)/shard_map/pallas_call | solution.py:37
  5.1 8.5 %all-to-all-start = ((f32[16,104,128]{2,1,0:T(8,128)}), f32[16,104,128]{2,1,0:T(8,128)}, u32[]{:S(2)}, u32[]{:S(2)}) async-start(f32[16,104,128]{2,1,0:T(8,128)} %shard_map.137), calls=%async_computation | async-start | bytes 1703936 | tf_op jit(solution)/shard_map/all_to_all | solution.py:443
  13.6 1.7 %copy-done.7 = f32[1,1,1,768,768]{4,3,2,1,0:T(8,128)S(1)} copy-done((f32[1,1,1,768,768]{4,3,2,1,0:T(8,128)S(1)}, f32[1,1,1,768,768]{4,3,2,1,0:T(8,128)}, u32[]{:S(2)}) %copy-start.7) | copy-done | bytes 2359320
  15.3 1.7 %copy-done.8 = f32[1,1,1,768,768]{4,3,2,1,0:T(8,128)S(1)} copy-done((f32[1,1,1,768,768]{4,3,2,1,0:T(8,128)S(1)}, f32[1,1,1,768,768]{4,3,2,1,0:T(8,128)}, u32[]{:S(2)}) %copy-start.8) | copy-done | bytes 2359320
  16.9 3.4 %shard_map.138 = (f32[768,512]{1,0:T(8,128)S(1)}, f32[1,512]{1,0:T(1,128)S(1)}, f32[1,512]{1,0:T(1,128)S(1)}, bf16[256,384]{1,0:T(8,128)(2,1)S(1)}, bf16[768,256...) custom-call(s32[6]{0:T(128)S(1)} %bitcast.26, ...), custom_call_target="tpu_custom_call" | custom-call | flops 1811939328 | bytes 10223616 | tf_op jit(solution)/shard_map/pallas_call | solution.py:37
  23.6 10.9 %all-to-all-done.incoming_any = f32[16,104,128]{2,1,0:T(8,128)} async-done(((f32[16,104,128]{2,1,0:T(8,128)}), f32[16,104,128]{2,1,0:T(8,128)}, u32[]{:S(2)}, u32[]{:S(2)}) %all-to-all-start) | async-done | bytes 852000 | tf_op jit(solution)/shard_map/all_to_all | solution.py:443
  34.5 2.5 %shard_map.139 = f32[16,104,128]{2,1,0:T(8,128)S(1)} custom-call(f32[16,104,128]{2,1,0:T(8,128)} %all-to-all-done.incoming_any, f32[256,256]{1,0:T(8,128)} %bitcast.39, f32[1,512]{1,0:T(1,128)S(1)} %get-tuple-element.37.local_part_ref, f32[1,512]{1,0:T(1,128)S(1)} %get-tuple-element.38.square_ref), custom_call_target="tpu_custom_call" | custom-call | flops 603979776 | bytes 1572864 | tf_op jit(solution)/shard_map/pallas_call | solution.py:37
  37.1 26.5 %all_to_all.15.returned_ref = f32[16,104,128]{2,1,0:T(8,128)S(1)} all-to-all(f32[16,104,128]{2,1,0:T(8,128)S(1)} %shard_map.139), channel_id=1, replica_groups=mesh['blk'=4,'lat'=4,'depth'=2] {'blk','lat'}, dimensions={0} | all-to-all | bytes 1703936 | tf_op jit(solution)/shard_map/all_to_all | solution.py:443
  63.6 1.2 %shard_map.140 = (f32[768,512]{1,0:T(8,128)S(1)}, f32[8,128]{1,0:T(8,128)S(1)}, f32[128,512]{1,0:T(8,128)S(1)}, f32[128,512]{1,0:T(8,128)S(1)}, f32[128,512]{1,0...) custom-call(f32[16,104,128]{2,1,0:T(8,128)S(1)} %all_to_all.15.returned_ref, ...), custom_call_target="tpu_custom_call" | custom-call | flops 805306368 | bytes 6291456 | tf_op jit(solution)/shard_map/pallas_call | solution.py:37
  66.6 3.5 %collective-permute-start.2 = (f32[128,512]{1,0:T(8,128)S(1)}, f32[128,512]{1,0:T(8,128)S(1)}, u32[]{:S(2)}, u32[]{:S(2)}) collective-permute-start(f32[128,512]{1,0:T(8,128)S(1)} %get-tuple-element.49), channel_id=1, source_target_pairs={{0,2},{2,0},{4,6},{6,4},{1,3},{3,1},{5,7},{7,5},{8,10},{10,8},{12,... | collective-permute-start | bytes 786440 | tf_op jit(solution)/shard_map/ppermute | solution.py:298
  71.6 2.8 %collective-permute-start.5 = (f32[128,512]{1,0:T(8,128)S(1)}, f32[128,512]{1,0:T(8,128)S(1)}, u32[]{:S(2)}, u32[]{:S(2)}) collective-permute-start(f32[128,512]{1,0:T(8,128)S(1)} %get-tuple-element.54), channel_id=1, source_target_pairs={{0,24},{8,0},{16,8},{24,16},{1,25},{9,1},{17,9},{25,17},{2,26},{10... | collective-permute-start | bytes 786440 | tf_op jit(solution)/shard_map/ppermute | solution.py:298
  74.4 4.4 %collective-permute-done.2.refs_2_ = f32[128,512]{1,0:T(8,128)S(1)} collective-permute-done((f32[128,512]{1,0:T(8,128)S(1)}, f32[128,512]{1,0:T(8,128)S(1)}, u32[]{:S(2)}, u32[]{:S(2)}) %collective-permute-start.2) | collective-permute-done | bytes 262176 | tf_op jit(solution)/shard_map/ppermute | solution.py:298
  78.9 3.3 %shard_map.141 = (f32[1,512]{1,0:T(1,128)}, f32[1,512]{1,0:T(1,128)S(1)}, f32[1,512]{1,0:T(1,128)S(1)}, f32[640,512]{1,0:T(8,128)S(1)}, f32[768,512]{1,0:T(8,128)S(1)}) custom-call(s32[6]{0:T(128)S(1)} %bitcast.27, f32[8,128]{1,0:T(8,128)S(1)} %get-tuple-element.43.sums_ref, f32[1,512]{1,0:T(1,128)S(1)} %bitcast.34, ...), custom_call_target="tpu_custom_call" | custom-call | flops 1207959552 | bytes 8650752 | tf_op jit(solution)/shard_map/pallas_call | solution.py:37
  82.2 1.4 %shard_map.142 = (f32[128,512]{1,0:T(8,128)S(1)}, f32[768,512]{1,0:T(8,128)S(1)}, f32[128,512]{1,0:T(8,128)S(1)}, f32[128,512]{1,0:T(8,128)S(1)}, f32[128,512]{1...) custom-call(s32[6]{0:T(128)S(1)} %bitcast.28, f32[1,512]{1,0:T(1,128)S(1)} %get-tuple-element.51.beta_ref, ...), custom_call_target="tpu_custom_call" | custom-call | flops 301989888 | bytes 8650752 | tf_op jit(solution)/shard_map/pallas_call | solution.py:37
  83.5 1.5 %collective-permute-start.6 = (f32[128,512]{1,0:T(8,128)S(1)}, f32[128,512]{1,0:T(8,128)S(1)}, u32[]{:S(2)}, u32[]{:S(2)}) collective-permute-start(f32[128,512]{1,0:T(8,128)S(1)} %get-tuple-element.56), channel_id=1, source_target_pairs={{0,8},{8,16},{16,24},{24,0},{1,9},{9,17},{17,25},{25,1},{2,10},{10... | collective-permute-start | bytes 786440 | tf_op jit(solution)/shard_map/ppermute | solution.py:298
  85.7 2.4 %collective-permute-start.8 = (f32[128,512]{1,0:T(8,128)S(1)}, f32[128,512]{1,0:T(8,128)S(1)}, u32[]{:S(2)}, u32[]{:S(2)}) collective-permute-start(f32[128,512]{1,0:T(8,128)S(1)} %get-tuple-element.58), channel_id=1, source_target_pairs={{0,24},{8,0},{16,8},{24,16},{1,25},{9,1},{17,9},{25,17},{2,26},{10... | collective-permute-start | bytes 786440 | tf_op jit(solution)/shard_map/ppermute | solution.py:298
  88.1 3.1 %collective-permute-start.9 = (f32[128,512]{1,0:T(8,128)S(1)}, f32[128,512]{1,0:T(8,128)S(1)}, u32[]{:S(2)}, u32[]{:S(2)}) collective-permute-start(f32[128,512]{1,0:T(8,128)S(1)} %get-tuple-element.59), channel_id=1, source_target_pairs={{0,2},{2,0},{4,6},{6,4},{1,3},{3,1},{5,7},{7,5},{8,10},{10,8},{12,... | collective-permute-start | bytes 786440 | tf_op jit(solution)/shard_map/ppermute | solution.py:298
  91.2 3.4 %collective-permute-done.6.arrived.refs_0_ = f32[128,512]{1,0:T(8,128)S(1)} collective-permute-done((f32[128,512]{1,0:T(8,128)S(1)}, f32[128,512]{1,0:T(8,128)S(1)}, u32[]{:S(2)}, u32[]{:S(2)}) %collective-permute-start.6) | collective-permute-done | bytes 262176 | tf_op jit(solution)/shard_map/ppermute | solution.py:298
  96.9 2.6 %collective-permute-done.9.refs_3_ = f32[128,512]{1,0:T(8,128)S(1)} collective-permute-done((f32[128,512]{1,0:T(8,128)S(1)}, f32[128,512]{1,0:T(8,128)S(1)}, u32[]{:S(2)}, u32[]{:S(2)}) %collective-permute-start.9) | collective-permute-done | bytes 262176 | tf_op jit(solution)/shard_map/ppermute | solution.py:298
  99.5 1.6 %shard_map.144 = (f32[768,512]{1,0:T(8,128)S(1)}, f32[32,2,4,128]{3,2,1,0:T(4,128)}) custom-call(s32[6]{0:T(128)S(1)} %bitcast.30, f32[768,512]{1,0:T(8,128)S(1)} %get-tuple-element.55.schur_ref, f32[128,512]{1,0:T(8,128)S(1)} %collective-permute-done.6.arrived.refs_0_, f32[128,512]{1,0:T(8,128)S(1)} %collective-permute-done.7.refs_1_, ...), custom_call_target="tpu_custom_call" | custom-call | flops 1572864 | bytes 4718592 | tf_op jit(solution)/shard_map/pallas_call | solution.py:37
  102.3 4.6 %all-to-all-start.2 = ((f32[32,2,4,128]{3,2,1,0:T(4,128)}), f32[32,2,4,128]{3,2,1,0:T(4,128)S(1)}, u32[]{:S(2)}, u32[]{:S(2)}) async-start(f32[32,2,4,128]{3,2,1,0:T(4,128)} %get-tuple-element.62), calls=%async_computation.2 | async-start | bytes 262144 | tf_op jit(solution)/shard_map/all_to_all | solution.py:443
  108.1 7.0 %all-to-all-done.2.sums_ref = f32[32,2,4,128]{3,2,1,0:T(4,128)S(1)} async-done(((f32[32,2,4,128]{3,2,1,0:T(4,128)}), f32[32,2,4,128]{3,2,1,0:T(4,128)S(1)}, u32[]{:S(2)}, u32[]{:S(2)}) %all-to-all-start.2) | async-done | bytes 131104 | tf_op jit(solution)/shard_map/all_to_all | solution.py:443
  115.1 1.4 %copy-done.10 = f32[768,512]{1,0:T(8,128)S(1)} copy-done((f32[768,512]{1,0:T(8,128)S(1)}, f32[768,512]{1,0:T(8,128)}, u32[]{:S(2)}) %copy-start.10) | copy-done | bytes 1572888
  116.5 2.4 %shard_map.145 = (f32[768,512]{1,0:T(8,128)}, f32[1,512]{1,0:T(1,128)}, f32[1,512]{1,0:T(1,128)}) custom-call(s32[6]{0:T(128)S(1)} %bitcast.31, f32[32,2,4,128]{3,2,1,0:T(4,128)S(1)} %all-to-all-done.2.sums_ref, f32[1,512]{1,0:T(1,128)S(1)} %copy-done.16, f32[1,512]{1,0:T(1,128)S(1)} %get-tuple-element.64.square_ref, f32[768,512]{1,0:T(8,128)S(1)} %bitcast.18, ...), custom_call_target="tpu_custom_call" | custom-call | flops 1572864 | bytes 4718592 | tf_op jit(solution)/shard_map/pallas_call | solution.py:37
  (49 shorter events, 11.8 us)
Async XLA Ops:
  0.6 12.9 %copy-start.6 = (f32[1,1,1,768,256]{4,3,2,1,0:T(8,128)S(1)}, f32[1,1,1,768,256]{4,3,2,1,0:T(8,128)}, u32[]{:S(2)}) copy-start(f32[1,1,1,768,256]{4,3,2,1,0:T(8,128)} %param.16) | copy-start | bytes 2359300
  5.0 8.5 %copy-start = (f32[1,1,1,768,512]{4,3,2,1,0:T(8,128)S(1)}, f32[1,1,1,768,512]{4,3,2,1,0:T(8,128)}, u32[]{:S(2)}) copy-start(f32[1,1,1,768,512]{4,3,2,1,0:T(8,128)} %param.11) | copy-start | bytes 4718596
  5.0 8.5 %copy-start.13 = (s32[1,1,1,6]{3,2,1,0:T(1,128)S(1)}, s32[1,1,1,6]{3,2,1,0:T(1,128)}, u32[]{:S(2)}) copy-start(s32[1,1,1,6]{3,2,1,0:T(1,128)} %param.10) | copy-start | bytes 76
  5.1 8.5 %copy-start.14 = (s32[1,1,1,256,1]{3,4,2,1,0:T(1,128)S(1)}, s32[1,1,1,256,1]{3,4,2,1,0:T(1,128)}, u32[]{:S(2)}) copy-start(s32[1,1,1,256,1]{3,4,2,1,0:T(1,128)} %param.18) | copy-start | bytes 3076
  5.1 29.5 %all-to-all-start = ((f32[16,104,128]{2,1,0:T(8,128)}), f32[16,104,128]{2,1,0:T(8,128)}, u32[]{:S(2)}, u32[]{:S(2)}) async-start(f32[16,104,128]{2,1,0:T(8,128)} %shard_map.137), calls=%async_computation | async-start | bytes 1703936 | tf_op jit(solution)/shard_map/all_to_all | solution.py:443
  34.5 29.1 %copy-start.12 = (f32[768,512]{1,0:T(8,128)S(1)}, f32[768,512]{1,0:T(8,128)}, u32[]{:S(2)}) copy-start(f32[768,512]{1,0:T(8,128)} %copy-done.11) | copy-start | bytes 4718596
  37.1 41.8 %copy-start.5 = (bf16[768,768]{1,0:T(8,128)(2,1)S(1)}, bf16[768,768]{1,0:T(8,128)(2,1)}, u32[]{:S(2)}) copy-start(bf16[768,768]{1,0:T(8,128)(2,1)} %copy-done.4) | copy-start | bytes 3538948
  63.6 15.3 %copy-start.1 = (f32[1,1,1,768,512]{4,3,2,1,0:T(8,128)S(1)}, f32[1,1,1,768,512]{4,3,2,1,0:T(8,128)}, u32[]{:S(2)}) copy-start(f32[1,1,1,768,512]{4,3,2,1,0:T(8,128)} %param.12) | copy-start | bytes 4718596
  63.6 15.3 %copy-start.3 = (bf16[768,768]{1,0:T(8,128)(2,1)S(1)}, bf16[768,768]{1,0:T(8,128)(2,1)}, u32[]{:S(2)}) copy-start(bf16[768,768]{1,0:T(8,128)(2,1)} %copy-done.2) | copy-start | bytes 3538948
  63.6 15.3 %copy-start.15 = (f32[512]{0:T(512)S(1)}, f32[512]{0:T(512)}, u32[]{:S(2)}) copy-start(f32[512]{0:T(512)} %param.13) | copy-start | bytes 6148
  64.8 9.6 %collective-permute-start = (f32[128,512]{1,0:T(8,128)S(1)}, f32[128,512]{1,0:T(8,128)S(1)}, u32[]{:S(2)}, u32[]{:S(2)}) collective-permute-start(f32[128,512]{1,0:T(8,128)S(1)} %get-tuple-element.47), channel_id=1, source_target_pairs={{2,4},{4,2},{3,5},{5,3},{10,12},{12,10},{11,13},{13,11},{18,20},{2... | collective-permute-start | bytes 786440 | tf_op jit(solution)/shard_map/ppermute | solution.py:298
  65.5 8.9 %collective-permute-start.1 = (f32[128,512]{1,0:T(8,128)S(1)}, f32[128,512]{1,0:T(8,128)S(1)}, u32[]{:S(2)}, u32[]{:S(2)}) collective-permute-start(f32[128,512]{1,0:T(8,128)S(1)} %get-tuple-element.48), channel_id=1, source_target_pairs={{0,8},{8,16},{16,24},{24,0},{1,9},{9,17},{17,25},{25,1},{2,10},{10... | collective-permute-start | bytes 786440 | tf_op jit(solution)/shard_map/ppermute | solution.py:298
  66.6 12.3 %collective-permute-start.2 = (f32[128,512]{1,0:T(8,128)S(1)}, f32[128,512]{1,0:T(8,128)S(1)}, u32[]{:S(2)}, u32[]{:S(2)}) collective-permute-start(f32[128,512]{1,0:T(8,128)S(1)} %get-tuple-element.49), channel_id=1, source_target_pairs={{0,2},{2,0},{4,6},{6,4},{1,3},{3,1},{5,7},{7,5},{8,10},{10,8},{12,... | collective-permute-start | bytes 786440 | tf_op jit(solution)/shard_map/ppermute | solution.py:298
  70.1 8.8 %collective-permute-start.3 = (f32[128,512]{1,0:T(8,128)S(1)}, f32[128,512]{1,0:T(8,128)S(1)}, u32[]{:S(2)}, u32[]{:S(2)}) collective-permute-start(f32[128,512]{1,0:T(8,128)S(1)} %get-tuple-element.50), channel_id=1, source_target_pairs={{0,1},{1,0},{2,3},{3,2},{4,5},{5,4},{6,7},{7,6},{8,9},{9,8},{10,11... | collective-permute-start | bytes 786440 | tf_op jit(solution)/shard_map/ppermute | solution.py:298
  70.1 1.5 %collective-permute-start.4 = (f32[8,128]{1,0:T(8,128)S(1)}, f32[8,128]{1,0:T(8,128)S(1)}, u32[]{:S(2)}, u32[]{:S(2)}) collective-permute-start(f32[8,128]{1,0:T(8,128)S(1)} %get-tuple-element.43.sums_ref), channel_id=1, source_target_pairs={{0,1},{1,0},{2,3},{3,2},{4,5},{5,4},{6,7},{7,6},{8,9},{9,8},{10,11... | collective-permute-start | bytes 12296 | tf_op jit(solution)/shard_map/ppermute | solution.py:539
  71.6 10.6 %collective-permute-start.5 = (f32[128,512]{1,0:T(8,128)S(1)}, f32[128,512]{1,0:T(8,128)S(1)}, u32[]{:S(2)}, u32[]{:S(2)}) collective-permute-start(f32[128,512]{1,0:T(8,128)S(1)} %get-tuple-element.54), channel_id=1, source_target_pairs={{0,24},{8,0},{16,8},{24,16},{1,25},{9,1},{17,9},{25,17},{2,26},{10... | collective-permute-start | bytes 786440 | tf_op jit(solution)/shard_map/ppermute | solution.py:298
  83.5 11.1 %collective-permute-start.6 = (f32[128,512]{1,0:T(8,128)S(1)}, f32[128,512]{1,0:T(8,128)S(1)}, u32[]{:S(2)}, u32[]{:S(2)}) collective-permute-start(f32[128,512]{1,0:T(8,128)S(1)} %get-tuple-element.56), channel_id=1, source_target_pairs={{0,8},{8,16},{16,24},{24,0},{1,9},{9,17},{17,25},{25,1},{2,10},{10... | collective-permute-start | bytes 786440 | tf_op jit(solution)/shard_map/ppermute | solution.py:298
  85.0 10.9 %collective-permute-start.7 = (f32[128,512]{1,0:T(8,128)S(1)}, f32[128,512]{1,0:T(8,128)S(1)}, u32[]{:S(2)}, u32[]{:S(2)}) collective-permute-start(f32[128,512]{1,0:T(8,128)S(1)} %get-tuple-element.57), channel_id=1, source_target_pairs={{2,4},{4,2},{3,5},{5,3},{10,12},{12,10},{11,13},{13,11},{18,20},{2... | collective-permute-start | bytes 786440 | tf_op jit(solution)/shard_map/ppermute | solution.py:298
  85.7 11.2 %collective-permute-start.8 = (f32[128,512]{1,0:T(8,128)S(1)}, f32[128,512]{1,0:T(8,128)S(1)}, u32[]{:S(2)}, u32[]{:S(2)}) collective-permute-start(f32[128,512]{1,0:T(8,128)S(1)} %get-tuple-element.58), channel_id=1, source_target_pairs={{0,24},{8,0},{16,8},{24,16},{1,25},{9,1},{17,9},{25,17},{2,26},{10... | collective-permute-start | bytes 786440 | tf_op jit(solution)/shard_map/ppermute | solution.py:298
  88.1 11.4 %collective-permute-start.9 = (f32[128,512]{1,0:T(8,128)S(1)}, f32[128,512]{1,0:T(8,128)S(1)}, u32[]{:S(2)}, u32[]{:S(2)}) collective-permute-start(f32[128,512]{1,0:T(8,128)S(1)} %get-tuple-element.59), channel_id=1, source_target_pairs={{0,2},{2,0},{4,6},{6,4},{1,3},{3,1},{5,7},{7,5},{8,10},{10,8},{12,... | collective-permute-start | bytes 786440 | tf_op jit(solution)/shard_map/ppermute | solution.py:298
  91.2 8.3 %collective-permute-start.10 = (f32[128,512]{1,0:T(8,128)S(1)}, f32[128,512]{1,0:T(8,128)S(1)}, u32[]{:S(2)}, u32[]{:S(2)}) collective-permute-start(f32[128,512]{1,0:T(8,128)S(1)} %get-tuple-element.60), channel_id=1, source_target_pairs={{0,1},{1,0},{2,3},{3,2},{4,5},{5,4},{6,7},{7,6},{8,9},{9,8},{10,11... | collective-permute-start | bytes 786440 | tf_op jit(solution)/shard_map/ppermute | solution.py:298
  95.8 3.7 %collective-permute-start.11 = (f32[8,128]{1,0:T(8,128)S(1)}, f32[8,128]{1,0:T(8,128)S(1)}, u32[]{:S(2)}, u32[]{:S(2)}) collective-permute-start(f32[8,128]{1,0:T(8,128)S(1)} %shard_map.143.refs_5_), channel_id=1, source_target_pairs={{0,1},{1,0},{2,3},{3,2},{4,5},{5,4},{6,7},{7,6},{8,9},{9,8},{10,11... | collective-permute-start | bytes 12296 | tf_op jit(solution)/shard_map/ppermute | solution.py:575
  102.3 12.8 %all-to-all-start.2 = ((f32[32,2,4,128]{3,2,1,0:T(4,128)}), f32[32,2,4,128]{3,2,1,0:T(4,128)S(1)}, u32[]{:S(2)}, u32[]{:S(2)}) async-start(f32[32,2,4,128]{3,2,1,0:T(4,128)} %get-tuple-element.62), calls=%async_computation.2 | async-start | bytes 262144 | tf_op jit(solution)/shard_map/all_to_all | solution.py:443
  106.9 8.2 %copy-start.16 = (f32[1,512]{1,0:T(1,128)S(1)}, f32[1,512]{1,0:T(1,128)}, u32[]{:S(2)}) copy-start(f32[1,512]{1,0:T(1,128)} %get-tuple-element.63.rho_ref) | copy-start | bytes 6148
  (7 other events, 9.1 us)

commit v8 on v7

--- a/solution.py
+++ b/solution.py
@@ -191,8 +191,10 @@
     local_ref[...] = local
     part_ref[...] = jnp.sum(live * local, axis=0, keepdims=True)
     square_ref[...] = jnp.sum(live * live, axis=0, keepdims=True)
-    for i in range(2):
-        refs[2 * i][...], refs[2 * i + 1][...] = parts(whole[i][...])
+    refs[0][...], refs[1][...] = parts(whole[0][...])
+    for i, face in enumerate(NEAR + FAR):
+        at = slice(i * rows, (i + 1) * rows)
+        refs[2][:, at], refs[3][:, at] = parts(whole[1][:, face * rows : (face + 1) * rows])
     primal, slots = table_ref.shape
     rank_row, own_col = ranks(owner_ref[...].astype(f32))
     (rank_col,) = columns(rank_row)
@@ -250,8 +252,10 @@
 AXIS_AT = {"blk": 0, "lat": 2, "depth": 4}
 
 
-FIRST = [("lat", 1), ("blk", "up"), ("lat", 0), ("depth", 1), ("depth", 0), ("blk", "down")]
-SECOND = [("blk", "up"), ("lat", 1), ("blk", "down"), ("lat", 0), ("depth", 1), ("depth", 0)]
+FIRST = [("blk", "up"), ("lat", "up"), ("depth", 1), ("depth", 0), ("blk", "down"), ("lat", "down")]
+SECOND = [("blk", "up"), ("lat", "up"), ("blk", "down"), ("lat", "down"), ("depth", 1), ("depth", 0)]
+NEAR = (0, 2, 4, 5)
+FAR = (1, 3)
 
 
 def moves(order):
@@ -262,7 +266,8 @@
     devices = lax.axis_size(axis)
     if way in ("up", "down"):
         by = 1 if way == "up" else -1
-        return [(i, (i + by) % devices) for i in range(devices)]
+        ends = [(i, i + by) for i in range(devices)]
+        return [(i, j % devices) for i, j in ends if axis == "blk" or j in range(devices)]
     return [pair for i in range(way, devices - 1, 2) for pair in ((i, i + 1), (i + 1, i))]
 
 
@@ -282,13 +287,13 @@
 
 def got_face(got, face):
     axis, side = ("blk", "lat", "depth")[face // 2], face % 2
-    if axis == "blk":
-        return got["blk", "down" if side else "up"][...]
+    if axis != "depth":
+        return got[axis, "down" if side else "up"][...]
     total = None
-    for (axis_of, way), ref in got.items():
-        if axis_of == axis:
+    for way in (0, 1):
+        if (axis, way) in got:
             mine = sends_plus(axis, way) == (side == 1)
-            piece = jnp.where(mine, ref[...], 0.0)
+            piece = jnp.where(mine, got[axis, way][...], 0.0)
             total = piece if total is None else total + piece
     return total
 
@@ -335,42 +340,43 @@
     rho_out[...] = rho
     beta_out[...] = beta
     square_out[...] = unfolded(sums, folds, folds)
-    for i, face in enumerate((0, 2, 3, 4, 5)):
+    for i, face in enumerate(NEAR):
         near_ref[i * rows : (i + 1) * rows, :] = new_direction(
             len_ref, beta, image_ref, prev_ref, got, face, rows
         )
-    high, low = parts(near_ref[...])
-    last = 2 * rows
-    image_out[...] = product(
-        (high_ref[:, last:], low_ref[:, last:]), (high[rows:], low[rows:])
-    ) + product((high_ref[:, :rows], low_ref[:, :rows]), (high[:rows], low[:rows]))
+    first = len(NEAR) * rows
+    image_out[...] = product((high_ref[:, :first], low_ref[:, :first]), parts(near_ref[...]))
 
 
 def far_kernel(keys, len_ref, beta_ref, image_ref, prev_ref, high_ref, low_ref, near_ref, near_image_ref, *refs):
     got, refs = dict(zip(keys, refs)), refs[len(keys) :]
     far_ref, schur_out, *face_refs = refs
     rows = image_ref.shape[0] // 6
-    far = new_direction(len_ref, beta_ref[...], image_ref, prev_ref, got, 1, rows)
-    far_ref[...] = far
-    at = slice(rows, 2 * rows)
-    image = near_image_ref[...] + product((high_ref[:, at], low_ref[:, at]), parts(far))
+    beta = beta_ref[...]
+    for i, face in enumerate(FAR):
+        far_ref[i * rows : (i + 1) * rows, :] = new_direction(
+            len_ref, beta, image_ref, prev_ref, got, face, rows
+        )
+    first = len(NEAR) * rows
+    image = near_image_ref[...] + product(
+        (high_ref[:, first:], low_ref[:, first:]), parts(far_ref[...])
+    )
     schur_out[...] = image
     put_faces(image, rows, SECOND, face_refs)
 
 
 def store_kernel(near_ref, far_ref, direction_out, sems):
-    rows = far_ref.shape[0]
-    copies = [
-        pltpu.make_async_copy(
-            near_ref.at[pl.ds(0, rows)], direction_out.at[pl.ds(0, rows)], sems.at[0]
-        ),
-        pltpu.make_async_copy(far_ref, direction_out.at[pl.ds(rows, rows)], sems.at[1]),
-        pltpu.make_async_copy(
-            near_ref.at[pl.ds(rows, 4 * rows)],
-            direction_out.at[pl.ds(2 * rows, 4 * rows)],
-            sems.at[2],
-        ),
-    ]
+    rows = far_ref.shape[0] // len(FAR)
+    copies = []
+    for ref, faces in ((near_ref, NEAR), (far_ref, FAR)):
+        for i, face in enumerate(faces):
+            copies.append(
+                pltpu.make_async_copy(
+                    ref.at[pl.ds(i * rows, rows)],
+                    direction_out.at[pl.ds(face * rows, rows)],
+                    sems.at[face],
+                )
+            )
     for copy in copies:
         copy.start()
     for copy in copies:
@@ -378,10 +384,13 @@
 
 
 def products_kernel(len_ref, near_ref, far_ref, schur_ref, residual_ref, arrived, out_ref):
-    rows = far_ref.shape[0]
+    rows = schur_ref.shape[0] // 6
     image = schur_ref[...]
-    near = near_ref[...]
-    direction = jnp.concatenate([near[:rows], far_ref[...], near[rows:]], axis=0)
+    blocks = {}
+    for ref, faces in ((near_ref, NEAR), (far_ref, FAR)):
+        for i, face in enumerate(faces):
+            blocks[face] = ref[i * rows : (i + 1) * rows, :]
+    direction = jnp.concatenate([blocks[face] for face in range(6)], axis=0)
     live = jnp.concatenate(
         [masked(len_ref, residual_ref, face, rows) for face in range(6)], axis=0
     )
@@ -391,7 +400,7 @@
         out_ref[j : j + 1, :] = piece
 
 
-def applied_kernel(pair_depth, len_ref, schur_ref, *refs):
+def applied_kernel(pair_depth, len_ref, stored, schur_ref, *refs):
     keys = moves(SECOND)
     got, refs = dict(zip(keys, refs)), refs[len(keys) :]
     products, (applied_ref, spread_ref) = refs[:-2], refs[-2:]
@@ -408,8 +417,10 @@
     halves = [products[:folds], products[folds : 2 * folds]]
     if pair_depth:
         halves = [jnp.where(lax.axis_index("depth") == 0, *halves)]
-    for i, half in enumerate([*halves, jnp.concatenate(folded(total), axis=0)]):
-        spread_ref[:, i, :, :] = jnp.broadcast_to(half[None], (spread_ref.shape[0], folds, LANES))
+    halves = [[half[j : j + 1] for j in range(folds)] for half in halves]
+    for i, half in enumerate([*halves, folded(total)]):
+        for j, piece in enumerate(half):
+            spread_ref[:, i, j, :] = jnp.broadcast_to(piece, (spread_ref.shape[0], LANES))
 
 
 def finish_kernel(pair_depth, scale, len_ref, sums_ref, rho_ref, square_ref, residual_ref, applied_ref, new_out, alpha_ref, norm_ref, new_ref, sems):
@@ -539,11 +550,11 @@
         sums = [sums, lax.ppermute(sums, "depth", route("depth", 0))]
     else:
         sums = [to_all(sums, "depth")]
-    near_keys = [key for key in keys if key != ("blk", "down")]
-    far_keys = [("blk", "down")]
+    far_keys = [("blk", "down"), ("lat", "down")]
+    near_keys = [key for key in keys if key not in far_keys]
     rho, beta, square, near, near_image = call(
         functools.partial(near_kernel, pair_depth, scale, near_keys),
-        [row, row, row, shape_of(5 * rows, width), whole],
+        [row, row, row, shape_of(len(NEAR) * rows, width), whole],
         [lengths, sums[0], prev_rho.reshape(1, width), image, prev_direction, *schur_halves]
         + [got[key] for key in near_keys]
         + sums[1:],
@@ -553,11 +564,11 @@
     )
     far, schur_image, *outward = call(
         functools.partial(far_kernel, far_keys),
-        [face, whole, *faces],
+        [shape_of(len(FAR) * rows, width), whole, *faces],
         [lengths, beta, image, prev_direction, *schur_halves, near, near_image]
         + [got[key] for key in far_keys],
         smem=(0,),
-        flops=height * height * width,
+        flops=2 * height * height * width,
         moved=4 * height * (height + 4 * width),
     )
     got = exchange(outward, SECOND)
@@ -579,13 +590,14 @@
         [near, far],
         far_out=(0,),
         moved=8 * height * width,
-        scratch=[pltpu.SemaphoreType.DMA((3,))],
+        scratch=[pltpu.SemaphoreType.DMA((6,))],
     )
     applied, spread_sums = call(
         functools.partial(applied_kernel, pair_depth),
         [whole, shape_of(devices, 2 if pair_depth else 3, folds, LANES)],
-        [lengths, schur_image, *got, *products],
+        [lengths, direction, schur_image, *got, *products],
         smem=(0,),
+        far=(1,),
         flops=4 * height * width,
         moved=12 * height * width,
     )

time: 119 us -> 114 us (0.958)
  blocking collectives: 26.5 us -> 37.2 us
  waiting for transfers between devices: 30.5 us -> 20.2 us
  starting transfers between devices: 29.3 us -> 26.5 us
  Pallas kernels: 22.6 us -> 21.2 us
  local copies, waits for them, and re-layouts: 9.12 us -> 7.73 us
    all_to_all x1 -> x2, blocking collectives: 26.5 us -> 37.2 us  [to_all(): return lax.all_to_all(x, axes, split_axis=0, concat_axis=0, tiled=True)]
    all_to_all x2 -> x1, waiting for transfers between devices: 18 us -> 9.71 us  [to_all(): return lax.all_to_all(x, axes, split_axis=0, concat_axis=0, tiled=True)]
    all_to_all x2 -> x1, starting transfers between devices: 13.1 us -> 8.49 us  [to_all(): return lax.all_to_all(x, axes, split_axis=0, concat_axis=0, tiled=True)]
    ppermute x10, starting transfers between devices: 15.7 us -> 17.4 us  [exchange(): lax.ppermute(block, axis, route(axis, way))]
    unnamed x34 -> x38, local copies, waits for them, and re-layouts: 9.12 us -> 7.73 us
    pallas_call x10, Pallas kernels: 22.6 us -> 21.2 us  [call(): pl.pallas_call(body, out_shape=list(outs), in_specs=in_specs, out_specs=o...]
  transfers between devices with their start and end apart: 14 -> 13, of which waited for: 7 -> 7; matrix products, arithmetic and copies ran while one was open for 0% -> 0% of each run, Pallas kernels for 8% -> 7%
where the time goes in v8:
time: 114 us
  blocking collectives  37.2 us (33%)
  starting transfers between devices  26.5 us (23%)
  Pallas kernels  21.2 us (19%)
  waiting for transfers between devices  20.2 us (18%)
  local copies, waits for them, and re-layouts  7.73 us (7%)
    all_to_all x2, blocking collectives, to_all(): return lax.all_to_all(x, axes, split_axis=0, concat_axis=0, tiled=True)  37.2 us
    pallas_call x10, Pallas kernels, call(): pl.pallas_call(body, out_shape=list(outs), in_specs=in_specs, out_specs=o...  21.2 us
    ppermute x10, starting transfers between devices, exchange(): lax.ppermute(block, axis, route(axis, way))  17.4 us
    ppermute x10, waiting for transfers between devices, exchange(): lax.ppermute(block, axis, route(axis, way))  10.5 us
    all_to_all x1, waiting for transfers between devices, to_all(): return lax.all_to_all(x, axes, split_axis=0, concat_axis=0, tiled=True)  9.71 us
    all_to_all x1, starting transfers between devices, to_all(): return lax.all_to_all(x, axes, split_axis=0, concat_axis=0, tiled=True)  8.49 us
    unnamed x38, local copies, waits for them, and re-layouts  7.73 us
  transfers between devices with their start and end apart: 13, of which 7 were waited for; matrix products, arithmetic and copies ran while one was open for 0% of the time, Pallas kernels for 7%

profile of v8, /device:TPU:0, one launch (start us, length us, event | category | flops | bytes accessed | tf_op | source)
XLA Modules:
  0.0 113.7 jit_solution(11959402035684361543)
XLA Ops:
  0.6 4.4 %shard_map.137 = f32[16,104,128]{2,1,0:T(8,128)} custom-call(s32[6]{0:T(128)} %bitcast.25, s32[1,256]{1,0:T(1,128)} %bitcast.32, s32[1,256]{1,0:T(1,128)} %bitcast.37, f32[768,512]{1,0:T(8,128)} %bitcast.15, f32[768,256]{1,0:T(8,128)} %bitcast.21), custom_call_target="tpu_custom_call" | custom-call | flops 603979776 | bytes 3145728 | tf_op jit(solution)/shard_map/pallas_call | solution.py:37
  5.1 8.5 %all-to-all-start = ((f32[16,104,128]{2,1,0:T(8,128)}), f32[16,104,128]{2,1,0:T(8,128)}, u32[]{:S(2)}, u32[]{:S(2)}) async-start(f32[16,104,128]{2,1,0:T(8,128)} %shard_map.137), calls=%async_computation | async-start | bytes 1703936 | tf_op jit(solution)/shard_map/all_to_all | solution.py:454
  13.6 1.7 %copy-done.5 = f32[1,1,1,768,768]{4,3,2,1,0:T(8,128)S(1)} copy-done((f32[1,1,1,768,768]{4,3,2,1,0:T(8,128)S(1)}, f32[1,1,1,768,768]{4,3,2,1,0:T(8,128)}, u32[]{:S(2)}) %copy-start.5) | copy-done | bytes 2359320
  15.3 1.7 %copy-done.6 = f32[1,1,1,768,768]{4,3,2,1,0:T(8,128)S(1)} copy-done((f32[1,1,1,768,768]{4,3,2,1,0:T(8,128)S(1)}, f32[1,1,1,768,768]{4,3,2,1,0:T(8,128)}, u32[]{:S(2)}) %copy-start.6) | copy-done | bytes 2359320
  16.9 3.5 %shard_map.138 = (f32[768,512]{1,0:T(8,128)S(1)}, f32[1,512]{1,0:T(1,128)S(1)}, f32[1,512]{1,0:T(1,128)S(1)}, bf16[256,384]{1,0:T(8,128)(2,1)S(1)}, bf16[768,256...) custom-call(s32[6]{0:T(128)S(1)} %bitcast.26, ...), custom_call_target="tpu_custom_call" | custom-call | flops 1811939328 | bytes 10223616 | tf_op jit(solution)/shard_map/pallas_call | solution.py:37
  24.8 9.7 %all-to-all-done.incoming_any = f32[16,104,128]{2,1,0:T(8,128)} async-done(((f32[16,104,128]{2,1,0:T(8,128)}), f32[16,104,128]{2,1,0:T(8,128)}, u32[]{:S(2)}, u32[]{:S(2)}) %all-to-all-start) | async-done | bytes 852000 | tf_op jit(solution)/shard_map/all_to_all | solution.py:454
  34.5 2.6 %shard_map.139 = f32[16,104,128]{2,1,0:T(8,128)S(1)} custom-call(f32[16,104,128]{2,1,0:T(8,128)} %all-to-all-done.incoming_any, f32[256,256]{1,0:T(8,128)} %bitcast.39, f32[1,512]{1,0:T(1,128)S(1)} %get-tuple-element.37.local_part_ref, f32[1,512]{1,0:T(1,128)S(1)} %get-tuple-element.38.square_ref), custom_call_target="tpu_custom_call" | custom-call | flops 603979776 | bytes 1572864 | tf_op jit(solution)/shard_map/pallas_call | solution.py:37
  37.1 26.4 %all_to_all.15.returned_ref = f32[16,104,128]{2,1,0:T(8,128)S(1)} all-to-all(f32[16,104,128]{2,1,0:T(8,128)S(1)} %shard_map.139), channel_id=1, replica_groups=mesh['blk'=4,'lat'=4,'depth'=2] {'blk','lat'}, dimensions={0} | all-to-all | bytes 1703936 | tf_op jit(solution)/shard_map/all_to_all | solution.py:454
  63.5 1.2 %shard_map.140 = (f32[768,512]{1,0:T(8,128)S(1)}, f32[8,128]{1,0:T(8,128)S(1)}, f32[128,512]{1,0:T(8,128)S(1)}, f32[128,512]{1,0:T(8,128)S(1)}, f32[128,512]{1,0...) custom-call(f32[16,104,128]{2,1,0:T(8,128)S(1)} %all_to_all.15.returned_ref, ...), custom_call_target="tpu_custom_call" | custom-call | flops 805306368 | bytes 6291456 | tf_op jit(solution)/shard_map/pallas_call | solution.py:37
  65.8 2.5 %collective-permute-start.1 = (f32[128,512]{1,0:T(8,128)S(1)}, f32[128,512]{1,0:T(8,128)S(1)}, u32[]{:S(2)}, u32[]{:S(2)}) collective-permute-start(f32[128,512]{1,0:T(8,128)S(1)} %get-tuple-element.48), channel_id=1, source_target_pairs={{0,2},{2,4},{4,6},{1,3},{3,5},{5,7},{8,10},{10,12},{12,14},{9,11},... | collective-permute-start | bytes 786440 | tf_op jit(solution)/shard_map/ppermute | solution.py:303
  68.9 2.8 %collective-permute-start.4 = (f32[128,512]{1,0:T(8,128)S(1)}, f32[128,512]{1,0:T(8,128)S(1)}, u32[]{:S(2)}, u32[]{:S(2)}) collective-permute-start(f32[128,512]{1,0:T(8,128)S(1)} %get-tuple-element.53), channel_id=1, source_target_pairs={{0,24},{8,0},{16,8},{24,16},{1,25},{9,1},{17,9},{25,17},{2,26},{10... | collective-permute-start | bytes 786440 | tf_op jit(solution)/shard_map/ppermute | solution.py:303
  71.7 1.3 %collective-permute-start.5 = (f32[128,512]{1,0:T(8,128)S(1)}, f32[128,512]{1,0:T(8,128)S(1)}, u32[]{:S(2)}, u32[]{:S(2)}) collective-permute-start(f32[128,512]{1,0:T(8,128)S(1)} %get-tuple-element.54), channel_id=1, source_target_pairs={{2,0},{4,2},{6,4},{3,1},{5,3},{7,5},{10,8},{12,10},{14,12},{11,9},... | collective-permute-start | bytes 786440 | tf_op jit(solution)/shard_map/ppermute | solution.py:303
  73.3 2.6 %shard_map.141 = (f32[1,512]{1,0:T(1,128)}, f32[1,512]{1,0:T(1,128)S(1)}, f32[1,512]{1,0:T(1,128)S(1)}, f32[512,512]{1,0:T(8,128)S(1)}, f32[768,512]{1,0:T(8,128)S(1)}) custom-call(s32[6]{0:T(128)S(1)} %bitcast.27, f32[8,128]{1,0:T(8,128)S(1)} %get-tuple-element.43.sums_ref, f32[1,512]{1,0:T(1,128)S(1)} %bitcast.34, ...), custom_call_target="tpu_custom_call" | custom-call | flops 1207959552 | bytes 8650752 | tf_op jit(solution)/shard_map/pallas_call | solution.py:37
  75.9 2.7 %collective-permute-done.4.refs_0_ = f32[128,512]{1,0:T(8,128)S(1)} collective-permute-done((f32[128,512]{1,0:T(8,128)S(1)}, f32[128,512]{1,0:T(8,128)S(1)}, u32[]{:S(2)}, u32[]{:S(2)}) %collective-permute-start.4) | collective-permute-done | bytes 262176 | tf_op jit(solution)/shard_map/ppermute | solution.py:303
  78.6 3.0 %collective-permute-done.5.refs_1_ = f32[128,512]{1,0:T(8,128)S(1)} collective-permute-done((f32[128,512]{1,0:T(8,128)S(1)}, f32[128,512]{1,0:T(8,128)S(1)}, u32[]{:S(2)}, u32[]{:S(2)}) %collective-permute-start.5) | collective-permute-done | bytes 262176 | tf_op jit(solution)/shard_map/ppermute | solution.py:303
  81.6 1.4 %shard_map.142 = (f32[256,512]{1,0:T(8,128)S(1)}, f32[768,512]{1,0:T(8,128)S(1)}, f32[128,512]{1,0:T(8,128)S(1)}, f32[128,512]{1,0:T(8,128)S(1)}, f32[128,512]{1...) custom-call(s32[6]{0:T(128)S(1)} %bitcast.28, f32[1,512]{1,0:T(1,128)S(1)} %get-tuple-element.51.beta_ref, ...), custom_call_target="tpu_custom_call" | custom-call | flops 603979776 | bytes 8650752 | tf_op jit(solution)/shard_map/pallas_call | solution.py:37
  83.1 4.5 %collective-permute-start.7 = (f32[128,512]{1,0:T(8,128)S(1)}, f32[128,512]{1,0:T(8,128)S(1)}, u32[]{:S(2)}, u32[]{:S(2)}) collective-permute-start(f32[128,512]{1,0:T(8,128)S(1)} %get-tuple-element.58), channel_id=1, source_target_pairs={{0,2},{2,4},{4,6},{1,3},{3,5},{5,7},{8,10},{10,12},{12,14},{9,11},... | collective-permute-start | bytes 786440 | tf_op jit(solution)/shard_map/ppermute | solution.py:303
  87.6 3.9 %collective-permute-start.8 = (f32[128,512]{1,0:T(8,128)S(1)}, f32[128,512]{1,0:T(8,128)S(1)}, u32[]{:S(2)}, u32[]{:S(2)}) collective-permute-start(f32[128,512]{1,0:T(8,128)S(1)} %get-tuple-element.59), channel_id=1, source_target_pairs={{0,24},{8,0},{16,8},{24,16},{1,25},{9,1},{17,9},{25,17},{2,26},{10... | collective-permute-start | bytes 786440 | tf_op jit(solution)/shard_map/ppermute | solution.py:303
  91.4 1.3 %collective-permute-start.9 = (f32[128,512]{1,0:T(8,128)S(1)}, f32[128,512]{1,0:T(8,128)S(1)}, u32[]{:S(2)}, u32[]{:S(2)}) collective-permute-start(f32[128,512]{1,0:T(8,128)S(1)} %get-tuple-element.60), channel_id=1, source_target_pairs={{2,0},{4,2},{6,4},{3,1},{5,3},{7,5},{10,8},{12,10},{14,12},{11,9},... | collective-permute-start | bytes 786440 | tf_op jit(solution)/shard_map/ppermute | solution.py:303
  94.5 1.2 %shard_map.143.stored = f32[768,512]{1,0:T(8,128)} custom-call(f32[512,512]{1,0:T(8,128)S(1)} %get-tuple-element.50.near_ref, f32[256,512]{1,0:T(8,128)S(1)} %get-tuple-element.55.far_ref), custom_call_target="tpu_custom_call" | custom-call | bytes 3145728 | tf_op jit(solution)/shard_map/pallas_call | solution.py:37
  95.8 1.9 %collective-permute-done.8.refs_2_ = f32[128,512]{1,0:T(8,128)S(1)} collective-permute-done((f32[128,512]{1,0:T(8,128)S(1)}, f32[128,512]{1,0:T(8,128)S(1)}, u32[]{:S(2)}, u32[]{:S(2)}) %collective-permute-start.8) | collective-permute-done | bytes 262176 | tf_op jit(solution)/shard_map/ppermute | solution.py:303
  97.6 2.1 %collective-permute-done.9.refs_3_ = f32[128,512]{1,0:T(8,128)S(1)} collective-permute-done((f32[128,512]{1,0:T(8,128)S(1)}, f32[128,512]{1,0:T(8,128)S(1)}, u32[]{:S(2)}, u32[]{:S(2)}) %collective-permute-start.9) | collective-permute-done | bytes 262176 | tf_op jit(solution)/shard_map/ppermute | solution.py:303
  100.5 10.8 %all_to_all.16.sums_ref = f32[32,2,4,128]{3,2,1,0:T(4,128)S(1)} all-to-all(f32[32,2,4,128]{3,2,1,0:T(4,128)S(1)} %get-tuple-element.62), channel_id=1, replica_groups=mesh['blk'=4,'lat'=4,'depth'=2] {'blk','lat','depth'}, dimensions={0} | all-to-all | bytes 262144 | tf_op jit(solution)/shard_map/all_to_all | solution.py:454
  111.3 2.4 %shard_map.146 = (f32[768,512]{1,0:T(8,128)}, f32[1,512]{1,0:T(1,128)}, f32[1,512]{1,0:T(1,128)}) custom-call(s32[6]{0:T(128)S(1)} %bitcast.31, f32[32,2,4,128]{3,2,1,0:T(4,128)S(1)} %all_to_all.16.sums_ref, f32[1,512]{1,0:T(1,128)S(1)} %copy-done.18, f32[1,512]{1,0:T(1,128)S(1)} %get-tuple-element.64.square_ref, f32[768,512]{1,0:T(8,128)S(1)} %bitcast.18, ...), custom_call_target="tpu_custom_call" | custom-call | flops 1572864 | bytes 4718592 | tf_op jit(solution)/shard_map/pallas_call | solution.py:37
  (52 shorter events, 9.0 us)
Async XLA Ops:
  0.6 12.9 %copy-start.4 = (f32[1,1,1,768,256]{4,3,2,1,0:T(8,128)S(1)}, f32[1,1,1,768,256]{4,3,2,1,0:T(8,128)}, u32[]{:S(2)}) copy-start(f32[1,1,1,768,256]{4,3,2,1,0:T(8,128)} %param.16) | copy-start | bytes 2359300
  5.0 8.5 %copy-start = (f32[1,1,1,768,512]{4,3,2,1,0:T(8,128)S(1)}, f32[1,1,1,768,512]{4,3,2,1,0:T(8,128)}, u32[]{:S(2)}) copy-start(f32[1,1,1,768,512]{4,3,2,1,0:T(8,128)} %param.11) | copy-start | bytes 4718596
  5.0 8.5 %copy-start.15 = (s32[1,1,1,6]{3,2,1,0:T(1,128)S(1)}, s32[1,1,1,6]{3,2,1,0:T(1,128)}, u32[]{:S(2)}) copy-start(s32[1,1,1,6]{3,2,1,0:T(1,128)} %param.10) | copy-start | bytes 76
  5.1 29.5 %all-to-all-start = ((f32[16,104,128]{2,1,0:T(8,128)}), f32[16,104,128]{2,1,0:T(8,128)}, u32[]{:S(2)}, u32[]{:S(2)}) async-start(f32[16,104,128]{2,1,0:T(8,128)} %shard_map.137), calls=%async_computation | async-start | bytes 1703936 | tf_op jit(solution)/shard_map/all_to_all | solution.py:454
  34.5 29.0 %copy-start.8 = (f32[768,512]{1,0:T(8,128)S(1)}, f32[768,512]{1,0:T(8,128)}, u32[]{:S(2)}) copy-start(f32[768,512]{1,0:T(8,128)} %copy-done.7) | copy-start | bytes 4718596
  34.5 29.0 %copy-start.10 = (bf16[768,256]{1,0:T(8,128)(2,1)S(1)}, bf16[768,256]{1,0:T(8,128)(2,1)}, u32[]{:S(2)}) copy-start(bf16[768,256]{1,0:T(8,128)(2,1)} %copy-done.9) | copy-start | bytes 1179652
  34.5 29.0 %copy-start.12 = (bf16[768,256]{1,0:T(8,128)(2,1)S(1)}, bf16[768,256]{1,0:T(8,128)(2,1)}, u32[]{:S(2)}) copy-start(bf16[768,256]{1,0:T(8,128)(2,1)} %copy-done.11) | copy-start | bytes 1179652
  34.5 29.0 %copy-start.14 = (bf16[256,384]{1,0:T(8,128)(2,1)S(1)}, bf16[256,384]{1,0:T(8,128)(2,1)}, u32[]{:S(2)}) copy-start(bf16[256,384]{1,0:T(8,128)(2,1)} %copy-done.13) | copy-start | bytes 589828
  63.5 9.8 %copy-start.1 = (f32[1,1,1,768,512]{4,3,2,1,0:T(8,128)S(1)}, f32[1,1,1,768,512]{4,3,2,1,0:T(8,128)}, u32[]{:S(2)}) copy-start(f32[1,1,1,768,512]{4,3,2,1,0:T(8,128)} %param.12) | copy-start | bytes 4718596
  63.5 9.8 %copy-start.3 = (bf16[768,768]{1,0:T(8,128)(2,1)S(1)}, bf16[768,768]{1,0:T(8,128)(2,1)}, u32[]{:S(2)}) copy-start(bf16[768,768]{1,0:T(8,128)(2,1)} %copy-done.2) | copy-start | bytes 3538948
  63.5 9.8 %copy-start.17 = (f32[512]{0:T(512)S(1)}, f32[512]{0:T(512)}, u32[]{:S(2)}) copy-start(f32[512]{0:T(512)} %param.13) | copy-start | bytes 6148
  64.8 8.5 %collective-permute-start = (f32[128,512]{1,0:T(8,128)S(1)}, f32[128,512]{1,0:T(8,128)S(1)}, u32[]{:S(2)}, u32[]{:S(2)}) collective-permute-start(f32[128,512]{1,0:T(8,128)S(1)} %get-tuple-element.47), channel_id=1, source_target_pairs={{0,8},{8,16},{16,24},{24,0},{1,9},{9,17},{17,25},{25,1},{2,10},{10... | collective-permute-start | bytes 786440 | tf_op jit(solution)/shard_map/ppermute | solution.py:303
  65.8 7.5 %collective-permute-start.1 = (f32[128,512]{1,0:T(8,128)S(1)}, f32[128,512]{1,0:T(8,128)S(1)}, u32[]{:S(2)}, u32[]{:S(2)}) collective-permute-start(f32[128,512]{1,0:T(8,128)S(1)} %get-tuple-element.48), channel_id=1, source_target_pairs={{0,2},{2,4},{4,6},{1,3},{3,5},{5,7},{8,10},{10,12},{12,14},{9,11},... | collective-permute-start | bytes 786440 | tf_op jit(solution)/shard_map/ppermute | solution.py:303
  68.3 5.0 %collective-permute-start.2 = (f32[128,512]{1,0:T(8,128)S(1)}, f32[128,512]{1,0:T(8,128)S(1)}, u32[]{:S(2)}, u32[]{:S(2)}) collective-permute-start(f32[128,512]{1,0:T(8,128)S(1)} %get-tuple-element.49), channel_id=1, source_target_pairs={{0,1},{1,0},{2,3},{3,2},{4,5},{5,4},{6,7},{7,6},{8,9},{9,8},{10,11... | collective-permute-start | bytes 786440 | tf_op jit(solution)/shard_map/ppermute | solution.py:303
  68.4 3.3 %collective-permute-start.3 = (f32[8,128]{1,0:T(8,128)S(1)}, f32[8,128]{1,0:T(8,128)S(1)}, u32[]{:S(2)}, u32[]{:S(2)}) collective-permute-start(f32[8,128]{1,0:T(8,128)S(1)} %get-tuple-element.43.sums_ref), channel_id=1, source_target_pairs={{0,1},{1,0},{2,3},{3,2},{4,5},{5,4},{6,7},{7,6},{8,9},{9,8},{10,11... | collective-permute-start | bytes 12296 | tf_op jit(solution)/shard_map/ppermute | solution.py:550
  68.9 9.7 %collective-permute-start.4 = (f32[128,512]{1,0:T(8,128)S(1)}, f32[128,512]{1,0:T(8,128)S(1)}, u32[]{:S(2)}, u32[]{:S(2)}) collective-permute-start(f32[128,512]{1,0:T(8,128)S(1)} %get-tuple-element.53), channel_id=1, source_target_pairs={{0,24},{8,0},{16,8},{24,16},{1,25},{9,1},{17,9},{25,17},{2,26},{10... | collective-permute-start | bytes 786440 | tf_op jit(solution)/shard_map/ppermute | solution.py:303
  71.7 9.9 %collective-permute-start.5 = (f32[128,512]{1,0:T(8,128)S(1)}, f32[128,512]{1,0:T(8,128)S(1)}, u32[]{:S(2)}, u32[]{:S(2)}) collective-permute-start(f32[128,512]{1,0:T(8,128)S(1)} %get-tuple-element.54), channel_id=1, source_target_pairs={{2,0},{4,2},{6,4},{3,1},{5,3},{7,5},{10,8},{12,10},{14,12},{11,9},... | collective-permute-start | bytes 786440 | tf_op jit(solution)/shard_map/ppermute | solution.py:303
  83.0 10.3 %collective-permute-start.6 = (f32[128,512]{1,0:T(8,128)S(1)}, f32[128,512]{1,0:T(8,128)S(1)}, u32[]{:S(2)}, u32[]{:S(2)}) collective-permute-start(f32[128,512]{1,0:T(8,128)S(1)} %get-tuple-element.57), channel_id=1, source_target_pairs={{0,8},{8,16},{16,24},{24,0},{1,9},{9,17},{17,25},{25,1},{2,10},{10... | collective-permute-start | bytes 786440 | tf_op jit(solution)/shard_map/ppermute | solution.py:303
  83.1 12.7 %collective-permute-start.7 = (f32[128,512]{1,0:T(8,128)S(1)}, f32[128,512]{1,0:T(8,128)S(1)}, u32[]{:S(2)}, u32[]{:S(2)}) collective-permute-start(f32[128,512]{1,0:T(8,128)S(1)} %get-tuple-element.58), channel_id=1, source_target_pairs={{0,2},{2,4},{4,6},{1,3},{3,5},{5,7},{8,10},{10,12},{12,14},{9,11},... | collective-permute-start | bytes 786440 | tf_op jit(solution)/shard_map/ppermute | solution.py:303
  87.6 10.0 %collective-permute-start.8 = (f32[128,512]{1,0:T(8,128)S(1)}, f32[128,512]{1,0:T(8,128)S(1)}, u32[]{:S(2)}, u32[]{:S(2)}) collective-permute-start(f32[128,512]{1,0:T(8,128)S(1)} %get-tuple-element.59), channel_id=1, source_target_pairs={{0,24},{8,0},{16,8},{24,16},{1,25},{9,1},{17,9},{25,17},{2,26},{10... | collective-permute-start | bytes 786440 | tf_op jit(solution)/shard_map/ppermute | solution.py:303
  91.4 8.3 %collective-permute-start.9 = (f32[128,512]{1,0:T(8,128)S(1)}, f32[128,512]{1,0:T(8,128)S(1)}, u32[]{:S(2)}, u32[]{:S(2)}) collective-permute-start(f32[128,512]{1,0:T(8,128)S(1)} %get-tuple-element.60), channel_id=1, source_target_pairs={{2,0},{4,2},{6,4},{3,1},{5,3},{7,5},{10,8},{12,10},{14,12},{11,9},... | collective-permute-start | bytes 786440 | tf_op jit(solution)/shard_map/ppermute | solution.py:303
  92.7 7.0 %collective-permute-start.10 = (f32[128,512]{1,0:T(8,128)S(1)}, f32[128,512]{1,0:T(8,128)S(1)}, u32[]{:S(2)}, u32[]{:S(2)}) collective-permute-start(f32[128,512]{1,0:T(8,128)S(1)} %get-tuple-element.61), channel_id=1, source_target_pairs={{0,1},{1,0},{2,3},{3,2},{4,5},{5,4},{6,7},{7,6},{8,9},{9,8},{10,11... | collective-permute-start | bytes 786440 | tf_op jit(solution)/shard_map/ppermute | solution.py:303
  94.5 5.2 %collective-permute-start.11 = (f32[8,128]{1,0:T(8,128)S(1)}, f32[8,128]{1,0:T(8,128)S(1)}, u32[]{:S(2)}, u32[]{:S(2)}) collective-permute-start(f32[8,128]{1,0:T(8,128)S(1)} %shard_map.144.refs_5_), channel_id=1, source_target_pairs={{0,1},{1,0},{2,3},{3,2},{4,5},{5,4},{6,7},{7,6},{8,9},{9,8},{10,11... | collective-permute-start | bytes 12296 | tf_op jit(solution)/shard_map/ppermute | solution.py:586
  95.7 15.6 %copy-start.18 = (f32[1,512]{1,0:T(1,128)S(1)}, f32[1,512]{1,0:T(1,128)}, u32[]{:S(2)}) copy-start(f32[1,512]{1,0:T(1,128)} %get-tuple-element.63.rho_ref) | copy-start | bytes 6148
  (8 other events, 16.2 us)

commit v9 on v8

--- a/solution.py
+++ b/solution.py
@@ -95,17 +95,19 @@
     return -(-rows // TILE) * TILE
 
 
-def put_slab(out_ref, block):
+def put_slab(out_ref, block, first=0):
     owners = out_ref.shape[0]
     for j in range(block.shape[1] // LANES):
         piece = block[:, j * LANES : (j + 1) * LANES]
-        out_ref[:, j * CAP : (j + 1) * CAP, :] = piece.reshape(owners, CAP, LANES)
-
-
-def get_slab(ref, pieces):
+        at = (first + j) * CAP
+        out_ref[:, at : at + CAP, :] = piece.reshape(owners, CAP, LANES)
+
+
+def get_slab(ref, first, last):
     slots = ref.shape[0] * CAP
     return jnp.concatenate(
-        [ref[:, j * CAP : (j + 1) * CAP, :].reshape(slots, LANES) for j in range(pieces)], axis=1
+        [ref[:, j * CAP : (j + 1) * CAP, :].reshape(slots, LANES) for j in range(first, last)],
+        axis=1,
     )
 
 
@@ -192,9 +194,9 @@
     part_ref[...] = jnp.sum(live * local, axis=0, keepdims=True)
     square_ref[...] = jnp.sum(live * live, axis=0, keepdims=True)
     refs[0][...], refs[1][...] = parts(whole[0][...])
-    for i, face in enumerate(NEAR + FAR):
+    for i, move in enumerate(NEAR + FAR):
         at = slice(i * rows, (i + 1) * rows)
-        refs[2][:, at], refs[3][:, at] = parts(whole[1][:, face * rows : (face + 1) * rows])
+        refs[2][:, at], refs[3][:, at] = parts(whole[1][:, rows_of(served(*move), rows)])
     primal, slots = table_ref.shape
     rank_row, own_col = ranks(owner_ref[...].astype(f32))
     (rank_col,) = columns(rank_row)
@@ -236,12 +238,17 @@
         copy.start()
     copies[0].wait()
     table = picker_table(names_ref, inverse_ref.shape[0]).astype(bf16)
-    for copy in copies[1:]:
+    copies[3].wait()
+    inverse = parts(inverse_ref[...])
+    products = []
+    for half, copy in enumerate(copies[1:3]):
         copy.wait()
-    summed = select(table, get_slab(slab_ref, pieces), LEFT_T)
-    solved = product(parts(inverse_ref[...]), parts(summed))
-    put_slab(answer_ref, select(table, solved))
-    total = local_part_ref[...] + 2.0 * jnp.sum(summed * solved, axis=0, keepdims=True)
+        first, last = (0, pieces // 2) if half == 0 else (pieces // 2, pieces)
+        summed = select(table, get_slab(slab_ref, first, last), LEFT_T)
+        solved = product(inverse, parts(summed))
+        put_slab(answer_ref, select(table, solved), first)
+        products.append(jnp.sum(summed * solved, axis=0, keepdims=True))
+    total = local_part_ref[...] + 2.0 * jnp.concatenate(products, axis=1)
     sums = folded(total) + folded(square_ref[...])
     sums += [jnp.zeros((1, LANES), f32)] * (tiles(len(sums)) - len(sums))
     answer_ref[:, pieces * CAP :, :] = jnp.broadcast_to(
@@ -249,13 +256,10 @@
     )
 
 
-AXIS_AT = {"blk": 0, "lat": 2, "depth": 4}
-
-
-FIRST = [("blk", "up"), ("lat", "up"), ("depth", 1), ("depth", 0), ("blk", "down"), ("lat", "down")]
-SECOND = [("blk", "up"), ("lat", "up"), ("blk", "down"), ("lat", "down"), ("depth", 1), ("depth", 0)]
-NEAR = (0, 2, 4, 5)
-FAR = (1, 3)
+NEAR = (("blk", "up"), ("lat", 0), ("depth", 0), ("depth", 1))
+FAR = (("blk", "down"), ("lat", 1))
+FIRST = NEAR + FAR
+SECOND = (("blk", "up"), ("lat", 0), ("blk", "down"), ("lat", 1), ("depth", 0), ("depth", 1))
 
 
 def moves(order):
@@ -266,36 +270,30 @@
     devices = lax.axis_size(axis)
     if way in ("up", "down"):
         by = 1 if way == "up" else -1
-        ends = [(i, i + by) for i in range(devices)]
-        return [(i, j % devices) for i, j in ends if axis == "blk" or j in range(devices)]
+        return [(i, (i + by) % devices) for i in range(devices)]
     return [pair for i in range(way, devices - 1, 2) for pair in ((i, i + 1), (i + 1, i))]
 
 
-def sends_plus(axis, way):
-    return lax.rem(lax.axis_index(axis), 2) == way
-
-
-def put_faces(image, rows, order, face_refs):
-    for ref, (axis, way) in zip(face_refs, moves(order), strict=True):
-        at = AXIS_AT[axis] * rows
-        minus, plus = image[at : at + rows, :], image[at + rows : at + 2 * rows, :]
-        if way in ("up", "down"):
-            ref[...] = plus if way == "up" else minus
-        else:
-            ref[...] = jnp.where(sends_plus(axis, way), plus, minus)
-
-
-def got_face(got, face):
-    axis, side = ("blk", "lat", "depth")[face // 2], face % 2
-    if axis != "depth":
-        return got[axis, "down" if side else "up"][...]
-    total = None
-    for way in (0, 1):
-        if (axis, way) in got:
-            mine = sends_plus(axis, way) == (side == 1)
-            piece = jnp.where(mine, got[axis, way][...], 0.0)
-            total = piece if total is None else total + piece
-    return total
+def served(axis, way):
+    if way in ("up", "down"):
+        return 0 if way == "up" else 1
+    plus = (lax.rem(lax.axis_index(axis), 2) == way).astype(jnp.int32)
+    return (2 if axis == "lat" else 4) + plus
+
+
+def sent(axis, way):
+    return 1 - served(axis, way) if axis == "blk" else served(axis, way)
+
+
+def rows_of(face, rows):
+    if isinstance(face, int):
+        return pl.ds(face * rows, rows)
+    return pl.ds(pl.multiple_of(face * rows, rows), rows)
+
+
+def put_faces(image_ref, rows, order, face_refs):
+    for ref, move in zip(face_refs, moves(order), strict=True):
+        ref[...] = image_ref[rows_of(sent(*move), rows), :]
 
 
 def exchange(faces, order):
@@ -309,10 +307,10 @@
     rows = local_ref.shape[0] // 6
     width = local_ref.shape[1]
     folds = width // LANES
-    correction = select(table_ref[...], get_slab(returned_ref, folds))
+    correction = select(table_ref[...], get_slab(returned_ref, 0, folds))
     image = local_ref[...] + product((high_ref[...], low_ref[...]), parts(correction))
     image_ref[...] = image
-    put_faces(image, rows, FIRST, face_refs)
+    put_faces(image_ref, rows, FIRST, face_refs)
     tail = jnp.sum(returned_ref[:, folds * CAP :, :], axis=0)
     if pair_depth:
         sums_ref[...] = tail
@@ -320,9 +318,14 @@
         sums_ref[...] = jnp.broadcast_to(tail[None], sums_ref.shape)
 
 
-def new_direction(len_ref, beta, image_ref, prev_ref, got, face, rows):
-    at = slice(face * rows, (face + 1) * rows)
-    precond = 0.5 * (image_ref[at, :] + got_face(got, face))
+def with_got(ref, at, got, move):
+    return ref[at, :] + got[move][...] if move in got else ref[at, :]
+
+
+def new_direction(len_ref, beta, image_ref, prev_ref, got, move, rows):
+    face = served(*move)
+    at = rows_of(face, rows)
+    precond = 0.5 * with_got(image_ref, at, got, move)
     return jnp.where(live_rows(len_ref, face, rows), precond + beta * prev_ref[at, :], 0.0)
 
 
@@ -340,9 +343,9 @@
     rho_out[...] = rho
     beta_out[...] = beta
     square_out[...] = unfolded(sums, folds, folds)
-    for i, face in enumerate(NEAR):
+    for i, move in enumerate(NEAR):
         near_ref[i * rows : (i + 1) * rows, :] = new_direction(
-            len_ref, beta, image_ref, prev_ref, got, face, rows
+            len_ref, beta, image_ref, prev_ref, got, move, rows
         )
     first = len(NEAR) * rows
     image_out[...] = product((high_ref[:, :first], low_ref[:, :first]), parts(near_ref[...]))
@@ -353,28 +356,28 @@
     far_ref, schur_out, *face_refs = refs
     rows = image_ref.shape[0] // 6
     beta = beta_ref[...]
-    for i, face in enumerate(FAR):
+    for i, move in enumerate(FAR):
         far_ref[i * rows : (i + 1) * rows, :] = new_direction(
-            len_ref, beta, image_ref, prev_ref, got, face, rows
+            len_ref, beta, image_ref, prev_ref, got, move, rows
         )
     first = len(NEAR) * rows
     image = near_image_ref[...] + product(
         (high_ref[:, first:], low_ref[:, first:]), parts(far_ref[...])
     )
     schur_out[...] = image
-    put_faces(image, rows, SECOND, face_refs)
+    put_faces(schur_out, rows, SECOND, face_refs)
 
 
 def store_kernel(near_ref, far_ref, direction_out, sems):
     rows = far_ref.shape[0] // len(FAR)
     copies = []
-    for ref, faces in ((near_ref, NEAR), (far_ref, FAR)):
-        for i, face in enumerate(faces):
+    for ref, served_moves in ((near_ref, NEAR), (far_ref, FAR)):
+        for i, move in enumerate(served_moves):
             copies.append(
                 pltpu.make_async_copy(
                     ref.at[pl.ds(i * rows, rows)],
-                    direction_out.at[pl.ds(face * rows, rows)],
-                    sems.at[face],
+                    direction_out.at[rows_of(served(*move), rows)],
+                    sems.at[len(copies)],
                 )
             )
     for copy in copies:
@@ -385,17 +388,16 @@
 
 def products_kernel(len_ref, near_ref, far_ref, schur_ref, residual_ref, arrived, out_ref):
     rows = schur_ref.shape[0] // 6
-    image = schur_ref[...]
-    blocks = {}
-    for ref, faces in ((near_ref, NEAR), (far_ref, FAR)):
-        for i, face in enumerate(faces):
-            blocks[face] = ref[i * rows : (i + 1) * rows, :]
-    direction = jnp.concatenate([blocks[face] for face in range(6)], axis=0)
-    live = jnp.concatenate(
-        [masked(len_ref, residual_ref, face, rows) for face in range(6)], axis=0
-    )
-    curve = 2.0 * jnp.sum(direction * image, axis=0, keepdims=True)
-    cross = 2.0 * jnp.sum(live * image, axis=0, keepdims=True)
+    curve = cross = jnp.zeros((1, schur_ref.shape[1]), f32)
+    for ref, served_moves in ((near_ref, NEAR), (far_ref, FAR)):
+        for i, move in enumerate(served_moves):
+            face = served(*move)
+            at = rows_of(face, rows)
+            image = schur_ref[at, :]
+            live = jnp.where(live_rows(len_ref, face, rows), residual_ref[at, :], 0.0)
+            direction = ref[i * rows : (i + 1) * rows, :]
+            curve += 2.0 * jnp.sum(direction * image, axis=0, keepdims=True)
+            cross += 2.0 * jnp.sum(live * image, axis=0, keepdims=True)
     for j, piece in enumerate(folded(curve) + folded(cross)):
         out_ref[j : j + 1, :] = piece
 
@@ -407,9 +409,10 @@
     rows = schur_ref.shape[0] // 6
     folds = schur_ref.shape[1] // LANES
     total = jnp.zeros((1, schur_ref.shape[1]), f32)
-    for face in range(6):
-        at = slice(face * rows, (face + 1) * rows)
-        applied = schur_ref[at, :] + got_face(got, face)
+    for move in SECOND:
+        face = served(*move)
+        at = rows_of(face, rows)
+        applied = with_got(schur_ref, at, got, move)
         applied = jnp.where(live_rows(len_ref, face, rows), applied, 0.0)
         applied_ref[at, :] = applied
         total += jnp.sum(applied * applied, axis=0, keepdims=True)
@@ -550,8 +553,7 @@
         sums = [sums, lax.ppermute(sums, "depth", route("depth", 0))]
     else:
         sums = [to_all(sums, "depth")]
-    far_keys = [("blk", "down"), ("lat", "down")]
-    near_keys = [key for key in keys if key not in far_keys]
+    near_keys, far_keys = moves(NEAR), moves(FAR)
     rho, beta, square, near, near_image = call(
         functools.partial(near_kernel, pair_depth, scale, near_keys),
         [row, row, row, shape_of(len(NEAR) * rows, width), whole],

time: 114 us -> 112 us (0.982)
  starting transfers between devices: 26.5 us -> 22.6 us
  blocking collectives: 37.2 us -> 39.1 us
  waiting for transfers between devices: 20.2 us -> 18.8 us
  Pallas kernels: 21.2 us -> 22.5 us
    ppermute x10, starting transfers between devices: 17.4 us -> 13.5 us  [exchange(): lax.ppermute(block, axis, route(axis, way))]
    all_to_all x2, blocking collectives: 37.2 us -> 39.1 us  [to_all(): return lax.all_to_all(x, axes, split_axis=0, concat_axis=0, tiled=True)]
    ppermute x10, waiting for transfers between devices: 10.5 us -> 9.02 us  [exchange(): lax.ppermute(block, axis, route(axis, way))]
    pallas_call x10, Pallas kernels: 21.2 us -> 22.5 us  [call(): pl.pallas_call(body, out_shape=list(outs), in_specs=in_specs, out_specs=o...]
  transfers between devices with their start and end apart: 13 -> 13, of which waited for: 7 -> 4; matrix products, arithmetic and copies ran while one was open for 0% -> 0% of each run, Pallas kernels for 7% -> 8%
where the time goes in v9:
time: 112 us; the launch traced here: 111 us
  blocking collectives  39.1 us (35%)
  starting transfers between devices  22.6 us (20%)
  Pallas kernels  22.5 us (20%)
  waiting for transfers between devices  18.8 us (17%)
  local copies, waits for them, and re-layouts  7.73 us (7%)
    all_to_all x2, blocking collectives, to_all(): return lax.all_to_all(x, axes, split_axis=0, concat_axis=0, tiled=True)  39.1 us
    pallas_call x10, Pallas kernels, call(): pl.pallas_call(body, out_shape=list(outs), in_specs=in_specs, out_specs=o...  22.5 us
    ppermute x10, starting transfers between devices, exchange(): lax.ppermute(block, axis, route(axis, way))  13.5 us
    all_to_all x1, waiting for transfers between devices, to_all(): return lax.all_to_all(x, axes, split_axis=0, concat_axis=0, tiled=True)  9.73 us
    ppermute x10, waiting for transfers between devices, exchange(): lax.ppermute(block, axis, route(axis, way))  9.02 us
    all_to_all x1, starting transfers between devices, to_all(): return lax.all_to_all(x, axes, split_axis=0, concat_axis=0, tiled=True)  8.49 us
    unnamed x38, local copies, waits for them, and re-layouts  7.73 us
  transfers between devices with their start and end apart: 13, of which 4 were waited for; matrix products, arithmetic and copies ran while one was open for 0% of the time, Pallas kernels for 8%

profile of v9, /device:TPU:0, one launch (start us, length us, event | category | flops | bytes accessed | tf_op | source)
XLA Modules:
  0.0 111.5 jit_solution(8397658120954837119)
XLA Ops:
  0.6 4.4 %shard_map.137 = f32[16,104,128]{2,1,0:T(8,128)} custom-call(s32[6]{0:T(128)} %bitcast.25, s32[1,256]{1,0:T(1,128)} %bitcast.32, s32[1,256]{1,0:T(1,128)} %bitcast.37, f32[768,512]{1,0:T(8,128)} %bitcast.15, f32[768,256]{1,0:T(8,128)} %bitcast.21), custom_call_target="tpu_custom_call" | custom-call | flops 603979776 | bytes 3145728 | tf_op jit(solution)/shard_map/pallas_call | solution.py:37
  5.1 8.5 %all-to-all-start = ((f32[16,104,128]{2,1,0:T(8,128)}), f32[16,104,128]{2,1,0:T(8,128)}, u32[]{:S(2)}, u32[]{:S(2)}) async-start(f32[16,104,128]{2,1,0:T(8,128)} %shard_map.137), calls=%async_computation | async-start | bytes 1703936 | tf_op jit(solution)/shard_map/all_to_all | solution.py:457
  13.6 1.7 %copy-done.5 = f32[1,1,1,768,768]{4,3,2,1,0:T(8,128)S(1)} copy-done((f32[1,1,1,768,768]{4,3,2,1,0:T(8,128)S(1)}, f32[1,1,1,768,768]{4,3,2,1,0:T(8,128)}, u32[]{:S(2)}) %copy-start.5) | copy-done | bytes 2359320
  15.3 1.7 %copy-done.6 = f32[1,1,1,768,768]{4,3,2,1,0:T(8,128)S(1)} copy-done((f32[1,1,1,768,768]{4,3,2,1,0:T(8,128)S(1)}, f32[1,1,1,768,768]{4,3,2,1,0:T(8,128)}, u32[]{:S(2)}) %copy-start.6) | copy-done | bytes 2359320
  16.9 3.5 %shard_map.138 = (f32[768,512]{1,0:T(8,128)S(1)}, f32[1,512]{1,0:T(1,128)S(1)}, f32[1,512]{1,0:T(1,128)S(1)}, bf16[256,384]{1,0:T(8,128)(2,1)S(1)}, bf16[768,256...) custom-call(s32[6]{0:T(128)S(1)} %bitcast.26, ...), custom_call_target="tpu_custom_call" | custom-call | flops 1811939328 | bytes 10223616 | tf_op jit(solution)/shard_map/pallas_call | solution.py:37
  20.5 1.0 copy-done.2
  21.5 1.1 %copy-done.7 = f32[768,512]{1,0:T(8,128)} copy-done((f32[768,512]{1,0:T(8,128)}, f32[768,512]{1,0:T(8,128)S(1)}, u32[]{:S(2)}) %copy-start.7) | copy-done | bytes 1572888
  24.8 9.7 %all-to-all-done.incoming_any = f32[16,104,128]{2,1,0:T(8,128)} async-done(((f32[16,104,128]{2,1,0:T(8,128)}), f32[16,104,128]{2,1,0:T(8,128)}, u32[]{:S(2)}, u32[]{:S(2)}) %all-to-all-start) | async-done | bytes 852000 | tf_op jit(solution)/shard_map/all_to_all | solution.py:457
  34.5 3.5 %shard_map.139 = f32[16,104,128]{2,1,0:T(8,128)S(1)} custom-call(f32[16,104,128]{2,1,0:T(8,128)} %all-to-all-done.incoming_any, f32[256,256]{1,0:T(8,128)} %bitcast.39, f32[1,512]{1,0:T(1,128)S(1)} %get-tuple-element.37.local_part_ref, f32[1,512]{1,0:T(1,128)S(1)} %get-tuple-element.38.square_ref), custom_call_target="tpu_custom_call" | custom-call | flops 603979776 | bytes 1572864 | tf_op jit(solution)/shard_map/pallas_call | solution.py:37
  38.1 26.4 %all_to_all.15.returned_ref = f32[16,104,128]{2,1,0:T(8,128)S(1)} all-to-all(f32[16,104,128]{2,1,0:T(8,128)S(1)} %shard_map.139), channel_id=1, replica_groups=mesh['blk'=4,'lat'=4,'depth'=2] {'blk','lat'}, dimensions={0} | all-to-all | bytes 1703936 | tf_op jit(solution)/shard_map/all_to_all | solution.py:457
  64.5 1.3 %shard_map.140 = (f32[768,512]{1,0:T(8,128)S(1)}, f32[8,128]{1,0:T(8,128)S(1)}, f32[128,512]{1,0:T(8,128)S(1)}, f32[128,512]{1,0:T(8,128)S(1)}, f32[128,512]{1,0...) custom-call(f32[16,104,128]{2,1,0:T(8,128)S(1)} %all_to_all.15.returned_ref, ...), custom_call_target="tpu_custom_call" | custom-call | flops 805306368 | bytes 6291456 | tf_op jit(solution)/shard_map/pallas_call | solution.py:37
  65.8 1.1 collective-permute-start
  67.9 2.8 %collective-permute-start.4 = (f32[128,512]{1,0:T(8,128)S(1)}, f32[128,512]{1,0:T(8,128)S(1)}, u32[]{:S(2)}, u32[]{:S(2)}) collective-permute-start(f32[128,512]{1,0:T(8,128)S(1)} %get-tuple-element.53), channel_id=1, source_target_pairs={{0,24},{8,0},{16,8},{24,16},{1,25},{9,1},{17,9},{25,17},{2,26},{10... | collective-permute-start | bytes 786440 | tf_op jit(solution)/shard_map/ppermute | solution.py:301
  71.4 5.1 %collective-permute-done.refs_0_ = f32[128,512]{1,0:T(8,128)S(1)} collective-permute-done((f32[128,512]{1,0:T(8,128)S(1)}, f32[128,512]{1,0:T(8,128)S(1)}, u32[]{:S(2)}, u32[]{:S(2)}) %collective-permute-start) | collective-permute-done | bytes 262176 | tf_op jit(solution)/shard_map/ppermute | solution.py:301
  76.5 2.6 %shard_map.141 = (f32[1,512]{1,0:T(1,128)}, f32[1,512]{1,0:T(1,128)S(1)}, f32[1,512]{1,0:T(1,128)S(1)}, f32[512,512]{1,0:T(8,128)S(1)}, f32[768,512]{1,0:T(8,128)S(1)}) custom-call(s32[6]{0:T(128)S(1)} %bitcast.27, f32[8,128]{1,0:T(8,128)S(1)} %get-tuple-element.43.sums_ref, f32[1,512]{1,0:T(1,128)S(1)} %bitcast.34, ...), custom_call_target="tpu_custom_call" | custom-call | flops 1207959552 | bytes 8650752 | tf_op jit(solution)/shard_map/pallas_call | solution.py:37
  79.1 1.5 %shard_map.142 = (f32[256,512]{1,0:T(8,128)S(1)}, f32[768,512]{1,0:T(8,128)S(1)}, f32[128,512]{1,0:T(8,128)S(1)}, f32[128,512]{1,0:T(8,128)S(1)}, f32[128,512]{1...) custom-call(s32[6]{0:T(128)S(1)} %bitcast.28, f32[1,512]{1,0:T(1,128)S(1)} %get-tuple-element.51.beta_ref, ...), custom_call_target="tpu_custom_call" | custom-call | flops 603979776 | bytes 8650752 | tf_op jit(solution)/shard_map/pallas_call | solution.py:37
  81.3 3.3 %collective-permute-start.7 = (f32[128,512]{1,0:T(8,128)S(1)}, f32[128,512]{1,0:T(8,128)S(1)}, u32[]{:S(2)}, u32[]{:S(2)}) collective-permute-start(f32[128,512]{1,0:T(8,128)S(1)} %get-tuple-element.58), channel_id=1, source_target_pairs={{0,2},{2,0},{4,6},{6,4},{1,3},{3,1},{5,7},{7,5},{8,10},{10,8},{12,... | collective-permute-start | bytes 786440 | tf_op jit(solution)/shard_map/ppermute | solution.py:301
  84.6 3.7 %collective-permute-start.8 = (f32[128,512]{1,0:T(8,128)S(1)}, f32[128,512]{1,0:T(8,128)S(1)}, u32[]{:S(2)}, u32[]{:S(2)}) collective-permute-start(f32[128,512]{1,0:T(8,128)S(1)} %get-tuple-element.59), channel_id=1, source_target_pairs={{0,24},{8,0},{16,8},{24,16},{1,25},{9,1},{17,9},{25,17},{2,26},{10... | collective-permute-start | bytes 786440 | tf_op jit(solution)/shard_map/ppermute | solution.py:301
  89.1 2.7 %collective-permute-done.6.arrived.refs_0_ = f32[128,512]{1,0:T(8,128)S(1)} collective-permute-done((f32[128,512]{1,0:T(8,128)S(1)}, f32[128,512]{1,0:T(8,128)S(1)}, u32[]{:S(2)}, u32[]{:S(2)}) %collective-permute-start.6) | collective-permute-done | bytes 262176 | tf_op jit(solution)/shard_map/ppermute | solution.py:301
  91.8 1.3 %shard_map.144.refs_5_ = f32[8,128]{1,0:T(8,128)S(1)} custom-call(s32[6]{0:T(128)S(1)} %bitcast.29, f32[512,512]{1,0:T(8,128)S(1)} %get-tuple-element.50.near_ref, f32[256,512]{1,0:T(8,128)S(1)} %get-tuple-element.55.far_ref, f32[768,512]{1,0:T(8,128)S(1)} %get-tuple-element.56.schur_ref, f32[768,512]{1,0:T(8,128)S(1)} %bitcast.17, ...), custom_call_target="tpu_custom_call" | custom-call | flops 1572864 | bytes 4718592 | tf_op jit(solution)/shard_map/pallas_call | solution.py:37
  93.1 1.2 %shard_map.143.stored = f32[768,512]{1,0:T(8,128)} custom-call(f32[512,512]{1,0:T(8,128)S(1)} %get-tuple-element.50.near_ref, f32[256,512]{1,0:T(8,128)S(1)} %get-tuple-element.55.far_ref), custom_call_target="tpu_custom_call" | custom-call | bytes 3145728 | tf_op jit(solution)/shard_map/pallas_call | solution.py:37
  94.4 1.2 %collective-permute-done.8.refs_2_ = f32[128,512]{1,0:T(8,128)S(1)} collective-permute-done((f32[128,512]{1,0:T(8,128)S(1)}, f32[128,512]{1,0:T(8,128)S(1)}, u32[]{:S(2)}, u32[]{:S(2)}) %collective-permute-start.8) | collective-permute-done | bytes 262176 | tf_op jit(solution)/shard_map/ppermute | solution.py:301
  96.4 12.7 %all_to_all.16.sums_ref = f32[32,2,4,128]{3,2,1,0:T(4,128)S(1)} all-to-all(f32[32,2,4,128]{3,2,1,0:T(4,128)S(1)} %get-tuple-element.62), channel_id=1, replica_groups=mesh['blk'=4,'lat'=4,'depth'=2] {'blk','lat','depth'}, dimensions={0} | all-to-all | bytes 262144 | tf_op jit(solution)/shard_map/all_to_all | solution.py:457
  109.1 2.4 %shard_map.146 = (f32[768,512]{1,0:T(8,128)}, f32[1,512]{1,0:T(1,128)}, f32[1,512]{1,0:T(1,128)}) custom-call(s32[6]{0:T(128)S(1)} %bitcast.31, f32[32,2,4,128]{3,2,1,0:T(4,128)S(1)} %all_to_all.16.sums_ref, f32[1,512]{1,0:T(1,128)S(1)} %copy-done.18, f32[1,512]{1,0:T(1,128)S(1)} %get-tuple-element.64.square_ref, f32[768,512]{1,0:T(8,128)S(1)} %bitcast.18, ...), custom_call_target="tpu_custom_call" | custom-call | flops 1572864 | bytes 4718592 | tf_op jit(solution)/shard_map/pallas_call | solution.py:37
  (52 shorter events, 6.3 us)
Async XLA Ops:
  0.6 12.9 %copy-start.4 = (f32[1,1,1,768,256]{4,3,2,1,0:T(8,128)S(1)}, f32[1,1,1,768,256]{4,3,2,1,0:T(8,128)}, u32[]{:S(2)}) copy-start(f32[1,1,1,768,256]{4,3,2,1,0:T(8,128)} %param.16) | copy-start | bytes 2359300
  5.0 8.5 %copy-start = (f32[1,1,1,768,512]{4,3,2,1,0:T(8,128)S(1)}, f32[1,1,1,768,512]{4,3,2,1,0:T(8,128)}, u32[]{:S(2)}) copy-start(f32[1,1,1,768,512]{4,3,2,1,0:T(8,128)} %param.11) | copy-start | bytes 4718596
  5.0 8.5 %copy-start.15 = (s32[1,1,1,6]{3,2,1,0:T(1,128)S(1)}, s32[1,1,1,6]{3,2,1,0:T(1,128)}, u32[]{:S(2)}) copy-start(s32[1,1,1,6]{3,2,1,0:T(1,128)} %param.10) | copy-start | bytes 76
  5.1 29.5 %all-to-all-start = ((f32[16,104,128]{2,1,0:T(8,128)}), f32[16,104,128]{2,1,0:T(8,128)}, u32[]{:S(2)}, u32[]{:S(2)}) async-start(f32[16,104,128]{2,1,0:T(8,128)} %shard_map.137), calls=%async_computation | async-start | bytes 1703936 | tf_op jit(solution)/shard_map/all_to_all | solution.py:457
  34.5 29.9 %copy-start.8 = (f32[768,512]{1,0:T(8,128)S(1)}, f32[768,512]{1,0:T(8,128)}, u32[]{:S(2)}) copy-start(f32[768,512]{1,0:T(8,128)} %copy-done.7) | copy-start | bytes 4718596
  34.5 29.9 %copy-start.10 = (bf16[768,256]{1,0:T(8,128)(2,1)S(1)}, bf16[768,256]{1,0:T(8,128)(2,1)}, u32[]{:S(2)}) copy-start(bf16[768,256]{1,0:T(8,128)(2,1)} %copy-done.9) | copy-start | bytes 1179652
  34.5 29.9 %copy-start.12 = (bf16[768,256]{1,0:T(8,128)(2,1)S(1)}, bf16[768,256]{1,0:T(8,128)(2,1)}, u32[]{:S(2)}) copy-start(bf16[768,256]{1,0:T(8,128)(2,1)} %copy-done.11) | copy-start | bytes 1179652
  34.5 29.9 %copy-start.14 = (bf16[256,384]{1,0:T(8,128)(2,1)S(1)}, bf16[256,384]{1,0:T(8,128)(2,1)}, u32[]{:S(2)}) copy-start(bf16[256,384]{1,0:T(8,128)(2,1)} %copy-done.13) | copy-start | bytes 589828
  64.5 12.1 %copy-start.1 = (f32[1,1,1,768,512]{4,3,2,1,0:T(8,128)S(1)}, f32[1,1,1,768,512]{4,3,2,1,0:T(8,128)}, u32[]{:S(2)}) copy-start(f32[1,1,1,768,512]{4,3,2,1,0:T(8,128)} %param.12) | copy-start | bytes 4718596
  64.5 12.1 %copy-start.3 = (bf16[768,768]{1,0:T(8,128)(2,1)S(1)}, bf16[768,768]{1,0:T(8,128)(2,1)}, u32[]{:S(2)}) copy-start(bf16[768,768]{1,0:T(8,128)(2,1)} %copy-done.2) | copy-start | bytes 3538948
  64.5 12.1 %copy-start.17 = (f32[512]{0:T(512)S(1)}, f32[512]{0:T(512)}, u32[]{:S(2)}) copy-start(f32[512]{0:T(512)} %param.13) | copy-start | bytes 6148
  65.8 10.7 %collective-permute-start = (f32[128,512]{1,0:T(8,128)S(1)}, f32[128,512]{1,0:T(8,128)S(1)}, u32[]{:S(2)}, u32[]{:S(2)}) collective-permute-start(f32[128,512]{1,0:T(8,128)S(1)} %get-tuple-element.47), channel_id=1, source_target_pairs={{0,8},{8,16},{16,24},{24,0},{1,9},{9,17},{17,25},{25,1},{2,10},{10... | collective-permute-start | bytes 786440 | tf_op jit(solution)/shard_map/ppermute | solution.py:301
  66.8 9.7 %collective-permute-start.1 = (f32[128,512]{1,0:T(8,128)S(1)}, f32[128,512]{1,0:T(8,128)S(1)}, u32[]{:S(2)}, u32[]{:S(2)}) collective-permute-start(f32[128,512]{1,0:T(8,128)S(1)} %get-tuple-element.48), channel_id=1, source_target_pairs={{0,2},{2,0},{4,6},{6,4},{1,3},{3,1},{5,7},{7,5},{8,10},{10,8},{12,... | collective-permute-start | bytes 786440 | tf_op jit(solution)/shard_map/ppermute | solution.py:301
  67.4 9.1 %collective-permute-start.2 = (f32[128,512]{1,0:T(8,128)S(1)}, f32[128,512]{1,0:T(8,128)S(1)}, u32[]{:S(2)}, u32[]{:S(2)}) collective-permute-start(f32[128,512]{1,0:T(8,128)S(1)} %get-tuple-element.49), channel_id=1, source_target_pairs={{0,1},{1,0},{2,3},{3,2},{4,5},{5,4},{6,7},{7,6},{8,9},{9,8},{10,11... | collective-permute-start | bytes 786440 | tf_op jit(solution)/shard_map/ppermute | solution.py:301
  67.4 3.3 %collective-permute-start.3 = (f32[8,128]{1,0:T(8,128)S(1)}, f32[8,128]{1,0:T(8,128)S(1)}, u32[]{:S(2)}, u32[]{:S(2)}) collective-permute-start(f32[8,128]{1,0:T(8,128)S(1)} %get-tuple-element.43.sums_ref), channel_id=1, source_target_pairs={{0,1},{1,0},{2,3},{3,2},{4,5},{5,4},{6,7},{7,6},{8,9},{9,8},{10,11... | collective-permute-start | bytes 12296 | tf_op jit(solution)/shard_map/ppermute | solution.py:553
  67.9 11.2 %collective-permute-start.4 = (f32[128,512]{1,0:T(8,128)S(1)}, f32[128,512]{1,0:T(8,128)S(1)}, u32[]{:S(2)}, u32[]{:S(2)}) collective-permute-start(f32[128,512]{1,0:T(8,128)S(1)} %get-tuple-element.53), channel_id=1, source_target_pairs={{0,24},{8,0},{16,8},{24,16},{1,25},{9,1},{17,9},{25,17},{2,26},{10... | collective-permute-start | bytes 786440 | tf_op jit(solution)/shard_map/ppermute | solution.py:301
  70.7 8.4 %collective-permute-start.5 = (f32[128,512]{1,0:T(8,128)S(1)}, f32[128,512]{1,0:T(8,128)S(1)}, u32[]{:S(2)}, u32[]{:S(2)}) collective-permute-start(f32[128,512]{1,0:T(8,128)S(1)} %get-tuple-element.54), channel_id=1, source_target_pairs={{2,4},{4,2},{3,5},{5,3},{10,12},{12,10},{11,13},{13,11},{18,20},{2... | collective-permute-start | bytes 786440 | tf_op jit(solution)/shard_map/ppermute | solution.py:301
  80.6 11.1 %collective-permute-start.6 = (f32[128,512]{1,0:T(8,128)S(1)}, f32[128,512]{1,0:T(8,128)S(1)}, u32[]{:S(2)}, u32[]{:S(2)}) collective-permute-start(f32[128,512]{1,0:T(8,128)S(1)} %get-tuple-element.57), channel_id=1, source_target_pairs={{0,8},{8,16},{16,24},{24,0},{1,9},{9,17},{17,25},{25,1},{2,10},{10... | collective-permute-start | bytes 786440 | tf_op jit(solution)/shard_map/ppermute | solution.py:301
  81.3 13.1 %collective-permute-start.7 = (f32[128,512]{1,0:T(8,128)S(1)}, f32[128,512]{1,0:T(8,128)S(1)}, u32[]{:S(2)}, u32[]{:S(2)}) collective-permute-start(f32[128,512]{1,0:T(8,128)S(1)} %get-tuple-element.58), channel_id=1, source_target_pairs={{0,2},{2,0},{4,6},{6,4},{1,3},{3,1},{5,7},{7,5},{8,10},{10,8},{12,... | collective-permute-start | bytes 786440 | tf_op jit(solution)/shard_map/ppermute | solution.py:301
  84.6 11.0 %collective-permute-start.8 = (f32[128,512]{1,0:T(8,128)S(1)}, f32[128,512]{1,0:T(8,128)S(1)}, u32[]{:S(2)}, u32[]{:S(2)}) collective-permute-start(f32[128,512]{1,0:T(8,128)S(1)} %get-tuple-element.59), channel_id=1, source_target_pairs={{0,24},{8,0},{16,8},{24,16},{1,25},{9,1},{17,9},{25,17},{2,26},{10... | collective-permute-start | bytes 786440 | tf_op jit(solution)/shard_map/ppermute | solution.py:301
  88.3 7.2 %collective-permute-start.9 = (f32[128,512]{1,0:T(8,128)S(1)}, f32[128,512]{1,0:T(8,128)S(1)}, u32[]{:S(2)}, u32[]{:S(2)}) collective-permute-start(f32[128,512]{1,0:T(8,128)S(1)} %get-tuple-element.60), channel_id=1, source_target_pairs={{2,4},{4,2},{3,5},{5,3},{10,12},{12,10},{11,13},{13,11},{18,20},{2... | collective-permute-start | bytes 786440 | tf_op jit(solution)/shard_map/ppermute | solution.py:301
  89.0 6.6 %collective-permute-start.10 = (f32[128,512]{1,0:T(8,128)S(1)}, f32[128,512]{1,0:T(8,128)S(1)}, u32[]{:S(2)}, u32[]{:S(2)}) collective-permute-start(f32[128,512]{1,0:T(8,128)S(1)} %get-tuple-element.61), channel_id=1, source_target_pairs={{0,1},{1,0},{2,3},{3,2},{4,5},{5,4},{6,7},{7,6},{8,9},{9,8},{10,11... | collective-permute-start | bytes 786440 | tf_op jit(solution)/shard_map/ppermute | solution.py:301
  93.1 2.5 %collective-permute-start.11 = (f32[8,128]{1,0:T(8,128)S(1)}, f32[8,128]{1,0:T(8,128)S(1)}, u32[]{:S(2)}, u32[]{:S(2)}) collective-permute-start(f32[8,128]{1,0:T(8,128)S(1)} %shard_map.144.refs_5_), channel_id=1, source_target_pairs={{0,1},{1,0},{2,3},{3,2},{4,5},{5,4},{6,7},{7,6},{8,9},{9,8},{10,11... | collective-permute-start | bytes 12296 | tf_op jit(solution)/shard_map/ppermute | solution.py:588
  94.3 14.8 %copy-start.18 = (f32[1,512]{1,0:T(1,128)S(1)}, f32[1,512]{1,0:T(1,128)}, u32[]{:S(2)}) copy-start(f32[1,512]{1,0:T(1,128)} %get-tuple-element.63.rho_ref) | copy-start | bytes 6148
  (8 other events, 16.2 us)

commit v10 on v9

--- a/solution.py
+++ b/solution.py
@@ -56,7 +56,6 @@
 
 
 PLAIN = ((1,), (0,))
-LEFT_T = ((0,), (0,))
 
 
 def product(a, b, dims=PLAIN):
@@ -91,23 +90,25 @@
     return jnp.concatenate([block[first + j : first + j + 1, :] for j in range(pieces)], axis=1)
 
 
+def id_rows(slots):
+    return -(-slots // LANES)
+
+
 def tiles(rows):
     return -(-rows // TILE) * TILE
 
 
-def put_slab(out_ref, block, first=0):
+def put_slab(out_ref, block):
     owners = out_ref.shape[0]
     for j in range(block.shape[1] // LANES):
         piece = block[:, j * LANES : (j + 1) * LANES]
-        at = (first + j) * CAP
-        out_ref[:, at : at + CAP, :] = piece.reshape(owners, CAP, LANES)
-
-
-def get_slab(ref, first, last):
+        out_ref[:, j * CAP : (j + 1) * CAP, :] = piece.reshape(owners, CAP, LANES)
+
+
+def get_slab(ref, pieces):
     slots = ref.shape[0] * CAP
     return jnp.concatenate(
-        [ref[:, j * CAP : (j + 1) * CAP, :].reshape(slots, LANES) for j in range(first, last)],
-        axis=1,
+        [ref[:, j * CAP : (j + 1) * CAP, :].reshape(slots, LANES) for j in range(pieces)], axis=1
     )
 
 
@@ -161,9 +162,9 @@
     rank_col, wanted_col = columns(rank_row, wanted_row)
     packer = one_hot(lax.broadcasted_iota(jnp.int32, (slots, primal), 0) == slot_row)
     to_owner = one_hot(lax.broadcasted_iota(jnp.int32, (owners, primal), 0) == owner_ref[...])
-    lane_at = lax.broadcasted_iota(jnp.int32, (primal, LANES), 1)
-    ranked = jnp.where(lane_at == rank_col.astype(jnp.int32), wanted_col, 0.0)
-    names = select(to_owner, ranked)
+    at_owner = lax.axis_index(LAYER) * CAP + rank_col.astype(jnp.int32)
+    place = lax.broadcasted_iota(jnp.int32, (primal, id_rows(slots) * LANES), 1)
+    names = select(to_owner, jnp.where(place == at_owner, wanted_col, 0.0))
     terms = None
     for pair in range(3):
         for copy in large[pair]:
@@ -173,13 +174,15 @@
             axis=0,
         )
         basis = basis_ref[2 * pair * rows : 2 * (pair + 1) * rows, :]
-        term = product(parts(basis), parts(weighted), LEFT_T)
+        term = product(parts(jnp.transpose(basis)), parts(weighted))
         terms = term if terms is None else terms + term
     put_slab(slab_ref, select(packer, terms))
-    tail = slab_ref.shape[1] - TILE
-    slab_ref[:, tail:, :] = jnp.broadcast_to(
-        names.reshape(owners, 1, LANES), (owners, TILE, LANES)
-    )
+    tail = slab_ref.shape[1] - tiles(id_rows(slots))
+    names = jnp.concatenate(
+        [names, jnp.zeros((owners, (slab_ref.shape[1] - tail) * LANES - names.shape[1]), f32)], axis=1
+    )
+    for j in range(slab_ref.shape[1] - tail):
+        slab_ref[:, tail + j, :] = names[:, j * LANES : (j + 1) * LANES]
 
 
 def local_kernel(len_ref, residual_ref, matrix_ref, owner_ref, *refs):
@@ -204,26 +207,15 @@
     table_ref[...] = one_hot(lax.broadcasted_iota(jnp.int32, (primal, slots), 1) == slot_col)
 
 
-def picker_table(names_ref, owned):
-    owners = names_ref.shape[0]
-    lane_at = lax.broadcasted_iota(jnp.int32, (CAP, LANES), 1)
-    rank_at = lax.broadcasted_iota(jnp.int32, (CAP, LANES), 0)
-    out_at = lax.broadcasted_iota(jnp.int32, (CAP, owned), 1).astype(f32) + 1.0
-    blocks = []
-    for source in range(owners):
-        names = names_ref[source, 0:1, :]
-        named = jnp.sum(jnp.where(lane_at == rank_at, names, 0.0), axis=1, keepdims=True)
-        blocks.append(jnp.where(out_at == named, 1.0, 0.0))
-    return jnp.concatenate(blocks, axis=0)
-
-
 def solve_kernel(incoming_any, inverse_any, local_part_ref, square_ref, answer_ref, *refs):
     names_ref, slab_ref, inverse_ref, sems = refs
     owners, height, _ = slab_ref.shape
     pieces = height // CAP
     half = pieces // 2 * CAP
     copies = [
-        pltpu.make_async_copy(incoming_any.at[:, pl.ds(height, TILE)], names_ref, sems.at[0]),
+        pltpu.make_async_copy(
+            incoming_any.at[:, pl.ds(height, names_ref.shape[1])], names_ref, sems.at[0]
+        ),
         pltpu.make_async_copy(
             incoming_any.at[:, pl.ds(0, half)], slab_ref.at[:, pl.ds(0, half)], sems.at[1]
         ),
@@ -237,18 +229,21 @@
     for copy in copies:
         copy.start()
     copies[0].wait()
-    table = picker_table(names_ref, inverse_ref.shape[0]).astype(bf16)
+    slots, owned = owners * CAP, inverse_ref.shape[0]
+    wanted = unfolded(jnp.sum(names_ref[...], axis=0), 0, id_rows(slots))[:, :slots]
+    (wanted_col,) = columns(wanted)
+    row_at = lax.broadcasted_iota(jnp.int32, (owned, slots), 0).astype(f32) + 1.0
+    col_at = lax.broadcasted_iota(jnp.int32, (slots, owned), 1).astype(f32) + 1.0
+    gather = one_hot(row_at == wanted)
+    table = one_hot(col_at == wanted_col)
     copies[3].wait()
     inverse = parts(inverse_ref[...])
-    products = []
-    for half, copy in enumerate(copies[1:3]):
+    for copy in copies[1:3]:
         copy.wait()
-        first, last = (0, pieces // 2) if half == 0 else (pieces // 2, pieces)
-        summed = select(table, get_slab(slab_ref, first, last), LEFT_T)
-        solved = product(inverse, parts(summed))
-        put_slab(answer_ref, select(table, solved), first)
-        products.append(jnp.sum(summed * solved, axis=0, keepdims=True))
-    total = local_part_ref[...] + 2.0 * jnp.concatenate(products, axis=1)
+    summed = select(gather, get_slab(slab_ref, pieces))
+    solved = product(inverse, parts(summed))
+    put_slab(answer_ref, select(table, solved))
+    total = local_part_ref[...] + 2.0 * jnp.sum(summed * solved, axis=0, keepdims=True)
     sums = folded(total) + folded(square_ref[...])
     sums += [jnp.zeros((1, LANES), f32)] * (tiles(len(sums)) - len(sums))
     answer_ref[:, pieces * CAP :, :] = jnp.broadcast_to(
@@ -307,7 +302,7 @@
     rows = local_ref.shape[0] // 6
     width = local_ref.shape[1]
     folds = width // LANES
-    correction = select(table_ref[...], get_slab(returned_ref, 0, folds))
+    correction = select(table_ref[...], get_slab(returned_ref, folds))
     image = local_ref[...] + product((high_ref[...], low_ref[...]), parts(correction))
     image_ref[...] = image
     put_faces(image_ref, rows, FIRST, face_refs)
@@ -481,6 +476,7 @@
     scale = 0.5 / (devices * height)
     folds = width // LANES
     tail = tiles(2 * folds)
+    id_tail = tiles(id_rows(slots))
 
     lengths = face_len.reshape(6)
     residual = residual.reshape(height, width)
@@ -497,7 +493,7 @@
 
     (outgoing,) = call(
         pack_kernel,
-        [shape_of(owners, folds * CAP + TILE, LANES)],
+        [shape_of(owners, folds * CAP + id_tail, LANES)],
         [lengths, owner, wanted, residual, basis],
         far=range(5),
         flops=6 * height * primal * width,
@@ -532,7 +528,7 @@
         flops=(8 * slots + 6 * owned) * owned * width,
         moved=8 * slots * width,
         scratch=[
-            pltpu.VMEM((owners, TILE, LANES), f32),
+            pltpu.VMEM((owners, id_tail, LANES), f32),
             pltpu.VMEM((owners, folds * CAP, LANES), f32),
             pltpu.VMEM((owned, owned), f32),
             pltpu.SemaphoreType.DMA((4,)),

time: 112 us -> 111 us (level)
  no operation moved by 1% of the time
where the time goes in v10:
time: 111 us
  blocking collectives  39 us (35%)
  starting transfers between devices  22.6 us (20%)
  Pallas kernels  21.6 us (19%)
  waiting for transfers between devices  18.8 us (17%)
  local copies, waits for them, and re-layouts  7.73 us (7%)
    all_to_all x2, blocking collectives, to_all(): return lax.all_to_all(x, axes, split_axis=0, concat_axis=0, tiled=True)  39 us
    pallas_call x10, Pallas kernels, call(): pl.pallas_call(body, out_shape=list(outs), in_specs=in_specs, out_specs=o...  21.6 us
    ppermute x10, starting transfers between devices, exchange(): lax.ppermute(block, axis, route(axis, way))  13.5 us
    all_to_all x1, waiting for transfers between devices, to_all(): return lax.all_to_all(x, axes, split_axis=0, concat_axis=0, tiled=True)  9.73 us
    ppermute x10, waiting for transfers between devices, exchange(): lax.ppermute(block, axis, route(axis, way))  9.02 us
    all_to_all x1, starting transfers between devices, to_all(): return lax.all_to_all(x, axes, split_axis=0, concat_axis=0, tiled=True)  8.5 us
    unnamed x38, local copies, waits for them, and re-layouts  7.73 us
  transfers between devices with their start and end apart: 13, of which 4 were waited for; matrix products, arithmetic and copies ran while one was open for 0% of the time, Pallas kernels for 8%

profile of v10, /device:TPU:0, one launch (start us, length us, event | category | flops | bytes accessed | tf_op | source)
XLA Modules:
  0.0 110.6 jit_solution(14340716002924325115)
XLA Ops:
  0.6 4.4 %shard_map.137 = f32[16,104,128]{2,1,0:T(8,128)} custom-call(s32[6]{0:T(128)} %bitcast.25, s32[1,256]{1,0:T(1,128)} %bitcast.32, s32[1,256]{1,0:T(1,128)} %bitcast.37, f32[768,512]{1,0:T(8,128)} %bitcast.15, f32[768,256]{1,0:T(8,128)} %bitcast.21), custom_call_target="tpu_custom_call" | custom-call | flops 603979776 | bytes 3145728 | tf_op jit(solution)/shard_map/pallas_call | solution.py:37
  5.1 8.5 %all-to-all-start = ((f32[16,104,128]{2,1,0:T(8,128)}), f32[16,104,128]{2,1,0:T(8,128)}, u32[]{:S(2)}, u32[]{:S(2)}) async-start(f32[16,104,128]{2,1,0:T(8,128)} %shard_map.137), calls=%async_computation | async-start | bytes 1703936 | tf_op jit(solution)/shard_map/all_to_all | solution.py:452
  13.7 1.7 %copy-done.5 = f32[1,1,1,768,768]{4,3,2,1,0:T(8,128)S(1)} copy-done((f32[1,1,1,768,768]{4,3,2,1,0:T(8,128)S(1)}, f32[1,1,1,768,768]{4,3,2,1,0:T(8,128)}, u32[]{:S(2)}) %copy-start.5) | copy-done | bytes 2359320
  15.3 1.7 %copy-done.6 = f32[1,1,1,768,768]{4,3,2,1,0:T(8,128)S(1)} copy-done((f32[1,1,1,768,768]{4,3,2,1,0:T(8,128)S(1)}, f32[1,1,1,768,768]{4,3,2,1,0:T(8,128)}, u32[]{:S(2)}) %copy-start.6) | copy-done | bytes 2359320
  17.0 3.5 %shard_map.138 = (f32[768,512]{1,0:T(8,128)S(1)}, f32[1,512]{1,0:T(1,128)S(1)}, f32[1,512]{1,0:T(1,128)S(1)}, bf16[256,384]{1,0:T(8,128)(2,1)S(1)}, bf16[768,256...) custom-call(s32[6]{0:T(128)S(1)} %bitcast.26, ...), custom_call_target="tpu_custom_call" | custom-call | flops 1811939328 | bytes 10223616 | tf_op jit(solution)/shard_map/pallas_call | solution.py:37
  20.5 1.0 copy-done.2
  21.5 1.1 %copy-done.7 = f32[768,512]{1,0:T(8,128)} copy-done((f32[768,512]{1,0:T(8,128)}, f32[768,512]{1,0:T(8,128)S(1)}, u32[]{:S(2)}) %copy-start.7) | copy-done | bytes 1572888
  24.8 9.7 %all-to-all-done.incoming_any = f32[16,104,128]{2,1,0:T(8,128)} async-done(((f32[16,104,128]{2,1,0:T(8,128)}), f32[16,104,128]{2,1,0:T(8,128)}, u32[]{:S(2)}, u32[]{:S(2)}) %all-to-all-start) | async-done | bytes 852000 | tf_op jit(solution)/shard_map/all_to_all | solution.py:452
  34.6 2.6 %shard_map.139 = f32[16,104,128]{2,1,0:T(8,128)S(1)} custom-call(f32[16,104,128]{2,1,0:T(8,128)} %all-to-all-done.incoming_any, f32[256,256]{1,0:T(8,128)} %bitcast.39, f32[1,512]{1,0:T(1,128)S(1)} %get-tuple-element.37.local_part_ref, f32[1,512]{1,0:T(1,128)S(1)} %get-tuple-element.38.square_ref), custom_call_target="tpu_custom_call" | custom-call | flops 603979776 | bytes 1572864 | tf_op jit(solution)/shard_map/pallas_call | solution.py:37
  37.2 26.4 %all_to_all.15.returned_ref = f32[16,104,128]{2,1,0:T(8,128)S(1)} all-to-all(f32[16,104,128]{2,1,0:T(8,128)S(1)} %shard_map.139), channel_id=1, replica_groups=mesh['blk'=4,'lat'=4,'depth'=2] {'blk','lat'}, dimensions={0} | all-to-all | bytes 1703936 | tf_op jit(solution)/shard_map/all_to_all | solution.py:452
  63.6 1.3 %shard_map.140 = (f32[768,512]{1,0:T(8,128)S(1)}, f32[8,128]{1,0:T(8,128)S(1)}, f32[128,512]{1,0:T(8,128)S(1)}, f32[128,512]{1,0:T(8,128)S(1)}, f32[128,512]{1,0...) custom-call(f32[16,104,128]{2,1,0:T(8,128)S(1)} %all_to_all.15.returned_ref, ...), custom_call_target="tpu_custom_call" | custom-call | flops 805306368 | bytes 6291456 | tf_op jit(solution)/shard_map/pallas_call | solution.py:37
  64.9 1.1 collective-permute-start
  67.0 2.8 %collective-permute-start.4 = (f32[128,512]{1,0:T(8,128)S(1)}, f32[128,512]{1,0:T(8,128)S(1)}, u32[]{:S(2)}, u32[]{:S(2)}) collective-permute-start(f32[128,512]{1,0:T(8,128)S(1)} %get-tuple-element.53), channel_id=1, source_target_pairs={{0,24},{8,0},{16,8},{24,16},{1,25},{9,1},{17,9},{25,17},{2,26},{10... | collective-permute-start | bytes 786440 | tf_op jit(solution)/shard_map/ppermute | solution.py:296
  70.5 5.1 %collective-permute-done.refs_0_ = f32[128,512]{1,0:T(8,128)S(1)} collective-permute-done((f32[128,512]{1,0:T(8,128)S(1)}, f32[128,512]{1,0:T(8,128)S(1)}, u32[]{:S(2)}, u32[]{:S(2)}) %collective-permute-start) | collective-permute-done | bytes 262176 | tf_op jit(solution)/shard_map/ppermute | solution.py:296
  75.7 2.6 %shard_map.141 = (f32[1,512]{1,0:T(1,128)}, f32[1,512]{1,0:T(1,128)S(1)}, f32[1,512]{1,0:T(1,128)S(1)}, f32[512,512]{1,0:T(8,128)S(1)}, f32[768,512]{1,0:T(8,128)S(1)}) custom-call(s32[6]{0:T(128)S(1)} %bitcast.27, f32[8,128]{1,0:T(8,128)S(1)} %get-tuple-element.43.sums_ref, f32[1,512]{1,0:T(1,128)S(1)} %bitcast.34, ...), custom_call_target="tpu_custom_call" | custom-call | flops 1207959552 | bytes 8650752 | tf_op jit(solution)/shard_map/pallas_call | solution.py:37
  78.2 1.5 %shard_map.142 = (f32[256,512]{1,0:T(8,128)S(1)}, f32[768,512]{1,0:T(8,128)S(1)}, f32[128,512]{1,0:T(8,128)S(1)}, f32[128,512]{1,0:T(8,128)S(1)}, f32[128,512]{1...) custom-call(s32[6]{0:T(128)S(1)} %bitcast.28, f32[1,512]{1,0:T(1,128)S(1)} %get-tuple-element.51.beta_ref, ...), custom_call_target="tpu_custom_call" | custom-call | flops 603979776 | bytes 8650752 | tf_op jit(solution)/shard_map/pallas_call | solution.py:37
  80.4 3.3 %collective-permute-start.7 = (f32[128,512]{1,0:T(8,128)S(1)}, f32[128,512]{1,0:T(8,128)S(1)}, u32[]{:S(2)}, u32[]{:S(2)}) collective-permute-start(f32[128,512]{1,0:T(8,128)S(1)} %get-tuple-element.58), channel_id=1, source_target_pairs={{0,2},{2,0},{4,6},{6,4},{1,3},{3,1},{5,7},{7,5},{8,10},{10,8},{12,... | collective-permute-start | bytes 786440 | tf_op jit(solution)/shard_map/ppermute | solution.py:296
  83.7 3.7 %collective-permute-start.8 = (f32[128,512]{1,0:T(8,128)S(1)}, f32[128,512]{1,0:T(8,128)S(1)}, u32[]{:S(2)}, u32[]{:S(2)}) collective-permute-start(f32[128,512]{1,0:T(8,128)S(1)} %get-tuple-element.59), channel_id=1, source_target_pairs={{0,24},{8,0},{16,8},{24,16},{1,25},{9,1},{17,9},{25,17},{2,26},{10... | collective-permute-start | bytes 786440 | tf_op jit(solution)/shard_map/ppermute | solution.py:296
  88.2 2.7 %collective-permute-done.6.arrived.refs_0_ = f32[128,512]{1,0:T(8,128)S(1)} collective-permute-done((f32[128,512]{1,0:T(8,128)S(1)}, f32[128,512]{1,0:T(8,128)S(1)}, u32[]{:S(2)}, u32[]{:S(2)}) %collective-permute-start.6) | collective-permute-done | bytes 262176 | tf_op jit(solution)/shard_map/ppermute | solution.py:296
  90.9 1.3 %shard_map.144.refs_5_ = f32[8,128]{1,0:T(8,128)S(1)} custom-call(s32[6]{0:T(128)S(1)} %bitcast.29, f32[512,512]{1,0:T(8,128)S(1)} %get-tuple-element.50.near_ref, f32[256,512]{1,0:T(8,128)S(1)} %get-tuple-element.55.far_ref, f32[768,512]{1,0:T(8,128)S(1)} %get-tuple-element.56.schur_ref, f32[768,512]{1,0:T(8,128)S(1)} %bitcast.17, ...), custom_call_target="tpu_custom_call" | custom-call | flops 1572864 | bytes 4718592 | tf_op jit(solution)/shard_map/pallas_call | solution.py:37
  92.3 1.2 %shard_map.143.stored = f32[768,512]{1,0:T(8,128)} custom-call(f32[512,512]{1,0:T(8,128)S(1)} %get-tuple-element.50.near_ref, f32[256,512]{1,0:T(8,128)S(1)} %get-tuple-element.55.far_ref), custom_call_target="tpu_custom_call" | custom-call | bytes 3145728 | tf_op jit(solution)/shard_map/pallas_call | solution.py:37
  93.5 1.2 %collective-permute-done.8.refs_2_ = f32[128,512]{1,0:T(8,128)S(1)} collective-permute-done((f32[128,512]{1,0:T(8,128)S(1)}, f32[128,512]{1,0:T(8,128)S(1)}, u32[]{:S(2)}, u32[]{:S(2)}) %collective-permute-start.8) | collective-permute-done | bytes 262176 | tf_op jit(solution)/shard_map/ppermute | solution.py:296
  95.5 12.7 %all_to_all.16.sums_ref = f32[32,2,4,128]{3,2,1,0:T(4,128)S(1)} all-to-all(f32[32,2,4,128]{3,2,1,0:T(4,128)S(1)} %get-tuple-element.62), channel_id=1, replica_groups=mesh['blk'=4,'lat'=4,'depth'=2] {'blk','lat','depth'}, dimensions={0} | all-to-all | bytes 262144 | tf_op jit(solution)/shard_map/all_to_all | solution.py:452
  108.2 2.4 %shard_map.146 = (f32[768,512]{1,0:T(8,128)}, f32[1,512]{1,0:T(1,128)}, f32[1,512]{1,0:T(1,128)}) custom-call(s32[6]{0:T(128)S(1)} %bitcast.31, f32[32,2,4,128]{3,2,1,0:T(4,128)S(1)} %all_to_all.16.sums_ref, f32[1,512]{1,0:T(1,128)S(1)} %copy-done.18, f32[1,512]{1,0:T(1,128)S(1)} %get-tuple-element.64.square_ref, f32[768,512]{1,0:T(8,128)S(1)} %bitcast.18, ...), custom_call_target="tpu_custom_call" | custom-call | flops 1572864 | bytes 4718592 | tf_op jit(solution)/shard_map/pallas_call | solution.py:37
  (52 shorter events, 6.3 us)
Async XLA Ops:
  0.6 13.0 %copy-start.4 = (f32[1,1,1,768,256]{4,3,2,1,0:T(8,128)S(1)}, f32[1,1,1,768,256]{4,3,2,1,0:T(8,128)}, u32[]{:S(2)}) copy-start(f32[1,1,1,768,256]{4,3,2,1,0:T(8,128)} %param.16) | copy-start | bytes 2359300
  5.1 8.6 %copy-start = (f32[1,1,1,768,512]{4,3,2,1,0:T(8,128)S(1)}, f32[1,1,1,768,512]{4,3,2,1,0:T(8,128)}, u32[]{:S(2)}) copy-start(f32[1,1,1,768,512]{4,3,2,1,0:T(8,128)} %param.11) | copy-start | bytes 4718596
  5.1 8.6 %copy-start.15 = (s32[1,1,1,6]{3,2,1,0:T(1,128)S(1)}, s32[1,1,1,6]{3,2,1,0:T(1,128)}, u32[]{:S(2)}) copy-start(s32[1,1,1,6]{3,2,1,0:T(1,128)} %param.10) | copy-start | bytes 76
  5.1 29.5 %all-to-all-start = ((f32[16,104,128]{2,1,0:T(8,128)}), f32[16,104,128]{2,1,0:T(8,128)}, u32[]{:S(2)}, u32[]{:S(2)}) async-start(f32[16,104,128]{2,1,0:T(8,128)} %shard_map.137), calls=%async_computation | async-start | bytes 1703936 | tf_op jit(solution)/shard_map/all_to_all | solution.py:452
  34.6 29.0 %copy-start.8 = (f32[768,512]{1,0:T(8,128)S(1)}, f32[768,512]{1,0:T(8,128)}, u32[]{:S(2)}) copy-start(f32[768,512]{1,0:T(8,128)} %copy-done.7) | copy-start | bytes 4718596
  34.6 29.0 %copy-start.10 = (bf16[768,256]{1,0:T(8,128)(2,1)S(1)}, bf16[768,256]{1,0:T(8,128)(2,1)}, u32[]{:S(2)}) copy-start(bf16[768,256]{1,0:T(8,128)(2,1)} %copy-done.9) | copy-start | bytes 1179652
  34.6 29.0 %copy-start.12 = (bf16[768,256]{1,0:T(8,128)(2,1)S(1)}, bf16[768,256]{1,0:T(8,128)(2,1)}, u32[]{:S(2)}) copy-start(bf16[768,256]{1,0:T(8,128)(2,1)} %copy-done.11) | copy-start | bytes 1179652
  34.6 29.0 %copy-start.14 = (bf16[256,384]{1,0:T(8,128)(2,1)S(1)}, bf16[256,384]{1,0:T(8,128)(2,1)}, u32[]{:S(2)}) copy-start(bf16[256,384]{1,0:T(8,128)(2,1)} %copy-done.13) | copy-start | bytes 589828
  63.6 12.1 %copy-start.1 = (f32[1,1,1,768,512]{4,3,2,1,0:T(8,128)S(1)}, f32[1,1,1,768,512]{4,3,2,1,0:T(8,128)}, u32[]{:S(2)}) copy-start(f32[1,1,1,768,512]{4,3,2,1,0:T(8,128)} %param.12) | copy-start | bytes 4718596
  63.6 12.1 %copy-start.3 = (bf16[768,768]{1,0:T(8,128)(2,1)S(1)}, bf16[768,768]{1,0:T(8,128)(2,1)}, u32[]{:S(2)}) copy-start(bf16[768,768]{1,0:T(8,128)(2,1)} %copy-done.2) | copy-start | bytes 3538948
  63.6 12.1 %copy-start.17 = (f32[512]{0:T(512)S(1)}, f32[512]{0:T(512)}, u32[]{:S(2)}) copy-start(f32[512]{0:T(512)} %param.13) | copy-start | bytes 6148
  64.9 10.7 %collective-permute-start = (f32[128,512]{1,0:T(8,128)S(1)}, f32[128,512]{1,0:T(8,128)S(1)}, u32[]{:S(2)}, u32[]{:S(2)}) collective-permute-start(f32[128,512]{1,0:T(8,128)S(1)} %get-tuple-element.47), channel_id=1, source_target_pairs={{0,8},{8,16},{16,24},{24,0},{1,9},{9,17},{17,25},{25,1},{2,10},{10... | collective-permute-start | bytes 786440 | tf_op jit(solution)/shard_map/ppermute | solution.py:296
  66.0 9.7 %collective-permute-start.1 = (f32[128,512]{1,0:T(8,128)S(1)}, f32[128,512]{1,0:T(8,128)S(1)}, u32[]{:S(2)}, u32[]{:S(2)}) collective-permute-start(f32[128,512]{1,0:T(8,128)S(1)} %get-tuple-element.48), channel_id=1, source_target_pairs={{0,2},{2,0},{4,6},{6,4},{1,3},{3,1},{5,7},{7,5},{8,10},{10,8},{12,... | collective-permute-start | bytes 786440 | tf_op jit(solution)/shard_map/ppermute | solution.py:296
  66.5 9.1 %collective-permute-start.2 = (f32[128,512]{1,0:T(8,128)S(1)}, f32[128,512]{1,0:T(8,128)S(1)}, u32[]{:S(2)}, u32[]{:S(2)}) collective-permute-start(f32[128,512]{1,0:T(8,128)S(1)} %get-tuple-element.49), channel_id=1, source_target_pairs={{0,1},{1,0},{2,3},{3,2},{4,5},{5,4},{6,7},{7,6},{8,9},{9,8},{10,11... | collective-permute-start | bytes 786440 | tf_op jit(solution)/shard_map/ppermute | solution.py:296
  66.5 3.3 %collective-permute-start.3 = (f32[8,128]{1,0:T(8,128)S(1)}, f32[8,128]{1,0:T(8,128)S(1)}, u32[]{:S(2)}, u32[]{:S(2)}) collective-permute-start(f32[8,128]{1,0:T(8,128)S(1)} %get-tuple-element.43.sums_ref), channel_id=1, source_target_pairs={{0,1},{1,0},{2,3},{3,2},{4,5},{5,4},{6,7},{7,6},{8,9},{9,8},{10,11... | collective-permute-start | bytes 12296 | tf_op jit(solution)/shard_map/ppermute | solution.py:549
  67.0 11.2 %collective-permute-start.4 = (f32[128,512]{1,0:T(8,128)S(1)}, f32[128,512]{1,0:T(8,128)S(1)}, u32[]{:S(2)}, u32[]{:S(2)}) collective-permute-start(f32[128,512]{1,0:T(8,128)S(1)} %get-tuple-element.53), channel_id=1, source_target_pairs={{0,24},{8,0},{16,8},{24,16},{1,25},{9,1},{17,9},{25,17},{2,26},{10... | collective-permute-start | bytes 786440 | tf_op jit(solution)/shard_map/ppermute | solution.py:296
  69.9 8.4 %collective-permute-start.5 = (f32[128,512]{1,0:T(8,128)S(1)}, f32[128,512]{1,0:T(8,128)S(1)}, u32[]{:S(2)}, u32[]{:S(2)}) collective-permute-start(f32[128,512]{1,0:T(8,128)S(1)} %get-tuple-element.54), channel_id=1, source_target_pairs={{2,4},{4,2},{3,5},{5,3},{10,12},{12,10},{11,13},{13,11},{18,20},{2... | collective-permute-start | bytes 786440 | tf_op jit(solution)/shard_map/ppermute | solution.py:296
  79.8 11.1 %collective-permute-start.6 = (f32[128,512]{1,0:T(8,128)S(1)}, f32[128,512]{1,0:T(8,128)S(1)}, u32[]{:S(2)}, u32[]{:S(2)}) collective-permute-start(f32[128,512]{1,0:T(8,128)S(1)} %get-tuple-element.57), channel_id=1, source_target_pairs={{0,8},{8,16},{16,24},{24,0},{1,9},{9,17},{17,25},{25,1},{2,10},{10... | collective-permute-start | bytes 786440 | tf_op jit(solution)/shard_map/ppermute | solution.py:296
  80.4 13.1 %collective-permute-start.7 = (f32[128,512]{1,0:T(8,128)S(1)}, f32[128,512]{1,0:T(8,128)S(1)}, u32[]{:S(2)}, u32[]{:S(2)}) collective-permute-start(f32[128,512]{1,0:T(8,128)S(1)} %get-tuple-element.58), channel_id=1, source_target_pairs={{0,2},{2,0},{4,6},{6,4},{1,3},{3,1},{5,7},{7,5},{8,10},{10,8},{12,... | collective-permute-start | bytes 786440 | tf_op jit(solution)/shard_map/ppermute | solution.py:296
  83.7 11.0 %collective-permute-start.8 = (f32[128,512]{1,0:T(8,128)S(1)}, f32[128,512]{1,0:T(8,128)S(1)}, u32[]{:S(2)}, u32[]{:S(2)}) collective-permute-start(f32[128,512]{1,0:T(8,128)S(1)} %get-tuple-element.59), channel_id=1, source_target_pairs={{0,24},{8,0},{16,8},{24,16},{1,25},{9,1},{17,9},{25,17},{2,26},{10... | collective-permute-start | bytes 786440 | tf_op jit(solution)/shard_map/ppermute | solution.py:296
  87.5 7.2 %collective-permute-start.9 = (f32[128,512]{1,0:T(8,128)S(1)}, f32[128,512]{1,0:T(8,128)S(1)}, u32[]{:S(2)}, u32[]{:S(2)}) collective-permute-start(f32[128,512]{1,0:T(8,128)S(1)} %get-tuple-element.60), channel_id=1, source_target_pairs={{2,4},{4,2},{3,5},{5,3},{10,12},{12,10},{11,13},{13,11},{18,20},{2... | collective-permute-start | bytes 786440 | tf_op jit(solution)/shard_map/ppermute | solution.py:296
  88.1 6.6 %collective-permute-start.10 = (f32[128,512]{1,0:T(8,128)S(1)}, f32[128,512]{1,0:T(8,128)S(1)}, u32[]{:S(2)}, u32[]{:S(2)}) collective-permute-start(f32[128,512]{1,0:T(8,128)S(1)} %get-tuple-element.61), channel_id=1, source_target_pairs={{0,1},{1,0},{2,3},{3,2},{4,5},{5,4},{6,7},{7,6},{8,9},{9,8},{10,11... | collective-permute-start | bytes 786440 | tf_op jit(solution)/shard_map/ppermute | solution.py:296
  92.2 2.5 %collective-permute-start.11 = (f32[8,128]{1,0:T(8,128)S(1)}, f32[8,128]{1,0:T(8,128)S(1)}, u32[]{:S(2)}, u32[]{:S(2)}) collective-permute-start(f32[8,128]{1,0:T(8,128)S(1)} %shard_map.144.refs_5_), channel_id=1, source_target_pairs={{0,1},{1,0},{2,3},{3,2},{4,5},{5,4},{6,7},{7,6},{8,9},{9,8},{10,11... | collective-permute-start | bytes 12296 | tf_op jit(solution)/shard_map/ppermute | solution.py:584
  93.5 14.8 %copy-start.18 = (f32[1,512]{1,0:T(1,128)S(1)}, f32[1,512]{1,0:T(1,128)}, u32[]{:S(2)}) copy-start(f32[1,512]{1,0:T(1,128)} %get-tuple-element.63.rho_ref) | copy-start | bytes 6148
  (8 other events, 16.2 us)

commit v11 on v10

--- a/solution.py
+++ b/solution.py
@@ -9,7 +9,7 @@
 
 CAP = 24
 AXES = ("blk", "lat", "depth")
-LAYER = ("blk", "lat")
+LAYER = ("lat", "blk")
 LANES = 128
 TILE = 8
 f32 = jnp.float32
@@ -116,6 +116,12 @@
     spare = [jnp.zeros_like(rows[0])] * (TILE - len(rows))
     turned = jnp.transpose(jnp.concatenate([*rows, *spare], axis=0))
     return [turned[:, i : i + 1] for i in range(len(rows))]
+
+
+def position(owner):
+    lats = lax.axis_size("lat")
+    blk = jnp.floor((owner.astype(f32) + 0.5) * (1.0 / lats))
+    return (owner.astype(f32) - lats * blk) * lax.axis_size("blk") + blk
 
 
 def ranks(own_row):
@@ -155,13 +161,15 @@
             copy.start()
     for copy in small:
         copy.wait()
-    own_row = owner_ref[...].astype(f32)
+    own_row = position(owner_ref[...])
     wanted_row = row_ref[...].astype(f32) + 1.0
     rank_row, _ = ranks(own_row)
     slot_row = (own_row * CAP + rank_row).astype(jnp.int32)
     rank_col, wanted_col = columns(rank_row, wanted_row)
     packer = one_hot(lax.broadcasted_iota(jnp.int32, (slots, primal), 0) == slot_row)
-    to_owner = one_hot(lax.broadcasted_iota(jnp.int32, (owners, primal), 0) == owner_ref[...])
+    to_owner = one_hot(
+        lax.broadcasted_iota(jnp.int32, (owners, primal), 0) == own_row.astype(jnp.int32)
+    )
     at_owner = lax.axis_index(LAYER) * CAP + rank_col.astype(jnp.int32)
     place = lax.broadcasted_iota(jnp.int32, (primal, id_rows(slots) * LANES), 1)
     names = select(to_owner, jnp.where(place == at_owner, wanted_col, 0.0))
@@ -201,7 +209,7 @@
         at = slice(i * rows, (i + 1) * rows)
         refs[2][:, at], refs[3][:, at] = parts(whole[1][:, rows_of(served(*move), rows)])
     primal, slots = table_ref.shape
-    rank_row, own_col = ranks(owner_ref[...].astype(f32))
+    rank_row, own_col = ranks(position(owner_ref[...]))
     (rank_col,) = columns(rank_row)
     slot_col = (own_col * CAP + rank_col).astype(jnp.int32)
     table_ref[...] = one_hot(lax.broadcasted_iota(jnp.int32, (primal, slots), 1) == slot_col)

time: 111 us -> 113 us (1.018)
  waiting for transfers between devices: 18.8 us -> 24.2 us
  starting transfers between devices: 22.6 us -> 20.9 us
  blocking collectives: 39 us -> 37.6 us
    ppermute x10, waiting for transfers between devices: 9.02 us -> 12.1 us  [exchange(): lax.ppermute(block, axis, route(axis, way))]
    all_to_all x1, waiting for transfers between devices: 9.73 us -> 12.1 us  [to_all(): return lax.all_to_all(x, axes, split_axis=0, concat_axis=0, tiled=True)]
    ppermute x10, starting transfers between devices: 13.5 us -> 11.8 us  [exchange(): lax.ppermute(block, axis, route(axis, way))]
    all_to_all x2, blocking collectives: 39 us -> 37.6 us  [to_all(): return lax.all_to_all(x, axes, split_axis=0, concat_axis=0, tiled=True)]
  transfers between devices with their start and end apart: 13 -> 13, of which waited for: 4 -> 5; matrix products, arithmetic and copies ran while one was open for 0% -> 0% of each run, Pallas kernels for 8% -> 8%
where the time goes in v11:
time: 113 us
  blocking collectives  37.6 us (33%)
  waiting for transfers between devices  24.2 us (21%)
  Pallas kernels  21.6 us (19%)
  starting transfers between devices  20.9 us (18%)
  local copies, waits for them, and re-layouts  7.73 us (7%)
    all_to_all x2, blocking collectives, to_all(): return lax.all_to_all(x, axes, split_axis=0, concat_axis=0, tiled=True)  37.6 us
    pallas_call x10, Pallas kernels, call(): pl.pallas_call(body, out_shape=list(outs), in_specs=in_specs, out_specs=o...  21.6 us
    ppermute x10, waiting for transfers between devices, exchange(): lax.ppermute(block, axis, route(axis, way))  12.1 us
    all_to_all x1, waiting for transfers between devices, to_all(): return lax.all_to_all(x, axes, split_axis=0, concat_axis=0, tiled=True)  12.1 us
    ppermute x10, starting transfers between devices, exchange(): lax.ppermute(block, axis, route(axis, way))  11.8 us
    all_to_all x1, starting transfers between devices, to_all(): return lax.all_to_all(x, axes, split_axis=0, concat_axis=0, tiled=True)  8.5 us
    unnamed x38, local copies, waits for them, and re-layouts  7.73 us
  transfers between devices with their start and end apart: 13, of which 5 were waited for; matrix products, arithmetic and copies ran while one was open for 0% of the time, Pallas kernels for 8%

profile of v11, /device:TPU:0, one launch (start us, length us, event | category | flops | bytes accessed | tf_op | source)
XLA Modules:
  0.0 112.9 jit_solution(9040652586416002741)
XLA Ops:
  0.6 4.4 %shard_map.137 = f32[16,104,128]{2,1,0:T(8,128)} custom-call(s32[6]{0:T(128)} %bitcast.25, s32[1,256]{1,0:T(1,128)} %bitcast.32, s32[1,256]{1,0:T(1,128)} %bitcast.37, f32[768,512]{1,0:T(8,128)} %bitcast.15, f32[768,256]{1,0:T(8,128)} %bitcast.21), custom_call_target="tpu_custom_call" | custom-call | flops 603979776 | bytes 3145728 | tf_op jit(solution)/shard_map/pallas_call | solution.py:37
  5.1 8.5 %all-to-all-start = ((f32[16,104,128]{2,1,0:T(8,128)}), f32[16,104,128]{2,1,0:T(8,128)}, u32[]{:S(2)}, u32[]{:S(2)}) async-start(f32[16,104,128]{2,1,0:T(8,128)} %shard_map.137), calls=%async_computation | async-start | bytes 1703936 | tf_op jit(solution)/shard_map/all_to_all | solution.py:460
  13.7 1.7 %copy-done.5 = f32[1,1,1,768,768]{4,3,2,1,0:T(8,128)S(1)} copy-done((f32[1,1,1,768,768]{4,3,2,1,0:T(8,128)S(1)}, f32[1,1,1,768,768]{4,3,2,1,0:T(8,128)}, u32[]{:S(2)}) %copy-start.5) | copy-done | bytes 2359320
  15.3 1.7 %copy-done.6 = f32[1,1,1,768,768]{4,3,2,1,0:T(8,128)S(1)} copy-done((f32[1,1,1,768,768]{4,3,2,1,0:T(8,128)S(1)}, f32[1,1,1,768,768]{4,3,2,1,0:T(8,128)}, u32[]{:S(2)}) %copy-start.6) | copy-done | bytes 2359320
  17.0 3.5 %shard_map.138 = (f32[768,512]{1,0:T(8,128)S(1)}, f32[1,512]{1,0:T(1,128)S(1)}, f32[1,512]{1,0:T(1,128)S(1)}, bf16[256,384]{1,0:T(8,128)(2,1)S(1)}, bf16[768,256...) custom-call(s32[6]{0:T(128)S(1)} %bitcast.26, ...), custom_call_target="tpu_custom_call" | custom-call | flops 1811939328 | bytes 10223616 | tf_op jit(solution)/shard_map/pallas_call | solution.py:37
  20.5 1.0 copy-done.2
  21.5 1.1 %copy-done.7 = f32[768,512]{1,0:T(8,128)} copy-done((f32[768,512]{1,0:T(8,128)}, f32[768,512]{1,0:T(8,128)S(1)}, u32[]{:S(2)}) %copy-start.7) | copy-done | bytes 1572888
  24.8 12.1 %all-to-all-done.incoming_any = f32[16,104,128]{2,1,0:T(8,128)} async-done(((f32[16,104,128]{2,1,0:T(8,128)}), f32[16,104,128]{2,1,0:T(8,128)}, u32[]{:S(2)}, u32[]{:S(2)}) %all-to-all-start) | async-done | bytes 852000 | tf_op jit(solution)/shard_map/all_to_all | solution.py:460
  37.0 2.6 %shard_map.139 = f32[16,104,128]{2,1,0:T(8,128)S(1)} custom-call(f32[16,104,128]{2,1,0:T(8,128)} %all-to-all-done.incoming_any, f32[256,256]{1,0:T(8,128)} %bitcast.39, f32[1,512]{1,0:T(1,128)S(1)} %get-tuple-element.37.local_part_ref, f32[1,512]{1,0:T(1,128)S(1)} %get-tuple-element.38.square_ref), custom_call_target="tpu_custom_call" | custom-call | flops 603979776 | bytes 1572864 | tf_op jit(solution)/shard_map/pallas_call | solution.py:37
  39.6 26.0 %all_to_all.15.returned_ref = f32[16,104,128]{2,1,0:T(8,128)S(1)} all-to-all(f32[16,104,128]{2,1,0:T(8,128)S(1)} %shard_map.139), channel_id=1, replica_groups=mesh['blk'=4,'lat'=4,'depth'=2] {'lat','blk'}, dimensions={0} | all-to-all | bytes 1703936 | tf_op jit(solution)/shard_map/all_to_all | solution.py:460
  65.7 1.3 %shard_map.140 = (f32[768,512]{1,0:T(8,128)S(1)}, f32[8,128]{1,0:T(8,128)S(1)}, f32[128,512]{1,0:T(8,128)S(1)}, f32[128,512]{1,0:T(8,128)S(1)}, f32[128,512]{1,0...) custom-call(f32[16,104,128]{2,1,0:T(8,128)S(1)} %all_to_all.15.returned_ref, ...), custom_call_target="tpu_custom_call" | custom-call | flops 805306368 | bytes 6291456 | tf_op jit(solution)/shard_map/pallas_call | solution.py:37
  68.2 3.1 %collective-permute-start.4 = (f32[128,512]{1,0:T(8,128)S(1)}, f32[128,512]{1,0:T(8,128)S(1)}, u32[]{:S(2)}, u32[]{:S(2)}) collective-permute-start(f32[128,512]{1,0:T(8,128)S(1)} %get-tuple-element.53), channel_id=1, source_target_pairs={{0,24},{8,0},{16,8},{24,16},{1,25},{9,1},{17,9},{25,17},{2,26},{10... | collective-permute-start | bytes 786440 | tf_op jit(solution)/shard_map/ppermute | solution.py:304
  72.0 6.1 %collective-permute-done.refs_0_ = f32[128,512]{1,0:T(8,128)S(1)} collective-permute-done((f32[128,512]{1,0:T(8,128)S(1)}, f32[128,512]{1,0:T(8,128)S(1)}, u32[]{:S(2)}, u32[]{:S(2)}) %collective-permute-start) | collective-permute-done | bytes 262176 | tf_op jit(solution)/shard_map/ppermute | solution.py:304
  78.1 2.6 %shard_map.141 = (f32[1,512]{1,0:T(1,128)}, f32[1,512]{1,0:T(1,128)S(1)}, f32[1,512]{1,0:T(1,128)S(1)}, f32[512,512]{1,0:T(8,128)S(1)}, f32[768,512]{1,0:T(8,128)S(1)}) custom-call(s32[6]{0:T(128)S(1)} %bitcast.27, f32[8,128]{1,0:T(8,128)S(1)} %get-tuple-element.43.sums_ref, f32[1,512]{1,0:T(1,128)S(1)} %bitcast.34, ...), custom_call_target="tpu_custom_call" | custom-call | flops 1207959552 | bytes 8650752 | tf_op jit(solution)/shard_map/pallas_call | solution.py:37
  81.4 1.5 %shard_map.142 = (f32[256,512]{1,0:T(8,128)S(1)}, f32[768,512]{1,0:T(8,128)S(1)}, f32[128,512]{1,0:T(8,128)S(1)}, f32[128,512]{1,0:T(8,128)S(1)}, f32[128,512]{1...) custom-call(s32[6]{0:T(128)S(1)} %bitcast.28, f32[1,512]{1,0:T(1,128)S(1)} %get-tuple-element.51.beta_ref, ...), custom_call_target="tpu_custom_call" | custom-call | flops 603979776 | bytes 8650752 | tf_op jit(solution)/shard_map/pallas_call | solution.py:37
  83.6 2.2 %collective-permute-start.7 = (f32[128,512]{1,0:T(8,128)S(1)}, f32[128,512]{1,0:T(8,128)S(1)}, u32[]{:S(2)}, u32[]{:S(2)}) collective-permute-start(f32[128,512]{1,0:T(8,128)S(1)} %get-tuple-element.58), channel_id=1, source_target_pairs={{0,2},{2,0},{4,6},{6,4},{1,3},{3,1},{5,7},{7,5},{8,10},{10,8},{12,... | collective-permute-start | bytes 786440 | tf_op jit(solution)/shard_map/ppermute | solution.py:304
  85.8 3.7 %collective-permute-start.8 = (f32[128,512]{1,0:T(8,128)S(1)}, f32[128,512]{1,0:T(8,128)S(1)}, u32[]{:S(2)}, u32[]{:S(2)}) collective-permute-start(f32[128,512]{1,0:T(8,128)S(1)} %get-tuple-element.59), channel_id=1, source_target_pairs={{0,24},{8,0},{16,8},{24,16},{1,25},{9,1},{17,9},{25,17},{2,26},{10... | collective-permute-start | bytes 786440 | tf_op jit(solution)/shard_map/ppermute | solution.py:304
  90.3 3.8 %collective-permute-done.6.arrived.refs_0_ = f32[128,512]{1,0:T(8,128)S(1)} collective-permute-done((f32[128,512]{1,0:T(8,128)S(1)}, f32[128,512]{1,0:T(8,128)S(1)}, u32[]{:S(2)}, u32[]{:S(2)}) %collective-permute-start.6) | collective-permute-done | bytes 262176 | tf_op jit(solution)/shard_map/ppermute | solution.py:304
  94.0 1.3 %shard_map.144.refs_5_ = f32[8,128]{1,0:T(8,128)S(1)} custom-call(s32[6]{0:T(128)S(1)} %bitcast.29, f32[512,512]{1,0:T(8,128)S(1)} %get-tuple-element.50.near_ref, f32[256,512]{1,0:T(8,128)S(1)} %get-tuple-element.55.far_ref, f32[768,512]{1,0:T(8,128)S(1)} %get-tuple-element.56.schur_ref, f32[768,512]{1,0:T(8,128)S(1)} %bitcast.17, ...), custom_call_target="tpu_custom_call" | custom-call | flops 1572864 | bytes 4718592 | tf_op jit(solution)/shard_map/pallas_call | solution.py:37
  95.4 1.2 %shard_map.143.stored = f32[768,512]{1,0:T(8,128)} custom-call(f32[512,512]{1,0:T(8,128)S(1)} %get-tuple-element.50.near_ref, f32[256,512]{1,0:T(8,128)S(1)} %get-tuple-element.55.far_ref), custom_call_target="tpu_custom_call" | custom-call | bytes 3145728 | tf_op jit(solution)/shard_map/pallas_call | solution.py:37
  96.6 1.5 %collective-permute-done.8.refs_2_ = f32[128,512]{1,0:T(8,128)S(1)} collective-permute-done((f32[128,512]{1,0:T(8,128)S(1)}, f32[128,512]{1,0:T(8,128)S(1)}, u32[]{:S(2)}, u32[]{:S(2)}) %collective-permute-start.8) | collective-permute-done | bytes 262176 | tf_op jit(solution)/shard_map/ppermute | solution.py:304
  98.2 0.8 shard_map.145
  99.0 11.6 %all_to_all.16.sums_ref = f32[32,2,4,128]{3,2,1,0:T(4,128)S(1)} all-to-all(f32[32,2,4,128]{3,2,1,0:T(4,128)S(1)} %get-tuple-element.62), channel_id=1, replica_groups=mesh['blk'=4,'lat'=4,'depth'=2] {'blk','lat','depth'}, dimensions={0} | all-to-all | bytes 262144 | tf_op jit(solution)/shard_map/all_to_all | solution.py:460
  110.6 2.4 %shard_map.146 = (f32[768,512]{1,0:T(8,128)}, f32[1,512]{1,0:T(1,128)}, f32[1,512]{1,0:T(1,128)}) custom-call(s32[6]{0:T(128)S(1)} %bitcast.31, f32[32,2,4,128]{3,2,1,0:T(4,128)S(1)} %all_to_all.16.sums_ref, f32[1,512]{1,0:T(1,128)S(1)} %copy-done.18, f32[1,512]{1,0:T(1,128)S(1)} %get-tuple-element.64.square_ref, f32[768,512]{1,0:T(8,128)S(1)} %bitcast.18, ...), custom_call_target="tpu_custom_call" | custom-call | flops 1572864 | bytes 4718592 | tf_op jit(solution)/shard_map/pallas_call | solution.py:37
  (52 shorter events, 6.3 us)
Async XLA Ops:
  0.6 13.0 %copy-start.4 = (f32[1,1,1,768,256]{4,3,2,1,0:T(8,128)S(1)}, f32[1,1,1,768,256]{4,3,2,1,0:T(8,128)}, u32[]{:S(2)}) copy-start(f32[1,1,1,768,256]{4,3,2,1,0:T(8,128)} %param.16) | copy-start | bytes 2359300
  5.1 8.6 %copy-start = (f32[1,1,1,768,512]{4,3,2,1,0:T(8,128)S(1)}, f32[1,1,1,768,512]{4,3,2,1,0:T(8,128)}, u32[]{:S(2)}) copy-start(f32[1,1,1,768,512]{4,3,2,1,0:T(8,128)} %param.11) | copy-start | bytes 4718596
  5.1 8.6 %copy-start.15 = (s32[1,1,1,6]{3,2,1,0:T(1,128)S(1)}, s32[1,1,1,6]{3,2,1,0:T(1,128)}, u32[]{:S(2)}) copy-start(s32[1,1,1,6]{3,2,1,0:T(1,128)} %param.10) | copy-start | bytes 76
  5.1 31.8 %all-to-all-start = ((f32[16,104,128]{2,1,0:T(8,128)}), f32[16,104,128]{2,1,0:T(8,128)}, u32[]{:S(2)}, u32[]{:S(2)}) async-start(f32[16,104,128]{2,1,0:T(8,128)} %shard_map.137), calls=%async_computation | async-start | bytes 1703936 | tf_op jit(solution)/shard_map/all_to_all | solution.py:460
  36.9 28.7 %copy-start.8 = (f32[768,512]{1,0:T(8,128)S(1)}, f32[768,512]{1,0:T(8,128)}, u32[]{:S(2)}) copy-start(f32[768,512]{1,0:T(8,128)} %copy-done.7) | copy-start | bytes 4718596
  36.9 28.7 %copy-start.10 = (bf16[768,256]{1,0:T(8,128)(2,1)S(1)}, bf16[768,256]{1,0:T(8,128)(2,1)}, u32[]{:S(2)}) copy-start(bf16[768,256]{1,0:T(8,128)(2,1)} %copy-done.9) | copy-start | bytes 1179652
  36.9 28.7 %copy-start.12 = (bf16[768,256]{1,0:T(8,128)(2,1)S(1)}, bf16[768,256]{1,0:T(8,128)(2,1)}, u32[]{:S(2)}) copy-start(bf16[768,256]{1,0:T(8,128)(2,1)} %copy-done.11) | copy-start | bytes 1179652
  37.0 28.7 %copy-start.14 = (bf16[256,384]{1,0:T(8,128)(2,1)S(1)}, bf16[256,384]{1,0:T(8,128)(2,1)}, u32[]{:S(2)}) copy-start(bf16[256,384]{1,0:T(8,128)(2,1)} %copy-done.13) | copy-start | bytes 589828
  65.6 12.5 %copy-start.1 = (f32[1,1,1,768,512]{4,3,2,1,0:T(8,128)S(1)}, f32[1,1,1,768,512]{4,3,2,1,0:T(8,128)}, u32[]{:S(2)}) copy-start(f32[1,1,1,768,512]{4,3,2,1,0:T(8,128)} %param.12) | copy-start | bytes 4718596
  65.7 12.5 %copy-start.3 = (bf16[768,768]{1,0:T(8,128)(2,1)S(1)}, bf16[768,768]{1,0:T(8,128)(2,1)}, u32[]{:S(2)}) copy-start(bf16[768,768]{1,0:T(8,128)(2,1)} %copy-done.2) | copy-start | bytes 3538948
  65.7 12.5 %copy-start.17 = (f32[512]{0:T(512)S(1)}, f32[512]{0:T(512)}, u32[]{:S(2)}) copy-start(f32[512]{0:T(512)} %param.13) | copy-start | bytes 6148
  67.0 11.1 %collective-permute-start = (f32[128,512]{1,0:T(8,128)S(1)}, f32[128,512]{1,0:T(8,128)S(1)}, u32[]{:S(2)}, u32[]{:S(2)}) collective-permute-start(f32[128,512]{1,0:T(8,128)S(1)} %get-tuple-element.47), channel_id=1, source_target_pairs={{0,8},{8,16},{16,24},{24,0},{1,9},{9,17},{17,25},{25,1},{2,10},{10... | collective-permute-start | bytes 786440 | tf_op jit(solution)/shard_map/ppermute | solution.py:304
  67.0 11.1 %collective-permute-start.1 = (f32[128,512]{1,0:T(8,128)S(1)}, f32[128,512]{1,0:T(8,128)S(1)}, u32[]{:S(2)}, u32[]{:S(2)}) collective-permute-start(f32[128,512]{1,0:T(8,128)S(1)} %get-tuple-element.48), channel_id=1, source_target_pairs={{0,2},{2,0},{4,6},{6,4},{1,3},{3,1},{5,7},{7,5},{8,10},{10,8},{12,... | collective-permute-start | bytes 786440 | tf_op jit(solution)/shard_map/ppermute | solution.py:304
  67.7 10.4 %collective-permute-start.2 = (f32[128,512]{1,0:T(8,128)S(1)}, f32[128,512]{1,0:T(8,128)S(1)}, u32[]{:S(2)}, u32[]{:S(2)}) collective-permute-start(f32[128,512]{1,0:T(8,128)S(1)} %get-tuple-element.49), channel_id=1, source_target_pairs={{0,1},{1,0},{2,3},{3,2},{4,5},{5,4},{6,7},{7,6},{8,9},{9,8},{10,11... | collective-permute-start | bytes 786440 | tf_op jit(solution)/shard_map/ppermute | solution.py:304
  67.7 3.7 %collective-permute-start.3 = (f32[8,128]{1,0:T(8,128)S(1)}, f32[8,128]{1,0:T(8,128)S(1)}, u32[]{:S(2)}, u32[]{:S(2)}) collective-permute-start(f32[8,128]{1,0:T(8,128)S(1)} %get-tuple-element.43.sums_ref), channel_id=1, source_target_pairs={{0,1},{1,0},{2,3},{3,2},{4,5},{5,4},{6,7},{7,6},{8,9},{9,8},{10,11... | collective-permute-start | bytes 12296 | tf_op jit(solution)/shard_map/ppermute | solution.py:557
  68.2 13.2 %collective-permute-start.4 = (f32[128,512]{1,0:T(8,128)S(1)}, f32[128,512]{1,0:T(8,128)S(1)}, u32[]{:S(2)}, u32[]{:S(2)}) collective-permute-start(f32[128,512]{1,0:T(8,128)S(1)} %get-tuple-element.53), channel_id=1, source_target_pairs={{0,24},{8,0},{16,8},{24,16},{1,25},{9,1},{17,9},{25,17},{2,26},{10... | collective-permute-start | bytes 786440 | tf_op jit(solution)/shard_map/ppermute | solution.py:304
  71.4 10.1 %collective-permute-start.5 = (f32[128,512]{1,0:T(8,128)S(1)}, f32[128,512]{1,0:T(8,128)S(1)}, u32[]{:S(2)}, u32[]{:S(2)}) collective-permute-start(f32[128,512]{1,0:T(8,128)S(1)} %get-tuple-element.54), channel_id=1, source_target_pairs={{2,4},{4,2},{3,5},{5,3},{10,12},{12,10},{11,13},{13,11},{18,20},{2... | collective-permute-start | bytes 786440 | tf_op jit(solution)/shard_map/ppermute | solution.py:304
  83.0 11.1 %collective-permute-start.6 = (f32[128,512]{1,0:T(8,128)S(1)}, f32[128,512]{1,0:T(8,128)S(1)}, u32[]{:S(2)}, u32[]{:S(2)}) collective-permute-start(f32[128,512]{1,0:T(8,128)S(1)} %get-tuple-element.57), channel_id=1, source_target_pairs={{0,8},{8,16},{16,24},{24,0},{1,9},{9,17},{17,25},{25,1},{2,10},{10... | collective-permute-start | bytes 786440 | tf_op jit(solution)/shard_map/ppermute | solution.py:304
  83.6 13.0 %collective-permute-start.7 = (f32[128,512]{1,0:T(8,128)S(1)}, f32[128,512]{1,0:T(8,128)S(1)}, u32[]{:S(2)}, u32[]{:S(2)}) collective-permute-start(f32[128,512]{1,0:T(8,128)S(1)} %get-tuple-element.58), channel_id=1, source_target_pairs={{0,2},{2,0},{4,6},{6,4},{1,3},{3,1},{5,7},{7,5},{8,10},{10,8},{12,... | collective-permute-start | bytes 786440 | tf_op jit(solution)/shard_map/ppermute | solution.py:304
  85.8 12.4 %collective-permute-start.8 = (f32[128,512]{1,0:T(8,128)S(1)}, f32[128,512]{1,0:T(8,128)S(1)}, u32[]{:S(2)}, u32[]{:S(2)}) collective-permute-start(f32[128,512]{1,0:T(8,128)S(1)} %get-tuple-element.59), channel_id=1, source_target_pairs={{0,24},{8,0},{16,8},{24,16},{1,25},{9,1},{17,9},{25,17},{2,26},{10... | collective-permute-start | bytes 786440 | tf_op jit(solution)/shard_map/ppermute | solution.py:304
  89.5 8.6 %collective-permute-start.9 = (f32[128,512]{1,0:T(8,128)S(1)}, f32[128,512]{1,0:T(8,128)S(1)}, u32[]{:S(2)}, u32[]{:S(2)}) collective-permute-start(f32[128,512]{1,0:T(8,128)S(1)} %get-tuple-element.60), channel_id=1, source_target_pairs={{2,4},{4,2},{3,5},{5,3},{10,12},{12,10},{11,13},{13,11},{18,20},{2... | collective-permute-start | bytes 786440 | tf_op jit(solution)/shard_map/ppermute | solution.py:304
  90.2 8.0 %collective-permute-start.10 = (f32[128,512]{1,0:T(8,128)S(1)}, f32[128,512]{1,0:T(8,128)S(1)}, u32[]{:S(2)}, u32[]{:S(2)}) collective-permute-start(f32[128,512]{1,0:T(8,128)S(1)} %get-tuple-element.61), channel_id=1, source_target_pairs={{0,1},{1,0},{2,3},{3,2},{4,5},{5,4},{6,7},{7,6},{8,9},{9,8},{10,11... | collective-permute-start | bytes 786440 | tf_op jit(solution)/shard_map/ppermute | solution.py:304
  95.3 2.8 %collective-permute-start.11 = (f32[8,128]{1,0:T(8,128)S(1)}, f32[8,128]{1,0:T(8,128)S(1)}, u32[]{:S(2)}, u32[]{:S(2)}) collective-permute-start(f32[8,128]{1,0:T(8,128)S(1)} %shard_map.144.refs_5_), channel_id=1, source_target_pairs={{0,1},{1,0},{2,3},{3,2},{4,5},{5,4},{6,7},{7,6},{8,9},{9,8},{10,11... | collective-permute-start | bytes 12296 | tf_op jit(solution)/shard_map/ppermute | solution.py:592
  96.6 14.0 %copy-start.18 = (f32[1,512]{1,0:T(1,128)S(1)}, f32[1,512]{1,0:T(1,128)}, u32[]{:S(2)}) copy-start(f32[1,512]{1,0:T(1,128)} %get-tuple-element.63.rho_ref) | copy-start | bytes 6148
  (8 other events, 16.2 us)

commit v12 on v10

--- a/solution.py
+++ b/solution.py
@@ -140,19 +140,16 @@
         )
     ]
     large = []
-    for pair in range(3):
-        at = pl.ds(2 * pair * rows, 2 * rows)
-        large.append(
-            (
-                pltpu.make_async_copy(residual_any.at[at], residual_ref.at[at], sems.at[pair, 0]),
-                pltpu.make_async_copy(basis_any.at[at], basis_ref.at[at], sems.at[pair, 1]),
-            )
-        )
+    for face in range(6):
+        at = pl.ds(face * rows, rows)
+        large += [
+            pltpu.make_async_copy(residual_any.at[at], residual_ref.at[at], sems.at[face, 0]),
+            pltpu.make_async_copy(basis_any.at[at], basis_ref.at[at], sems.at[face, 1]),
+        ]
     for copy in small:
         copy.start()
-    for pair in large:
-        for copy in pair:
-            copy.start()
+    for copy in large:
+        copy.start()
     for copy in small:
         copy.wait()
     own_row = owner_ref[...].astype(f32)
@@ -167,7 +164,7 @@
     names = select(to_owner, jnp.where(place == at_owner, wanted_col, 0.0))
     terms = None
     for pair in range(3):
-        for copy in large[pair]:
+        for copy in large[4 * pair : 4 * pair + 4]:
             copy.wait()
         weighted = jnp.concatenate(
             [0.5 * masked(len_ref, residual_ref, 2 * pair + side, rows) for side in range(2)],
@@ -189,17 +186,27 @@
     whole, refs = refs[:2], refs[2:]
     local_ref, part_ref, square_ref, table_ref, refs = *refs[:4], refs[4:]
     rows = residual_ref.shape[0] // 6
-    live = jnp.concatenate(
-        [masked(len_ref, residual_ref, face, rows) for face in range(6)], axis=0
-    )
-    local = product(parts(matrix_ref[...]), parts(0.5 * live))
-    local_ref[...] = local
-    part_ref[...] = jnp.sum(live * local, axis=0, keepdims=True)
-    square_ref[...] = jnp.sum(live * live, axis=0, keepdims=True)
-    refs[0][...], refs[1][...] = parts(whole[0][...])
-    for i, move in enumerate(NEAR + FAR):
-        at = slice(i * rows, (i + 1) * rows)
-        refs[2][:, at], refs[3][:, at] = parts(whole[1][:, rows_of(served(*move), rows)])
+    weighted = parts(
+        jnp.concatenate(
+            [0.5 * masked(len_ref, residual_ref, face, rows) for face in range(6)], axis=0
+        )
+    )
+    part = square = jnp.zeros((1, residual_ref.shape[1]), f32)
+    for i, move in enumerate(FIRST):
+        face = served(*move)
+        at, to = rows_of(face, rows), slice(i * rows, (i + 1) * rows)
+        local = product(parts(matrix_ref[at, :]), weighted)
+        local_ref[to, :] = local
+        live = jnp.where(live_rows(len_ref, face, rows), residual_ref[at, :], 0.0)
+        part += jnp.sum(live * local, axis=0, keepdims=True)
+        square += jnp.sum(live * live, axis=0, keepdims=True)
+        refs[0][to, :], refs[1][to, :] = parts(whole[0][at, :])
+        for j, other in enumerate(FIRST):
+            across = rows_of(served(*other), rows)
+            over = slice(j * rows, (j + 1) * rows)
+            refs[2][to, over], refs[3][to, over] = parts(whole[1][at, across])
+    part_ref[...] = part
+    square_ref[...] = square
     primal, slots = table_ref.shape
     rank_row, own_col = ranks(owner_ref[...].astype(f32))
     (rank_col,) = columns(rank_row)
@@ -277,7 +284,7 @@
 
 
 def sent(axis, way):
-    return 1 - served(axis, way) if axis == "blk" else served(axis, way)
+    return (axis, "down" if way == "up" else "up") if axis == "blk" else (axis, way)
 
 
 def rows_of(face, rows):
@@ -286,26 +293,30 @@
     return pl.ds(pl.multiple_of(face * rows, rows), rows)
 
 
-def put_faces(image_ref, rows, order, face_refs):
-    for ref, move in zip(face_refs, moves(order), strict=True):
-        ref[...] = image_ref[rows_of(sent(*move), rows), :]
-
-
-def exchange(faces, order):
-    return [
-        lax.ppermute(block, axis, route(axis, way))
-        for block, (axis, way) in zip(faces, moves(order), strict=True)
-    ]
-
-
-def image_kernel(pair_depth, returned_ref, table_ref, high_ref, low_ref, local_ref, image_ref, sums_ref, *face_refs):
-    rows = local_ref.shape[0] // 6
+def sending(order):
+    return [sent(*move) for move in order]
+
+
+def put_blocks(image, refs, order):
+    rows = refs[0].shape[0]
+    for ref, move in zip(refs, sending(order), strict=True):
+        i = FIRST.index(move)
+        ref[...] = image[i * rows : (i + 1) * rows, :]
+
+
+def exchange(blocks, order):
+    return {
+        (axis, way): lax.ppermute(blocks[sent(axis, way)], axis, route(axis, way))
+        for axis, way in moves(order)
+    }
+
+
+def image_kernel(pair_depth, returned_ref, table_ref, high_ref, low_ref, local_ref, sums_ref, *image_refs):
     width = local_ref.shape[1]
     folds = width // LANES
     correction = select(table_ref[...], get_slab(returned_ref, folds))
     image = local_ref[...] + product((high_ref[...], low_ref[...]), parts(correction))
-    image_ref[...] = image
-    put_faces(image_ref, rows, FIRST, face_refs)
+    put_blocks(image, image_refs, FIRST)
     tail = jnp.sum(returned_ref[:, folds * CAP :, :], axis=0)
     if pair_depth:
         sums_ref[...] = tail
@@ -313,26 +324,28 @@
         sums_ref[...] = jnp.broadcast_to(tail[None], sums_ref.shape)
 
 
-def with_got(ref, at, got, move):
-    return ref[at, :] + got[move][...] if move in got else ref[at, :]
+def with_got(block, got, move):
+    return block + got[move][...] if move in got else block
 
 
 def new_direction(len_ref, beta, image_ref, prev_ref, got, move, rows):
     face = served(*move)
-    at = rows_of(face, rows)
-    precond = 0.5 * with_got(image_ref, at, got, move)
-    return jnp.where(live_rows(len_ref, face, rows), precond + beta * prev_ref[at, :], 0.0)
-
-
-def near_kernel(pair_depth, scale, keys, len_ref, sums_ref, prev_rho_ref, image_ref, prev_ref, high_ref, low_ref, *refs):
+    precond = 0.5 * with_got(image_ref[...], got, move)
+    return jnp.where(
+        live_rows(len_ref, face, rows), precond + beta * prev_ref[rows_of(face, rows), :], 0.0
+    )
+
+
+def near_kernel(pair_depth, scale, keys, len_ref, sums_ref, prev_rho_ref, prev_ref, high_ref, low_ref, *refs):
+    images, refs = refs[: len(NEAR)], refs[len(NEAR) :]
     got, refs = dict(zip(keys, refs)), refs[len(keys) :]
     if pair_depth:
         sums, refs = sums_ref[...] + refs[0][...], refs[1:]
     else:
         sums = jnp.sum(sums_ref[...], axis=0)
     rho_out, beta_out, square_out, near_ref, image_out = refs
-    rows = image_ref.shape[0] // 6
-    folds = image_ref.shape[1] // LANES
+    rows = images[0].shape[0]
+    folds = images[0].shape[1] // LANES
     rho = scale * unfolded(sums, 0, folds)
     beta = rho / prev_rho_ref[...]
     rho_out[...] = rho
@@ -340,27 +353,26 @@
     square_out[...] = unfolded(sums, folds, folds)
     for i, move in enumerate(NEAR):
         near_ref[i * rows : (i + 1) * rows, :] = new_direction(
-            len_ref, beta, image_ref, prev_ref, got, move, rows
+            len_ref, beta, images[i], prev_ref, got, move, rows
         )
     first = len(NEAR) * rows
     image_out[...] = product((high_ref[:, :first], low_ref[:, :first]), parts(near_ref[...]))
 
 
-def far_kernel(keys, len_ref, beta_ref, image_ref, prev_ref, high_ref, low_ref, near_ref, near_image_ref, *refs):
-    got, refs = dict(zip(keys, refs)), refs[len(keys) :]
-    far_ref, schur_out, *face_refs = refs
-    rows = image_ref.shape[0] // 6
+def far_kernel(keys, len_ref, beta_ref, prev_ref, high_ref, low_ref, near_image_ref, *refs):
+    images, refs = refs[: len(FAR)], refs[len(FAR) :]
+    got, (far_ref, *schur_refs) = dict(zip(keys, refs)), refs[len(keys) :]
+    rows = images[0].shape[0]
     beta = beta_ref[...]
     for i, move in enumerate(FAR):
         far_ref[i * rows : (i + 1) * rows, :] = new_direction(
-            len_ref, beta, image_ref, prev_ref, got, move, rows
+            len_ref, beta, images[i], prev_ref, got, move, rows
         )
     first = len(NEAR) * rows
     image = near_image_ref[...] + product(
         (high_ref[:, first:], low_ref[:, first:]), parts(far_ref[...])
     )
-    schur_out[...] = image
-    put_faces(schur_out, rows, SECOND, face_refs)
+    put_blocks(image, schur_refs, SECOND)
 
 
 def store_kernel(near_ref, far_ref, direction_out, sems):
@@ -381,35 +393,33 @@
         copy.wait()
 
 
-def products_kernel(len_ref, near_ref, far_ref, schur_ref, residual_ref, arrived, out_ref):
-    rows = schur_ref.shape[0] // 6
-    curve = cross = jnp.zeros((1, schur_ref.shape[1]), f32)
-    for ref, served_moves in ((near_ref, NEAR), (far_ref, FAR)):
-        for i, move in enumerate(served_moves):
-            face = served(*move)
-            at = rows_of(face, rows)
-            image = schur_ref[at, :]
-            live = jnp.where(live_rows(len_ref, face, rows), residual_ref[at, :], 0.0)
-            direction = ref[i * rows : (i + 1) * rows, :]
-            curve += 2.0 * jnp.sum(direction * image, axis=0, keepdims=True)
-            cross += 2.0 * jnp.sum(live * image, axis=0, keepdims=True)
+def products_kernel(len_ref, near_ref, far_ref, residual_ref, arrived, *refs):
+    schur_refs, out_ref = refs[:-1], refs[-1]
+    rows, width = schur_refs[0].shape
+    curve = cross = jnp.zeros((1, width), f32)
+    for i, (move, schur_ref) in enumerate(zip(FIRST, schur_refs, strict=True)):
+        face = served(*move)
+        image = schur_ref[...]
+        live = jnp.where(live_rows(len_ref, face, rows), residual_ref[rows_of(face, rows), :], 0.0)
+        ref, first = (near_ref, i) if i < len(NEAR) else (far_ref, i - len(NEAR))
+        direction = ref[first * rows : (first + 1) * rows, :]
+        curve += 2.0 * jnp.sum(direction * image, axis=0, keepdims=True)
+        cross += 2.0 * jnp.sum(live * image, axis=0, keepdims=True)
     for j, piece in enumerate(folded(curve) + folded(cross)):
         out_ref[j : j + 1, :] = piece
 
 
-def applied_kernel(pair_depth, len_ref, stored, schur_ref, *refs):
-    keys = moves(SECOND)
+def applied_kernel(pair_depth, keys, len_ref, stored, *refs):
+    schur_refs, refs = refs[: len(FIRST)], refs[len(FIRST) :]
     got, refs = dict(zip(keys, refs)), refs[len(keys) :]
     products, (applied_ref, spread_ref) = refs[:-2], refs[-2:]
-    rows = schur_ref.shape[0] // 6
-    folds = schur_ref.shape[1] // LANES
-    total = jnp.zeros((1, schur_ref.shape[1]), f32)
-    for move in SECOND:
-        face = served(*move)
-        at = rows_of(face, rows)
-        applied = with_got(schur_ref, at, got, move)
-        applied = jnp.where(live_rows(len_ref, face, rows), applied, 0.0)
-        applied_ref[at, :] = applied
+    rows, width = schur_refs[0].shape
+    folds = width // LANES
+    total = jnp.zeros((1, width), f32)
+    for i, (move, schur_ref) in enumerate(zip(FIRST, schur_refs, strict=True)):
+        applied = with_got(schur_ref[...], got, move)
+        applied = jnp.where(live_rows(len_ref, served(*move), rows), applied, 0.0)
+        applied_ref[i * rows : (i + 1) * rows, :] = applied
         total += jnp.sum(applied * applied, axis=0, keepdims=True)
     products = sum(ref[...] for ref in products)
     halves = [products[:folds], products[folds : 2 * folds]]
@@ -438,11 +448,12 @@
         square_ref[...] - 2.0 * alpha * cross + alpha * alpha * applied_square
     )
     copies = []
-    for face in range(6):
-        at = slice(face * rows, (face + 1) * rows)
-        new_ref[at, :] = masked(len_ref, residual_ref, face, rows) - alpha * applied_ref[at, :]
-        where = pl.ds(face * rows, rows)
-        copies.append(pltpu.make_async_copy(new_ref.at[where], new_out.at[where], sems.at[face]))
+    for i, move in enumerate(FIRST):
+        face = served(*move)
+        at, to = rows_of(face, rows), pl.ds(i * rows, rows)
+        live = jnp.where(live_rows(len_ref, face, rows), residual_ref[at, :], 0.0)
+        new_ref[to, :] = live - alpha * applied_ref[to, :]
+        copies.append(pltpu.make_async_copy(new_ref.at[to], new_out.at[at], sems.at[i]))
         copies[-1].start()
     for copy in copies:
         copy.wait()
@@ -504,7 +515,7 @@
             pltpu.VMEM((1, primal), jnp.int32),
             pltpu.VMEM((height, width), f32),
             pltpu.VMEM((height, primal), f32),
-            pltpu.SemaphoreType.DMA((3, 2)),
+            pltpu.SemaphoreType.DMA((6, 2)),
             pltpu.SemaphoreType.DMA((3,)),
         ],
     )
@@ -535,16 +546,16 @@
         ],
     )
     returned = to_all(answers, LAYER)
-    keys = moves(FIRST)
-    faces = [face] * len(keys)
-    image, sums, *outward = call(
+    faces = [face] * len(FIRST)
+    sums, *image = call(
         functools.partial(image_kernel, pair_depth),
-        [whole, shape_of(tail, LANES) if pair_depth else shape_of(layers, tail, LANES), *faces],
+        [shape_of(tail, LANES) if pair_depth else shape_of(layers, tail, LANES), *faces],
         [returned, table, *basis_halves, local],
         flops=(6 * height + 4 * slots) * primal * width,
         moved=16 * height * width,
     )
-    got = dict(zip(keys, exchange(outward, FIRST)))
+    image = dict(zip(sending(FIRST), image))
+    got = exchange(image, FIRST)
     if pair_depth:
         sums = [sums, lax.ppermute(sums, "depth", route("depth", 0))]
     else:
@@ -553,29 +564,33 @@
     rho, beta, square, near, near_image = call(
         functools.partial(near_kernel, pair_depth, scale, near_keys),
         [row, row, row, shape_of(len(NEAR) * rows, width), whole],
-        [lengths, sums[0], prev_rho.reshape(1, width), image, prev_direction, *schur_halves]
+        [lengths, sums[0], prev_rho.reshape(1, width), prev_direction, *schur_halves]
+        + [image[move] for move in NEAR]
         + [got[key] for key in near_keys]
         + sums[1:],
         smem=(0,),
         flops=4 * height * height * width,
         moved=4 * height * (height + 4 * width),
     )
-    far, schur_image, *outward = call(
+    far, *schur_image = call(
         functools.partial(far_kernel, far_keys),
-        [shape_of(len(FAR) * rows, width), whole, *faces],
-        [lengths, beta, image, prev_direction, *schur_halves, near, near_image]
+        [shape_of(len(FAR) * rows, width), *faces],
+        [lengths, beta, prev_direction, *schur_halves, near_image]
+        + [image[move] for move in FAR]
         + [got[key] for key in far_keys],
         smem=(0,),
         flops=2 * height * height * width,
         moved=4 * height * (height + 4 * width),
     )
-    got = exchange(outward, SECOND)
+    schur_image = dict(zip(sending(SECOND), schur_image))
+    got = exchange(schur_image, SECOND)
+    schur_image = [schur_image[move] for move in FIRST]
     (products,) = call(
         products_kernel,
         [shape_of(2 * folds, LANES)],
-        [lengths, near, far, schur_image, residual, got[0]],
+        [lengths, near, far, residual, got[SECOND[0]], *schur_image],
         smem=(0,),
-        loose=(5,),
+        loose=(4,),
         flops=4 * height * width,
         moved=12 * height * width,
     )
@@ -591,9 +606,9 @@
         scratch=[pltpu.SemaphoreType.DMA((6,))],
     )
     applied, spread_sums = call(
-        functools.partial(applied_kernel, pair_depth),
+        functools.partial(applied_kernel, pair_depth, list(got)),
         [whole, shape_of(devices, 2 if pair_depth else 3, folds, LANES)],
-        [lengths, direction, schur_image, *got, *products],
+        [lengths, direction, *schur_image, *got.values(), *products],
         smem=(0,),
         far=(1,),
         flops=4 * height * width,

time: 111 us -> 113 us (1.018)
  waiting for transfers between devices: 18.8 us -> 23.4 us
  starting transfers between devices: 22.6 us -> 19.9 us
    ppermute x10, waiting for transfers between devices: 9.02 us -> 13.3 us  [exchange(): lax.ppermute(blocks[sent(axis, way)], axis, route(axis, way))]
    ppermute x10, starting transfers between devices: 13.5 us -> 11.1 us  [exchange(): lax.ppermute(blocks[sent(axis, way)], axis, route(axis, way))]
  transfers between devices with their start and end apart: 13 -> 13, of which waited for: 4 -> 6; matrix products, arithmetic and copies ran while one was open for 0% -> 0% of each run, Pallas kernels for 8% -> 7%
where the time goes in v12:
time: 113 us
  blocking collectives  39.7 us (35%)
  waiting for transfers between devices  23.4 us (21%)
  Pallas kernels  21.3 us (19%)
  starting transfers between devices  19.9 us (18%)
  local copies, waits for them, and re-layouts  7.73 us (7%)
    all_to_all x2, blocking collectives, to_all(): return lax.all_to_all(x, axes, split_axis=0, concat_axis=0, tiled=True)  39.7 us
    pallas_call x10, Pallas kernels, call(): pl.pallas_call(body, out_shape=list(outs), in_specs=in_specs, out_specs=o...  21.3 us
    ppermute x10, waiting for transfers between devices, exchange(): lax.ppermute(blocks[sent(axis, way)], axis, route(axis, way))  13.3 us
    ppermute x10, starting transfers between devices, exchange(): lax.ppermute(blocks[sent(axis, way)], axis, route(axis, way))  11.1 us
    all_to_all x1, waiting for transfers between devices, to_all(): return lax.all_to_all(x, axes, split_axis=0, concat_axis=0, tiled=True)  10.1 us
    all_to_all x1, starting transfers between devices, to_all(): return lax.all_to_all(x, axes, split_axis=0, concat_axis=0, tiled=True)  8.5 us
    unnamed x38, local copies, waits for them, and re-layouts  7.73 us
  transfers between devices with their start and end apart: 13, of which 6 were waited for; matrix products, arithmetic and copies ran while one was open for 0% of the time, Pallas kernels for 7%

profile of v12, /device:TPU:0, one launch (start us, length us, event | category | flops | bytes accessed | tf_op | source)
XLA Modules:
  0.0 112.9 jit_solution(4107965644264234067)
XLA Ops:
  0.6 4.6 %shard_map.137 = f32[16,104,128]{2,1,0:T(8,128)} custom-call(s32[6]{0:T(128)} %bitcast.25, s32[1,256]{1,0:T(1,128)} %bitcast.32, s32[1,256]{1,0:T(1,128)} %bitcast.37, f32[768,512]{1,0:T(8,128)} %bitcast.15, f32[768,256]{1,0:T(8,128)} %bitcast.21), custom_call_target="tpu_custom_call" | custom-call | flops 603979776 | bytes 3145728 | tf_op jit(solution)/shard_map/pallas_call | solution.py:37
  5.3 8.5 %all-to-all-start = ((f32[16,104,128]{2,1,0:T(8,128)}), f32[16,104,128]{2,1,0:T(8,128)}, u32[]{:S(2)}, u32[]{:S(2)}) async-start(f32[16,104,128]{2,1,0:T(8,128)} %shard_map.137), calls=%async_computation | async-start | bytes 1703936 | tf_op jit(solution)/shard_map/all_to_all | solution.py:463
  13.9 1.7 %copy-done.5 = f32[1,1,1,768,768]{4,3,2,1,0:T(8,128)S(1)} copy-done((f32[1,1,1,768,768]{4,3,2,1,0:T(8,128)S(1)}, f32[1,1,1,768,768]{4,3,2,1,0:T(8,128)}, u32[]{:S(2)}) %copy-start.5) | copy-done | bytes 2359320
  15.5 1.7 %copy-done.6 = f32[1,1,1,768,768]{4,3,2,1,0:T(8,128)S(1)} copy-done((f32[1,1,1,768,768]{4,3,2,1,0:T(8,128)S(1)}, f32[1,1,1,768,768]{4,3,2,1,0:T(8,128)}, u32[]{:S(2)}) %copy-start.6) | copy-done | bytes 2359320
  17.2 3.1 %shard_map.138 = (f32[768,512]{1,0:T(8,128)S(1)}, f32[1,512]{1,0:T(1,128)S(1)}, f32[1,512]{1,0:T(1,128)S(1)}, bf16[256,384]{1,0:T(8,128)(2,1)S(1)}, bf16[768,256...) custom-call(s32[6]{0:T(128)S(1)} %bitcast.26, ...), custom_call_target="tpu_custom_call" | custom-call | flops 1811939328 | bytes 10223616 | tf_op jit(solution)/shard_map/pallas_call | solution.py:37
  21.4 1.1 %copy-done.7 = f32[768,512]{1,0:T(8,128)} copy-done((f32[768,512]{1,0:T(8,128)}, f32[768,512]{1,0:T(8,128)S(1)}, u32[]{:S(2)}) %copy-start.7) | copy-done | bytes 1572888
  24.7 10.1 %all-to-all-done.incoming_any = f32[16,104,128]{2,1,0:T(8,128)} async-done(((f32[16,104,128]{2,1,0:T(8,128)}), f32[16,104,128]{2,1,0:T(8,128)}, u32[]{:S(2)}, u32[]{:S(2)}) %all-to-all-start) | async-done | bytes 852000 | tf_op jit(solution)/shard_map/all_to_all | solution.py:463
  34.8 2.6 %shard_map.139 = f32[16,104,128]{2,1,0:T(8,128)S(1)} custom-call(f32[16,104,128]{2,1,0:T(8,128)} %all-to-all-done.incoming_any, f32[256,256]{1,0:T(8,128)} %bitcast.39, f32[1,512]{1,0:T(1,128)S(1)} %get-tuple-element.37.local_part_ref, f32[1,512]{1,0:T(1,128)S(1)} %get-tuple-element.38.square_ref), custom_call_target="tpu_custom_call" | custom-call | flops 603979776 | bytes 1572864 | tf_op jit(solution)/shard_map/pallas_call | solution.py:37
  37.4 26.4 %all_to_all.15.returned_ref = f32[16,104,128]{2,1,0:T(8,128)S(1)} all-to-all(f32[16,104,128]{2,1,0:T(8,128)S(1)} %shard_map.139), channel_id=1, replica_groups=mesh['blk'=4,'lat'=4,'depth'=2] {'blk','lat'}, dimensions={0} | all-to-all | bytes 1703936 | tf_op jit(solution)/shard_map/all_to_all | solution.py:463
  63.8 1.2 %shard_map.140 = (f32[8,128]{1,0:T(8,128)S(1)}, f32[128,512]{1,0:T(8,128)S(1)}, f32[128,512]{1,0:T(8,128)S(1)}, f32[128,512]{1,0:T(8,128)S(1)}, f32[128,512]{1,0...) custom-call(f32[16,104,128]{2,1,0:T(8,128)S(1)} %all_to_all.15.returned_ref, ...), custom_call_target="tpu_custom_call" | custom-call | flops 805306368 | bytes 6291456 | tf_op jit(solution)/shard_map/pallas_call | solution.py:37
  65.7 1.0 collective-permute-start
  66.9 2.8 %collective-permute-start.4 = (f32[128,512]{1,0:T(8,128)S(1)}, f32[128,512]{1,0:T(8,128)S(1)}, u32[]{:S(2)}, u32[]{:S(2)}) collective-permute-start(f32[128,512]{1,0:T(8,128)S(1)} %get-tuple-element.46.refs_0_), channel_id=1, source_target_pairs={{0,24},{8,0},{16,8},{24,16},{1,25},{9,1},{17,9},{25,17},{2,26},{10... | collective-permute-start | bytes 786440 | tf_op jit(solution)/shard_map/ppermute | solution.py:309
  70.4 1.1 collective-permute-done.1.refs_5_
  71.5 5.1 %collective-permute-done.refs_4_ = f32[128,512]{1,0:T(8,128)S(1)} collective-permute-done((f32[128,512]{1,0:T(8,128)S(1)}, f32[128,512]{1,0:T(8,128)S(1)}, u32[]{:S(2)}, u32[]{:S(2)}) %collective-permute-start) | collective-permute-done | bytes 262176 | tf_op jit(solution)/shard_map/ppermute | solution.py:309
  76.6 2.6 %shard_map.141 = (f32[1,512]{1,0:T(1,128)}, f32[1,512]{1,0:T(1,128)S(1)}, f32[1,512]{1,0:T(1,128)S(1)}, f32[512,512]{1,0:T(8,128)S(1)}, f32[768,512]{1,0:T(8,128)S(1)}) custom-call(s32[6]{0:T(128)S(1)} %bitcast.27, f32[8,128]{1,0:T(8,128)S(1)} %get-tuple-element.43.sums_ref, f32[1,512]{1,0:T(1,128)S(1)} %bitcast.34, f32[768,512]{1,0:T(8,128)S(1)} %bitcast.19, ...), custom_call_target="tpu_custom_call" | custom-call | flops 1207959552 | bytes 8650752 | tf_op jit(solution)/shard_map/pallas_call | solution.py:37
  79.2 1.8 %collective-permute-done.4.refs_2_ = f32[128,512]{1,0:T(8,128)S(1)} collective-permute-done((f32[128,512]{1,0:T(8,128)S(1)}, f32[128,512]{1,0:T(8,128)S(1)}, u32[]{:S(2)}, u32[]{:S(2)}) %collective-permute-start.4) | collective-permute-done | bytes 262176 | tf_op jit(solution)/shard_map/ppermute | solution.py:309
  81.0 1.4 %shard_map.142 = (f32[256,512]{1,0:T(8,128)S(1)}, f32[128,512]{1,0:T(8,128)S(1)}, f32[128,512]{1,0:T(8,128)S(1)}, f32[128,512]{1,0:T(8,128)S(1)}, f32[128,512]{1...) custom-call(s32[6]{0:T(128)S(1)} %bitcast.28, f32[1,512]{1,0:T(1,128)S(1)} %get-tuple-element.52.beta_ref, ...), custom_call_target="tpu_custom_call" | custom-call | flops 603979776 | bytes 8650752 | tf_op jit(solution)/shard_map/pallas_call | solution.py:37
  83.3 3.0 %collective-permute-start.8 = (f32[128,512]{1,0:T(8,128)S(1)}, f32[128,512]{1,0:T(8,128)S(1)}, u32[]{:S(2)}, u32[]{:S(2)}) collective-permute-start(f32[128,512]{1,0:T(8,128)S(1)} %get-tuple-element.56.refs_0_), channel_id=1, source_target_pairs={{0,24},{8,0},{16,8},{24,16},{1,25},{9,1},{17,9},{25,17},{2,26},{10... | collective-permute-start | bytes 786440 | tf_op jit(solution)/shard_map/ppermute | solution.py:309
  86.3 1.5 %collective-permute-start.7 = (f32[128,512]{1,0:T(8,128)S(1)}, f32[128,512]{1,0:T(8,128)S(1)}, u32[]{:S(2)}, u32[]{:S(2)}) collective-permute-start(f32[128,512]{1,0:T(8,128)S(1)} %get-tuple-element.57.refs_1_), channel_id=1, source_target_pairs={{0,2},{2,0},{4,6},{6,4},{1,3},{3,1},{5,7},{7,5},{8,10},{10,8},{12,... | collective-permute-start | bytes 786440 | tf_op jit(solution)/shard_map/ppermute | solution.py:309
  88.5 5.1 %collective-permute-done.6.arrived.refs_6_ = f32[128,512]{1,0:T(8,128)S(1)} collective-permute-done((f32[128,512]{1,0:T(8,128)S(1)}, f32[128,512]{1,0:T(8,128)S(1)}, u32[]{:S(2)}, u32[]{:S(2)}) %collective-permute-start.6) | collective-permute-done | bytes 262176 | tf_op jit(solution)/shard_map/ppermute | solution.py:309
  93.5 1.3 %shard_map.144.refs_11_ = f32[8,128]{1,0:T(8,128)S(1)} custom-call(s32[6]{0:T(128)S(1)} %bitcast.29, f32[512,512]{1,0:T(8,128)S(1)} %get-tuple-element.51.near_ref, f32[256,512]{1,0:T(8,128)S(1)} %get-tuple-element.55.far_ref, f32[768,512]{1,0:T(8,128)S(1)} %bitcast.17, f32[128,512]{1,0:T(8,128)S(1)} %collective-permute-done.6.arrived.refs_6_, ...), custom_call_target="tpu_custom_call" | custom-call | flops 1572864 | bytes 4718592 | tf_op jit(solution)/shard_map/pallas_call | solution.py:37
  94.9 1.2 %shard_map.143.stored = f32[768,512]{1,0:T(8,128)} custom-call(f32[512,512]{1,0:T(8,128)S(1)} %get-tuple-element.51.near_ref, f32[256,512]{1,0:T(8,128)S(1)} %get-tuple-element.55.far_ref), custom_call_target="tpu_custom_call" | custom-call | bytes 3145728 | tf_op jit(solution)/shard_map/pallas_call | solution.py:37
  97.2 13.4 %all_to_all.16.sums_ref = f32[32,2,4,128]{3,2,1,0:T(4,128)S(1)} all-to-all(f32[32,2,4,128]{3,2,1,0:T(4,128)S(1)} %get-tuple-element.62), channel_id=1, replica_groups=mesh['blk'=4,'lat'=4,'depth'=2] {'blk','lat','depth'}, dimensions={0} | all-to-all | bytes 262144 | tf_op jit(solution)/shard_map/all_to_all | solution.py:463
  110.5 2.4 %shard_map.146 = (f32[768,512]{1,0:T(8,128)}, f32[1,512]{1,0:T(1,128)}, f32[1,512]{1,0:T(1,128)}) custom-call(s32[6]{0:T(128)S(1)} %bitcast.31, f32[32,2,4,128]{3,2,1,0:T(4,128)S(1)} %all_to_all.16.sums_ref, f32[1,512]{1,0:T(1,128)S(1)} %copy-done.18, f32[1,512]{1,0:T(1,128)S(1)} %get-tuple-element.64.square_ref, f32[768,512]{1,0:T(8,128)S(1)} %bitcast.18, ...), custom_call_target="tpu_custom_call" | custom-call | flops 1572864 | bytes 4718592 | tf_op jit(solution)/shard_map/pallas_call | solution.py:37
  (52 shorter events, 7.4 us)
Async XLA Ops:
  0.6 13.2 %copy-start.4 = (f32[1,1,1,768,256]{4,3,2,1,0:T(8,128)S(1)}, f32[1,1,1,768,256]{4,3,2,1,0:T(8,128)}, u32[]{:S(2)}) copy-start(f32[1,1,1,768,256]{4,3,2,1,0:T(8,128)} %param.16) | copy-start | bytes 2359300
  5.3 8.6 %copy-start = (f32[1,1,1,768,512]{4,3,2,1,0:T(8,128)S(1)}, f32[1,1,1,768,512]{4,3,2,1,0:T(8,128)}, u32[]{:S(2)}) copy-start(f32[1,1,1,768,512]{4,3,2,1,0:T(8,128)} %param.11) | copy-start | bytes 4718596
  5.3 8.6 %copy-start.15 = (s32[1,1,1,6]{3,2,1,0:T(1,128)S(1)}, s32[1,1,1,6]{3,2,1,0:T(1,128)}, u32[]{:S(2)}) copy-start(s32[1,1,1,6]{3,2,1,0:T(1,128)} %param.10) | copy-start | bytes 76
  5.3 29.4 %all-to-all-start = ((f32[16,104,128]{2,1,0:T(8,128)}), f32[16,104,128]{2,1,0:T(8,128)}, u32[]{:S(2)}, u32[]{:S(2)}) async-start(f32[16,104,128]{2,1,0:T(8,128)} %shard_map.137), calls=%async_computation | async-start | bytes 1703936 | tf_op jit(solution)/shard_map/all_to_all | solution.py:463
  34.8 29.0 %copy-start.8 = (f32[768,512]{1,0:T(8,128)S(1)}, f32[768,512]{1,0:T(8,128)}, u32[]{:S(2)}) copy-start(f32[768,512]{1,0:T(8,128)} %copy-done.7) | copy-start | bytes 4718596
  34.8 29.0 %copy-start.10 = (bf16[768,256]{1,0:T(8,128)(2,1)S(1)}, bf16[768,256]{1,0:T(8,128)(2,1)}, u32[]{:S(2)}) copy-start(bf16[768,256]{1,0:T(8,128)(2,1)} %copy-done.9) | copy-start | bytes 1179652
  34.8 29.0 %copy-start.12 = (bf16[768,256]{1,0:T(8,128)(2,1)S(1)}, bf16[768,256]{1,0:T(8,128)(2,1)}, u32[]{:S(2)}) copy-start(bf16[768,256]{1,0:T(8,128)(2,1)} %copy-done.11) | copy-start | bytes 1179652
  34.8 29.0 %copy-start.14 = (bf16[256,384]{1,0:T(8,128)(2,1)S(1)}, bf16[256,384]{1,0:T(8,128)(2,1)}, u32[]{:S(2)}) copy-start(bf16[256,384]{1,0:T(8,128)(2,1)} %copy-done.13) | copy-start | bytes 589828
  63.8 12.8 %copy-start.1 = (f32[1,1,1,768,512]{4,3,2,1,0:T(8,128)S(1)}, f32[1,1,1,768,512]{4,3,2,1,0:T(8,128)}, u32[]{:S(2)}) copy-start(f32[1,1,1,768,512]{4,3,2,1,0:T(8,128)} %param.12) | copy-start | bytes 4718596
  63.8 12.8 %copy-start.3 = (bf16[768,768]{1,0:T(8,128)(2,1)S(1)}, bf16[768,768]{1,0:T(8,128)(2,1)}, u32[]{:S(2)}) copy-start(bf16[768,768]{1,0:T(8,128)(2,1)} %copy-done.2) | copy-start | bytes 3538948
  63.8 12.8 %copy-start.17 = (f32[512]{0:T(512)S(1)}, f32[512]{0:T(512)}, u32[]{:S(2)}) copy-start(f32[512]{0:T(512)} %param.13) | copy-start | bytes 6148
  65.0 6.4 %collective-permute-start.1 = (f32[128,512]{1,0:T(8,128)S(1)}, f32[128,512]{1,0:T(8,128)S(1)}, u32[]{:S(2)}, u32[]{:S(2)}) collective-permute-start(f32[128,512]{1,0:T(8,128)S(1)} %get-tuple-element.47.refs_1_), channel_id=1, source_target_pairs={{0,2},{2,0},{4,6},{6,4},{1,3},{3,1},{5,7},{7,5},{8,10},{10,8},{12,... | collective-permute-start | bytes 786440 | tf_op jit(solution)/shard_map/ppermute | solution.py:309
  65.6 5.8 %collective-permute-start.2 = (f32[128,512]{1,0:T(8,128)S(1)}, f32[128,512]{1,0:T(8,128)S(1)}, u32[]{:S(2)}, u32[]{:S(2)}) collective-permute-start(f32[128,512]{1,0:T(8,128)S(1)} %get-tuple-element.48.refs_2_), channel_id=1, source_target_pairs={{0,1},{1,0},{2,3},{3,2},{4,5},{5,4},{6,7},{7,6},{8,9},{9,8},{10,11... | collective-permute-start | bytes 786440 | tf_op jit(solution)/shard_map/ppermute | solution.py:309
  65.7 10.9 %collective-permute-start = (f32[128,512]{1,0:T(8,128)S(1)}, f32[128,512]{1,0:T(8,128)S(1)}, u32[]{:S(2)}, u32[]{:S(2)}) collective-permute-start(f32[128,512]{1,0:T(8,128)S(1)} %get-tuple-element.50.refs_0_), channel_id=1, source_target_pairs={{0,8},{8,16},{16,24},{24,0},{1,9},{9,17},{17,25},{25,1},{2,10},{10... | collective-permute-start | bytes 786440 | tf_op jit(solution)/shard_map/ppermute | solution.py:309
  66.7 3.1 %collective-permute-start.3 = (f32[8,128]{1,0:T(8,128)S(1)}, f32[8,128]{1,0:T(8,128)S(1)}, u32[]{:S(2)}, u32[]{:S(2)}) collective-permute-start(f32[8,128]{1,0:T(8,128)S(1)} %get-tuple-element.43.sums_ref), channel_id=1, source_target_pairs={{0,1},{1,0},{2,3},{3,2},{4,5},{5,4},{6,7},{7,6},{8,9},{9,8},{10,11... | collective-permute-start | bytes 12296 | tf_op jit(solution)/shard_map/ppermute | solution.py:560
  66.9 14.1 %collective-permute-start.4 = (f32[128,512]{1,0:T(8,128)S(1)}, f32[128,512]{1,0:T(8,128)S(1)}, u32[]{:S(2)}, u32[]{:S(2)}) collective-permute-start(f32[128,512]{1,0:T(8,128)S(1)} %get-tuple-element.46.refs_0_), channel_id=1, source_target_pairs={{0,24},{8,0},{16,8},{24,16},{1,25},{9,1},{17,9},{25,17},{2,26},{10... | collective-permute-start | bytes 786440 | tf_op jit(solution)/shard_map/ppermute | solution.py:309
  69.7 11.3 %collective-permute-start.5 = (f32[128,512]{1,0:T(8,128)S(1)}, f32[128,512]{1,0:T(8,128)S(1)}, u32[]{:S(2)}, u32[]{:S(2)}) collective-permute-start(f32[128,512]{1,0:T(8,128)S(1)} %get-tuple-element.54.refs_1_), channel_id=1, source_target_pairs={{2,4},{4,2},{3,5},{5,3},{10,12},{12,10},{11,13},{13,11},{18,20},{2... | collective-permute-start | bytes 786440 | tf_op jit(solution)/shard_map/ppermute | solution.py:309
  82.4 11.1 %collective-permute-start.6 = (f32[128,512]{1,0:T(8,128)S(1)}, f32[128,512]{1,0:T(8,128)S(1)}, u32[]{:S(2)}, u32[]{:S(2)}) collective-permute-start(f32[128,512]{1,0:T(8,128)S(1)} %get-tuple-element.60.refs_4_), channel_id=1, source_target_pairs={{0,8},{8,16},{16,24},{24,0},{1,9},{9,17},{17,25},{25,1},{2,10},{10... | collective-permute-start | bytes 786440 | tf_op jit(solution)/shard_map/ppermute | solution.py:309
  83.3 13.0 %collective-permute-start.8 = (f32[128,512]{1,0:T(8,128)S(1)}, f32[128,512]{1,0:T(8,128)S(1)}, u32[]{:S(2)}, u32[]{:S(2)}) collective-permute-start(f32[128,512]{1,0:T(8,128)S(1)} %get-tuple-element.56.refs_0_), channel_id=1, source_target_pairs={{0,24},{8,0},{16,8},{24,16},{1,25},{9,1},{17,9},{25,17},{2,26},{10... | collective-permute-start | bytes 786440 | tf_op jit(solution)/shard_map/ppermute | solution.py:309
  86.3 10.0 %collective-permute-start.7 = (f32[128,512]{1,0:T(8,128)S(1)}, f32[128,512]{1,0:T(8,128)S(1)}, u32[]{:S(2)}, u32[]{:S(2)}) collective-permute-start(f32[128,512]{1,0:T(8,128)S(1)} %get-tuple-element.57.refs_1_), channel_id=1, source_target_pairs={{0,2},{2,0},{4,6},{6,4},{1,3},{3,1},{5,7},{7,5},{8,10},{10,8},{12,... | collective-permute-start | bytes 786440 | tf_op jit(solution)/shard_map/ppermute | solution.py:309
  87.8 8.5 %collective-permute-start.10 = (f32[128,512]{1,0:T(8,128)S(1)}, f32[128,512]{1,0:T(8,128)S(1)}, u32[]{:S(2)}, u32[]{:S(2)}) collective-permute-start(f32[128,512]{1,0:T(8,128)S(1)} %get-tuple-element.58.refs_2_), channel_id=1, source_target_pairs={{0,1},{1,0},{2,3},{3,2},{4,5},{5,4},{6,7},{7,6},{8,9},{9,8},{10,11... | collective-permute-start | bytes 786440 | tf_op jit(solution)/shard_map/ppermute | solution.py:309
  87.8 8.5 %collective-permute-start.9 = (f32[128,512]{1,0:T(8,128)S(1)}, f32[128,512]{1,0:T(8,128)S(1)}, u32[]{:S(2)}, u32[]{:S(2)}) collective-permute-start(f32[128,512]{1,0:T(8,128)S(1)} %get-tuple-element.61.refs_5_), channel_id=1, source_target_pairs={{2,4},{4,2},{3,5},{5,3},{10,12},{12,10},{11,13},{13,11},{18,20},{2... | collective-permute-start | bytes 786440 | tf_op jit(solution)/shard_map/ppermute | solution.py:309
  94.8 1.5 %collective-permute-start.11 = (f32[8,128]{1,0:T(8,128)S(1)}, f32[8,128]{1,0:T(8,128)S(1)}, u32[]{:S(2)}, u32[]{:S(2)}) collective-permute-start(f32[8,128]{1,0:T(8,128)S(1)} %shard_map.144.refs_11_), channel_id=1, source_target_pairs={{0,1},{1,0},{2,3},{3,2},{4,5},{5,4},{6,7},{7,6},{8,9},{9,8},{10,11... | collective-permute-start | bytes 12296 | tf_op jit(solution)/shard_map/ppermute | solution.py:599
  96.1 14.4 %copy-start.18 = (f32[1,512]{1,0:T(1,128)S(1)}, f32[1,512]{1,0:T(1,128)}, u32[]{:S(2)}) copy-start(f32[1,512]{1,0:T(1,128)} %get-tuple-element.63.rho_ref) | copy-start | bytes 6148
  (8 other events, 16.2 us)

commit v13 on v10

--- a/solution.py
+++ b/solution.py
@@ -8,7 +8,7 @@
 from jax.sharding import PartitionSpec as P
 
 CAP = 24
-AXES = ("blk", "lat", "depth")
+AXES = ("depth", "blk", "lat")
 LAYER = ("blk", "lat")
 LANES = 128
 TILE = 8
@@ -155,6 +155,18 @@
             copy.start()
     for copy in small:
         copy.wait()
+
+    def term_of(pair):
+        for copy in large[pair]:
+            copy.wait()
+        weighted = jnp.concatenate(
+            [0.5 * masked(len_ref, residual_ref, 2 * pair + side, rows) for side in range(2)],
+            axis=0,
+        )
+        basis = basis_ref[2 * pair * rows : 2 * (pair + 1) * rows, :]
+        return product(parts(jnp.transpose(basis)), parts(weighted))
+
+    terms = term_of(0)
     own_row = owner_ref[...].astype(f32)
     wanted_row = row_ref[...].astype(f32) + 1.0
     rank_row, _ = ranks(own_row)
@@ -165,17 +177,8 @@
     at_owner = lax.axis_index(LAYER) * CAP + rank_col.astype(jnp.int32)
     place = lax.broadcasted_iota(jnp.int32, (primal, id_rows(slots) * LANES), 1)
     names = select(to_owner, jnp.where(place == at_owner, wanted_col, 0.0))
-    terms = None
-    for pair in range(3):
-        for copy in large[pair]:
-            copy.wait()
-        weighted = jnp.concatenate(
-            [0.5 * masked(len_ref, residual_ref, 2 * pair + side, rows) for side in range(2)],
-            axis=0,
-        )
-        basis = basis_ref[2 * pair * rows : 2 * (pair + 1) * rows, :]
-        term = product(parts(jnp.transpose(basis)), parts(weighted))
-        terms = term if terms is None else terms + term
+    terms += term_of(1)
+    terms += term_of(2)
     put_slab(slab_ref, select(packer, terms))
     tail = slab_ref.shape[1] - tiles(id_rows(slots))
     names = jnp.concatenate(
@@ -415,23 +418,22 @@
     halves = [products[:folds], products[folds : 2 * folds]]
     if pair_depth:
         halves = [jnp.where(lax.axis_index("depth") == 0, *halves)]
-    halves = [[half[j : j + 1] for j in range(folds)] for half in halves]
-    for i, half in enumerate([*halves, folded(total)]):
-        for j, piece in enumerate(half):
-            spread_ref[:, i, j, :] = jnp.broadcast_to(piece, (spread_ref.shape[0], LANES))
+    block = jnp.concatenate([*halves, *folded(total)], axis=0)
+    spread_ref[...] = jnp.broadcast_to(block[None], spread_ref.shape)
 
 
 def finish_kernel(pair_depth, scale, len_ref, sums_ref, rho_ref, square_ref, residual_ref, applied_ref, new_out, alpha_ref, norm_ref, new_ref, sems):
     rows = applied_ref.shape[0] // 6
-    devices, _, folds, _ = sums_ref.shape
+    devices, height, _ = sums_ref.shape
     if pair_depth:
-        pairs = sums_ref[...].reshape(devices // 2, 2, 2, folds, LANES)
-        pairs = jnp.sum(pairs, axis=0)
-        sums = [pairs[0, 0], pairs[1, 0], pairs[0, 1] + pairs[1, 1]]
+        folds = height // 2
+        layers = [jnp.sum(sums_ref[: devices // 2], axis=0), jnp.sum(sums_ref[devices // 2 :], axis=0)]
+        curve, cross = [unfolded(layer, 0, folds) for layer in layers]
+        applied_square = unfolded(layers[0] + layers[1], folds, folds)
     else:
+        folds = height // 3
         total = jnp.sum(sums_ref[...], axis=0)
-        sums = [total[i] for i in range(3)]
-    curve, cross, applied_square = [unfolded(x, 0, folds) for x in sums]
+        curve, cross, applied_square = [unfolded(total, i * folds, folds) for i in range(3)]
     alpha = rho_ref[...] / (scale * curve)
     alpha_ref[...] = alpha
     norm_ref[...] = scale * (
@@ -592,7 +594,7 @@
     )
     applied, spread_sums = call(
         functools.partial(applied_kernel, pair_depth),
-        [whole, shape_of(devices, 2 if pair_depth else 3, folds, LANES)],
+        [whole, shape_of(devices, (2 if pair_depth else 3) * folds, LANES)],
         [lengths, direction, schur_image, *got, *products],
         smem=(0,),
         far=(1,),

time: 111 us -> 110 us (level)
  no operation moved by 1% of the time
where the time goes in v13:
time: 110 us
  blocking collectives  38.7 us (35%)
  starting transfers between devices  22.6 us (21%)
  Pallas kernels  21.3 us (19%)
  waiting for transfers between devices  18.7 us (17%)
  local copies, waits for them, and re-layouts  7.73 us (7%)
    all_to_all x2, blocking collectives, to_all(): return lax.all_to_all(x, axes, split_axis=0, concat_axis=0, tiled=True)  38.7 us
    pallas_call x10, Pallas kernels, call(): pl.pallas_call(body, out_shape=list(outs), in_specs=in_specs, out_specs=o...  21.3 us
    ppermute x10, starting transfers between devices, exchange(): lax.ppermute(block, axis, route(axis, way))  13.5 us
    all_to_all x1, waiting for transfers between devices, to_all(): return lax.all_to_all(x, axes, split_axis=0, concat_axis=0, tiled=True)  9.71 us
    ppermute x10, waiting for transfers between devices, exchange(): lax.ppermute(block, axis, route(axis, way))  9.02 us
    all_to_all x1, starting transfers between devices, to_all(): return lax.all_to_all(x, axes, split_axis=0, concat_axis=0, tiled=True)  8.5 us
    unnamed x38, local copies, waits for them, and re-layouts  7.73 us
  transfers between devices with their start and end apart: 13, of which 4 were waited for; matrix products, arithmetic and copies ran while one was open for 0% of the time, Pallas kernels for 8%

profile of v13, /device:TPU:0, one launch (start us, length us, event | category | flops | bytes accessed | tf_op | source)
XLA Modules:
  0.0 109.9 jit_solution(9605098962318055338)
XLA Ops:
  0.6 4.1 %shard_map.137 = f32[16,104,128]{2,1,0:T(8,128)} custom-call(s32[6]{0:T(128)} %bitcast.25, s32[1,256]{1,0:T(1,128)} %bitcast.32, s32[1,256]{1,0:T(1,128)} %bitcast.37, f32[768,512]{1,0:T(8,128)} %bitcast.15, f32[768,256]{1,0:T(8,128)} %bitcast.21), custom_call_target="tpu_custom_call" | custom-call | flops 603979776 | bytes 3145728 | tf_op jit(solution)/shard_map/pallas_call | solution.py:37
  4.8 8.5 %all-to-all-start = ((f32[16,104,128]{2,1,0:T(8,128)}), f32[16,104,128]{2,1,0:T(8,128)}, u32[]{:S(2)}, u32[]{:S(2)}) async-start(f32[16,104,128]{2,1,0:T(8,128)} %shard_map.137), calls=%async_computation | async-start | bytes 1703936 | tf_op jit(solution)/shard_map/all_to_all | solution.py:454
  13.3 1.7 %copy-done.5 = f32[1,1,1,768,768]{4,3,2,1,0:T(8,128)S(1)} copy-done((f32[1,1,1,768,768]{4,3,2,1,0:T(8,128)S(1)}, f32[1,1,1,768,768]{4,3,2,1,0:T(8,128)}, u32[]{:S(2)}) %copy-start.5) | copy-done | bytes 2359320
  15.0 1.7 %copy-done.6 = f32[1,1,1,768,768]{4,3,2,1,0:T(8,128)S(1)} copy-done((f32[1,1,1,768,768]{4,3,2,1,0:T(8,128)S(1)}, f32[1,1,1,768,768]{4,3,2,1,0:T(8,128)}, u32[]{:S(2)}) %copy-start.6) | copy-done | bytes 2359320
  16.7 3.5 %shard_map.138 = (f32[768,512]{1,0:T(8,128)S(1)}, f32[1,512]{1,0:T(1,128)S(1)}, f32[1,512]{1,0:T(1,128)S(1)}, bf16[256,384]{1,0:T(8,128)(2,1)S(1)}, bf16[768,256...) custom-call(s32[6]{0:T(128)S(1)} %bitcast.26, ...), custom_call_target="tpu_custom_call" | custom-call | flops 1811939328 | bytes 10223616 | tf_op jit(solution)/shard_map/pallas_call | solution.py:37
  20.2 1.0 copy-done.2
  21.2 1.1 %copy-done.7 = f32[768,512]{1,0:T(8,128)} copy-done((f32[768,512]{1,0:T(8,128)}, f32[768,512]{1,0:T(8,128)S(1)}, u32[]{:S(2)}) %copy-start.7) | copy-done | bytes 1572888
  24.5 9.7 %all-to-all-done.incoming_any = f32[16,104,128]{2,1,0:T(8,128)} async-done(((f32[16,104,128]{2,1,0:T(8,128)}), f32[16,104,128]{2,1,0:T(8,128)}, u32[]{:S(2)}, u32[]{:S(2)}) %all-to-all-start) | async-done | bytes 852000 | tf_op jit(solution)/shard_map/all_to_all | solution.py:454
  34.3 2.6 %shard_map.139 = f32[16,104,128]{2,1,0:T(8,128)S(1)} custom-call(f32[16,104,128]{2,1,0:T(8,128)} %all-to-all-done.incoming_any, f32[256,256]{1,0:T(8,128)} %bitcast.39, f32[1,512]{1,0:T(1,128)S(1)} %get-tuple-element.37.local_part_ref, f32[1,512]{1,0:T(1,128)S(1)} %get-tuple-element.38.square_ref), custom_call_target="tpu_custom_call" | custom-call | flops 603979776 | bytes 1572864 | tf_op jit(solution)/shard_map/pallas_call | solution.py:37
  36.9 26.4 %all_to_all.15.returned_ref = f32[16,104,128]{2,1,0:T(8,128)S(1)} all-to-all(f32[16,104,128]{2,1,0:T(8,128)S(1)} %shard_map.139), channel_id=1, replica_groups=mesh['blk'=4,'lat'=4,'depth'=2] {'blk','lat'}, dimensions={0} | all-to-all | bytes 1703936 | tf_op jit(solution)/shard_map/all_to_all | solution.py:454
  63.3 1.3 %shard_map.140 = (f32[768,512]{1,0:T(8,128)S(1)}, f32[8,128]{1,0:T(8,128)S(1)}, f32[128,512]{1,0:T(8,128)S(1)}, f32[128,512]{1,0:T(8,128)S(1)}, f32[128,512]{1,0...) custom-call(f32[16,104,128]{2,1,0:T(8,128)S(1)} %all_to_all.15.returned_ref, ...), custom_call_target="tpu_custom_call" | custom-call | flops 805306368 | bytes 6291456 | tf_op jit(solution)/shard_map/pallas_call | solution.py:37
  64.6 1.1 collective-permute-start
  66.7 2.8 %collective-permute-start.4 = (f32[128,512]{1,0:T(8,128)S(1)}, f32[128,512]{1,0:T(8,128)S(1)}, u32[]{:S(2)}, u32[]{:S(2)}) collective-permute-start(f32[128,512]{1,0:T(8,128)S(1)} %get-tuple-element.53), channel_id=1, source_target_pairs={{0,24},{8,0},{16,8},{24,16},{1,25},{9,1},{17,9},{25,17},{2,26},{10... | collective-permute-start | bytes 786440 | tf_op jit(solution)/shard_map/ppermute | solution.py:299
  70.2 5.1 %collective-permute-done.refs_0_ = f32[128,512]{1,0:T(8,128)S(1)} collective-permute-done((f32[128,512]{1,0:T(8,128)S(1)}, f32[128,512]{1,0:T(8,128)S(1)}, u32[]{:S(2)}, u32[]{:S(2)}) %collective-permute-start) | collective-permute-done | bytes 262176 | tf_op jit(solution)/shard_map/ppermute | solution.py:299
  75.3 2.6 %shard_map.141 = (f32[1,512]{1,0:T(1,128)}, f32[1,512]{1,0:T(1,128)S(1)}, f32[1,512]{1,0:T(1,128)S(1)}, f32[512,512]{1,0:T(8,128)S(1)}, f32[768,512]{1,0:T(8,128)S(1)}) custom-call(s32[6]{0:T(128)S(1)} %bitcast.27, f32[8,128]{1,0:T(8,128)S(1)} %get-tuple-element.43.sums_ref, f32[1,512]{1,0:T(1,128)S(1)} %bitcast.34, ...), custom_call_target="tpu_custom_call" | custom-call | flops 1207959552 | bytes 8650752 | tf_op jit(solution)/shard_map/pallas_call | solution.py:37
  77.9 1.5 %shard_map.142 = (f32[256,512]{1,0:T(8,128)S(1)}, f32[768,512]{1,0:T(8,128)S(1)}, f32[128,512]{1,0:T(8,128)S(1)}, f32[128,512]{1,0:T(8,128)S(1)}, f32[128,512]{1...) custom-call(s32[6]{0:T(128)S(1)} %bitcast.28, f32[1,512]{1,0:T(1,128)S(1)} %get-tuple-element.51.beta_ref, ...), custom_call_target="tpu_custom_call" | custom-call | flops 603979776 | bytes 8650752 | tf_op jit(solution)/shard_map/pallas_call | solution.py:37
  80.1 3.3 %collective-permute-start.7 = (f32[128,512]{1,0:T(8,128)S(1)}, f32[128,512]{1,0:T(8,128)S(1)}, u32[]{:S(2)}, u32[]{:S(2)}) collective-permute-start(f32[128,512]{1,0:T(8,128)S(1)} %get-tuple-element.58), channel_id=1, source_target_pairs={{0,2},{2,0},{4,6},{6,4},{1,3},{3,1},{5,7},{7,5},{8,10},{10,8},{12,... | collective-permute-start | bytes 786440 | tf_op jit(solution)/shard_map/ppermute | solution.py:299
  83.4 3.7 %collective-permute-start.8 = (f32[128,512]{1,0:T(8,128)S(1)}, f32[128,512]{1,0:T(8,128)S(1)}, u32[]{:S(2)}, u32[]{:S(2)}) collective-permute-start(f32[128,512]{1,0:T(8,128)S(1)} %get-tuple-element.59), channel_id=1, source_target_pairs={{0,24},{8,0},{16,8},{24,16},{1,25},{9,1},{17,9},{25,17},{2,26},{10... | collective-permute-start | bytes 786440 | tf_op jit(solution)/shard_map/ppermute | solution.py:299
  87.9 2.7 %collective-permute-done.6.arrived.refs_0_ = f32[128,512]{1,0:T(8,128)S(1)} collective-permute-done((f32[128,512]{1,0:T(8,128)S(1)}, f32[128,512]{1,0:T(8,128)S(1)}, u32[]{:S(2)}, u32[]{:S(2)}) %collective-permute-start.6) | collective-permute-done | bytes 262176 | tf_op jit(solution)/shard_map/ppermute | solution.py:299
  90.6 1.3 %shard_map.144.refs_5_ = f32[8,128]{1,0:T(8,128)S(1)} custom-call(s32[6]{0:T(128)S(1)} %bitcast.29, f32[512,512]{1,0:T(8,128)S(1)} %get-tuple-element.50.near_ref, f32[256,512]{1,0:T(8,128)S(1)} %get-tuple-element.55.far_ref, f32[768,512]{1,0:T(8,128)S(1)} %get-tuple-element.56.schur_ref, f32[768,512]{1,0:T(8,128)S(1)} %bitcast.17, ...), custom_call_target="tpu_custom_call" | custom-call | flops 1572864 | bytes 4718592 | tf_op jit(solution)/shard_map/pallas_call | solution.py:37
  92.0 1.2 %shard_map.143.stored = f32[768,512]{1,0:T(8,128)} custom-call(f32[512,512]{1,0:T(8,128)S(1)} %get-tuple-element.50.near_ref, f32[256,512]{1,0:T(8,128)S(1)} %get-tuple-element.55.far_ref), custom_call_target="tpu_custom_call" | custom-call | bytes 3145728 | tf_op jit(solution)/shard_map/pallas_call | solution.py:37
  93.2 1.2 %collective-permute-done.8.refs_2_ = f32[128,512]{1,0:T(8,128)S(1)} collective-permute-done((f32[128,512]{1,0:T(8,128)S(1)}, f32[128,512]{1,0:T(8,128)S(1)}, u32[]{:S(2)}, u32[]{:S(2)}) %collective-permute-start.8) | collective-permute-done | bytes 262176 | tf_op jit(solution)/shard_map/ppermute | solution.py:299
  95.2 12.4 %all_to_all.16.sums_ref = f32[32,8,128]{2,1,0:T(8,128)S(1)} all-to-all(f32[32,8,128]{2,1,0:T(8,128)S(1)} %get-tuple-element.62), channel_id=1, replica_groups=mesh['blk'=4,'lat'=4,'depth'=2] {'depth','blk','lat'}, dimensions={0} | all-to-all | bytes 262144 | tf_op jit(solution)/shard_map/all_to_all | solution.py:454
  107.6 2.4 %shard_map.146 = (f32[768,512]{1,0:T(8,128)}, f32[1,512]{1,0:T(1,128)}, f32[1,512]{1,0:T(1,128)}) custom-call(s32[6]{0:T(128)S(1)} %bitcast.31, f32[32,8,128]{2,1,0:T(8,128)S(1)} %all_to_all.16.sums_ref, f32[1,512]{1,0:T(1,128)S(1)} %copy-done.18, f32[1,512]{1,0:T(1,128)S(1)} %get-tuple-element.64.square_ref, f32[768,512]{1,0:T(8,128)S(1)} %bitcast.18, ...), custom_call_target="tpu_custom_call" | custom-call | flops 1572864 | bytes 4718592 | tf_op jit(solution)/shard_map/pallas_call | solution.py:37
  (52 shorter events, 6.3 us)
Async XLA Ops:
  0.6 12.7 %copy-start.4 = (f32[1,1,1,768,256]{4,3,2,1,0:T(8,128)S(1)}, f32[1,1,1,768,256]{4,3,2,1,0:T(8,128)}, u32[]{:S(2)}) copy-start(f32[1,1,1,768,256]{4,3,2,1,0:T(8,128)} %param.16) | copy-start | bytes 2359300
  4.7 8.6 %copy-start = (f32[1,1,1,768,512]{4,3,2,1,0:T(8,128)S(1)}, f32[1,1,1,768,512]{4,3,2,1,0:T(8,128)}, u32[]{:S(2)}) copy-start(f32[1,1,1,768,512]{4,3,2,1,0:T(8,128)} %param.11) | copy-start | bytes 4718596
  4.8 8.6 %copy-start.15 = (s32[1,1,1,6]{3,2,1,0:T(1,128)S(1)}, s32[1,1,1,6]{3,2,1,0:T(1,128)}, u32[]{:S(2)}) copy-start(s32[1,1,1,6]{3,2,1,0:T(1,128)} %param.10) | copy-start | bytes 76
  4.8 29.5 %all-to-all-start = ((f32[16,104,128]{2,1,0:T(8,128)}), f32[16,104,128]{2,1,0:T(8,128)}, u32[]{:S(2)}, u32[]{:S(2)}) async-start(f32[16,104,128]{2,1,0:T(8,128)} %shard_map.137), calls=%async_computation | async-start | bytes 1703936 | tf_op jit(solution)/shard_map/all_to_all | solution.py:454
  34.2 29.0 %copy-start.8 = (f32[768,512]{1,0:T(8,128)S(1)}, f32[768,512]{1,0:T(8,128)}, u32[]{:S(2)}) copy-start(f32[768,512]{1,0:T(8,128)} %copy-done.7) | copy-start | bytes 4718596
  34.2 29.0 %copy-start.10 = (bf16[768,256]{1,0:T(8,128)(2,1)S(1)}, bf16[768,256]{1,0:T(8,128)(2,1)}, u32[]{:S(2)}) copy-start(bf16[768,256]{1,0:T(8,128)(2,1)} %copy-done.9) | copy-start | bytes 1179652
  34.2 29.0 %copy-start.12 = (bf16[768,256]{1,0:T(8,128)(2,1)S(1)}, bf16[768,256]{1,0:T(8,128)(2,1)}, u32[]{:S(2)}) copy-start(bf16[768,256]{1,0:T(8,128)(2,1)} %copy-done.11) | copy-start | bytes 1179652
  34.3 29.0 %copy-start.14 = (bf16[256,384]{1,0:T(8,128)(2,1)S(1)}, bf16[256,384]{1,0:T(8,128)(2,1)}, u32[]{:S(2)}) copy-start(bf16[256,384]{1,0:T(8,128)(2,1)} %copy-done.13) | copy-start | bytes 589828
  63.3 12.1 %copy-start.1 = (f32[1,1,1,768,512]{4,3,2,1,0:T(8,128)S(1)}, f32[1,1,1,768,512]{4,3,2,1,0:T(8,128)}, u32[]{:S(2)}) copy-start(f32[1,1,1,768,512]{4,3,2,1,0:T(8,128)} %param.12) | copy-start | bytes 4718596
  63.3 12.1 %copy-start.3 = (bf16[768,768]{1,0:T(8,128)(2,1)S(1)}, bf16[768,768]{1,0:T(8,128)(2,1)}, u32[]{:S(2)}) copy-start(bf16[768,768]{1,0:T(8,128)(2,1)} %copy-done.2) | copy-start | bytes 3538948
  63.3 12.1 %copy-start.17 = (f32[512]{0:T(512)S(1)}, f32[512]{0:T(512)}, u32[]{:S(2)}) copy-start(f32[512]{0:T(512)} %param.13) | copy-start | bytes 6148
  64.6 10.7 %collective-permute-start = (f32[128,512]{1,0:T(8,128)S(1)}, f32[128,512]{1,0:T(8,128)S(1)}, u32[]{:S(2)}, u32[]{:S(2)}) collective-permute-start(f32[128,512]{1,0:T(8,128)S(1)} %get-tuple-element.47), channel_id=1, source_target_pairs={{0,8},{8,16},{16,24},{24,0},{1,9},{9,17},{17,25},{25,1},{2,10},{10... | collective-permute-start | bytes 786440 | tf_op jit(solution)/shard_map/ppermute | solution.py:299
  65.6 9.7 %collective-permute-start.1 = (f32[128,512]{1,0:T(8,128)S(1)}, f32[128,512]{1,0:T(8,128)S(1)}, u32[]{:S(2)}, u32[]{:S(2)}) collective-permute-start(f32[128,512]{1,0:T(8,128)S(1)} %get-tuple-element.48), channel_id=1, source_target_pairs={{0,2},{2,0},{4,6},{6,4},{1,3},{3,1},{5,7},{7,5},{8,10},{10,8},{12,... | collective-permute-start | bytes 786440 | tf_op jit(solution)/shard_map/ppermute | solution.py:299
  66.2 9.1 %collective-permute-start.2 = (f32[128,512]{1,0:T(8,128)S(1)}, f32[128,512]{1,0:T(8,128)S(1)}, u32[]{:S(2)}, u32[]{:S(2)}) collective-permute-start(f32[128,512]{1,0:T(8,128)S(1)} %get-tuple-element.49), channel_id=1, source_target_pairs={{0,1},{1,0},{2,3},{3,2},{4,5},{5,4},{6,7},{7,6},{8,9},{9,8},{10,11... | collective-permute-start | bytes 786440 | tf_op jit(solution)/shard_map/ppermute | solution.py:299
  66.2 3.3 %collective-permute-start.3 = (f32[8,128]{1,0:T(8,128)S(1)}, f32[8,128]{1,0:T(8,128)S(1)}, u32[]{:S(2)}, u32[]{:S(2)}) collective-permute-start(f32[8,128]{1,0:T(8,128)S(1)} %get-tuple-element.43.sums_ref), channel_id=1, source_target_pairs={{0,1},{1,0},{2,3},{3,2},{4,5},{5,4},{6,7},{7,6},{8,9},{9,8},{10,11... | collective-permute-start | bytes 12296 | tf_op jit(solution)/shard_map/ppermute | solution.py:551
  66.7 11.2 %collective-permute-start.4 = (f32[128,512]{1,0:T(8,128)S(1)}, f32[128,512]{1,0:T(8,128)S(1)}, u32[]{:S(2)}, u32[]{:S(2)}) collective-permute-start(f32[128,512]{1,0:T(8,128)S(1)} %get-tuple-element.53), channel_id=1, source_target_pairs={{0,24},{8,0},{16,8},{24,16},{1,25},{9,1},{17,9},{25,17},{2,26},{10... | collective-permute-start | bytes 786440 | tf_op jit(solution)/shard_map/ppermute | solution.py:299
  69.5 8.4 %collective-permute-start.5 = (f32[128,512]{1,0:T(8,128)S(1)}, f32[128,512]{1,0:T(8,128)S(1)}, u32[]{:S(2)}, u32[]{:S(2)}) collective-permute-start(f32[128,512]{1,0:T(8,128)S(1)} %get-tuple-element.54), channel_id=1, source_target_pairs={{2,4},{4,2},{3,5},{5,3},{10,12},{12,10},{11,13},{13,11},{18,20},{2... | collective-permute-start | bytes 786440 | tf_op jit(solution)/shard_map/ppermute | solution.py:299
  79.4 11.1 %collective-permute-start.6 = (f32[128,512]{1,0:T(8,128)S(1)}, f32[128,512]{1,0:T(8,128)S(1)}, u32[]{:S(2)}, u32[]{:S(2)}) collective-permute-start(f32[128,512]{1,0:T(8,128)S(1)} %get-tuple-element.57), channel_id=1, source_target_pairs={{0,8},{8,16},{16,24},{24,0},{1,9},{9,17},{17,25},{25,1},{2,10},{10... | collective-permute-start | bytes 786440 | tf_op jit(solution)/shard_map/ppermute | solution.py:299
  80.1 13.1 %collective-permute-start.7 = (f32[128,512]{1,0:T(8,128)S(1)}, f32[128,512]{1,0:T(8,128)S(1)}, u32[]{:S(2)}, u32[]{:S(2)}) collective-permute-start(f32[128,512]{1,0:T(8,128)S(1)} %get-tuple-element.58), channel_id=1, source_target_pairs={{0,2},{2,0},{4,6},{6,4},{1,3},{3,1},{5,7},{7,5},{8,10},{10,8},{12,... | collective-permute-start | bytes 786440 | tf_op jit(solution)/shard_map/ppermute | solution.py:299
  83.4 11.0 %collective-permute-start.8 = (f32[128,512]{1,0:T(8,128)S(1)}, f32[128,512]{1,0:T(8,128)S(1)}, u32[]{:S(2)}, u32[]{:S(2)}) collective-permute-start(f32[128,512]{1,0:T(8,128)S(1)} %get-tuple-element.59), channel_id=1, source_target_pairs={{0,24},{8,0},{16,8},{24,16},{1,25},{9,1},{17,9},{25,17},{2,26},{10... | collective-permute-start | bytes 786440 | tf_op jit(solution)/shard_map/ppermute | solution.py:299
  87.1 7.2 %collective-permute-start.9 = (f32[128,512]{1,0:T(8,128)S(1)}, f32[128,512]{1,0:T(8,128)S(1)}, u32[]{:S(2)}, u32[]{:S(2)}) collective-permute-start(f32[128,512]{1,0:T(8,128)S(1)} %get-tuple-element.60), channel_id=1, source_target_pairs={{2,4},{4,2},{3,5},{5,3},{10,12},{12,10},{11,13},{13,11},{18,20},{2... | collective-permute-start | bytes 786440 | tf_op jit(solution)/shard_map/ppermute | solution.py:299
  87.8 6.6 %collective-permute-start.10 = (f32[128,512]{1,0:T(8,128)S(1)}, f32[128,512]{1,0:T(8,128)S(1)}, u32[]{:S(2)}, u32[]{:S(2)}) collective-permute-start(f32[128,512]{1,0:T(8,128)S(1)} %get-tuple-element.61), channel_id=1, source_target_pairs={{0,1},{1,0},{2,3},{3,2},{4,5},{5,4},{6,7},{7,6},{8,9},{9,8},{10,11... | collective-permute-start | bytes 786440 | tf_op jit(solution)/shard_map/ppermute | solution.py:299
  91.9 2.5 %collective-permute-start.11 = (f32[8,128]{1,0:T(8,128)S(1)}, f32[8,128]{1,0:T(8,128)S(1)}, u32[]{:S(2)}, u32[]{:S(2)}) collective-permute-start(f32[8,128]{1,0:T(8,128)S(1)} %shard_map.144.refs_5_), channel_id=1, source_target_pairs={{0,1},{1,0},{2,3},{3,2},{4,5},{5,4},{6,7},{7,6},{8,9},{9,8},{10,11... | collective-permute-start | bytes 12296 | tf_op jit(solution)/shard_map/ppermute | solution.py:586
  93.1 14.4 %copy-start.18 = (f32[1,512]{1,0:T(1,128)S(1)}, f32[1,512]{1,0:T(1,128)}, u32[]{:S(2)}) copy-start(f32[1,512]{1,0:T(1,128)} %get-tuple-element.63.rho_ref) | copy-start | bytes 6148
  (8 other events, 16.2 us)

commit v14 on v13

--- a/solution.py
+++ b/solution.py
@@ -102,13 +102,13 @@
     owners = out_ref.shape[0]
     for j in range(block.shape[1] // LANES):
         piece = block[:, j * LANES : (j + 1) * LANES]
-        out_ref[:, j * CAP : (j + 1) * CAP, :] = piece.reshape(owners, CAP, LANES)
+        out_ref[:, j * CAP : (j + 1) * CAP, 0, :] = piece.reshape(owners, CAP, LANES)
 
 
 def get_slab(ref, pieces):
     slots = ref.shape[0] * CAP
     return jnp.concatenate(
-        [ref[:, j * CAP : (j + 1) * CAP, :].reshape(slots, LANES) for j in range(pieces)], axis=1
+        [ref[:, j * CAP : (j + 1) * CAP, 0, :].reshape(slots, LANES) for j in range(pieces)], axis=1
     )
 
 
@@ -156,6 +156,8 @@
     for copy in small:
         copy.wait()
 
+    squares = []
+
     def term_of(pair):
         for copy in large[pair]:
             copy.wait()
@@ -164,6 +166,7 @@
             axis=0,
         )
         basis = basis_ref[2 * pair * rows : 2 * (pair + 1) * rows, :]
+        squares.append(jnp.sum(weighted * weighted, axis=0, keepdims=True))
         return product(parts(jnp.transpose(basis)), parts(weighted))
 
     terms = term_of(0)
@@ -180,17 +183,15 @@
     terms += term_of(1)
     terms += term_of(2)
     put_slab(slab_ref, select(packer, terms))
-    tail = slab_ref.shape[1] - tiles(id_rows(slots))
-    names = jnp.concatenate(
-        [names, jnp.zeros((owners, (slab_ref.shape[1] - tail) * LANES - names.shape[1]), f32)], axis=1
-    )
-    for j in range(slab_ref.shape[1] - tail):
-        slab_ref[:, tail + j, :] = names[:, j * LANES : (j + 1) * LANES]
+    square = 4.0 * (squares[0] + squares[1] + squares[2])
+    pieces = folded(names) + [jnp.broadcast_to(x, (owners, LANES)) for x in folded(square)]
+    for j, piece in enumerate(pieces):
+        slab_ref[:, slab_ref.shape[1] - len(pieces) + j, 0, :] = piece
 
 
 def local_kernel(len_ref, residual_ref, matrix_ref, owner_ref, *refs):
     whole, refs = refs[:2], refs[2:]
-    local_ref, part_ref, square_ref, table_ref, refs = *refs[:4], refs[4:]
+    local_ref, part_ref, table_ref, refs = *refs[:3], refs[3:]
     rows = residual_ref.shape[0] // 6
     live = jnp.concatenate(
         [masked(len_ref, residual_ref, face, rows) for face in range(6)], axis=0
@@ -198,7 +199,6 @@
     local = product(parts(matrix_ref[...]), parts(0.5 * live))
     local_ref[...] = local
     part_ref[...] = jnp.sum(live * local, axis=0, keepdims=True)
-    square_ref[...] = jnp.sum(live * live, axis=0, keepdims=True)
     refs[0][...], refs[1][...] = parts(whole[0][...])
     for i, move in enumerate(NEAR + FAR):
         at = slice(i * rows, (i + 1) * rows)
@@ -210,9 +210,9 @@
     table_ref[...] = one_hot(lax.broadcasted_iota(jnp.int32, (primal, slots), 1) == slot_col)
 
 
-def solve_kernel(incoming_any, inverse_any, local_part_ref, square_ref, answer_ref, *refs):
+def solve_kernel(incoming_any, inverse_any, local_part_ref, answer_ref, square_ref, *refs):
     names_ref, slab_ref, inverse_ref, sems = refs
-    owners, height, _ = slab_ref.shape
+    owners, height, _, _ = slab_ref.shape
     pieces = height // CAP
     half = pieces // 2 * CAP
     copies = [
@@ -233,7 +233,10 @@
         copy.start()
     copies[0].wait()
     slots, owned = owners * CAP, inverse_ref.shape[0]
-    wanted = unfolded(jnp.sum(names_ref[...], axis=0), 0, id_rows(slots))[:, :slots]
+    told = [jnp.sum(names_ref[:, j, 0, :], axis=0, keepdims=True) for j in range(names_ref.shape[1])]
+    for j, piece in enumerate(told[id_rows(slots) :]):
+        square_ref[j : j + 1, :] = piece
+    wanted = jnp.concatenate(told[: id_rows(slots)], axis=1)[:, :slots]
     (wanted_col,) = columns(wanted)
     row_at = lax.broadcasted_iota(jnp.int32, (owned, slots), 0).astype(f32) + 1.0
     col_at = lax.broadcasted_iota(jnp.int32, (slots, owned), 1).astype(f32) + 1.0
@@ -247,11 +250,8 @@
     solved = product(inverse, parts(summed))
     put_slab(answer_ref, select(table, solved))
     total = local_part_ref[...] + 2.0 * jnp.sum(summed * solved, axis=0, keepdims=True)
-    sums = folded(total) + folded(square_ref[...])
-    sums += [jnp.zeros((1, LANES), f32)] * (tiles(len(sums)) - len(sums))
-    answer_ref[:, pieces * CAP :, :] = jnp.broadcast_to(
-        jnp.concatenate(sums, axis=0)[None], (owners, len(sums), LANES)
-    )
+    for j, piece in enumerate(folded(total)):
+        answer_ref[:, height + j, 0, :] = jnp.broadcast_to(piece, (owners, LANES))
 
 
 NEAR = (("blk", "up"), ("lat", 0), ("depth", 0), ("depth", 1))
@@ -301,7 +301,7 @@
     ]
 
 
-def image_kernel(pair_depth, returned_ref, table_ref, high_ref, low_ref, local_ref, image_ref, sums_ref, *face_refs):
+def image_kernel(pair_depth, returned_ref, square_ref, table_ref, high_ref, low_ref, local_ref, image_ref, sums_ref, *face_refs):
     rows = local_ref.shape[0] // 6
     width = local_ref.shape[1]
     folds = width // LANES
@@ -309,7 +309,14 @@
     image = local_ref[...] + product((high_ref[...], low_ref[...]), parts(correction))
     image_ref[...] = image
     put_faces(image_ref, rows, FIRST, face_refs)
-    tail = jnp.sum(returned_ref[:, folds * CAP :, :], axis=0)
+    tail = jnp.concatenate(
+        [
+            jnp.sum(returned_ref[:, folds * CAP + j, 0, :], axis=0, keepdims=True)
+            for j in range(folds)
+        ]
+        + [square_ref[...]],
+        axis=0,
+    )
     if pair_depth:
         sums_ref[...] = tail
     else:
@@ -477,8 +484,8 @@
     pair_depth = layers == 2
     scale = 0.5 / (devices * height)
     folds = width // LANES
-    tail = tiles(2 * folds)
-    id_tail = tiles(id_rows(slots))
+    tail = 2 * folds
+    id_tail = id_rows(slots) + folds
 
     lengths = face_len.reshape(6)
     residual = residual.reshape(height, width)
@@ -495,7 +502,7 @@
 
     (outgoing,) = call(
         pack_kernel,
-        [shape_of(owners, folds * CAP + id_tail, LANES)],
+        [shape_of(owners, folds * CAP + id_tail, 1, LANES)],
         [lengths, owner, wanted, residual, basis],
         far=range(5),
         flops=6 * height * primal * width,
@@ -511,9 +518,9 @@
         ],
     )
     incoming = to_all(outgoing, LAYER)
-    local, local_part, square, table, *halves = call(
+    local, local_part, table, *halves = call(
         local_kernel,
-        [whole, row, row, shape_of(primal, slots, dtype=bf16)]
+        [whole, row, shape_of(primal, slots, dtype=bf16)]
         + [shape_of(height, primal, dtype=bf16)] * 2
         + [shape_of(height, height, dtype=bf16)] * 2,
         [lengths, residual, neumann, owner, basis, schur],
@@ -522,16 +529,16 @@
         moved=4 * height * (3 * height + 2 * width),
     )
     basis_halves, schur_halves = halves[:2], halves[2:]
-    (answers,) = call(
+    answers, square = call(
         solve_kernel,
-        [shape_of(owners, folds * CAP + tail, LANES)],
-        [incoming, inverse, local_part, square],
+        [shape_of(owners, folds * CAP + folds, 1, LANES), shape_of(folds, LANES)],
+        [incoming, inverse, local_part],
         far=range(2),
         flops=(8 * slots + 6 * owned) * owned * width,
         moved=8 * slots * width,
         scratch=[
-            pltpu.VMEM((owners, id_tail, LANES), f32),
-            pltpu.VMEM((owners, folds * CAP, LANES), f32),
+            pltpu.VMEM((owners, id_tail, 1, LANES), f32),
+            pltpu.VMEM((owners, folds * CAP, 1, LANES), f32),
             pltpu.VMEM((owned, owned), f32),
             pltpu.SemaphoreType.DMA((4,)),
         ],
@@ -542,7 +549,7 @@
     image, sums, *outward = call(
         functools.partial(image_kernel, pair_depth),
         [whole, shape_of(tail, LANES) if pair_depth else shape_of(layers, tail, LANES), *faces],
-        [returned, table, *basis_halves, local],
+        [returned, square, table, *basis_halves, local],
         flops=(6 * height + 4 * slots) * primal * width,
         moved=16 * height * width,
     )

time: 110 us -> 111 us (level)
  Pallas kernels: 21.3 us -> 22.6 us
    pallas_call x10, Pallas kernels: 21.3 us -> 22.6 us  [call(): pl.pallas_call(body, out_shape=list(outs), in_specs=in_specs, out_specs=o...]
where the time goes in v14:
time: 111 us
  blocking collectives  37.9 us (34%)
  Pallas kernels  22.6 us (20%)
  starting transfers between devices  22.6 us (20%)
  waiting for transfers between devices  18.8 us (17%)
  local copies, waits for them, and re-layouts  7.72 us (7%)
    all_to_all x2, blocking collectives, to_all(): return lax.all_to_all(x, axes, split_axis=0, concat_axis=0, tiled=True)  37.9 us
    pallas_call x10, Pallas kernels, call(): pl.pallas_call(body, out_shape=list(outs), in_specs=in_specs, out_specs=o...  22.6 us
    ppermute x10, starting transfers between devices, exchange(): lax.ppermute(block, axis, route(axis, way))  13.5 us
    all_to_all x1, waiting for transfers between devices, to_all(): return lax.all_to_all(x, axes, split_axis=0, concat_axis=0, tiled=True)  9.61 us
    ppermute x10, waiting for transfers between devices, exchange(): lax.ppermute(block, axis, route(axis, way))  9.17 us
    all_to_all x1, starting transfers between devices, to_all(): return lax.all_to_all(x, axes, split_axis=0, concat_axis=0, tiled=True)  8.5 us
    unnamed x38, local copies, waits for them, and re-layouts  7.72 us
  transfers between devices with their start and end apart: 13, of which 4 were waited for; matrix products, arithmetic and copies ran while one was open for 0% of the time, Pallas kernels for 8%

profile of v14, /device:TPU:0, one launch (start us, length us, event | category | flops | bytes accessed | tf_op | source)
XLA Modules:
  0.0 110.5 jit_solution(15480258359375912148)
XLA Ops:
  0.6 4.5 %shard_map.137 = f32[16,103,1,128]{3,2,1,0:T(1,128)} custom-call(s32[6]{0:T(128)} %bitcast.25, s32[1,256]{1,0:T(1,128)} %bitcast.32, s32[1,256]{1,0:T(1,128)} %bitcast.37, f32[768,512]{1,0:T(8,128)} %bitcast.15, f32[768,256]{1,0:T(8,128)} %bitcast.21), custom_call_target="tpu_custom_call" | custom-call | flops 603979776 | bytes 3145728 | tf_op jit(solution)/shard_map/pallas_call | solution.py:37
  5.2 8.5 %all-to-all-start = ((f32[16,103,1,128]{3,2,1,0:T(1,128)}), f32[16,103,1,128]{3,2,1,0:T(1,128)}, u32[]{:S(2)}, u32[]{:S(2)}) async-start(f32[16,103,1,128]{3,2,1,0:T(1,128)} %shard_map.137), calls=%async_computation | async-start | bytes 1687552 | tf_op jit(solution)/shard_map/all_to_all | solution.py:461
  13.7 1.7 %copy-done.5 = f32[1,1,1,768,768]{4,3,2,1,0:T(8,128)S(1)} copy-done((f32[1,1,1,768,768]{4,3,2,1,0:T(8,128)S(1)}, f32[1,1,1,768,768]{4,3,2,1,0:T(8,128)}, u32[]{:S(2)}) %copy-start.5) | copy-done | bytes 2359320
  15.4 1.7 %copy-done.6 = f32[1,1,1,768,768]{4,3,2,1,0:T(8,128)S(1)} copy-done((f32[1,1,1,768,768]{4,3,2,1,0:T(8,128)S(1)}, f32[1,1,1,768,768]{4,3,2,1,0:T(8,128)}, u32[]{:S(2)}) %copy-start.6) | copy-done | bytes 2359320
  17.0 3.5 %shard_map.138 = (f32[768,512]{1,0:T(8,128)S(1)}, f32[1,512]{1,0:T(1,128)S(1)}, bf16[256,384]{1,0:T(8,128)(2,1)S(1)}, bf16[768,256]{1,0:T(8,128)(2,1)S(1)}, bf16...) custom-call(s32[6]{0:T(128)S(1)} %bitcast.26, f32[768,512]{1,0:T(8,128)S(1)} %bitcast.16, ...), custom_call_target="tpu_custom_call" | custom-call | flops 1811939328 | bytes 10223616 | tf_op jit(solution)/shard_map/pallas_call | solution.py:37
  20.5 1.0 copy-done.2
  21.5 1.1 %copy-done.7 = f32[768,512]{1,0:T(8,128)} copy-done((f32[768,512]{1,0:T(8,128)}, f32[768,512]{1,0:T(8,128)S(1)}, u32[]{:S(2)}) %copy-start.7) | copy-done | bytes 1572888
  24.9 9.6 %all-to-all-done.incoming_any = f32[16,103,1,128]{3,2,1,0:T(1,128)} async-done(((f32[16,103,1,128]{3,2,1,0:T(1,128)}), f32[16,103,1,128]{3,2,1,0:T(1,128)}, u32[]{:S(2)}, u32[]{:S(2)}) %all-to-all-start) | async-done | bytes 843808 | tf_op jit(solution)/shard_map/all_to_all | solution.py:461
  34.5 3.3 %shard_map.139 = (f32[16,100,1,128]{3,2,1,0:T(1,128)S(1)}, f32[4,128]{1,0:T(4,128)S(1)}) custom-call(f32[16,103,1,128]{3,2,1,0:T(1,128)} %all-to-all-done.incoming_any, f32[256,256]{1,0:T(8,128)} %bitcast.39, f32[1,512]{1,0:T(1,128)S(1)} %get-tuple-element.38.local_part_ref), custom_call_target="tpu_custom_call" | custom-call | flops 603979776 | bytes 1572864 | tf_op jit(solution)/shard_map/pallas_call | solution.py:37
  37.8 25.7 %all_to_all.15.returned_ref = f32[16,100,1,128]{3,2,1,0:T(1,128)S(1)} all-to-all(f32[16,100,1,128]{3,2,1,0:T(1,128)S(1)} %get-tuple-element.39), channel_id=1, replica_groups=mesh['blk'=4,'lat'=4,'depth'=2] {'blk','lat'}, dimensions={0} | all-to-all | bytes 1638400 | tf_op jit(solution)/shard_map/all_to_all | solution.py:461
  63.5 1.6 %shard_map.140 = (f32[768,512]{1,0:T(8,128)S(1)}, f32[8,128]{1,0:T(8,128)S(1)}, f32[128,512]{1,0:T(8,128)S(1)}, f32[128,512]{1,0:T(8,128)S(1)}, f32[128,512]{1,0...) custom-call(f32[16,100,1,128]{3,2,1,0:T(1,128)S(1)} %all_to_all.15.returned_ref, ...), custom_call_target="tpu_custom_call" | custom-call | flops 805306368 | bytes 6291456 | tf_op jit(solution)/shard_map/pallas_call | solution.py:37
  65.2 1.0 collective-permute-start
  67.3 2.9 %collective-permute-start.4 = (f32[128,512]{1,0:T(8,128)S(1)}, f32[128,512]{1,0:T(8,128)S(1)}, u32[]{:S(2)}, u32[]{:S(2)}) collective-permute-start(f32[128,512]{1,0:T(8,128)S(1)} %get-tuple-element.55), channel_id=1, source_target_pairs={{0,24},{8,0},{16,8},{24,16},{1,25},{9,1},{17,9},{25,17},{2,26},{10... | collective-permute-start | bytes 786440 | tf_op jit(solution)/shard_map/ppermute | solution.py:299
  70.8 5.1 %collective-permute-done.refs_0_ = f32[128,512]{1,0:T(8,128)S(1)} collective-permute-done((f32[128,512]{1,0:T(8,128)S(1)}, f32[128,512]{1,0:T(8,128)S(1)}, u32[]{:S(2)}, u32[]{:S(2)}) %collective-permute-start) | collective-permute-done | bytes 262176 | tf_op jit(solution)/shard_map/ppermute | solution.py:299
  75.9 2.6 %shard_map.141 = (f32[1,512]{1,0:T(1,128)}, f32[1,512]{1,0:T(1,128)S(1)}, f32[1,512]{1,0:T(1,128)S(1)}, f32[512,512]{1,0:T(8,128)S(1)}, f32[768,512]{1,0:T(8,128)S(1)}) custom-call(s32[6]{0:T(128)S(1)} %bitcast.27, f32[8,128]{1,0:T(8,128)S(1)} %get-tuple-element.45.sums_ref, f32[1,512]{1,0:T(1,128)S(1)} %bitcast.34, ...), custom_call_target="tpu_custom_call" | custom-call | flops 1207959552 | bytes 8650752 | tf_op jit(solution)/shard_map/pallas_call | solution.py:37
  78.5 1.5 %shard_map.142 = (f32[256,512]{1,0:T(8,128)S(1)}, f32[768,512]{1,0:T(8,128)S(1)}, f32[128,512]{1,0:T(8,128)S(1)}, f32[128,512]{1,0:T(8,128)S(1)}, f32[128,512]{1...) custom-call(s32[6]{0:T(128)S(1)} %bitcast.28, f32[1,512]{1,0:T(1,128)S(1)} %get-tuple-element.53.beta_ref, ...), custom_call_target="tpu_custom_call" | custom-call | flops 603979776 | bytes 8650752 | tf_op jit(solution)/shard_map/pallas_call | solution.py:37
  80.6 3.3 %collective-permute-start.7 = (f32[128,512]{1,0:T(8,128)S(1)}, f32[128,512]{1,0:T(8,128)S(1)}, u32[]{:S(2)}, u32[]{:S(2)}) collective-permute-start(f32[128,512]{1,0:T(8,128)S(1)} %get-tuple-element.60), channel_id=1, source_target_pairs={{0,2},{2,0},{4,6},{6,4},{1,3},{3,1},{5,7},{7,5},{8,10},{10,8},{12,... | collective-permute-start | bytes 786440 | tf_op jit(solution)/shard_map/ppermute | solution.py:299
  84.0 3.7 %collective-permute-start.8 = (f32[128,512]{1,0:T(8,128)S(1)}, f32[128,512]{1,0:T(8,128)S(1)}, u32[]{:S(2)}, u32[]{:S(2)}) collective-permute-start(f32[128,512]{1,0:T(8,128)S(1)} %get-tuple-element.61), channel_id=1, source_target_pairs={{0,24},{8,0},{16,8},{24,16},{1,25},{9,1},{17,9},{25,17},{2,26},{10... | collective-permute-start | bytes 786440 | tf_op jit(solution)/shard_map/ppermute | solution.py:299
  88.5 2.7 %collective-permute-done.6.arrived.refs_0_ = f32[128,512]{1,0:T(8,128)S(1)} collective-permute-done((f32[128,512]{1,0:T(8,128)S(1)}, f32[128,512]{1,0:T(8,128)S(1)}, u32[]{:S(2)}, u32[]{:S(2)}) %collective-permute-start.6) | collective-permute-done | bytes 262176 | tf_op jit(solution)/shard_map/ppermute | solution.py:299
  91.2 1.3 %shard_map.144.refs_5_ = f32[8,128]{1,0:T(8,128)S(1)} custom-call(s32[6]{0:T(128)S(1)} %bitcast.29, f32[512,512]{1,0:T(8,128)S(1)} %get-tuple-element.52.near_ref, f32[256,512]{1,0:T(8,128)S(1)} %get-tuple-element.57.far_ref, f32[768,512]{1,0:T(8,128)S(1)} %get-tuple-element.58.schur_ref, f32[768,512]{1,0:T(8,128)S(1)} %bitcast.17, ...), custom_call_target="tpu_custom_call" | custom-call | flops 1572864 | bytes 4718592 | tf_op jit(solution)/shard_map/pallas_call | solution.py:37
  92.5 1.2 %shard_map.143.stored = f32[768,512]{1,0:T(8,128)} custom-call(f32[512,512]{1,0:T(8,128)S(1)} %get-tuple-element.52.near_ref, f32[256,512]{1,0:T(8,128)S(1)} %get-tuple-element.57.far_ref), custom_call_target="tpu_custom_call" | custom-call | bytes 3145728 | tf_op jit(solution)/shard_map/pallas_call | solution.py:37
  93.8 1.3 %collective-permute-done.8.refs_2_ = f32[128,512]{1,0:T(8,128)S(1)} collective-permute-done((f32[128,512]{1,0:T(8,128)S(1)}, f32[128,512]{1,0:T(8,128)S(1)}, u32[]{:S(2)}, u32[]{:S(2)}) %collective-permute-start.8) | collective-permute-done | bytes 262176 | tf_op jit(solution)/shard_map/ppermute | solution.py:299
  95.9 12.2 %all_to_all.16.sums_ref = f32[32,8,128]{2,1,0:T(8,128)S(1)} all-to-all(f32[32,8,128]{2,1,0:T(8,128)S(1)} %get-tuple-element.64), channel_id=1, replica_groups=mesh['blk'=4,'lat'=4,'depth'=2] {'depth','blk','lat'}, dimensions={0} | all-to-all | bytes 262144 | tf_op jit(solution)/shard_map/all_to_all | solution.py:461
  108.1 2.4 %shard_map.146 = (f32[768,512]{1,0:T(8,128)}, f32[1,512]{1,0:T(1,128)}, f32[1,512]{1,0:T(1,128)}) custom-call(s32[6]{0:T(128)S(1)} %bitcast.31, f32[32,8,128]{2,1,0:T(8,128)S(1)} %all_to_all.16.sums_ref, f32[1,512]{1,0:T(1,128)S(1)} %copy-done.18, f32[1,512]{1,0:T(1,128)S(1)} %get-tuple-element.66.square_ref, f32[768,512]{1,0:T(8,128)S(1)} %bitcast.18, ...), custom_call_target="tpu_custom_call" | custom-call | flops 1572864 | bytes 4718592 | tf_op jit(solution)/shard_map/pallas_call | solution.py:37
  (52 shorter events, 6.2 us)
Async XLA Ops:
  0.6 13.0 %copy-start.4 = (f32[1,1,1,768,256]{4,3,2,1,0:T(8,128)S(1)}, f32[1,1,1,768,256]{4,3,2,1,0:T(8,128)}, u32[]{:S(2)}) copy-start(f32[1,1,1,768,256]{4,3,2,1,0:T(8,128)} %param.16) | copy-start | bytes 2359300
  5.1 8.6 %copy-start = (f32[1,1,1,768,512]{4,3,2,1,0:T(8,128)S(1)}, f32[1,1,1,768,512]{4,3,2,1,0:T(8,128)}, u32[]{:S(2)}) copy-start(f32[1,1,1,768,512]{4,3,2,1,0:T(8,128)} %param.11) | copy-start | bytes 4718596
  5.1 8.6 %copy-start.15 = (s32[1,1,1,6]{3,2,1,0:T(1,128)S(1)}, s32[1,1,1,6]{3,2,1,0:T(1,128)}, u32[]{:S(2)}) copy-start(s32[1,1,1,6]{3,2,1,0:T(1,128)} %param.10) | copy-start | bytes 76
  5.2 29.3 %all-to-all-start = ((f32[16,103,1,128]{3,2,1,0:T(1,128)}), f32[16,103,1,128]{3,2,1,0:T(1,128)}, u32[]{:S(2)}, u32[]{:S(2)}) async-start(f32[16,103,1,128]{3,2,1,0:T(1,128)} %shard_map.137), calls=%async_computation | async-start | bytes 1687552 | tf_op jit(solution)/shard_map/all_to_all | solution.py:461
  34.5 29.0 %copy-start.8 = (f32[768,512]{1,0:T(8,128)S(1)}, f32[768,512]{1,0:T(8,128)}, u32[]{:S(2)}) copy-start(f32[768,512]{1,0:T(8,128)} %copy-done.7) | copy-start | bytes 4718596
  34.5 29.0 %copy-start.10 = (bf16[768,256]{1,0:T(8,128)(2,1)S(1)}, bf16[768,256]{1,0:T(8,128)(2,1)}, u32[]{:S(2)}) copy-start(bf16[768,256]{1,0:T(8,128)(2,1)} %copy-done.9) | copy-start | bytes 1179652
  34.5 29.0 %copy-start.12 = (bf16[768,256]{1,0:T(8,128)(2,1)S(1)}, bf16[768,256]{1,0:T(8,128)(2,1)}, u32[]{:S(2)}) copy-start(bf16[768,256]{1,0:T(8,128)(2,1)} %copy-done.11) | copy-start | bytes 1179652
  34.5 29.0 %copy-start.14 = (bf16[256,384]{1,0:T(8,128)(2,1)S(1)}, bf16[256,384]{1,0:T(8,128)(2,1)}, u32[]{:S(2)}) copy-start(bf16[256,384]{1,0:T(8,128)(2,1)} %copy-done.13) | copy-start | bytes 589828
  63.5 12.4 %copy-start.1 = (f32[1,1,1,768,512]{4,3,2,1,0:T(8,128)S(1)}, f32[1,1,1,768,512]{4,3,2,1,0:T(8,128)}, u32[]{:S(2)}) copy-start(f32[1,1,1,768,512]{4,3,2,1,0:T(8,128)} %param.12) | copy-start | bytes 4718596
  63.5 12.4 %copy-start.3 = (bf16[768,768]{1,0:T(8,128)(2,1)S(1)}, bf16[768,768]{1,0:T(8,128)(2,1)}, u32[]{:S(2)}) copy-start(bf16[768,768]{1,0:T(8,128)(2,1)} %copy-done.2) | copy-start | bytes 3538948
  63.5 12.4 %copy-start.17 = (f32[512]{0:T(512)S(1)}, f32[512]{0:T(512)}, u32[]{:S(2)}) copy-start(f32[512]{0:T(512)} %param.13) | copy-start | bytes 6148
  65.2 10.7 %collective-permute-start = (f32[128,512]{1,0:T(8,128)S(1)}, f32[128,512]{1,0:T(8,128)S(1)}, u32[]{:S(2)}, u32[]{:S(2)}) collective-permute-start(f32[128,512]{1,0:T(8,128)S(1)} %get-tuple-element.49), channel_id=1, source_target_pairs={{0,8},{8,16},{16,24},{24,0},{1,9},{9,17},{17,25},{25,1},{2,10},{10... | collective-permute-start | bytes 786440 | tf_op jit(solution)/shard_map/ppermute | solution.py:299
  66.2 9.7 %collective-permute-start.1 = (f32[128,512]{1,0:T(8,128)S(1)}, f32[128,512]{1,0:T(8,128)S(1)}, u32[]{:S(2)}, u32[]{:S(2)}) collective-permute-start(f32[128,512]{1,0:T(8,128)S(1)} %get-tuple-element.50), channel_id=1, source_target_pairs={{0,2},{2,0},{4,6},{6,4},{1,3},{3,1},{5,7},{7,5},{8,10},{10,8},{12,... | collective-permute-start | bytes 786440 | tf_op jit(solution)/shard_map/ppermute | solution.py:299
  66.7 9.2 %collective-permute-start.2 = (f32[128,512]{1,0:T(8,128)S(1)}, f32[128,512]{1,0:T(8,128)S(1)}, u32[]{:S(2)}, u32[]{:S(2)}) collective-permute-start(f32[128,512]{1,0:T(8,128)S(1)} %get-tuple-element.51), channel_id=1, source_target_pairs={{0,1},{1,0},{2,3},{3,2},{4,5},{5,4},{6,7},{7,6},{8,9},{9,8},{10,11... | collective-permute-start | bytes 786440 | tf_op jit(solution)/shard_map/ppermute | solution.py:299
  66.7 3.4 %collective-permute-start.3 = (f32[8,128]{1,0:T(8,128)S(1)}, f32[8,128]{1,0:T(8,128)S(1)}, u32[]{:S(2)}, u32[]{:S(2)}) collective-permute-start(f32[8,128]{1,0:T(8,128)S(1)} %get-tuple-element.45.sums_ref), channel_id=1, source_target_pairs={{0,1},{1,0},{2,3},{3,2},{4,5},{5,4},{6,7},{7,6},{8,9},{9,8},{10,11... | collective-permute-start | bytes 12296 | tf_op jit(solution)/shard_map/ppermute | solution.py:558
  67.3 11.2 %collective-permute-start.4 = (f32[128,512]{1,0:T(8,128)S(1)}, f32[128,512]{1,0:T(8,128)S(1)}, u32[]{:S(2)}, u32[]{:S(2)}) collective-permute-start(f32[128,512]{1,0:T(8,128)S(1)} %get-tuple-element.55), channel_id=1, source_target_pairs={{0,24},{8,0},{16,8},{24,16},{1,25},{9,1},{17,9},{25,17},{2,26},{10... | collective-permute-start | bytes 786440 | tf_op jit(solution)/shard_map/ppermute | solution.py:299
  70.1 8.4 %collective-permute-start.5 = (f32[128,512]{1,0:T(8,128)S(1)}, f32[128,512]{1,0:T(8,128)S(1)}, u32[]{:S(2)}, u32[]{:S(2)}) collective-permute-start(f32[128,512]{1,0:T(8,128)S(1)} %get-tuple-element.56), channel_id=1, source_target_pairs={{2,4},{4,2},{3,5},{5,3},{10,12},{12,10},{11,13},{13,11},{18,20},{2... | collective-permute-start | bytes 786440 | tf_op jit(solution)/shard_map/ppermute | solution.py:299
  80.0 11.1 %collective-permute-start.6 = (f32[128,512]{1,0:T(8,128)S(1)}, f32[128,512]{1,0:T(8,128)S(1)}, u32[]{:S(2)}, u32[]{:S(2)}) collective-permute-start(f32[128,512]{1,0:T(8,128)S(1)} %get-tuple-element.59), channel_id=1, source_target_pairs={{0,8},{8,16},{16,24},{24,0},{1,9},{9,17},{17,25},{25,1},{2,10},{10... | collective-permute-start | bytes 786440 | tf_op jit(solution)/shard_map/ppermute | solution.py:299
  80.6 13.1 %collective-permute-start.7 = (f32[128,512]{1,0:T(8,128)S(1)}, f32[128,512]{1,0:T(8,128)S(1)}, u32[]{:S(2)}, u32[]{:S(2)}) collective-permute-start(f32[128,512]{1,0:T(8,128)S(1)} %get-tuple-element.60), channel_id=1, source_target_pairs={{0,2},{2,0},{4,6},{6,4},{1,3},{3,1},{5,7},{7,5},{8,10},{10,8},{12,... | collective-permute-start | bytes 786440 | tf_op jit(solution)/shard_map/ppermute | solution.py:299
  84.0 11.1 %collective-permute-start.8 = (f32[128,512]{1,0:T(8,128)S(1)}, f32[128,512]{1,0:T(8,128)S(1)}, u32[]{:S(2)}, u32[]{:S(2)}) collective-permute-start(f32[128,512]{1,0:T(8,128)S(1)} %get-tuple-element.61), channel_id=1, source_target_pairs={{0,24},{8,0},{16,8},{24,16},{1,25},{9,1},{17,9},{25,17},{2,26},{10... | collective-permute-start | bytes 786440 | tf_op jit(solution)/shard_map/ppermute | solution.py:299
  87.7 7.4 %collective-permute-start.9 = (f32[128,512]{1,0:T(8,128)S(1)}, f32[128,512]{1,0:T(8,128)S(1)}, u32[]{:S(2)}, u32[]{:S(2)}) collective-permute-start(f32[128,512]{1,0:T(8,128)S(1)} %get-tuple-element.62), channel_id=1, source_target_pairs={{2,4},{4,2},{3,5},{5,3},{10,12},{12,10},{11,13},{13,11},{18,20},{2... | collective-permute-start | bytes 786440 | tf_op jit(solution)/shard_map/ppermute | solution.py:299
  88.4 6.7 %collective-permute-start.10 = (f32[128,512]{1,0:T(8,128)S(1)}, f32[128,512]{1,0:T(8,128)S(1)}, u32[]{:S(2)}, u32[]{:S(2)}) collective-permute-start(f32[128,512]{1,0:T(8,128)S(1)} %get-tuple-element.63), channel_id=1, source_target_pairs={{0,1},{1,0},{2,3},{3,2},{4,5},{5,4},{6,7},{7,6},{8,9},{9,8},{10,11... | collective-permute-start | bytes 786440 | tf_op jit(solution)/shard_map/ppermute | solution.py:299
  92.5 2.6 %collective-permute-start.11 = (f32[8,128]{1,0:T(8,128)S(1)}, f32[8,128]{1,0:T(8,128)S(1)}, u32[]{:S(2)}, u32[]{:S(2)}) collective-permute-start(f32[8,128]{1,0:T(8,128)S(1)} %shard_map.144.refs_5_), channel_id=1, source_target_pairs={{0,1},{1,0},{2,3},{3,2},{4,5},{5,4},{6,7},{7,6},{8,9},{9,8},{10,11... | collective-permute-start | bytes 12296 | tf_op jit(solution)/shard_map/ppermute | solution.py:593
  93.7 14.4 %copy-start.18 = (f32[1,512]{1,0:T(1,128)S(1)}, f32[1,512]{1,0:T(1,128)}, u32[]{:S(2)}) copy-start(f32[1,512]{1,0:T(1,128)} %get-tuple-element.65.rho_ref) | copy-start | bytes 6148
  (8 other events, 16.2 us)

commit v15 on v13

--- a/solution.py
+++ b/solution.py
@@ -116,6 +116,34 @@
     spare = [jnp.zeros_like(rows[0])] * (TILE - len(rows))
     turned = jnp.transpose(jnp.concatenate([*rows, *spare], axis=0))
     return [turned[:, i : i + 1] for i in range(len(rows))]
+
+
+def position(owner):
+    blks, lats = lax.axis_size("blk"), lax.axis_size("lat")
+    owner = owner.astype(f32)
+    blk = jnp.floor((owner + 0.5) * (1.0 / lats))
+    turned = (owner - lats * blk) * blks + blk
+    return jnp.where(lax.rem(lax.axis_index("depth"), 2) == 0, owner, turned)
+
+
+def own_position():
+    blk, lat, depth = (lax.axis_index(axis) for axis in ("blk", "lat", "depth"))
+    blks, lats = lax.axis_size("blk"), lax.axis_size("lat")
+    return jnp.where(lax.rem(depth, 2) == 0, blk * lats + lat, lat * blks + blk)
+
+
+def to_layer(x):
+    blks, lats, layers = (lax.axis_size(axis) for axis in ("blk", "lat", "depth"))
+    groups = []
+    for layer in range(layers):
+        if layer % 2 == 0:
+            order = [(blk, lat) for blk in range(blks) for lat in range(lats)]
+        else:
+            order = [(blk, lat) for lat in range(lats) for blk in range(blks)]
+        groups.append([(blk * lats + lat) * layers + layer for blk, lat in order])
+    return lax.all_to_all(
+        x, ("blk", "lat", "depth"), 0, 0, axis_index_groups=groups, tiled=True
+    )
 
 
 def ranks(own_row):
@@ -167,14 +195,16 @@
         return product(parts(jnp.transpose(basis)), parts(weighted))
 
     terms = term_of(0)
-    own_row = owner_ref[...].astype(f32)
+    own_row = position(owner_ref[...])
     wanted_row = row_ref[...].astype(f32) + 1.0
     rank_row, _ = ranks(own_row)
     slot_row = (own_row * CAP + rank_row).astype(jnp.int32)
     rank_col, wanted_col = columns(rank_row, wanted_row)
     packer = one_hot(lax.broadcasted_iota(jnp.int32, (slots, primal), 0) == slot_row)
-    to_owner = one_hot(lax.broadcasted_iota(jnp.int32, (owners, primal), 0) == owner_ref[...])
-    at_owner = lax.axis_index(LAYER) * CAP + rank_col.astype(jnp.int32)
+    to_owner = one_hot(
+        lax.broadcasted_iota(jnp.int32, (owners, primal), 0) == own_row.astype(jnp.int32)
+    )
+    at_owner = own_position() * CAP + rank_col.astype(jnp.int32)
     place = lax.broadcasted_iota(jnp.int32, (primal, id_rows(slots) * LANES), 1)
     names = select(to_owner, jnp.where(place == at_owner, wanted_col, 0.0))
     terms += term_of(1)
@@ -204,7 +234,7 @@
         at = slice(i * rows, (i + 1) * rows)
         refs[2][:, at], refs[3][:, at] = parts(whole[1][:, rows_of(served(*move), rows)])
     primal, slots = table_ref.shape
-    rank_row, own_col = ranks(owner_ref[...].astype(f32))
+    rank_row, own_col = ranks(position(owner_ref[...]))
     (rank_col,) = columns(rank_row)
     slot_col = (own_col * CAP + rank_col).astype(jnp.int32)
     table_ref[...] = one_hot(lax.broadcasted_iota(jnp.int32, (primal, slots), 1) == slot_col)
@@ -510,7 +540,7 @@
             pltpu.SemaphoreType.DMA((3,)),
         ],
     )
-    incoming = to_all(outgoing, LAYER)
+    incoming = to_layer(outgoing)
     local, local_part, square, table, *halves = call(
         local_kernel,
         [whole, row, row, shape_of(primal, slots, dtype=bf16)]
@@ -536,7 +566,7 @@
             pltpu.SemaphoreType.DMA((4,)),
         ],
     )
-    returned = to_all(answers, LAYER)
+    returned = to_layer(answers)
     keys = moves(FIRST)
     faces = [face] * len(keys)
     image, sums, *outward = call(

time: 110 us -> 113 us (1.027)
  waiting for transfers between devices: 18.7 us -> 22 us
  starting transfers between devices: 22.6 us -> 20.8 us
  blocking collectives: 38.7 us -> 39.9 us
    all_to_all x0 -> x1, blocking collectives: none -> 27.9 us  [to_layer(): lax.all_to_all(x, ('blk', 'lat', 'depth'), 0, 0, axis_index_groups=groups...]
    all_to_all x2 -> x1, blocking collectives: 38.7 us -> 11.9 us  [to_all(): return lax.all_to_all(x, axes, split_axis=0, concat_axis=0, tiled=True)]
    ppermute x10, waiting for transfers between devices: 9.02 us -> 12.2 us  [exchange(): lax.ppermute(block, axis, route(axis, way))]
    ppermute x10, starting transfers between devices: 13.5 us -> 11.7 us  [exchange(): lax.ppermute(block, axis, route(axis, way))]
  transfers between devices with their start and end apart: 13 -> 13, of which waited for: 4 -> 5; matrix products, arithmetic and copies ran while one was open for 0% -> 0% of each run, Pallas kernels for 8% -> 7%
where the time goes in v15:
time: 113 us; the launch traced here: 112 us
  blocking collectives  39.9 us (35%)
  waiting for transfers between devices  22 us (19%)
  Pallas kernels  21.1 us (19%)
  starting transfers between devices  20.8 us (18%)
  local copies, waits for them, and re-layouts  7.73 us (7%)
    all_to_all x1, blocking collectives, to_layer(): lax.all_to_all(x, ('blk', 'lat', 'depth'), 0, 0, axis_index_groups=groups...  27.9 us
    pallas_call x10, Pallas kernels, call(): pl.pallas_call(body, out_shape=list(outs), in_specs=in_specs, out_specs=o...  21.1 us
    ppermute x10, waiting for transfers between devices, exchange(): lax.ppermute(block, axis, route(axis, way))  12.2 us
    all_to_all x1, blocking collectives, to_all(): return lax.all_to_all(x, axes, split_axis=0, concat_axis=0, tiled=True)  11.9 us
    ppermute x10, starting transfers between devices, exchange(): lax.ppermute(block, axis, route(axis, way))  11.7 us
    all_to_all x1, waiting for transfers between devices, to_layer(): lax.all_to_all(x, ('blk', 'lat', 'depth'), 0, 0, axis_index_groups=groups...  9.82 us
    all_to_all x1, starting transfers between devices, to_layer(): lax.all_to_all(x, ('blk', 'lat', 'depth'), 0, 0, axis_index_groups=groups...  8.5 us
    unnamed x38, local copies, waits for them, and re-layouts  7.73 us
  transfers between devices with their start and end apart: 13, of which 5 were waited for; matrix products, arithmetic and copies ran while one was open for 0% of the time, Pallas kernels for 7%

profile of v15, /device:TPU:0, one launch (start us, length us, event | category | flops | bytes accessed | tf_op | source)
XLA Modules:
  0.0 112.4 jit_solution(4618079619372492960)
XLA Ops:
  0.6 4.1 %shard_map.137 = f32[16,104,128]{2,1,0:T(8,128)} custom-call(s32[6]{0:T(128)} %bitcast.25, s32[1,256]{1,0:T(1,128)} %bitcast.32, s32[1,256]{1,0:T(1,128)} %bitcast.37, f32[768,512]{1,0:T(8,128)} %bitcast.15, f32[768,256]{1,0:T(8,128)} %bitcast.21), custom_call_target="tpu_custom_call" | custom-call | flops 603979776 | bytes 3145728 | tf_op jit(solution)/shard_map/pallas_call | solution.py:37
  4.8 8.5 %all-to-all-start = ((f32[16,104,128]{2,1,0:T(8,128)}), f32[16,104,128]{2,1,0:T(8,128)}, u32[]{:S(2)}, u32[]{:S(2)}) async-start(f32[16,104,128]{2,1,0:T(8,128)} %shard_map.137), calls=%async_computation | async-start | bytes 1703936 | tf_op jit(solution)/shard_map/all_to_all | solution.py:144
  13.3 1.7 %copy-done.5 = f32[1,1,1,768,768]{4,3,2,1,0:T(8,128)S(1)} copy-done((f32[1,1,1,768,768]{4,3,2,1,0:T(8,128)S(1)}, f32[1,1,1,768,768]{4,3,2,1,0:T(8,128)}, u32[]{:S(2)}) %copy-start.5) | copy-done | bytes 2359320
  15.0 1.7 %copy-done.6 = f32[1,1,1,768,768]{4,3,2,1,0:T(8,128)S(1)} copy-done((f32[1,1,1,768,768]{4,3,2,1,0:T(8,128)S(1)}, f32[1,1,1,768,768]{4,3,2,1,0:T(8,128)}, u32[]{:S(2)}) %copy-start.6) | copy-done | bytes 2359320
  16.7 3.3 %shard_map.138 = (f32[768,512]{1,0:T(8,128)S(1)}, f32[1,512]{1,0:T(1,128)S(1)}, f32[1,512]{1,0:T(1,128)S(1)}, bf16[256,384]{1,0:T(8,128)(2,1)S(1)}, bf16[768,256...) custom-call(s32[6]{0:T(128)S(1)} %bitcast.26, ...), custom_call_target="tpu_custom_call" | custom-call | flops 1811939328 | bytes 10223616 | tf_op jit(solution)/shard_map/pallas_call | solution.py:37
  20.0 1.0 copy-done.2
  21.0 1.1 %copy-done.7 = f32[768,512]{1,0:T(8,128)} copy-done((f32[768,512]{1,0:T(8,128)}, f32[768,512]{1,0:T(8,128)S(1)}, u32[]{:S(2)}) %copy-start.7) | copy-done | bytes 1572888
  24.4 9.8 %all-to-all-done.incoming_any = f32[16,104,128]{2,1,0:T(8,128)} async-done(((f32[16,104,128]{2,1,0:T(8,128)}), f32[16,104,128]{2,1,0:T(8,128)}, u32[]{:S(2)}, u32[]{:S(2)}) %all-to-all-start) | async-done | bytes 852000 | tf_op jit(solution)/shard_map/all_to_all | solution.py:144
  34.2 2.6 %shard_map.139 = f32[16,104,128]{2,1,0:T(8,128)S(1)} custom-call(f32[16,104,128]{2,1,0:T(8,128)} %all-to-all-done.incoming_any, f32[256,256]{1,0:T(8,128)} %bitcast.39, f32[1,512]{1,0:T(1,128)S(1)} %get-tuple-element.37.local_part_ref, f32[1,512]{1,0:T(1,128)S(1)} %get-tuple-element.38.square_ref), custom_call_target="tpu_custom_call" | custom-call | flops 603979776 | bytes 1572864 | tf_op jit(solution)/shard_map/pallas_call | solution.py:37
  36.8 27.9 %all_to_all.15.returned_ref = f32[16,104,128]{2,1,0:T(8,128)S(1)} all-to-all(f32[16,104,128]{2,1,0:T(8,128)S(1)} %shard_map.139), channel_id=1, replica_groups={{0,2,4,6,8,10,12,14,16,18,20,22,24,26,28,30},{1,9,17,25,3,11,19,27,5,13..., dimensions={0} | all-to-all | bytes 1703936 | tf_op jit(solution)/shard_map/all_to_all | solution.py:144
  64.8 1.3 %shard_map.140 = (f32[768,512]{1,0:T(8,128)S(1)}, f32[8,128]{1,0:T(8,128)S(1)}, f32[128,512]{1,0:T(8,128)S(1)}, f32[128,512]{1,0:T(8,128)S(1)}, f32[128,512]{1,0...) custom-call(f32[16,104,128]{2,1,0:T(8,128)S(1)} %all_to_all.15.returned_ref, ...), custom_call_target="tpu_custom_call" | custom-call | flops 805306368 | bytes 6291456 | tf_op jit(solution)/shard_map/pallas_call | solution.py:37
  66.1 1.1 collective-permute-start
  68.2 2.8 %collective-permute-start.4 = (f32[128,512]{1,0:T(8,128)S(1)}, f32[128,512]{1,0:T(8,128)S(1)}, u32[]{:S(2)}, u32[]{:S(2)}) collective-permute-start(f32[128,512]{1,0:T(8,128)S(1)} %get-tuple-element.53), channel_id=1, source_target_pairs={{0,24},{8,0},{16,8},{24,16},{1,25},{9,1},{17,9},{25,17},{2,26},{10... | collective-permute-start | bytes 786440 | tf_op jit(solution)/shard_map/ppermute | solution.py:329
  71.7 5.5 %collective-permute-done.refs_0_ = f32[128,512]{1,0:T(8,128)S(1)} collective-permute-done((f32[128,512]{1,0:T(8,128)S(1)}, f32[128,512]{1,0:T(8,128)S(1)}, u32[]{:S(2)}, u32[]{:S(2)}) %collective-permute-start) | collective-permute-done | bytes 262176 | tf_op jit(solution)/shard_map/ppermute | solution.py:329
  77.3 2.6 %shard_map.141 = (f32[1,512]{1,0:T(1,128)}, f32[1,512]{1,0:T(1,128)S(1)}, f32[1,512]{1,0:T(1,128)S(1)}, f32[512,512]{1,0:T(8,128)S(1)}, f32[768,512]{1,0:T(8,128)S(1)}) custom-call(s32[6]{0:T(128)S(1)} %bitcast.27, f32[8,128]{1,0:T(8,128)S(1)} %get-tuple-element.43.sums_ref, f32[1,512]{1,0:T(1,128)S(1)} %bitcast.34, ...), custom_call_target="tpu_custom_call" | custom-call | flops 1207959552 | bytes 8650752 | tf_op jit(solution)/shard_map/pallas_call | solution.py:37
  79.8 1.4 %collective-permute-done.4.refs_0_ = f32[128,512]{1,0:T(8,128)S(1)} collective-permute-done((f32[128,512]{1,0:T(8,128)S(1)}, f32[128,512]{1,0:T(8,128)S(1)}, u32[]{:S(2)}, u32[]{:S(2)}) %collective-permute-start.4) | collective-permute-done | bytes 262176 | tf_op jit(solution)/shard_map/ppermute | solution.py:329
  81.2 1.5 %shard_map.142 = (f32[256,512]{1,0:T(8,128)S(1)}, f32[768,512]{1,0:T(8,128)S(1)}, f32[128,512]{1,0:T(8,128)S(1)}, f32[128,512]{1,0:T(8,128)S(1)}, f32[128,512]{1...) custom-call(s32[6]{0:T(128)S(1)} %bitcast.28, f32[1,512]{1,0:T(1,128)S(1)} %get-tuple-element.51.beta_ref, ...), custom_call_target="tpu_custom_call" | custom-call | flops 603979776 | bytes 8650752 | tf_op jit(solution)/shard_map/pallas_call | solution.py:37
  83.4 1.5 %collective-permute-start.7 = (f32[128,512]{1,0:T(8,128)S(1)}, f32[128,512]{1,0:T(8,128)S(1)}, u32[]{:S(2)}, u32[]{:S(2)}) collective-permute-start(f32[128,512]{1,0:T(8,128)S(1)} %get-tuple-element.58), channel_id=1, source_target_pairs={{0,2},{2,0},{4,6},{6,4},{1,3},{3,1},{5,7},{7,5},{8,10},{10,8},{12,... | collective-permute-start | bytes 786440 | tf_op jit(solution)/shard_map/ppermute | solution.py:329
  84.9 3.7 %collective-permute-start.8 = (f32[128,512]{1,0:T(8,128)S(1)}, f32[128,512]{1,0:T(8,128)S(1)}, u32[]{:S(2)}, u32[]{:S(2)}) collective-permute-start(f32[128,512]{1,0:T(8,128)S(1)} %get-tuple-element.59), channel_id=1, source_target_pairs={{0,24},{8,0},{16,8},{24,16},{1,25},{9,1},{17,9},{25,17},{2,26},{10... | collective-permute-start | bytes 786440 | tf_op jit(solution)/shard_map/ppermute | solution.py:329
  89.4 4.4 %collective-permute-done.6.arrived.refs_0_ = f32[128,512]{1,0:T(8,128)S(1)} collective-permute-done((f32[128,512]{1,0:T(8,128)S(1)}, f32[128,512]{1,0:T(8,128)S(1)}, u32[]{:S(2)}, u32[]{:S(2)}) %collective-permute-start.6) | collective-permute-done | bytes 262176 | tf_op jit(solution)/shard_map/ppermute | solution.py:329
  93.8 1.3 %shard_map.144.refs_5_ = f32[8,128]{1,0:T(8,128)S(1)} custom-call(s32[6]{0:T(128)S(1)} %bitcast.29, f32[512,512]{1,0:T(8,128)S(1)} %get-tuple-element.50.near_ref, f32[256,512]{1,0:T(8,128)S(1)} %get-tuple-element.55.far_ref, f32[768,512]{1,0:T(8,128)S(1)} %get-tuple-element.56.schur_ref, f32[768,512]{1,0:T(8,128)S(1)} %bitcast.17, ...), custom_call_target="tpu_custom_call" | custom-call | flops 1572864 | bytes 4718592 | tf_op jit(solution)/shard_map/pallas_call | solution.py:37
  95.2 1.2 %shard_map.143.stored = f32[768,512]{1,0:T(8,128)} custom-call(f32[512,512]{1,0:T(8,128)S(1)} %get-tuple-element.50.near_ref, f32[256,512]{1,0:T(8,128)S(1)} %get-tuple-element.55.far_ref), custom_call_target="tpu_custom_call" | custom-call | bytes 3145728 | tf_op jit(solution)/shard_map/pallas_call | solution.py:37
  98.1 11.9 %all_to_all.16.sums_ref = f32[32,8,128]{2,1,0:T(8,128)S(1)} all-to-all(f32[32,8,128]{2,1,0:T(8,128)S(1)} %get-tuple-element.62), channel_id=1, replica_groups=mesh['blk'=4,'lat'=4,'depth'=2] {'depth','blk','lat'}, dimensions={0} | all-to-all | bytes 262144 | tf_op jit(solution)/shard_map/all_to_all | solution.py:484
  110.0 2.4 %shard_map.146 = (f32[768,512]{1,0:T(8,128)}, f32[1,512]{1,0:T(1,128)}, f32[1,512]{1,0:T(1,128)}) custom-call(s32[6]{0:T(128)S(1)} %bitcast.31, f32[32,8,128]{2,1,0:T(8,128)S(1)} %all_to_all.16.sums_ref, f32[1,512]{1,0:T(1,128)S(1)} %copy-done.18, f32[1,512]{1,0:T(1,128)S(1)} %get-tuple-element.64.square_ref, f32[768,512]{1,0:T(8,128)S(1)} %bitcast.18, ...), custom_call_target="tpu_custom_call" | custom-call | flops 1572864 | bytes 4718592 | tf_op jit(solution)/shard_map/pallas_call | solution.py:37
  (52 shorter events, 7.1 us)
Async XLA Ops:
  0.6 12.7 %copy-start.4 = (f32[1,1,1,768,256]{4,3,2,1,0:T(8,128)S(1)}, f32[1,1,1,768,256]{4,3,2,1,0:T(8,128)}, u32[]{:S(2)}) copy-start(f32[1,1,1,768,256]{4,3,2,1,0:T(8,128)} %param.16) | copy-start | bytes 2359300
  4.7 8.6 %copy-start = (f32[1,1,1,768,512]{4,3,2,1,0:T(8,128)S(1)}, f32[1,1,1,768,512]{4,3,2,1,0:T(8,128)}, u32[]{:S(2)}) copy-start(f32[1,1,1,768,512]{4,3,2,1,0:T(8,128)} %param.11) | copy-start | bytes 4718596
  4.8 8.6 %copy-start.15 = (s32[1,1,1,6]{3,2,1,0:T(1,128)S(1)}, s32[1,1,1,6]{3,2,1,0:T(1,128)}, u32[]{:S(2)}) copy-start(s32[1,1,1,6]{3,2,1,0:T(1,128)} %param.10) | copy-start | bytes 76
  4.8 29.4 %all-to-all-start = ((f32[16,104,128]{2,1,0:T(8,128)}), f32[16,104,128]{2,1,0:T(8,128)}, u32[]{:S(2)}, u32[]{:S(2)}) async-start(f32[16,104,128]{2,1,0:T(8,128)} %shard_map.137), calls=%async_computation | async-start | bytes 1703936 | tf_op jit(solution)/shard_map/all_to_all | solution.py:144
  34.2 30.6 %copy-start.8 = (f32[768,512]{1,0:T(8,128)S(1)}, f32[768,512]{1,0:T(8,128)}, u32[]{:S(2)}) copy-start(f32[768,512]{1,0:T(8,128)} %copy-done.7) | copy-start | bytes 4718596
  34.2 30.6 %copy-start.10 = (bf16[768,256]{1,0:T(8,128)(2,1)S(1)}, bf16[768,256]{1,0:T(8,128)(2,1)}, u32[]{:S(2)}) copy-start(bf16[768,256]{1,0:T(8,128)(2,1)} %copy-done.9) | copy-start | bytes 1179652
  34.2 30.6 %copy-start.12 = (bf16[768,256]{1,0:T(8,128)(2,1)S(1)}, bf16[768,256]{1,0:T(8,128)(2,1)}, u32[]{:S(2)}) copy-start(bf16[768,256]{1,0:T(8,128)(2,1)} %copy-done.11) | copy-start | bytes 1179652
  34.2 30.6 %copy-start.14 = (bf16[256,384]{1,0:T(8,128)(2,1)S(1)}, bf16[256,384]{1,0:T(8,128)(2,1)}, u32[]{:S(2)}) copy-start(bf16[256,384]{1,0:T(8,128)(2,1)} %copy-done.13) | copy-start | bytes 589828
  64.8 12.5 %copy-start.1 = (f32[1,1,1,768,512]{4,3,2,1,0:T(8,128)S(1)}, f32[1,1,1,768,512]{4,3,2,1,0:T(8,128)}, u32[]{:S(2)}) copy-start(f32[1,1,1,768,512]{4,3,2,1,0:T(8,128)} %param.12) | copy-start | bytes 4718596
  64.8 12.5 %copy-start.3 = (bf16[768,768]{1,0:T(8,128)(2,1)S(1)}, bf16[768,768]{1,0:T(8,128)(2,1)}, u32[]{:S(2)}) copy-start(bf16[768,768]{1,0:T(8,128)(2,1)} %copy-done.2) | copy-start | bytes 3538948
  64.8 12.5 %copy-start.17 = (f32[512]{0:T(512)S(1)}, f32[512]{0:T(512)}, u32[]{:S(2)}) copy-start(f32[512]{0:T(512)} %param.13) | copy-start | bytes 6148
  66.1 11.1 %collective-permute-start = (f32[128,512]{1,0:T(8,128)S(1)}, f32[128,512]{1,0:T(8,128)S(1)}, u32[]{:S(2)}, u32[]{:S(2)}) collective-permute-start(f32[128,512]{1,0:T(8,128)S(1)} %get-tuple-element.47), channel_id=1, source_target_pairs={{0,8},{8,16},{16,24},{24,0},{1,9},{9,17},{17,25},{25,1},{2,10},{10... | collective-permute-start | bytes 786440 | tf_op jit(solution)/shard_map/ppermute | solution.py:329
  67.2 10.1 %collective-permute-start.1 = (f32[128,512]{1,0:T(8,128)S(1)}, f32[128,512]{1,0:T(8,128)S(1)}, u32[]{:S(2)}, u32[]{:S(2)}) collective-permute-start(f32[128,512]{1,0:T(8,128)S(1)} %get-tuple-element.48), channel_id=1, source_target_pairs={{0,2},{2,0},{4,6},{6,4},{1,3},{3,1},{5,7},{7,5},{8,10},{10,8},{12,... | collective-permute-start | bytes 786440 | tf_op jit(solution)/shard_map/ppermute | solution.py:329
  67.7 9.5 %collective-permute-start.2 = (f32[128,512]{1,0:T(8,128)S(1)}, f32[128,512]{1,0:T(8,128)S(1)}, u32[]{:S(2)}, u32[]{:S(2)}) collective-permute-start(f32[128,512]{1,0:T(8,128)S(1)} %get-tuple-element.49), channel_id=1, source_target_pairs={{0,1},{1,0},{2,3},{3,2},{4,5},{5,4},{6,7},{7,6},{8,9},{9,8},{10,11... | collective-permute-start | bytes 786440 | tf_op jit(solution)/shard_map/ppermute | solution.py:329
  67.7 3.3 %collective-permute-start.3 = (f32[8,128]{1,0:T(8,128)S(1)}, f32[8,128]{1,0:T(8,128)S(1)}, u32[]{:S(2)}, u32[]{:S(2)}) collective-permute-start(f32[8,128]{1,0:T(8,128)S(1)} %get-tuple-element.43.sums_ref), channel_id=1, source_target_pairs={{0,1},{1,0},{2,3},{3,2},{4,5},{5,4},{6,7},{7,6},{8,9},{9,8},{10,11... | collective-permute-start | bytes 12296 | tf_op jit(solution)/shard_map/ppermute | solution.py:581
  68.2 13.0 %collective-permute-start.4 = (f32[128,512]{1,0:T(8,128)S(1)}, f32[128,512]{1,0:T(8,128)S(1)}, u32[]{:S(2)}, u32[]{:S(2)}) collective-permute-start(f32[128,512]{1,0:T(8,128)S(1)} %get-tuple-element.53), channel_id=1, source_target_pairs={{0,24},{8,0},{16,8},{24,16},{1,25},{9,1},{17,9},{25,17},{2,26},{10... | collective-permute-start | bytes 786440 | tf_op jit(solution)/shard_map/ppermute | solution.py:329
  71.1 10.2 %collective-permute-start.5 = (f32[128,512]{1,0:T(8,128)S(1)}, f32[128,512]{1,0:T(8,128)S(1)}, u32[]{:S(2)}, u32[]{:S(2)}) collective-permute-start(f32[128,512]{1,0:T(8,128)S(1)} %get-tuple-element.54), channel_id=1, source_target_pairs={{2,4},{4,2},{3,5},{5,3},{10,12},{12,10},{11,13},{13,11},{18,20},{2... | collective-permute-start | bytes 786440 | tf_op jit(solution)/shard_map/ppermute | solution.py:329
  82.8 11.1 %collective-permute-start.6 = (f32[128,512]{1,0:T(8,128)S(1)}, f32[128,512]{1,0:T(8,128)S(1)}, u32[]{:S(2)}, u32[]{:S(2)}) collective-permute-start(f32[128,512]{1,0:T(8,128)S(1)} %get-tuple-element.57), channel_id=1, source_target_pairs={{0,8},{8,16},{16,24},{24,0},{1,9},{9,17},{17,25},{25,1},{2,10},{10... | collective-permute-start | bytes 786440 | tf_op jit(solution)/shard_map/ppermute | solution.py:329
  83.4 13.0 %collective-permute-start.7 = (f32[128,512]{1,0:T(8,128)S(1)}, f32[128,512]{1,0:T(8,128)S(1)}, u32[]{:S(2)}, u32[]{:S(2)}) collective-permute-start(f32[128,512]{1,0:T(8,128)S(1)} %get-tuple-element.58), channel_id=1, source_target_pairs={{0,2},{2,0},{4,6},{6,4},{1,3},{3,1},{5,7},{7,5},{8,10},{10,8},{12,... | collective-permute-start | bytes 786440 | tf_op jit(solution)/shard_map/ppermute | solution.py:329
  84.9 12.4 %collective-permute-start.8 = (f32[128,512]{1,0:T(8,128)S(1)}, f32[128,512]{1,0:T(8,128)S(1)}, u32[]{:S(2)}, u32[]{:S(2)}) collective-permute-start(f32[128,512]{1,0:T(8,128)S(1)} %get-tuple-element.59), channel_id=1, source_target_pairs={{0,24},{8,0},{16,8},{24,16},{1,25},{9,1},{17,9},{25,17},{2,26},{10... | collective-permute-start | bytes 786440 | tf_op jit(solution)/shard_map/ppermute | solution.py:329
  88.6 8.6 %collective-permute-start.9 = (f32[128,512]{1,0:T(8,128)S(1)}, f32[128,512]{1,0:T(8,128)S(1)}, u32[]{:S(2)}, u32[]{:S(2)}) collective-permute-start(f32[128,512]{1,0:T(8,128)S(1)} %get-tuple-element.60), channel_id=1, source_target_pairs={{2,4},{4,2},{3,5},{5,3},{10,12},{12,10},{11,13},{13,11},{18,20},{2... | collective-permute-start | bytes 786440 | tf_op jit(solution)/shard_map/ppermute | solution.py:329
  89.3 8.0 %collective-permute-start.10 = (f32[128,512]{1,0:T(8,128)S(1)}, f32[128,512]{1,0:T(8,128)S(1)}, u32[]{:S(2)}, u32[]{:S(2)}) collective-permute-start(f32[128,512]{1,0:T(8,128)S(1)} %get-tuple-element.61), channel_id=1, source_target_pairs={{0,1},{1,0},{2,3},{3,2},{4,5},{5,4},{6,7},{7,6},{8,9},{9,8},{10,11... | collective-permute-start | bytes 786440 | tf_op jit(solution)/shard_map/ppermute | solution.py:329
  95.1 2.2 %collective-permute-start.11 = (f32[8,128]{1,0:T(8,128)S(1)}, f32[8,128]{1,0:T(8,128)S(1)}, u32[]{:S(2)}, u32[]{:S(2)}) collective-permute-start(f32[8,128]{1,0:T(8,128)S(1)} %shard_map.144.refs_5_), channel_id=1, source_target_pairs={{0,1},{1,0},{2,3},{3,2},{4,5},{5,4},{6,7},{7,6},{8,9},{9,8},{10,11... | collective-permute-start | bytes 12296 | tf_op jit(solution)/shard_map/ppermute | solution.py:616
  96.4 13.6 %copy-start.18 = (f32[1,512]{1,0:T(1,128)S(1)}, f32[1,512]{1,0:T(1,128)}, u32[]{:S(2)}) copy-start(f32[1,512]{1,0:T(1,128)} %get-tuple-element.63.rho_ref) | copy-start | bytes 6148
  (8 other events, 16.2 us)

commit v16 on v15

--- a/solution.py
+++ b/solution.py
@@ -105,11 +105,10 @@
         out_ref[:, j * CAP : (j + 1) * CAP, :] = piece.reshape(owners, CAP, LANES)
 
 
-def get_slab(ref, pieces):
-    slots = ref.shape[0] * CAP
-    return jnp.concatenate(
-        [ref[:, j * CAP : (j + 1) * CAP, :].reshape(slots, LANES) for j in range(pieces)], axis=1
-    )
+def get_slab(ref, pieces, first=0, last=None):
+    last = ref.shape[0] if last is None else last
+    columns_of = [ref[first:last, j * CAP : (j + 1) * CAP, :] for j in range(pieces)]
+    return jnp.concatenate([x.reshape((last - first) * CAP, LANES) for x in columns_of], axis=1)
 
 
 def columns(*rows):
@@ -118,32 +117,32 @@
     return [turned[:, i : i + 1] for i in range(len(rows))]
 
 
+def turn(lat):
+    return lat ^ (lat >> 1)
+
+
 def position(owner):
-    blks, lats = lax.axis_size("blk"), lax.axis_size("lat")
+    lats = lax.axis_size("lat")
     owner = owner.astype(f32)
-    blk = jnp.floor((owner + 0.5) * (1.0 / lats))
-    turned = (owner - lats * blk) * blks + blk
-    return jnp.where(lax.rem(lax.axis_index("depth"), 2) == 0, owner, turned)
+    lat = owner - lats * jnp.floor((owner + 0.5) * (1.0 / lats))
+    for one in range(lats):
+        owner = owner + jnp.where(lat == one, float(turn(one) - one), 0.0)
+    return owner
 
 
 def own_position():
-    blk, lat, depth = (lax.axis_index(axis) for axis in ("blk", "lat", "depth"))
-    blks, lats = lax.axis_size("blk"), lax.axis_size("lat")
-    return jnp.where(lax.rem(depth, 2) == 0, blk * lats + lat, lat * blks + blk)
+    lat = lax.axis_index("lat")
+    return lax.axis_index("blk") * lax.axis_size("lat") + turn(lat)
 
 
 def to_layer(x):
-    blks, lats, layers = (lax.axis_size(axis) for axis in ("blk", "lat", "depth"))
-    groups = []
-    for layer in range(layers):
-        if layer % 2 == 0:
-            order = [(blk, lat) for blk in range(blks) for lat in range(lats)]
-        else:
-            order = [(blk, lat) for lat in range(lats) for blk in range(blks)]
-        groups.append([(blk * lats + lat) * layers + layer for blk, lat in order])
-    return lax.all_to_all(
-        x, ("blk", "lat", "depth"), 0, 0, axis_index_groups=groups, tiled=True
-    )
+    lats = lax.axis_size("lat")
+    order = [
+        blk * lats + lat
+        for blk in range(lax.axis_size("blk"))
+        for lat in sorted(range(lats), key=turn)
+    ]
+    return lax.all_to_all(x, LAYER, 0, 0, axis_index_groups=[order], tiled=True)
 
 
 def ranks(own_row):
@@ -184,14 +183,16 @@
     for copy in small:
         copy.wait()
 
-    def term_of(pair):
-        for copy in large[pair]:
-            copy.wait()
+    def term_of(*pairs):
+        for pair in pairs:
+            for copy in large[pair]:
+                copy.wait()
+        first, last = 2 * pairs[0], 2 * pairs[-1] + 2
         weighted = jnp.concatenate(
-            [0.5 * masked(len_ref, residual_ref, 2 * pair + side, rows) for side in range(2)],
+            [0.5 * masked(len_ref, residual_ref, face, rows) for face in range(first, last)],
             axis=0,
         )
-        basis = basis_ref[2 * pair * rows : 2 * (pair + 1) * rows, :]
+        basis = basis_ref[first * rows : last * rows, :]
         return product(parts(jnp.transpose(basis)), parts(weighted))
 
     terms = term_of(0)
@@ -207,8 +208,7 @@
     at_owner = own_position() * CAP + rank_col.astype(jnp.int32)
     place = lax.broadcasted_iota(jnp.int32, (primal, id_rows(slots) * LANES), 1)
     names = select(to_owner, jnp.where(place == at_owner, wanted_col, 0.0))
-    terms += term_of(1)
-    terms += term_of(2)
+    terms += term_of(1, 2)
     put_slab(slab_ref, select(packer, terms))
     tail = slab_ref.shape[1] - tiles(id_rows(slots))
     names = jnp.concatenate(
@@ -244,17 +244,21 @@
     names_ref, slab_ref, inverse_ref, sems = refs
     owners, height, _ = slab_ref.shape
     pieces = height // CAP
-    half = pieces // 2 * CAP
+    slots, owned = owners * CAP, inverse_ref.shape[0]
+    cut = 2 * slots // 3 // LANES * LANES
+    lead = -(-cut // CAP)
     copies = [
         pltpu.make_async_copy(
             incoming_any.at[:, pl.ds(height, names_ref.shape[1])], names_ref, sems.at[0]
         ),
         pltpu.make_async_copy(
-            incoming_any.at[:, pl.ds(0, half)], slab_ref.at[:, pl.ds(0, half)], sems.at[1]
+            incoming_any.at[pl.ds(0, lead), pl.ds(0, height)],
+            slab_ref.at[pl.ds(0, lead)],
+            sems.at[1],
         ),
         pltpu.make_async_copy(
-            incoming_any.at[:, pl.ds(half, height - half)],
-            slab_ref.at[:, pl.ds(half, height - half)],
+            incoming_any.at[pl.ds(lead, owners - lead), pl.ds(0, height)],
+            slab_ref.at[pl.ds(lead, owners - lead)],
             sems.at[2],
         ),
         pltpu.make_async_copy(inverse_any, inverse_ref, sems.at[3]),
@@ -262,7 +266,6 @@
     for copy in copies:
         copy.start()
     copies[0].wait()
-    slots, owned = owners * CAP, inverse_ref.shape[0]
     wanted = unfolded(jnp.sum(names_ref[...], axis=0), 0, id_rows(slots))[:, :slots]
     (wanted_col,) = columns(wanted)
     row_at = lax.broadcasted_iota(jnp.int32, (owned, slots), 0).astype(f32) + 1.0
@@ -271,9 +274,12 @@
     table = one_hot(col_at == wanted_col)
     copies[3].wait()
     inverse = parts(inverse_ref[...])
-    for copy in copies[1:3]:
-        copy.wait()
-    summed = select(gather, get_slab(slab_ref, pieces))
+    copies[1].wait()
+    head = get_slab(slab_ref, pieces, 0, lead)
+    summed = select(gather[:, :cut], head[:cut])
+    copies[2].wait()
+    rest = jnp.concatenate([head[cut:], get_slab(slab_ref, pieces, lead, owners)], axis=0)
+    summed += select(gather[:, cut:], rest)
     solved = product(inverse, parts(summed))
     put_slab(answer_ref, select(table, solved))
     total = local_part_ref[...] + 2.0 * jnp.sum(summed * solved, axis=0, keepdims=True)

time: 113 us -> 110 us (0.973)
  waiting for transfers between devices: 22 us -> 19 us
  blocking collectives: 39.9 us -> 37.8 us
  starting transfers between devices: 20.8 us -> 22.9 us
    ppermute x10, waiting for transfers between devices: 12.2 us -> 10 us  [exchange(): lax.ppermute(block, axis, route(axis, way))]
    ppermute x10, starting transfers between devices: 11.7 us -> 13.8 us  [exchange(): lax.ppermute(block, axis, route(axis, way))]
    all_to_all x1, blocking collectives: 27.9 us -> 26.5 us  [to_layer(): return lax.all_to_all(x, LAYER, 0, 0, axis_index_groups=[order], tiled=True)]
  transfers between devices with their start and end apart: 13 -> 13, of which waited for: 5 -> 5; matrix products, arithmetic and copies ran while one was open for 0% -> 0% of each run, Pallas kernels for 7% -> 8%
where the time goes in v16:
time: 110 us; the launch traced here: 109 us
  blocking collectives  37.8 us (34%)
  starting transfers between devices  22.9 us (21%)
  Pallas kernels  21.2 us (19%)
  waiting for transfers between devices  19 us (17%)
  local copies, waits for them, and re-layouts  7.73 us (7%)
    all_to_all x1, blocking collectives, to_layer(): return lax.all_to_all(x, LAYER, 0, 0, axis_index_groups=[order], tiled=True)  26.5 us
    pallas_call x10, Pallas kernels, call(): pl.pallas_call(body, out_shape=list(outs), in_specs=in_specs, out_specs=o...  21.2 us
    ppermute x10, starting transfers between devices, exchange(): lax.ppermute(block, axis, route(axis, way))  13.8 us
    all_to_all x1, blocking collectives, to_all(): return lax.all_to_all(x, axes, split_axis=0, concat_axis=0, tiled=True)  11.3 us
    ppermute x10, waiting for transfers between devices, exchange(): lax.ppermute(block, axis, route(axis, way))  10 us
    all_to_all x1, waiting for transfers between devices, to_layer(): return lax.all_to_all(x, LAYER, 0, 0, axis_index_groups=[order], tiled=True)  8.96 us
    all_to_all x1, starting transfers between devices, to_layer(): return lax.all_to_all(x, LAYER, 0, 0, axis_index_groups=[order], tiled=True)  8.5 us
    unnamed x38, local copies, waits for them, and re-layouts  7.73 us
  transfers between devices with their start and end apart: 13, of which 5 were waited for; matrix products, arithmetic and copies ran while one was open for 0% of the time, Pallas kernels for 8%

profile of v16, /device:TPU:0, one launch (start us, length us, event | category | flops | bytes accessed | tf_op | source)
XLA Modules:
  0.0 109.4 jit_solution(16132430632871100243)
XLA Ops:
  0.6 4.0 %shard_map.137 = f32[16,104,128]{2,1,0:T(8,128)} custom-call(s32[6]{0:T(128)} %bitcast.25, s32[1,256]{1,0:T(1,128)} %bitcast.32, s32[1,256]{1,0:T(1,128)} %bitcast.37, f32[768,512]{1,0:T(8,128)} %bitcast.15, f32[768,256]{1,0:T(8,128)} %bitcast.21), custom_call_target="tpu_custom_call" | custom-call | flops 603979776 | bytes 3145728 | tf_op jit(solution)/shard_map/pallas_call | solution.py:37
  4.7 8.5 %all-to-all-start = ((f32[16,104,128]{2,1,0:T(8,128)}), f32[16,104,128]{2,1,0:T(8,128)}, u32[]{:S(2)}, u32[]{:S(2)}) async-start(f32[16,104,128]{2,1,0:T(8,128)} %shard_map.137), calls=%async_computation | async-start | bytes 1703936 | tf_op jit(solution)/shard_map/all_to_all | solution.py:145
  13.2 1.7 %copy-done.5 = f32[1,1,1,768,768]{4,3,2,1,0:T(8,128)S(1)} copy-done((f32[1,1,1,768,768]{4,3,2,1,0:T(8,128)S(1)}, f32[1,1,1,768,768]{4,3,2,1,0:T(8,128)}, u32[]{:S(2)}) %copy-start.5) | copy-done | bytes 2359320
  14.9 1.7 %copy-done.6 = f32[1,1,1,768,768]{4,3,2,1,0:T(8,128)S(1)} copy-done((f32[1,1,1,768,768]{4,3,2,1,0:T(8,128)S(1)}, f32[1,1,1,768,768]{4,3,2,1,0:T(8,128)}, u32[]{:S(2)}) %copy-start.6) | copy-done | bytes 2359320
  16.5 3.5 %shard_map.138 = (f32[768,512]{1,0:T(8,128)S(1)}, f32[1,512]{1,0:T(1,128)S(1)}, f32[1,512]{1,0:T(1,128)S(1)}, bf16[256,384]{1,0:T(8,128)(2,1)S(1)}, bf16[768,256...) custom-call(s32[6]{0:T(128)S(1)} %bitcast.26, ...), custom_call_target="tpu_custom_call" | custom-call | flops 1811939328 | bytes 10223616 | tf_op jit(solution)/shard_map/pallas_call | solution.py:37
  24.4 9.0 %all-to-all-done.incoming_any = f32[16,104,128]{2,1,0:T(8,128)} async-done(((f32[16,104,128]{2,1,0:T(8,128)}), f32[16,104,128]{2,1,0:T(8,128)}, u32[]{:S(2)}, u32[]{:S(2)}) %all-to-all-start) | async-done | bytes 852000 | tf_op jit(solution)/shard_map/all_to_all | solution.py:145
  33.4 2.7 %shard_map.139 = f32[16,104,128]{2,1,0:T(8,128)S(1)} custom-call(f32[16,104,128]{2,1,0:T(8,128)} %all-to-all-done.incoming_any, f32[256,256]{1,0:T(8,128)} %bitcast.39, f32[1,512]{1,0:T(1,128)S(1)} %get-tuple-element.37.local_part_ref, f32[1,512]{1,0:T(1,128)S(1)} %get-tuple-element.38.square_ref), custom_call_target="tpu_custom_call" | custom-call | flops 603979776 | bytes 1572864 | tf_op jit(solution)/shard_map/pallas_call | solution.py:37
  36.1 26.5 %all_to_all.15.returned_ref = f32[16,104,128]{2,1,0:T(8,128)S(1)} all-to-all(f32[16,104,128]{2,1,0:T(8,128)S(1)} %shard_map.139), channel_id=1, replica_groups={{0,2,6,4,8,10,14,12,16,18,22,20,24,26,30,28},{1,3,7,5,9,11,15,13,17,19,..., dimensions={0} | all-to-all | bytes 1703936 | tf_op jit(solution)/shard_map/all_to_all | solution.py:145
  62.6 1.3 %shard_map.140 = (f32[768,512]{1,0:T(8,128)S(1)}, f32[8,128]{1,0:T(8,128)S(1)}, f32[128,512]{1,0:T(8,128)S(1)}, f32[128,512]{1,0:T(8,128)S(1)}, f32[128,512]{1,0...) custom-call(f32[16,104,128]{2,1,0:T(8,128)S(1)} %all_to_all.15.returned_ref, ...), custom_call_target="tpu_custom_call" | custom-call | flops 805306368 | bytes 6291456 | tf_op jit(solution)/shard_map/pallas_call | solution.py:37
  63.9 1.2 %collective-permute-start = (f32[128,512]{1,0:T(8,128)S(1)}, f32[128,512]{1,0:T(8,128)S(1)}, u32[]{:S(2)}, u32[]{:S(2)}) collective-permute-start(f32[128,512]{1,0:T(8,128)S(1)} %get-tuple-element.47), channel_id=1, source_target_pairs={{0,8},{8,16},{16,24},{24,0},{1,9},{9,17},{17,25},{25,1},{2,10},{10... | collective-permute-start | bytes 786440 | tf_op jit(solution)/shard_map/ppermute | solution.py:335
  65.1 1.2 %collective-permute-start.1 = (f32[128,512]{1,0:T(8,128)S(1)}, f32[128,512]{1,0:T(8,128)S(1)}, u32[]{:S(2)}, u32[]{:S(2)}) collective-permute-start(f32[128,512]{1,0:T(8,128)S(1)} %get-tuple-element.48), channel_id=1, source_target_pairs={{0,2},{2,0},{4,6},{6,4},{1,3},{3,1},{5,7},{7,5},{8,10},{10,8},{12,... | collective-permute-start | bytes 786440 | tf_op jit(solution)/shard_map/ppermute | solution.py:335
  66.8 2.8 %collective-permute-start.4 = (f32[128,512]{1,0:T(8,128)S(1)}, f32[128,512]{1,0:T(8,128)S(1)}, u32[]{:S(2)}, u32[]{:S(2)}) collective-permute-start(f32[128,512]{1,0:T(8,128)S(1)} %get-tuple-element.53), channel_id=1, source_target_pairs={{0,24},{8,0},{16,8},{24,16},{1,25},{9,1},{17,9},{25,17},{2,26},{10... | collective-permute-start | bytes 786440 | tf_op jit(solution)/shard_map/ppermute | solution.py:335
  70.3 3.3 %collective-permute-done.refs_0_ = f32[128,512]{1,0:T(8,128)S(1)} collective-permute-done((f32[128,512]{1,0:T(8,128)S(1)}, f32[128,512]{1,0:T(8,128)S(1)}, u32[]{:S(2)}, u32[]{:S(2)}) %collective-permute-start) | collective-permute-done | bytes 262176 | tf_op jit(solution)/shard_map/ppermute | solution.py:335
  73.7 2.6 %shard_map.141 = (f32[1,512]{1,0:T(1,128)}, f32[1,512]{1,0:T(1,128)S(1)}, f32[1,512]{1,0:T(1,128)S(1)}, f32[512,512]{1,0:T(8,128)S(1)}, f32[768,512]{1,0:T(8,128)S(1)}) custom-call(s32[6]{0:T(128)S(1)} %bitcast.27, f32[8,128]{1,0:T(8,128)S(1)} %get-tuple-element.43.sums_ref, f32[1,512]{1,0:T(1,128)S(1)} %bitcast.34, ...), custom_call_target="tpu_custom_call" | custom-call | flops 1207959552 | bytes 8650752 | tf_op jit(solution)/shard_map/pallas_call | solution.py:37
  76.2 1.5 %collective-permute-done.4.refs_0_ = f32[128,512]{1,0:T(8,128)S(1)} collective-permute-done((f32[128,512]{1,0:T(8,128)S(1)}, f32[128,512]{1,0:T(8,128)S(1)}, u32[]{:S(2)}, u32[]{:S(2)}) %collective-permute-start.4) | collective-permute-done | bytes 262176 | tf_op jit(solution)/shard_map/ppermute | solution.py:335
  77.7 1.5 %shard_map.142 = (f32[256,512]{1,0:T(8,128)S(1)}, f32[768,512]{1,0:T(8,128)S(1)}, f32[128,512]{1,0:T(8,128)S(1)}, f32[128,512]{1,0:T(8,128)S(1)}, f32[128,512]{1...) custom-call(s32[6]{0:T(128)S(1)} %bitcast.28, f32[1,512]{1,0:T(1,128)S(1)} %get-tuple-element.51.beta_ref, ...), custom_call_target="tpu_custom_call" | custom-call | flops 603979776 | bytes 8650752 | tf_op jit(solution)/shard_map/pallas_call | solution.py:37
  79.9 3.0 %collective-permute-start.7 = (f32[128,512]{1,0:T(8,128)S(1)}, f32[128,512]{1,0:T(8,128)S(1)}, u32[]{:S(2)}, u32[]{:S(2)}) collective-permute-start(f32[128,512]{1,0:T(8,128)S(1)} %get-tuple-element.58), channel_id=1, source_target_pairs={{0,2},{2,0},{4,6},{6,4},{1,3},{3,1},{5,7},{7,5},{8,10},{10,8},{12,... | collective-permute-start | bytes 786440 | tf_op jit(solution)/shard_map/ppermute | solution.py:335
  82.8 3.6 %collective-permute-start.8 = (f32[128,512]{1,0:T(8,128)S(1)}, f32[128,512]{1,0:T(8,128)S(1)}, u32[]{:S(2)}, u32[]{:S(2)}) collective-permute-start(f32[128,512]{1,0:T(8,128)S(1)} %get-tuple-element.59), channel_id=1, source_target_pairs={{0,24},{8,0},{16,8},{24,16},{1,25},{9,1},{17,9},{25,17},{2,26},{10... | collective-permute-start | bytes 786440 | tf_op jit(solution)/shard_map/ppermute | solution.py:335
  87.2 3.1 %collective-permute-done.6.arrived.refs_0_ = f32[128,512]{1,0:T(8,128)S(1)} collective-permute-done((f32[128,512]{1,0:T(8,128)S(1)}, f32[128,512]{1,0:T(8,128)S(1)}, u32[]{:S(2)}, u32[]{:S(2)}) %collective-permute-start.6) | collective-permute-done | bytes 262176 | tf_op jit(solution)/shard_map/ppermute | solution.py:335
  90.3 1.3 %shard_map.144.refs_5_ = f32[8,128]{1,0:T(8,128)S(1)} custom-call(s32[6]{0:T(128)S(1)} %bitcast.29, f32[512,512]{1,0:T(8,128)S(1)} %get-tuple-element.50.near_ref, f32[256,512]{1,0:T(8,128)S(1)} %get-tuple-element.55.far_ref, f32[768,512]{1,0:T(8,128)S(1)} %get-tuple-element.56.schur_ref, f32[768,512]{1,0:T(8,128)S(1)} %bitcast.17, ...), custom_call_target="tpu_custom_call" | custom-call | flops 1572864 | bytes 4718592 | tf_op jit(solution)/shard_map/pallas_call | solution.py:37
  91.7 1.2 %shard_map.143.stored = f32[768,512]{1,0:T(8,128)} custom-call(f32[512,512]{1,0:T(8,128)S(1)} %get-tuple-element.50.near_ref, f32[256,512]{1,0:T(8,128)S(1)} %get-tuple-element.55.far_ref), custom_call_target="tpu_custom_call" | custom-call | bytes 3145728 | tf_op jit(solution)/shard_map/pallas_call | solution.py:37
  92.9 2.0 %collective-permute-done.8.refs_2_ = f32[128,512]{1,0:T(8,128)S(1)} collective-permute-done((f32[128,512]{1,0:T(8,128)S(1)}, f32[128,512]{1,0:T(8,128)S(1)}, u32[]{:S(2)}, u32[]{:S(2)}) %collective-permute-start.8) | collective-permute-done | bytes 262176 | tf_op jit(solution)/shard_map/ppermute | solution.py:335
  95.8 11.3 %all_to_all.16.sums_ref = f32[32,8,128]{2,1,0:T(8,128)S(1)} all-to-all(f32[32,8,128]{2,1,0:T(8,128)S(1)} %get-tuple-element.62), channel_id=1, replica_groups=mesh['blk'=4,'lat'=4,'depth'=2] {'depth','blk','lat'}, dimensions={0} | all-to-all | bytes 262144 | tf_op jit(solution)/shard_map/all_to_all | solution.py:490
  107.1 2.4 %shard_map.146 = (f32[768,512]{1,0:T(8,128)}, f32[1,512]{1,0:T(1,128)}, f32[1,512]{1,0:T(1,128)}) custom-call(s32[6]{0:T(128)S(1)} %bitcast.31, f32[32,8,128]{2,1,0:T(8,128)S(1)} %all_to_all.16.sums_ref, f32[1,512]{1,0:T(1,128)S(1)} %copy-done.18, f32[1,512]{1,0:T(1,128)S(1)} %get-tuple-element.64.square_ref, f32[768,512]{1,0:T(8,128)S(1)} %bitcast.18, ...), custom_call_target="tpu_custom_call" | custom-call | flops 1572864 | bytes 4718592 | tf_op jit(solution)/shard_map/pallas_call | solution.py:37
  (52 shorter events, 7.8 us)
Async XLA Ops:
  0.6 12.5 %copy-start.4 = (f32[1,1,1,768,256]{4,3,2,1,0:T(8,128)S(1)}, f32[1,1,1,768,256]{4,3,2,1,0:T(8,128)}, u32[]{:S(2)}) copy-start(f32[1,1,1,768,256]{4,3,2,1,0:T(8,128)} %param.16) | copy-start | bytes 2359300
  4.6 8.6 %copy-start = (f32[1,1,1,768,512]{4,3,2,1,0:T(8,128)S(1)}, f32[1,1,1,768,512]{4,3,2,1,0:T(8,128)}, u32[]{:S(2)}) copy-start(f32[1,1,1,768,512]{4,3,2,1,0:T(8,128)} %param.11) | copy-start | bytes 4718596
  4.6 8.6 %copy-start.15 = (s32[1,1,1,6]{3,2,1,0:T(1,128)S(1)}, s32[1,1,1,6]{3,2,1,0:T(1,128)}, u32[]{:S(2)}) copy-start(s32[1,1,1,6]{3,2,1,0:T(1,128)} %param.10) | copy-start | bytes 76
  4.7 28.7 %all-to-all-start = ((f32[16,104,128]{2,1,0:T(8,128)}), f32[16,104,128]{2,1,0:T(8,128)}, u32[]{:S(2)}, u32[]{:S(2)}) async-start(f32[16,104,128]{2,1,0:T(8,128)} %shard_map.137), calls=%async_computation | async-start | bytes 1703936 | tf_op jit(solution)/shard_map/all_to_all | solution.py:145
  33.4 29.1 %copy-start.8 = (f32[768,512]{1,0:T(8,128)S(1)}, f32[768,512]{1,0:T(8,128)}, u32[]{:S(2)}) copy-start(f32[768,512]{1,0:T(8,128)} %copy-done.7) | copy-start | bytes 4718596
  33.4 29.1 %copy-start.10 = (bf16[768,256]{1,0:T(8,128)(2,1)S(1)}, bf16[768,256]{1,0:T(8,128)(2,1)}, u32[]{:S(2)}) copy-start(bf16[768,256]{1,0:T(8,128)(2,1)} %copy-done.9) | copy-start | bytes 1179652
  33.4 29.1 %copy-start.12 = (bf16[768,256]{1,0:T(8,128)(2,1)S(1)}, bf16[768,256]{1,0:T(8,128)(2,1)}, u32[]{:S(2)}) copy-start(bf16[768,256]{1,0:T(8,128)(2,1)} %copy-done.11) | copy-start | bytes 1179652
  33.4 29.2 %copy-start.14 = (bf16[256,384]{1,0:T(8,128)(2,1)S(1)}, bf16[256,384]{1,0:T(8,128)(2,1)}, u32[]{:S(2)}) copy-start(bf16[256,384]{1,0:T(8,128)(2,1)} %copy-done.13) | copy-start | bytes 589828
  62.5 11.1 %copy-start.1 = (f32[1,1,1,768,512]{4,3,2,1,0:T(8,128)S(1)}, f32[1,1,1,768,512]{4,3,2,1,0:T(8,128)}, u32[]{:S(2)}) copy-start(f32[1,1,1,768,512]{4,3,2,1,0:T(8,128)} %param.12) | copy-start | bytes 4718596
  62.6 11.1 %copy-start.3 = (bf16[768,768]{1,0:T(8,128)(2,1)S(1)}, bf16[768,768]{1,0:T(8,128)(2,1)}, u32[]{:S(2)}) copy-start(bf16[768,768]{1,0:T(8,128)(2,1)} %copy-done.2) | copy-start | bytes 3538948
  62.6 11.1 %copy-start.17 = (f32[512]{0:T(512)S(1)}, f32[512]{0:T(512)}, u32[]{:S(2)}) copy-start(f32[512]{0:T(512)} %param.13) | copy-start | bytes 6148
  63.9 9.8 %collective-permute-start = (f32[128,512]{1,0:T(8,128)S(1)}, f32[128,512]{1,0:T(8,128)S(1)}, u32[]{:S(2)}, u32[]{:S(2)}) collective-permute-start(f32[128,512]{1,0:T(8,128)S(1)} %get-tuple-element.47), channel_id=1, source_target_pairs={{0,8},{8,16},{16,24},{24,0},{1,9},{9,17},{17,25},{25,1},{2,10},{10... | collective-permute-start | bytes 786440 | tf_op jit(solution)/shard_map/ppermute | solution.py:335
  65.1 8.6 %collective-permute-start.1 = (f32[128,512]{1,0:T(8,128)S(1)}, f32[128,512]{1,0:T(8,128)S(1)}, u32[]{:S(2)}, u32[]{:S(2)}) collective-permute-start(f32[128,512]{1,0:T(8,128)S(1)} %get-tuple-element.48), channel_id=1, source_target_pairs={{0,2},{2,0},{4,6},{6,4},{1,3},{3,1},{5,7},{7,5},{8,10},{10,8},{12,... | collective-permute-start | bytes 786440 | tf_op jit(solution)/shard_map/ppermute | solution.py:335
  66.3 7.3 %collective-permute-start.2 = (f32[128,512]{1,0:T(8,128)S(1)}, f32[128,512]{1,0:T(8,128)S(1)}, u32[]{:S(2)}, u32[]{:S(2)}) collective-permute-start(f32[128,512]{1,0:T(8,128)S(1)} %get-tuple-element.49), channel_id=1, source_target_pairs={{0,1},{1,0},{2,3},{3,2},{4,5},{5,4},{6,7},{7,6},{8,9},{9,8},{10,11... | collective-permute-start | bytes 786440 | tf_op jit(solution)/shard_map/ppermute | solution.py:335
  66.3 3.3 %collective-permute-start.3 = (f32[8,128]{1,0:T(8,128)S(1)}, f32[8,128]{1,0:T(8,128)S(1)}, u32[]{:S(2)}, u32[]{:S(2)}) collective-permute-start(f32[8,128]{1,0:T(8,128)S(1)} %get-tuple-element.43.sums_ref), channel_id=1, source_target_pairs={{0,1},{1,0},{2,3},{3,2},{4,5},{5,4},{6,7},{7,6},{8,9},{9,8},{10,11... | collective-permute-start | bytes 12296 | tf_op jit(solution)/shard_map/ppermute | solution.py:587
  66.8 10.9 %collective-permute-start.4 = (f32[128,512]{1,0:T(8,128)S(1)}, f32[128,512]{1,0:T(8,128)S(1)}, u32[]{:S(2)}, u32[]{:S(2)}) collective-permute-start(f32[128,512]{1,0:T(8,128)S(1)} %get-tuple-element.53), channel_id=1, source_target_pairs={{0,24},{8,0},{16,8},{24,16},{1,25},{9,1},{17,9},{25,17},{2,26},{10... | collective-permute-start | bytes 786440 | tf_op jit(solution)/shard_map/ppermute | solution.py:335
  69.6 8.1 %collective-permute-start.5 = (f32[128,512]{1,0:T(8,128)S(1)}, f32[128,512]{1,0:T(8,128)S(1)}, u32[]{:S(2)}, u32[]{:S(2)}) collective-permute-start(f32[128,512]{1,0:T(8,128)S(1)} %get-tuple-element.54), channel_id=1, source_target_pairs={{2,4},{4,2},{3,5},{5,3},{10,12},{12,10},{11,13},{13,11},{18,20},{2... | collective-permute-start | bytes 786440 | tf_op jit(solution)/shard_map/ppermute | solution.py:335
  79.2 11.1 %collective-permute-start.6 = (f32[128,512]{1,0:T(8,128)S(1)}, f32[128,512]{1,0:T(8,128)S(1)}, u32[]{:S(2)}, u32[]{:S(2)}) collective-permute-start(f32[128,512]{1,0:T(8,128)S(1)} %get-tuple-element.57), channel_id=1, source_target_pairs={{0,8},{8,16},{16,24},{24,0},{1,9},{9,17},{17,25},{25,1},{2,10},{10... | collective-permute-start | bytes 786440 | tf_op jit(solution)/shard_map/ppermute | solution.py:335
  79.9 13.0 %collective-permute-start.7 = (f32[128,512]{1,0:T(8,128)S(1)}, f32[128,512]{1,0:T(8,128)S(1)}, u32[]{:S(2)}, u32[]{:S(2)}) collective-permute-start(f32[128,512]{1,0:T(8,128)S(1)} %get-tuple-element.58), channel_id=1, source_target_pairs={{0,2},{2,0},{4,6},{6,4},{1,3},{3,1},{5,7},{7,5},{8,10},{10,8},{12,... | collective-permute-start | bytes 786440 | tf_op jit(solution)/shard_map/ppermute | solution.py:335
  82.8 12.1 %collective-permute-start.8 = (f32[128,512]{1,0:T(8,128)S(1)}, f32[128,512]{1,0:T(8,128)S(1)}, u32[]{:S(2)}, u32[]{:S(2)}) collective-permute-start(f32[128,512]{1,0:T(8,128)S(1)} %get-tuple-element.59), channel_id=1, source_target_pairs={{0,24},{8,0},{16,8},{24,16},{1,25},{9,1},{17,9},{25,17},{2,26},{10... | collective-permute-start | bytes 786440 | tf_op jit(solution)/shard_map/ppermute | solution.py:335
  86.4 8.5 %collective-permute-start.9 = (f32[128,512]{1,0:T(8,128)S(1)}, f32[128,512]{1,0:T(8,128)S(1)}, u32[]{:S(2)}, u32[]{:S(2)}) collective-permute-start(f32[128,512]{1,0:T(8,128)S(1)} %get-tuple-element.60), channel_id=1, source_target_pairs={{2,4},{4,2},{3,5},{5,3},{10,12},{12,10},{11,13},{13,11},{18,20},{2... | collective-permute-start | bytes 786440 | tf_op jit(solution)/shard_map/ppermute | solution.py:335
  87.1 7.9 %collective-permute-start.10 = (f32[128,512]{1,0:T(8,128)S(1)}, f32[128,512]{1,0:T(8,128)S(1)}, u32[]{:S(2)}, u32[]{:S(2)}) collective-permute-start(f32[128,512]{1,0:T(8,128)S(1)} %get-tuple-element.61), channel_id=1, source_target_pairs={{0,1},{1,0},{2,3},{3,2},{4,5},{5,4},{6,7},{7,6},{8,9},{9,8},{10,11... | collective-permute-start | bytes 786440 | tf_op jit(solution)/shard_map/ppermute | solution.py:335
  91.6 3.4 %collective-permute-start.11 = (f32[8,128]{1,0:T(8,128)S(1)}, f32[8,128]{1,0:T(8,128)S(1)}, u32[]{:S(2)}, u32[]{:S(2)}) collective-permute-start(f32[8,128]{1,0:T(8,128)S(1)} %shard_map.144.refs_5_), channel_id=1, source_target_pairs={{0,1},{1,0},{2,3},{3,2},{4,5},{5,4},{6,7},{7,6},{8,9},{9,8},{10,11... | collective-permute-start | bytes 12296 | tf_op jit(solution)/shard_map/ppermute | solution.py:622
  92.9 14.2 %copy-start.18 = (f32[1,512]{1,0:T(1,128)S(1)}, f32[1,512]{1,0:T(1,128)}, u32[]{:S(2)}) copy-start(f32[1,512]{1,0:T(1,128)} %get-tuple-element.63.rho_ref) | copy-start | bytes 6148
  (8 other events, 16.2 us)

commit v17 on v16

--- a/solution.py
+++ b/solution.py
@@ -420,7 +420,7 @@
         copy.wait()
 
 
-def products_kernel(len_ref, near_ref, far_ref, schur_ref, residual_ref, arrived, out_ref):
+def products_kernel(len_ref, near_ref, far_ref, schur_ref, residual_ref, arrived, stored, out_ref):
     rows = schur_ref.shape[0] // 6
     curve = cross = jnp.zeros((1, schur_ref.shape[1]), f32)
     for ref, served_moves in ((near_ref, NEAR), (far_ref, FAR)):
@@ -436,7 +436,7 @@
         out_ref[j : j + 1, :] = piece
 
 
-def applied_kernel(pair_depth, len_ref, stored, schur_ref, *refs):
+def applied_kernel(pair_depth, len_ref, schur_ref, *refs):
     keys = moves(SECOND)
     got, refs = dict(zip(keys, refs)), refs[len(keys) :]
     products, (applied_ref, spread_ref) = refs[:-2], refs[-2:]
@@ -608,18 +608,6 @@
         moved=4 * height * (height + 4 * width),
     )
     got = exchange(outward, SECOND)
-    (products,) = call(
-        products_kernel,
-        [shape_of(2 * folds, LANES)],
-        [lengths, near, far, schur_image, residual, got[0]],
-        smem=(0,),
-        loose=(5,),
-        flops=4 * height * width,
-        moved=12 * height * width,
-    )
-    products = [products]
-    if pair_depth:
-        products.append(lax.ppermute(products[0], "depth", route("depth", 0)))
     (direction,) = call(
         store_kernel,
         [whole],
@@ -628,12 +616,24 @@
         moved=8 * height * width,
         scratch=[pltpu.SemaphoreType.DMA((6,))],
     )
+    (products,) = call(
+        products_kernel,
+        [shape_of(2 * folds, LANES)],
+        [lengths, near, far, schur_image, residual, got[0], direction],
+        smem=(0,),
+        loose=(5,),
+        far=(6,),
+        flops=4 * height * width,
+        moved=12 * height * width,
+    )
+    products = [products]
+    if pair_depth:
+        products.append(lax.ppermute(products[0], "depth", route("depth", 0)))
     applied, spread_sums = call(
         functools.partial(applied_kernel, pair_depth),
         [whole, shape_of(devices, (2 if pair_depth else 3) * folds, LANES)],
-        [lengths, direction, schur_image, *got, *products],
+        [lengths, schur_image, *got, *products],
         smem=(0,),
-        far=(1,),
         flops=4 * height * width,
         moved=12 * height * width,
     )

time: 110 us -> 110 us (level)
  no operation moved by 1% of the time
where the time goes in v17:
time: 110 us; the launch traced here: 109 us
  blocking collectives  37.8 us (34%)
  starting transfers between devices  22.9 us (21%)
  Pallas kernels  21.2 us (19%)
  waiting for transfers between devices  19 us (17%)
  local copies, waits for them, and re-layouts  7.73 us (7%)
    all_to_all x1, blocking collectives, to_layer(): return lax.all_to_all(x, LAYER, 0, 0, axis_index_groups=[order], tiled=True)  26.5 us
    pallas_call x10, Pallas kernels, call(): pl.pallas_call(body, out_shape=list(outs), in_specs=in_specs, out_specs=o...  21.2 us
    ppermute x10, starting transfers between devices, exchange(): lax.ppermute(block, axis, route(axis, way))  13.8 us
    all_to_all x1, blocking collectives, to_all(): return lax.all_to_all(x, axes, split_axis=0, concat_axis=0, tiled=True)  11.3 us
    ppermute x10, waiting for transfers between devices, exchange(): lax.ppermute(block, axis, route(axis, way))  10 us
    all_to_all x1, waiting for transfers between devices, to_layer(): return lax.all_to_all(x, LAYER, 0, 0, axis_index_groups=[order], tiled=True)  8.96 us
    all_to_all x1, starting transfers between devices, to_layer(): return lax.all_to_all(x, LAYER, 0, 0, axis_index_groups=[order], tiled=True)  8.5 us
    unnamed x38, local copies, waits for them, and re-layouts  7.73 us
  transfers between devices with their start and end apart: 13, of which 5 were waited for; matrix products, arithmetic and copies ran while one was open for 0% of the time, Pallas kernels for 8%

profile of v17, /device:TPU:0, one launch (start us, length us, event | category | flops | bytes accessed | tf_op | source)
XLA Modules:
  0.0 109.4 jit_solution(15149489816864978145)
XLA Ops:
  0.6 4.0 %shard_map.137 = f32[16,104,128]{2,1,0:T(8,128)} custom-call(s32[6]{0:T(128)} %bitcast.25, s32[1,256]{1,0:T(1,128)} %bitcast.32, s32[1,256]{1,0:T(1,128)} %bitcast.37, f32[768,512]{1,0:T(8,128)} %bitcast.15, f32[768,256]{1,0:T(8,128)} %bitcast.21), custom_call_target="tpu_custom_call" | custom-call | flops 603979776 | bytes 3145728 | tf_op jit(solution)/shard_map/pallas_call | solution.py:37
  4.7 8.5 %all-to-all-start = ((f32[16,104,128]{2,1,0:T(8,128)}), f32[16,104,128]{2,1,0:T(8,128)}, u32[]{:S(2)}, u32[]{:S(2)}) async-start(f32[16,104,128]{2,1,0:T(8,128)} %shard_map.137), calls=%async_computation | async-start | bytes 1703936 | tf_op jit(solution)/shard_map/all_to_all | solution.py:145
  13.2 1.7 %copy-done.5 = f32[1,1,1,768,768]{4,3,2,1,0:T(8,128)S(1)} copy-done((f32[1,1,1,768,768]{4,3,2,1,0:T(8,128)S(1)}, f32[1,1,1,768,768]{4,3,2,1,0:T(8,128)}, u32[]{:S(2)}) %copy-start.5) | copy-done | bytes 2359320
  14.9 1.7 %copy-done.6 = f32[1,1,1,768,768]{4,3,2,1,0:T(8,128)S(1)} copy-done((f32[1,1,1,768,768]{4,3,2,1,0:T(8,128)S(1)}, f32[1,1,1,768,768]{4,3,2,1,0:T(8,128)}, u32[]{:S(2)}) %copy-start.6) | copy-done | bytes 2359320
  16.5 3.5 %shard_map.138 = (f32[768,512]{1,0:T(8,128)S(1)}, f32[1,512]{1,0:T(1,128)S(1)}, f32[1,512]{1,0:T(1,128)S(1)}, bf16[256,384]{1,0:T(8,128)(2,1)S(1)}, bf16[768,256...) custom-call(s32[6]{0:T(128)S(1)} %bitcast.26, ...), custom_call_target="tpu_custom_call" | custom-call | flops 1811939328 | bytes 10223616 | tf_op jit(solution)/shard_map/pallas_call | solution.py:37
  24.4 9.0 %all-to-all-done.incoming_any = f32[16,104,128]{2,1,0:T(8,128)} async-done(((f32[16,104,128]{2,1,0:T(8,128)}), f32[16,104,128]{2,1,0:T(8,128)}, u32[]{:S(2)}, u32[]{:S(2)}) %all-to-all-start) | async-done | bytes 852000 | tf_op jit(solution)/shard_map/all_to_all | solution.py:145
  33.4 2.7 %shard_map.139 = f32[16,104,128]{2,1,0:T(8,128)S(1)} custom-call(f32[16,104,128]{2,1,0:T(8,128)} %all-to-all-done.incoming_any, f32[256,256]{1,0:T(8,128)} %bitcast.39, f32[1,512]{1,0:T(1,128)S(1)} %get-tuple-element.37.local_part_ref, f32[1,512]{1,0:T(1,128)S(1)} %get-tuple-element.38.square_ref), custom_call_target="tpu_custom_call" | custom-call | flops 603979776 | bytes 1572864 | tf_op jit(solution)/shard_map/pallas_call | solution.py:37
  36.1 26.5 %all_to_all.15.returned_ref = f32[16,104,128]{2,1,0:T(8,128)S(1)} all-to-all(f32[16,104,128]{2,1,0:T(8,128)S(1)} %shard_map.139), channel_id=1, replica_groups={{0,2,6,4,8,10,14,12,16,18,22,20,24,26,30,28},{1,3,7,5,9,11,15,13,17,19,..., dimensions={0} | all-to-all | bytes 1703936 | tf_op jit(solution)/shard_map/all_to_all | solution.py:145
  62.6 1.3 %shard_map.140 = (f32[768,512]{1,0:T(8,128)S(1)}, f32[8,128]{1,0:T(8,128)S(1)}, f32[128,512]{1,0:T(8,128)S(1)}, f32[128,512]{1,0:T(8,128)S(1)}, f32[128,512]{1,0...) custom-call(f32[16,104,128]{2,1,0:T(8,128)S(1)} %all_to_all.15.returned_ref, ...), custom_call_target="tpu_custom_call" | custom-call | flops 805306368 | bytes 6291456 | tf_op jit(solution)/shard_map/pallas_call | solution.py:37
  63.9 1.2 %collective-permute-start = (f32[128,512]{1,0:T(8,128)S(1)}, f32[128,512]{1,0:T(8,128)S(1)}, u32[]{:S(2)}, u32[]{:S(2)}) collective-permute-start(f32[128,512]{1,0:T(8,128)S(1)} %get-tuple-element.47), channel_id=1, source_target_pairs={{0,8},{8,16},{16,24},{24,0},{1,9},{9,17},{17,25},{25,1},{2,10},{10... | collective-permute-start | bytes 786440 | tf_op jit(solution)/shard_map/ppermute | solution.py:335
  65.1 1.2 %collective-permute-start.1 = (f32[128,512]{1,0:T(8,128)S(1)}, f32[128,512]{1,0:T(8,128)S(1)}, u32[]{:S(2)}, u32[]{:S(2)}) collective-permute-start(f32[128,512]{1,0:T(8,128)S(1)} %get-tuple-element.48), channel_id=1, source_target_pairs={{0,2},{2,0},{4,6},{6,4},{1,3},{3,1},{5,7},{7,5},{8,10},{10,8},{12,... | collective-permute-start | bytes 786440 | tf_op jit(solution)/shard_map/ppermute | solution.py:335
  66.8 2.8 %collective-permute-start.4 = (f32[128,512]{1,0:T(8,128)S(1)}, f32[128,512]{1,0:T(8,128)S(1)}, u32[]{:S(2)}, u32[]{:S(2)}) collective-permute-start(f32[128,512]{1,0:T(8,128)S(1)} %get-tuple-element.53), channel_id=1, source_target_pairs={{0,24},{8,0},{16,8},{24,16},{1,25},{9,1},{17,9},{25,17},{2,26},{10... | collective-permute-start | bytes 786440 | tf_op jit(solution)/shard_map/ppermute | solution.py:335
  70.3 3.3 %collective-permute-done.refs_0_ = f32[128,512]{1,0:T(8,128)S(1)} collective-permute-done((f32[128,512]{1,0:T(8,128)S(1)}, f32[128,512]{1,0:T(8,128)S(1)}, u32[]{:S(2)}, u32[]{:S(2)}) %collective-permute-start) | collective-permute-done | bytes 262176 | tf_op jit(solution)/shard_map/ppermute | solution.py:335
  73.7 2.6 %shard_map.141 = (f32[1,512]{1,0:T(1,128)}, f32[1,512]{1,0:T(1,128)S(1)}, f32[1,512]{1,0:T(1,128)S(1)}, f32[512,512]{1,0:T(8,128)S(1)}, f32[768,512]{1,0:T(8,128)S(1)}) custom-call(s32[6]{0:T(128)S(1)} %bitcast.27, f32[8,128]{1,0:T(8,128)S(1)} %get-tuple-element.43.sums_ref, f32[1,512]{1,0:T(1,128)S(1)} %bitcast.34, ...), custom_call_target="tpu_custom_call" | custom-call | flops 1207959552 | bytes 8650752 | tf_op jit(solution)/shard_map/pallas_call | solution.py:37
  76.2 1.5 %collective-permute-done.4.refs_0_ = f32[128,512]{1,0:T(8,128)S(1)} collective-permute-done((f32[128,512]{1,0:T(8,128)S(1)}, f32[128,512]{1,0:T(8,128)S(1)}, u32[]{:S(2)}, u32[]{:S(2)}) %collective-permute-start.4) | collective-permute-done | bytes 262176 | tf_op jit(solution)/shard_map/ppermute | solution.py:335
  77.7 1.5 %shard_map.142 = (f32[256,512]{1,0:T(8,128)S(1)}, f32[768,512]{1,0:T(8,128)S(1)}, f32[128,512]{1,0:T(8,128)S(1)}, f32[128,512]{1,0:T(8,128)S(1)}, f32[128,512]{1...) custom-call(s32[6]{0:T(128)S(1)} %bitcast.28, f32[1,512]{1,0:T(1,128)S(1)} %get-tuple-element.50.beta_ref, ...), custom_call_target="tpu_custom_call" | custom-call | flops 603979776 | bytes 8650752 | tf_op jit(solution)/shard_map/pallas_call | solution.py:37
  79.9 3.0 %collective-permute-start.7 = (f32[128,512]{1,0:T(8,128)S(1)}, f32[128,512]{1,0:T(8,128)S(1)}, u32[]{:S(2)}, u32[]{:S(2)}) collective-permute-start(f32[128,512]{1,0:T(8,128)S(1)} %get-tuple-element.57), channel_id=1, source_target_pairs={{0,2},{2,0},{4,6},{6,4},{1,3},{3,1},{5,7},{7,5},{8,10},{10,8},{12,... | collective-permute-start | bytes 786440 | tf_op jit(solution)/shard_map/ppermute | solution.py:335
  82.8 3.6 %collective-permute-start.8 = (f32[128,512]{1,0:T(8,128)S(1)}, f32[128,512]{1,0:T(8,128)S(1)}, u32[]{:S(2)}, u32[]{:S(2)}) collective-permute-start(f32[128,512]{1,0:T(8,128)S(1)} %get-tuple-element.58), channel_id=1, source_target_pairs={{0,24},{8,0},{16,8},{24,16},{1,25},{9,1},{17,9},{25,17},{2,26},{10... | collective-permute-start | bytes 786440 | tf_op jit(solution)/shard_map/ppermute | solution.py:335
  87.2 1.2 %shard_map.143.stored = f32[768,512]{1,0:T(8,128)} custom-call(f32[512,512]{1,0:T(8,128)S(1)} %get-tuple-element.51.near_ref, f32[256,512]{1,0:T(8,128)S(1)} %get-tuple-element.61.far_ref), custom_call_target="tpu_custom_call" | custom-call | bytes 3145728 | tf_op jit(solution)/shard_map/pallas_call | solution.py:37
  88.4 1.9 %collective-permute-done.6.arrived.refs_0_ = f32[128,512]{1,0:T(8,128)S(1)} collective-permute-done((f32[128,512]{1,0:T(8,128)S(1)}, f32[128,512]{1,0:T(8,128)S(1)}, u32[]{:S(2)}, u32[]{:S(2)}) %collective-permute-start.6) | collective-permute-done | bytes 262176 | tf_op jit(solution)/shard_map/ppermute | solution.py:335
  90.3 1.3 %shard_map.144.refs_5_ = f32[8,128]{1,0:T(8,128)S(1)} custom-call(s32[6]{0:T(128)S(1)} %bitcast.29, f32[512,512]{1,0:T(8,128)S(1)} %get-tuple-element.51.near_ref, f32[256,512]{1,0:T(8,128)S(1)} %get-tuple-element.61.far_ref, f32[768,512]{1,0:T(8,128)S(1)} %get-tuple-element.55.schur_ref, f32[768,512]{1,0:T(8,128)S(1)} %bitcast.17, ...), custom_call_target="tpu_custom_call" | custom-call | flops 1572864 | bytes 4718592 | tf_op jit(solution)/shard_map/pallas_call | solution.py:37
  91.7 3.2 %collective-permute-done.8.refs_2_ = f32[128,512]{1,0:T(8,128)S(1)} collective-permute-done((f32[128,512]{1,0:T(8,128)S(1)}, f32[128,512]{1,0:T(8,128)S(1)}, u32[]{:S(2)}, u32[]{:S(2)}) %collective-permute-start.8) | collective-permute-done | bytes 262176 | tf_op jit(solution)/shard_map/ppermute | solution.py:335
  95.8 11.3 %all_to_all.16.sums_ref = f32[32,8,128]{2,1,0:T(8,128)S(1)} all-to-all(f32[32,8,128]{2,1,0:T(8,128)S(1)} %get-tuple-element.62), channel_id=1, replica_groups=mesh['blk'=4,'lat'=4,'depth'=2] {'depth','blk','lat'}, dimensions={0} | all-to-all | bytes 262144 | tf_op jit(solution)/shard_map/all_to_all | solution.py:490
  107.1 2.4 %shard_map.146 = (f32[768,512]{1,0:T(8,128)}, f32[1,512]{1,0:T(1,128)}, f32[1,512]{1,0:T(1,128)}) custom-call(s32[6]{0:T(128)S(1)} %bitcast.31, f32[32,8,128]{2,1,0:T(8,128)S(1)} %all_to_all.16.sums_ref, f32[1,512]{1,0:T(1,128)S(1)} %copy-done.18, f32[1,512]{1,0:T(1,128)S(1)} %get-tuple-element.64.square_ref, f32[768,512]{1,0:T(8,128)S(1)} %bitcast.18, ...), custom_call_target="tpu_custom_call" | custom-call | flops 1572864 | bytes 4718592 | tf_op jit(solution)/shard_map/pallas_call | solution.py:37
  (52 shorter events, 7.8 us)
Async XLA Ops:
  0.6 12.5 %copy-start.4 = (f32[1,1,1,768,256]{4,3,2,1,0:T(8,128)S(1)}, f32[1,1,1,768,256]{4,3,2,1,0:T(8,128)}, u32[]{:S(2)}) copy-start(f32[1,1,1,768,256]{4,3,2,1,0:T(8,128)} %param.16) | copy-start | bytes 2359300
  4.6 8.6 %copy-start = (f32[1,1,1,768,512]{4,3,2,1,0:T(8,128)S(1)}, f32[1,1,1,768,512]{4,3,2,1,0:T(8,128)}, u32[]{:S(2)}) copy-start(f32[1,1,1,768,512]{4,3,2,1,0:T(8,128)} %param.11) | copy-start | bytes 4718596
  4.6 8.6 %copy-start.15 = (s32[1,1,1,6]{3,2,1,0:T(1,128)S(1)}, s32[1,1,1,6]{3,2,1,0:T(1,128)}, u32[]{:S(2)}) copy-start(s32[1,1,1,6]{3,2,1,0:T(1,128)} %param.10) | copy-start | bytes 76
  4.7 28.7 %all-to-all-start = ((f32[16,104,128]{2,1,0:T(8,128)}), f32[16,104,128]{2,1,0:T(8,128)}, u32[]{:S(2)}, u32[]{:S(2)}) async-start(f32[16,104,128]{2,1,0:T(8,128)} %shard_map.137), calls=%async_computation | async-start | bytes 1703936 | tf_op jit(solution)/shard_map/all_to_all | solution.py:145
  33.4 29.1 %copy-start.8 = (f32[768,512]{1,0:T(8,128)S(1)}, f32[768,512]{1,0:T(8,128)}, u32[]{:S(2)}) copy-start(f32[768,512]{1,0:T(8,128)} %copy-done.7) | copy-start | bytes 4718596
  33.4 29.1 %copy-start.10 = (bf16[768,256]{1,0:T(8,128)(2,1)S(1)}, bf16[768,256]{1,0:T(8,128)(2,1)}, u32[]{:S(2)}) copy-start(bf16[768,256]{1,0:T(8,128)(2,1)} %copy-done.9) | copy-start | bytes 1179652
  33.4 29.1 %copy-start.12 = (bf16[768,256]{1,0:T(8,128)(2,1)S(1)}, bf16[768,256]{1,0:T(8,128)(2,1)}, u32[]{:S(2)}) copy-start(bf16[768,256]{1,0:T(8,128)(2,1)} %copy-done.11) | copy-start | bytes 1179652
  33.4 29.2 %copy-start.14 = (bf16[256,384]{1,0:T(8,128)(2,1)S(1)}, bf16[256,384]{1,0:T(8,128)(2,1)}, u32[]{:S(2)}) copy-start(bf16[256,384]{1,0:T(8,128)(2,1)} %copy-done.13) | copy-start | bytes 589828
  62.5 11.1 %copy-start.1 = (f32[1,1,1,768,512]{4,3,2,1,0:T(8,128)S(1)}, f32[1,1,1,768,512]{4,3,2,1,0:T(8,128)}, u32[]{:S(2)}) copy-start(f32[1,1,1,768,512]{4,3,2,1,0:T(8,128)} %param.12) | copy-start | bytes 4718596
  62.6 11.1 %copy-start.3 = (bf16[768,768]{1,0:T(8,128)(2,1)S(1)}, bf16[768,768]{1,0:T(8,128)(2,1)}, u32[]{:S(2)}) copy-start(bf16[768,768]{1,0:T(8,128)(2,1)} %copy-done.2) | copy-start | bytes 3538948
  62.6 11.1 %copy-start.17 = (f32[512]{0:T(512)S(1)}, f32[512]{0:T(512)}, u32[]{:S(2)}) copy-start(f32[512]{0:T(512)} %param.13) | copy-start | bytes 6148
  63.9 9.8 %collective-permute-start = (f32[128,512]{1,0:T(8,128)S(1)}, f32[128,512]{1,0:T(8,128)S(1)}, u32[]{:S(2)}, u32[]{:S(2)}) collective-permute-start(f32[128,512]{1,0:T(8,128)S(1)} %get-tuple-element.47), channel_id=1, source_target_pairs={{0,8},{8,16},{16,24},{24,0},{1,9},{9,17},{17,25},{25,1},{2,10},{10... | collective-permute-start | bytes 786440 | tf_op jit(solution)/shard_map/ppermute | solution.py:335
  65.1 8.6 %collective-permute-start.1 = (f32[128,512]{1,0:T(8,128)S(1)}, f32[128,512]{1,0:T(8,128)S(1)}, u32[]{:S(2)}, u32[]{:S(2)}) collective-permute-start(f32[128,512]{1,0:T(8,128)S(1)} %get-tuple-element.48), channel_id=1, source_target_pairs={{0,2},{2,0},{4,6},{6,4},{1,3},{3,1},{5,7},{7,5},{8,10},{10,8},{12,... | collective-permute-start | bytes 786440 | tf_op jit(solution)/shard_map/ppermute | solution.py:335
  66.3 7.3 %collective-permute-start.2 = (f32[128,512]{1,0:T(8,128)S(1)}, f32[128,512]{1,0:T(8,128)S(1)}, u32[]{:S(2)}, u32[]{:S(2)}) collective-permute-start(f32[128,512]{1,0:T(8,128)S(1)} %get-tuple-element.49), channel_id=1, source_target_pairs={{0,1},{1,0},{2,3},{3,2},{4,5},{5,4},{6,7},{7,6},{8,9},{9,8},{10,11... | collective-permute-start | bytes 786440 | tf_op jit(solution)/shard_map/ppermute | solution.py:335
  66.3 3.3 %collective-permute-start.3 = (f32[8,128]{1,0:T(8,128)S(1)}, f32[8,128]{1,0:T(8,128)S(1)}, u32[]{:S(2)}, u32[]{:S(2)}) collective-permute-start(f32[8,128]{1,0:T(8,128)S(1)} %get-tuple-element.43.sums_ref), channel_id=1, source_target_pairs={{0,1},{1,0},{2,3},{3,2},{4,5},{5,4},{6,7},{7,6},{8,9},{9,8},{10,11... | collective-permute-start | bytes 12296 | tf_op jit(solution)/shard_map/ppermute | solution.py:587
  66.8 10.9 %collective-permute-start.4 = (f32[128,512]{1,0:T(8,128)S(1)}, f32[128,512]{1,0:T(8,128)S(1)}, u32[]{:S(2)}, u32[]{:S(2)}) collective-permute-start(f32[128,512]{1,0:T(8,128)S(1)} %get-tuple-element.53), channel_id=1, source_target_pairs={{0,24},{8,0},{16,8},{24,16},{1,25},{9,1},{17,9},{25,17},{2,26},{10... | collective-permute-start | bytes 786440 | tf_op jit(solution)/shard_map/ppermute | solution.py:335
  69.6 8.1 %collective-permute-start.5 = (f32[128,512]{1,0:T(8,128)S(1)}, f32[128,512]{1,0:T(8,128)S(1)}, u32[]{:S(2)}, u32[]{:S(2)}) collective-permute-start(f32[128,512]{1,0:T(8,128)S(1)} %get-tuple-element.54), channel_id=1, source_target_pairs={{2,4},{4,2},{3,5},{5,3},{10,12},{12,10},{11,13},{13,11},{18,20},{2... | collective-permute-start | bytes 786440 | tf_op jit(solution)/shard_map/ppermute | solution.py:335
  79.2 11.1 %collective-permute-start.6 = (f32[128,512]{1,0:T(8,128)S(1)}, f32[128,512]{1,0:T(8,128)S(1)}, u32[]{:S(2)}, u32[]{:S(2)}) collective-permute-start(f32[128,512]{1,0:T(8,128)S(1)} %get-tuple-element.56), channel_id=1, source_target_pairs={{0,8},{8,16},{16,24},{24,0},{1,9},{9,17},{17,25},{25,1},{2,10},{10... | collective-permute-start | bytes 786440 | tf_op jit(solution)/shard_map/ppermute | solution.py:335
  79.9 11.8 %collective-permute-start.7 = (f32[128,512]{1,0:T(8,128)S(1)}, f32[128,512]{1,0:T(8,128)S(1)}, u32[]{:S(2)}, u32[]{:S(2)}) collective-permute-start(f32[128,512]{1,0:T(8,128)S(1)} %get-tuple-element.57), channel_id=1, source_target_pairs={{0,2},{2,0},{4,6},{6,4},{1,3},{3,1},{5,7},{7,5},{8,10},{10,8},{12,... | collective-permute-start | bytes 786440 | tf_op jit(solution)/shard_map/ppermute | solution.py:335
  82.8 12.1 %collective-permute-start.8 = (f32[128,512]{1,0:T(8,128)S(1)}, f32[128,512]{1,0:T(8,128)S(1)}, u32[]{:S(2)}, u32[]{:S(2)}) collective-permute-start(f32[128,512]{1,0:T(8,128)S(1)} %get-tuple-element.58), channel_id=1, source_target_pairs={{0,24},{8,0},{16,8},{24,16},{1,25},{9,1},{17,9},{25,17},{2,26},{10... | collective-permute-start | bytes 786440 | tf_op jit(solution)/shard_map/ppermute | solution.py:335
  86.4 8.5 %collective-permute-start.9 = (f32[128,512]{1,0:T(8,128)S(1)}, f32[128,512]{1,0:T(8,128)S(1)}, u32[]{:S(2)}, u32[]{:S(2)}) collective-permute-start(f32[128,512]{1,0:T(8,128)S(1)} %get-tuple-element.59), channel_id=1, source_target_pairs={{2,4},{4,2},{3,5},{5,3},{10,12},{12,10},{11,13},{13,11},{18,20},{2... | collective-permute-start | bytes 786440 | tf_op jit(solution)/shard_map/ppermute | solution.py:335
  87.1 7.9 %collective-permute-start.10 = (f32[128,512]{1,0:T(8,128)S(1)}, f32[128,512]{1,0:T(8,128)S(1)}, u32[]{:S(2)}, u32[]{:S(2)}) collective-permute-start(f32[128,512]{1,0:T(8,128)S(1)} %get-tuple-element.60), channel_id=1, source_target_pairs={{0,1},{1,0},{2,3},{3,2},{4,5},{5,4},{6,7},{7,6},{8,9},{9,8},{10,11... | collective-permute-start | bytes 786440 | tf_op jit(solution)/shard_map/ppermute | solution.py:335
  91.6 15.5 %copy-start.18 = (f32[1,512]{1,0:T(1,128)S(1)}, f32[1,512]{1,0:T(1,128)}, u32[]{:S(2)}) copy-start(f32[1,512]{1,0:T(1,128)} %get-tuple-element.63.rho_ref) | copy-start | bytes 6148
  91.6 3.3 %collective-permute-start.11 = (f32[8,128]{1,0:T(8,128)S(1)}, f32[8,128]{1,0:T(8,128)S(1)}, u32[]{:S(2)}, u32[]{:S(2)}) collective-permute-start(f32[8,128]{1,0:T(8,128)S(1)} %shard_map.144.refs_5_), channel_id=1, source_target_pairs={{0,1},{1,0},{2,3},{3,2},{4,5},{5,4},{6,7},{7,6},{8,9},{9,8},{10,11... | collective-permute-start | bytes 12296 | tf_op jit(solution)/shard_map/ppermute | solution.py:631
  (8 other events, 16.2 us)

commit v18 on v17

--- a/solution.py
+++ b/solution.py
@@ -117,34 +117,6 @@
     return [turned[:, i : i + 1] for i in range(len(rows))]
 
 
-def turn(lat):
-    return lat ^ (lat >> 1)
-
-
-def position(owner):
-    lats = lax.axis_size("lat")
-    owner = owner.astype(f32)
-    lat = owner - lats * jnp.floor((owner + 0.5) * (1.0 / lats))
-    for one in range(lats):
-        owner = owner + jnp.where(lat == one, float(turn(one) - one), 0.0)
-    return owner
-
-
-def own_position():
-    lat = lax.axis_index("lat")
-    return lax.axis_index("blk") * lax.axis_size("lat") + turn(lat)
-
-
-def to_layer(x):
-    lats = lax.axis_size("lat")
-    order = [
-        blk * lats + lat
-        for blk in range(lax.axis_size("blk"))
-        for lat in sorted(range(lats), key=turn)
-    ]
-    return lax.all_to_all(x, LAYER, 0, 0, axis_index_groups=[order], tiled=True)
-
-
 def ranks(own_row):
     primal = own_row.shape[1]
     (own_col,) = columns(own_row)
@@ -163,7 +135,7 @@
     small = [
         pltpu.make_async_copy(src, dst, small_sems.at[i])
         for i, (src, dst) in enumerate(
-            [(owner_any, owner_ref), (row_any, row_ref), (len_any, len_ref)]
+            [(len_any, len_ref), (owner_any, owner_ref), (row_any, row_ref)]
         )
     ]
     large = []
@@ -175,13 +147,9 @@
                 pltpu.make_async_copy(basis_any.at[at], basis_ref.at[at], sems.at[pair, 1]),
             )
         )
-    for copy in small:
+    for copy in [small[0], *large[0], *small[1:], *large[1], *large[2]]:
         copy.start()
-    for pair in large:
-        for copy in pair:
-            copy.start()
-    for copy in small:
-        copy.wait()
+    small[0].wait()
 
     def term_of(*pairs):
         for pair in pairs:
@@ -196,16 +164,16 @@
         return product(parts(jnp.transpose(basis)), parts(weighted))
 
     terms = term_of(0)
-    own_row = position(owner_ref[...])
+    for copy in small[1:]:
+        copy.wait()
+    own_row = owner_ref[...].astype(f32)
     wanted_row = row_ref[...].astype(f32) + 1.0
     rank_row, _ = ranks(own_row)
     slot_row = (own_row * CAP + rank_row).astype(jnp.int32)
     rank_col, wanted_col = columns(rank_row, wanted_row)
     packer = one_hot(lax.broadcasted_iota(jnp.int32, (slots, primal), 0) == slot_row)
-    to_owner = one_hot(
-        lax.broadcasted_iota(jnp.int32, (owners, primal), 0) == own_row.astype(jnp.int32)
-    )
-    at_owner = own_position() * CAP + rank_col.astype(jnp.int32)
+    to_owner = one_hot(lax.broadcasted_iota(jnp.int32, (owners, primal), 0) == owner_ref[...])
+    at_owner = lax.axis_index(LAYER) * CAP + rank_col.astype(jnp.int32)
     place = lax.broadcasted_iota(jnp.int32, (primal, id_rows(slots) * LANES), 1)
     names = select(to_owner, jnp.where(place == at_owner, wanted_col, 0.0))
     terms += term_of(1, 2)
@@ -234,7 +202,7 @@
         at = slice(i * rows, (i + 1) * rows)
         refs[2][:, at], refs[3][:, at] = parts(whole[1][:, rows_of(served(*move), rows)])
     primal, slots = table_ref.shape
-    rank_row, own_col = ranks(position(owner_ref[...]))
+    rank_row, own_col = ranks(owner_ref[...].astype(f32))
     (rank_col,) = columns(rank_row)
     slot_col = (own_col * CAP + rank_col).astype(jnp.int32)
     table_ref[...] = one_hot(lax.broadcasted_iota(jnp.int32, (primal, slots), 1) == slot_col)
@@ -546,7 +514,7 @@
             pltpu.SemaphoreType.DMA((3,)),
         ],
     )
-    incoming = to_layer(outgoing)
+    incoming = to_all(outgoing, LAYER)
     local, local_part, square, table, *halves = call(
         local_kernel,
         [whole, row, row, shape_of(primal, slots, dtype=bf16)]
@@ -572,7 +540,7 @@
             pltpu.SemaphoreType.DMA((4,)),
         ],
     )
-    returned = to_layer(answers)
+    returned = to_all(answers, LAYER)
     keys = moves(FIRST)
     faces = [face] * len(keys)
     image, sums, *outward = call(

time: 110 us -> 110 us (level)
    all_to_all x1 -> x2, blocking collectives: 11.3 us -> 38.7 us  [to_all(): return lax.all_to_all(x, axes, split_axis=0, concat_axis=0, tiled=True)]
    all_to_all x1 -> x0, blocking collectives: 26.5 us -> none  [to_layer(): return lax.all_to_all(x, LAYER, 0, 0, axis_index_groups=[order], tiled=True)]
  transfers between devices with their start and end apart: 13 -> 13, of which waited for: 5 -> 4; matrix products, arithmetic and copies ran while one was open for 0% -> 0% of each run, Pallas kernels for 8% -> 8%
where the time goes in v18:
time: 110 us
  blocking collectives  38.7 us (35%)
  starting transfers between devices  22.6 us (21%)
  Pallas kernels  21.4 us (19%)
  waiting for transfers between devices  18.8 us (17%)
  local copies, waits for them, and re-layouts  7.73 us (7%)
    all_to_all x2, blocking collectives, to_all(): return lax.all_to_all(x, axes, split_axis=0, concat_axis=0, tiled=True)  38.7 us
    pallas_call x10, Pallas kernels, call(): pl.pallas_call(body, out_shape=list(outs), in_specs=in_specs, out_specs=o...  21.4 us
    ppermute x10, starting transfers between devices, exchange(): lax.ppermute(block, axis, route(axis, way))  13.5 us
    all_to_all x1, waiting for transfers between devices, to_all(): return lax.all_to_all(x, axes, split_axis=0, concat_axis=0, tiled=True)  9.73 us
    ppermute x10, waiting for transfers between devices, exchange(): lax.ppermute(block, axis, route(axis, way))  9.02 us
    all_to_all x1, starting transfers between devices, to_all(): return lax.all_to_all(x, axes, split_axis=0, concat_axis=0, tiled=True)  8.5 us
    unnamed x38, local copies, waits for them, and re-layouts  7.73 us
  transfers between devices with their start and end apart: 13, of which 4 were waited for; matrix products, arithmetic and copies ran while one was open for 0% of the time, Pallas kernels for 8%

profile of v18, /device:TPU:0, one launch (start us, length us, event | category | flops | bytes accessed | tf_op | source)
XLA Modules:
  0.0 110.1 jit_solution(1093595304552952688)
XLA Ops:
  0.6 4.2 %shard_map.137 = f32[16,104,128]{2,1,0:T(8,128)} custom-call(s32[6]{0:T(128)} %bitcast.25, s32[1,256]{1,0:T(1,128)} %bitcast.32, s32[1,256]{1,0:T(1,128)} %bitcast.37, f32[768,512]{1,0:T(8,128)} %bitcast.15, f32[768,256]{1,0:T(8,128)} %bitcast.21), custom_call_target="tpu_custom_call" | custom-call | flops 603979776 | bytes 3145728 | tf_op jit(solution)/shard_map/pallas_call | solution.py:37
  4.9 8.5 %all-to-all-start = ((f32[16,104,128]{2,1,0:T(8,128)}), f32[16,104,128]{2,1,0:T(8,128)}, u32[]{:S(2)}, u32[]{:S(2)}) async-start(f32[16,104,128]{2,1,0:T(8,128)} %shard_map.137), calls=%async_computation | async-start | bytes 1703936 | tf_op jit(solution)/shard_map/all_to_all | solution.py:458
  13.5 1.7 %copy-done.5 = f32[1,1,1,768,768]{4,3,2,1,0:T(8,128)S(1)} copy-done((f32[1,1,1,768,768]{4,3,2,1,0:T(8,128)S(1)}, f32[1,1,1,768,768]{4,3,2,1,0:T(8,128)}, u32[]{:S(2)}) %copy-start.5) | copy-done | bytes 2359320
  15.1 1.7 %copy-done.6 = f32[1,1,1,768,768]{4,3,2,1,0:T(8,128)S(1)} copy-done((f32[1,1,1,768,768]{4,3,2,1,0:T(8,128)S(1)}, f32[1,1,1,768,768]{4,3,2,1,0:T(8,128)}, u32[]{:S(2)}) %copy-start.6) | copy-done | bytes 2359320
  16.8 3.5 %shard_map.138 = (f32[768,512]{1,0:T(8,128)S(1)}, f32[1,512]{1,0:T(1,128)S(1)}, f32[1,512]{1,0:T(1,128)S(1)}, bf16[256,384]{1,0:T(8,128)(2,1)S(1)}, bf16[768,256...) custom-call(s32[6]{0:T(128)S(1)} %bitcast.26, ...), custom_call_target="tpu_custom_call" | custom-call | flops 1811939328 | bytes 10223616 | tf_op jit(solution)/shard_map/pallas_call | solution.py:37
  20.3 1.0 copy-done.2
  21.3 1.1 %copy-done.7 = f32[768,512]{1,0:T(8,128)} copy-done((f32[768,512]{1,0:T(8,128)}, f32[768,512]{1,0:T(8,128)S(1)}, u32[]{:S(2)}) %copy-start.7) | copy-done | bytes 1572888
  24.6 9.7 %all-to-all-done.incoming_any = f32[16,104,128]{2,1,0:T(8,128)} async-done(((f32[16,104,128]{2,1,0:T(8,128)}), f32[16,104,128]{2,1,0:T(8,128)}, u32[]{:S(2)}, u32[]{:S(2)}) %all-to-all-start) | async-done | bytes 852000 | tf_op jit(solution)/shard_map/all_to_all | solution.py:458
  34.4 2.7 %shard_map.139 = f32[16,104,128]{2,1,0:T(8,128)S(1)} custom-call(f32[16,104,128]{2,1,0:T(8,128)} %all-to-all-done.incoming_any, f32[256,256]{1,0:T(8,128)} %bitcast.39, f32[1,512]{1,0:T(1,128)S(1)} %get-tuple-element.37.local_part_ref, f32[1,512]{1,0:T(1,128)S(1)} %get-tuple-element.38.square_ref), custom_call_target="tpu_custom_call" | custom-call | flops 603979776 | bytes 1572864 | tf_op jit(solution)/shard_map/pallas_call | solution.py:37
  37.1 26.4 %all_to_all.15.returned_ref = f32[16,104,128]{2,1,0:T(8,128)S(1)} all-to-all(f32[16,104,128]{2,1,0:T(8,128)S(1)} %shard_map.139), channel_id=1, replica_groups=mesh['blk'=4,'lat'=4,'depth'=2] {'blk','lat'}, dimensions={0} | all-to-all | bytes 1703936 | tf_op jit(solution)/shard_map/all_to_all | solution.py:458
  63.5 1.3 %shard_map.140 = (f32[768,512]{1,0:T(8,128)S(1)}, f32[8,128]{1,0:T(8,128)S(1)}, f32[128,512]{1,0:T(8,128)S(1)}, f32[128,512]{1,0:T(8,128)S(1)}, f32[128,512]{1,0...) custom-call(f32[16,104,128]{2,1,0:T(8,128)S(1)} %all_to_all.15.returned_ref, ...), custom_call_target="tpu_custom_call" | custom-call | flops 805306368 | bytes 6291456 | tf_op jit(solution)/shard_map/pallas_call | solution.py:37
  64.8 1.1 collective-permute-start
  66.9 2.8 %collective-permute-start.4 = (f32[128,512]{1,0:T(8,128)S(1)}, f32[128,512]{1,0:T(8,128)S(1)}, u32[]{:S(2)}, u32[]{:S(2)}) collective-permute-start(f32[128,512]{1,0:T(8,128)S(1)} %get-tuple-element.53), channel_id=1, source_target_pairs={{0,24},{8,0},{16,8},{24,16},{1,25},{9,1},{17,9},{25,17},{2,26},{10... | collective-permute-start | bytes 786440 | tf_op jit(solution)/shard_map/ppermute | solution.py:303
  70.4 5.1 %collective-permute-done.refs_0_ = f32[128,512]{1,0:T(8,128)S(1)} collective-permute-done((f32[128,512]{1,0:T(8,128)S(1)}, f32[128,512]{1,0:T(8,128)S(1)}, u32[]{:S(2)}, u32[]{:S(2)}) %collective-permute-start) | collective-permute-done | bytes 262176 | tf_op jit(solution)/shard_map/ppermute | solution.py:303
  75.5 2.6 %shard_map.141 = (f32[1,512]{1,0:T(1,128)}, f32[1,512]{1,0:T(1,128)S(1)}, f32[1,512]{1,0:T(1,128)S(1)}, f32[512,512]{1,0:T(8,128)S(1)}, f32[768,512]{1,0:T(8,128)S(1)}) custom-call(s32[6]{0:T(128)S(1)} %bitcast.27, f32[8,128]{1,0:T(8,128)S(1)} %get-tuple-element.43.sums_ref, f32[1,512]{1,0:T(1,128)S(1)} %bitcast.34, ...), custom_call_target="tpu_custom_call" | custom-call | flops 1207959552 | bytes 8650752 | tf_op jit(solution)/shard_map/pallas_call | solution.py:37
  78.1 1.5 %shard_map.142 = (f32[256,512]{1,0:T(8,128)S(1)}, f32[768,512]{1,0:T(8,128)S(1)}, f32[128,512]{1,0:T(8,128)S(1)}, f32[128,512]{1,0:T(8,128)S(1)}, f32[128,512]{1...) custom-call(s32[6]{0:T(128)S(1)} %bitcast.28, f32[1,512]{1,0:T(1,128)S(1)} %get-tuple-element.50.beta_ref, ...), custom_call_target="tpu_custom_call" | custom-call | flops 603979776 | bytes 8650752 | tf_op jit(solution)/shard_map/pallas_call | solution.py:37
  80.3 3.3 %collective-permute-start.7 = (f32[128,512]{1,0:T(8,128)S(1)}, f32[128,512]{1,0:T(8,128)S(1)}, u32[]{:S(2)}, u32[]{:S(2)}) collective-permute-start(f32[128,512]{1,0:T(8,128)S(1)} %get-tuple-element.57), channel_id=1, source_target_pairs={{0,2},{2,0},{4,6},{6,4},{1,3},{3,1},{5,7},{7,5},{8,10},{10,8},{12,... | collective-permute-start | bytes 786440 | tf_op jit(solution)/shard_map/ppermute | solution.py:303
  83.5 3.7 %collective-permute-start.8 = (f32[128,512]{1,0:T(8,128)S(1)}, f32[128,512]{1,0:T(8,128)S(1)}, u32[]{:S(2)}, u32[]{:S(2)}) collective-permute-start(f32[128,512]{1,0:T(8,128)S(1)} %get-tuple-element.58), channel_id=1, source_target_pairs={{0,24},{8,0},{16,8},{24,16},{1,25},{9,1},{17,9},{25,17},{2,26},{10... | collective-permute-start | bytes 786440 | tf_op jit(solution)/shard_map/ppermute | solution.py:303
  88.0 1.2 %shard_map.143.stored = f32[768,512]{1,0:T(8,128)} custom-call(f32[512,512]{1,0:T(8,128)S(1)} %get-tuple-element.51.near_ref, f32[256,512]{1,0:T(8,128)S(1)} %get-tuple-element.61.far_ref), custom_call_target="tpu_custom_call" | custom-call | bytes 3145728 | tf_op jit(solution)/shard_map/pallas_call | solution.py:37
  89.2 1.5 %collective-permute-done.6.arrived.refs_0_ = f32[128,512]{1,0:T(8,128)S(1)} collective-permute-done((f32[128,512]{1,0:T(8,128)S(1)}, f32[128,512]{1,0:T(8,128)S(1)}, u32[]{:S(2)}, u32[]{:S(2)}) %collective-permute-start.6) | collective-permute-done | bytes 262176 | tf_op jit(solution)/shard_map/ppermute | solution.py:303
  90.8 1.3 %shard_map.144.refs_5_ = f32[8,128]{1,0:T(8,128)S(1)} custom-call(s32[6]{0:T(128)S(1)} %bitcast.29, f32[512,512]{1,0:T(8,128)S(1)} %get-tuple-element.51.near_ref, f32[256,512]{1,0:T(8,128)S(1)} %get-tuple-element.61.far_ref, f32[768,512]{1,0:T(8,128)S(1)} %get-tuple-element.55.schur_ref, f32[768,512]{1,0:T(8,128)S(1)} %bitcast.17, ...), custom_call_target="tpu_custom_call" | custom-call | flops 1572864 | bytes 4718592 | tf_op jit(solution)/shard_map/pallas_call | solution.py:37
  92.1 2.4 %collective-permute-done.8.refs_2_ = f32[128,512]{1,0:T(8,128)S(1)} collective-permute-done((f32[128,512]{1,0:T(8,128)S(1)}, f32[128,512]{1,0:T(8,128)S(1)}, u32[]{:S(2)}, u32[]{:S(2)}) %collective-permute-start.8) | collective-permute-done | bytes 262176 | tf_op jit(solution)/shard_map/ppermute | solution.py:303
  95.4 12.4 %all_to_all.16.sums_ref = f32[32,8,128]{2,1,0:T(8,128)S(1)} all-to-all(f32[32,8,128]{2,1,0:T(8,128)S(1)} %get-tuple-element.62), channel_id=1, replica_groups=mesh['blk'=4,'lat'=4,'depth'=2] {'depth','blk','lat'}, dimensions={0} | all-to-all | bytes 262144 | tf_op jit(solution)/shard_map/all_to_all | solution.py:458
  107.7 2.4 %shard_map.146 = (f32[768,512]{1,0:T(8,128)}, f32[1,512]{1,0:T(1,128)}, f32[1,512]{1,0:T(1,128)}) custom-call(s32[6]{0:T(128)S(1)} %bitcast.31, f32[32,8,128]{2,1,0:T(8,128)S(1)} %all_to_all.16.sums_ref, f32[1,512]{1,0:T(1,128)S(1)} %copy-done.18, f32[1,512]{1,0:T(1,128)S(1)} %get-tuple-element.64.square_ref, f32[768,512]{1,0:T(8,128)S(1)} %bitcast.18, ...), custom_call_target="tpu_custom_call" | custom-call | flops 1572864 | bytes 4718592 | tf_op jit(solution)/shard_map/pallas_call | solution.py:37
  (52 shorter events, 6.3 us)
Async XLA Ops:
  0.6 12.8 %copy-start.4 = (f32[1,1,1,768,256]{4,3,2,1,0:T(8,128)S(1)}, f32[1,1,1,768,256]{4,3,2,1,0:T(8,128)}, u32[]{:S(2)}) copy-start(f32[1,1,1,768,256]{4,3,2,1,0:T(8,128)} %param.16) | copy-start | bytes 2359300
  4.9 8.6 %copy-start = (f32[1,1,1,768,512]{4,3,2,1,0:T(8,128)S(1)}, f32[1,1,1,768,512]{4,3,2,1,0:T(8,128)}, u32[]{:S(2)}) copy-start(f32[1,1,1,768,512]{4,3,2,1,0:T(8,128)} %param.11) | copy-start | bytes 4718596
  4.9 8.6 %copy-start.15 = (s32[1,1,1,6]{3,2,1,0:T(1,128)S(1)}, s32[1,1,1,6]{3,2,1,0:T(1,128)}, u32[]{:S(2)}) copy-start(s32[1,1,1,6]{3,2,1,0:T(1,128)} %param.10) | copy-start | bytes 76
  4.9 29.5 %all-to-all-start = ((f32[16,104,128]{2,1,0:T(8,128)}), f32[16,104,128]{2,1,0:T(8,128)}, u32[]{:S(2)}, u32[]{:S(2)}) async-start(f32[16,104,128]{2,1,0:T(8,128)} %shard_map.137), calls=%async_computation | async-start | bytes 1703936 | tf_op jit(solution)/shard_map/all_to_all | solution.py:458
  34.4 29.0 %copy-start.8 = (f32[768,512]{1,0:T(8,128)S(1)}, f32[768,512]{1,0:T(8,128)}, u32[]{:S(2)}) copy-start(f32[768,512]{1,0:T(8,128)} %copy-done.7) | copy-start | bytes 4718596
  34.4 29.0 %copy-start.10 = (bf16[768,256]{1,0:T(8,128)(2,1)S(1)}, bf16[768,256]{1,0:T(8,128)(2,1)}, u32[]{:S(2)}) copy-start(bf16[768,256]{1,0:T(8,128)(2,1)} %copy-done.9) | copy-start | bytes 1179652
  34.4 29.0 %copy-start.12 = (bf16[768,256]{1,0:T(8,128)(2,1)S(1)}, bf16[768,256]{1,0:T(8,128)(2,1)}, u32[]{:S(2)}) copy-start(bf16[768,256]{1,0:T(8,128)(2,1)} %copy-done.11) | copy-start | bytes 1179652
  34.4 29.0 %copy-start.14 = (bf16[256,384]{1,0:T(8,128)(2,1)S(1)}, bf16[256,384]{1,0:T(8,128)(2,1)}, u32[]{:S(2)}) copy-start(bf16[256,384]{1,0:T(8,128)(2,1)} %copy-done.13) | copy-start | bytes 589828
  63.4 12.1 %copy-start.1 = (f32[1,1,1,768,512]{4,3,2,1,0:T(8,128)S(1)}, f32[1,1,1,768,512]{4,3,2,1,0:T(8,128)}, u32[]{:S(2)}) copy-start(f32[1,1,1,768,512]{4,3,2,1,0:T(8,128)} %param.12) | copy-start | bytes 4718596
  63.4 12.1 %copy-start.3 = (bf16[768,768]{1,0:T(8,128)(2,1)S(1)}, bf16[768,768]{1,0:T(8,128)(2,1)}, u32[]{:S(2)}) copy-start(bf16[768,768]{1,0:T(8,128)(2,1)} %copy-done.2) | copy-start | bytes 3538948
  63.5 12.1 %copy-start.17 = (f32[512]{0:T(512)S(1)}, f32[512]{0:T(512)}, u32[]{:S(2)}) copy-start(f32[512]{0:T(512)} %param.13) | copy-start | bytes 6148
  64.8 10.7 %collective-permute-start = (f32[128,512]{1,0:T(8,128)S(1)}, f32[128,512]{1,0:T(8,128)S(1)}, u32[]{:S(2)}, u32[]{:S(2)}) collective-permute-start(f32[128,512]{1,0:T(8,128)S(1)} %get-tuple-element.47), channel_id=1, source_target_pairs={{0,8},{8,16},{16,24},{24,0},{1,9},{9,17},{17,25},{25,1},{2,10},{10... | collective-permute-start | bytes 786440 | tf_op jit(solution)/shard_map/ppermute | solution.py:303
  65.8 9.7 %collective-permute-start.1 = (f32[128,512]{1,0:T(8,128)S(1)}, f32[128,512]{1,0:T(8,128)S(1)}, u32[]{:S(2)}, u32[]{:S(2)}) collective-permute-start(f32[128,512]{1,0:T(8,128)S(1)} %get-tuple-element.48), channel_id=1, source_target_pairs={{0,2},{2,0},{4,6},{6,4},{1,3},{3,1},{5,7},{7,5},{8,10},{10,8},{12,... | collective-permute-start | bytes 786440 | tf_op jit(solution)/shard_map/ppermute | solution.py:303
  66.4 9.1 %collective-permute-start.2 = (f32[128,512]{1,0:T(8,128)S(1)}, f32[128,512]{1,0:T(8,128)S(1)}, u32[]{:S(2)}, u32[]{:S(2)}) collective-permute-start(f32[128,512]{1,0:T(8,128)S(1)} %get-tuple-element.49), channel_id=1, source_target_pairs={{0,1},{1,0},{2,3},{3,2},{4,5},{5,4},{6,7},{7,6},{8,9},{9,8},{10,11... | collective-permute-start | bytes 786440 | tf_op jit(solution)/shard_map/ppermute | solution.py:303
  66.4 3.3 %collective-permute-start.3 = (f32[8,128]{1,0:T(8,128)S(1)}, f32[8,128]{1,0:T(8,128)S(1)}, u32[]{:S(2)}, u32[]{:S(2)}) collective-permute-start(f32[8,128]{1,0:T(8,128)S(1)} %get-tuple-element.43.sums_ref), channel_id=1, source_target_pairs={{0,1},{1,0},{2,3},{3,2},{4,5},{5,4},{6,7},{7,6},{8,9},{9,8},{10,11... | collective-permute-start | bytes 12296 | tf_op jit(solution)/shard_map/ppermute | solution.py:555
  66.9 11.2 %collective-permute-start.4 = (f32[128,512]{1,0:T(8,128)S(1)}, f32[128,512]{1,0:T(8,128)S(1)}, u32[]{:S(2)}, u32[]{:S(2)}) collective-permute-start(f32[128,512]{1,0:T(8,128)S(1)} %get-tuple-element.53), channel_id=1, source_target_pairs={{0,24},{8,0},{16,8},{24,16},{1,25},{9,1},{17,9},{25,17},{2,26},{10... | collective-permute-start | bytes 786440 | tf_op jit(solution)/shard_map/ppermute | solution.py:303
  69.7 8.4 %collective-permute-start.5 = (f32[128,512]{1,0:T(8,128)S(1)}, f32[128,512]{1,0:T(8,128)S(1)}, u32[]{:S(2)}, u32[]{:S(2)}) collective-permute-start(f32[128,512]{1,0:T(8,128)S(1)} %get-tuple-element.54), channel_id=1, source_target_pairs={{2,4},{4,2},{3,5},{5,3},{10,12},{12,10},{11,13},{13,11},{18,20},{2... | collective-permute-start | bytes 786440 | tf_op jit(solution)/shard_map/ppermute | solution.py:303
  79.6 11.1 %collective-permute-start.6 = (f32[128,512]{1,0:T(8,128)S(1)}, f32[128,512]{1,0:T(8,128)S(1)}, u32[]{:S(2)}, u32[]{:S(2)}) collective-permute-start(f32[128,512]{1,0:T(8,128)S(1)} %get-tuple-element.56), channel_id=1, source_target_pairs={{0,8},{8,16},{16,24},{24,0},{1,9},{9,17},{17,25},{25,1},{2,10},{10... | collective-permute-start | bytes 786440 | tf_op jit(solution)/shard_map/ppermute | solution.py:303
  80.3 11.9 %collective-permute-start.7 = (f32[128,512]{1,0:T(8,128)S(1)}, f32[128,512]{1,0:T(8,128)S(1)}, u32[]{:S(2)}, u32[]{:S(2)}) collective-permute-start(f32[128,512]{1,0:T(8,128)S(1)} %get-tuple-element.57), channel_id=1, source_target_pairs={{0,2},{2,0},{4,6},{6,4},{1,3},{3,1},{5,7},{7,5},{8,10},{10,8},{12,... | collective-permute-start | bytes 786440 | tf_op jit(solution)/shard_map/ppermute | solution.py:303
  83.5 11.0 %collective-permute-start.8 = (f32[128,512]{1,0:T(8,128)S(1)}, f32[128,512]{1,0:T(8,128)S(1)}, u32[]{:S(2)}, u32[]{:S(2)}) collective-permute-start(f32[128,512]{1,0:T(8,128)S(1)} %get-tuple-element.58), channel_id=1, source_target_pairs={{0,24},{8,0},{16,8},{24,16},{1,25},{9,1},{17,9},{25,17},{2,26},{10... | collective-permute-start | bytes 786440 | tf_op jit(solution)/shard_map/ppermute | solution.py:303
  87.3 7.2 %collective-permute-start.9 = (f32[128,512]{1,0:T(8,128)S(1)}, f32[128,512]{1,0:T(8,128)S(1)}, u32[]{:S(2)}, u32[]{:S(2)}) collective-permute-start(f32[128,512]{1,0:T(8,128)S(1)} %get-tuple-element.59), channel_id=1, source_target_pairs={{2,4},{4,2},{3,5},{5,3},{10,12},{12,10},{11,13},{13,11},{18,20},{2... | collective-permute-start | bytes 786440 | tf_op jit(solution)/shard_map/ppermute | solution.py:303
  88.0 6.6 %collective-permute-start.10 = (f32[128,512]{1,0:T(8,128)S(1)}, f32[128,512]{1,0:T(8,128)S(1)}, u32[]{:S(2)}, u32[]{:S(2)}) collective-permute-start(f32[128,512]{1,0:T(8,128)S(1)} %get-tuple-element.60), channel_id=1, source_target_pairs={{0,1},{1,0},{2,3},{3,2},{4,5},{5,4},{6,7},{7,6},{8,9},{9,8},{10,11... | collective-permute-start | bytes 786440 | tf_op jit(solution)/shard_map/ppermute | solution.py:303
  92.0 15.7 %copy-start.18 = (f32[1,512]{1,0:T(1,128)S(1)}, f32[1,512]{1,0:T(1,128)}, u32[]{:S(2)}) copy-start(f32[1,512]{1,0:T(1,128)} %get-tuple-element.63.rho_ref) | copy-start | bytes 6148
  92.1 2.5 %collective-permute-start.11 = (f32[8,128]{1,0:T(8,128)S(1)}, f32[8,128]{1,0:T(8,128)S(1)}, u32[]{:S(2)}, u32[]{:S(2)}) collective-permute-start(f32[8,128]{1,0:T(8,128)S(1)} %shard_map.144.refs_5_), channel_id=1, source_target_pairs={{0,1},{1,0},{2,3},{3,2},{4,5},{5,4},{6,7},{7,6},{8,9},{9,8},{10,11... | collective-permute-start | bytes 12296 | tf_op jit(solution)/shard_map/ppermute | solution.py:599
  (8 other events, 16.2 us)

commit v19 on v16

--- a/solution.py
+++ b/solution.py
@@ -385,21 +385,36 @@
     image_out[...] = product((high_ref[:, :first], low_ref[:, :first]), parts(near_ref[...]))
 
 
-def far_kernel(keys, len_ref, beta_ref, image_ref, prev_ref, high_ref, low_ref, near_ref, near_image_ref, *refs):
+def far_kernel(keys, len_ref, beta_ref, image_ref, prev_ref, high_ref, low_ref, near_image_ref, *refs):
     got, refs = dict(zip(keys, refs)), refs[len(keys) :]
-    far_ref, schur_out, *face_refs = refs
+    far_ref, blk_ref, plus_ref = refs
     rows = image_ref.shape[0] // 6
     beta = beta_ref[...]
     for i, move in enumerate(FAR):
         far_ref[i * rows : (i + 1) * rows, :] = new_direction(
             len_ref, beta, image_ref, prev_ref, got, move, rows
         )
-    first = len(NEAR) * rows
-    image = near_image_ref[...] + product(
-        (high_ref[:, first:], low_ref[:, first:]), parts(far_ref[...])
-    )
-    schur_out[...] = image
-    put_faces(schur_out, rows, SECOND, face_refs)
+    first, height = len(NEAR) * rows, 2 * rows
+    image = near_image_ref[:height, :] + product(
+        (high_ref[:height, first:], low_ref[:height, first:]), parts(far_ref[...])
+    )
+    blk_ref[...] = image
+    plus_ref[...] = image[rows:]
+
+
+def rest_kernel(high_ref, low_ref, near_image_ref, far_ref, blk_ref, schur_out, *face_refs):
+    rows = near_image_ref.shape[0] // 6
+    first, height = len(NEAR) * rows, 2 * rows
+    schur_out[:height, :] = blk_ref[...]
+    schur_out[height:, :] = near_image_ref[height:, :] + product(
+        (high_ref[height:, first:], low_ref[height:, first:]), parts(far_ref[...])
+    )
+    for ref, move in zip(face_refs, sideways(), strict=True):
+        ref[...] = schur_out[rows_of(sent(*move), rows), :]
+
+
+def sideways():
+    return [move for move in moves(SECOND) if move != ("blk", "up")]
 
 
 def store_kernel(near_ref, far_ref, direction_out, sems):
@@ -598,15 +613,25 @@
         flops=4 * height * height * width,
         moved=4 * height * (height + 4 * width),
     )
-    far, schur_image, *outward = call(
+    far, blk_image, plus = call(
         functools.partial(far_kernel, far_keys),
-        [shape_of(len(FAR) * rows, width), whole, *faces],
-        [lengths, beta, image, prev_direction, *schur_halves, near, near_image]
+        [shape_of(len(FAR) * rows, width), shape_of(2 * rows, width), face],
+        [lengths, beta, image, prev_direction, *schur_halves, near_image]
         + [got[key] for key in far_keys],
         smem=(0,),
-        flops=2 * height * height * width,
-        moved=4 * height * (height + 4 * width),
-    )
+        flops=2 * height * rows * width,
+        moved=8 * height * width,
+    )
+    schur_image, *others = call(
+        rest_kernel,
+        [whole] + [face] * len(sideways()),
+        [*schur_halves, near_image, far, blk_image],
+        flops=4 * height * rows * width,
+        moved=8 * height * width,
+    )
+    outward = dict(zip(sideways(), others))
+    outward["blk", "up"] = plus
+    outward = [outward[move] for move in moves(SECOND)]
     got = exchange(outward, SECOND)
     (products,) = call(
         products_kernel,

time: 110 us -> 110 us (level)
    pallas_call x10 -> x11, Pallas kernels: 21.2 us -> 21.4 us  [call(): pl.pallas_call(body, out_shape=list(outs), in_specs=in_specs, out_specs=o...]
where the time goes in v19:
time: 110 us
  blocking collectives  38.5 us (35%)
  starting transfers between devices  23 us (21%)
  Pallas kernels  21.4 us (19%)
  waiting for transfers between devices  18.2 us (17%)
  local copies, waits for them, and re-layouts  7.72 us (7%)
    all_to_all x1, blocking collectives, to_layer(): return lax.all_to_all(x, LAYER, 0, 0, axis_index_groups=[order], tiled=True)  26.5 us
    pallas_call x11, Pallas kernels, call(): pl.pallas_call(body, out_shape=list(outs), in_specs=in_specs, out_specs=o...  21.4 us
    ppermute x10, starting transfers between devices, exchange(): lax.ppermute(block, axis, route(axis, way))  13.9 us
    all_to_all x1, blocking collectives, to_all(): return lax.all_to_all(x, axes, split_axis=0, concat_axis=0, tiled=True)  12 us
    ppermute x10, waiting for transfers between devices, exchange(): lax.ppermute(block, axis, route(axis, way))  9.24 us
    all_to_all x1, waiting for transfers between devices, to_layer(): return lax.all_to_all(x, LAYER, 0, 0, axis_index_groups=[order], tiled=True)  8.98 us
    all_to_all x1, starting transfers between devices, to_layer(): return lax.all_to_all(x, LAYER, 0, 0, axis_index_groups=[order], tiled=True)  8.5 us
    unnamed x38, local copies, waits for them, and re-layouts  7.72 us
  transfers between devices with their start and end apart: 13, of which 5 were waited for; matrix products, arithmetic and copies ran while one was open for 0% of the time, Pallas kernels for 8%

profile of v19, /device:TPU:0, one launch (start us, length us, event | category | flops | bytes accessed | tf_op | source)
XLA Modules:
  0.0 109.7 jit_solution(5232868190209456716)
XLA Ops:
  0.6 4.0 %shard_map.137 = f32[16,104,128]{2,1,0:T(8,128)} custom-call(s32[6]{0:T(128)} %bitcast.25, s32[1,256]{1,0:T(1,128)} %bitcast.32, s32[1,256]{1,0:T(1,128)} %bitcast.37, f32[768,512]{1,0:T(8,128)} %bitcast.15, f32[768,256]{1,0:T(8,128)} %bitcast.21), custom_call_target="tpu_custom_call" | custom-call | flops 603979776 | bytes 3145728 | tf_op jit(solution)/shard_map/pallas_call | solution.py:37
  4.7 8.5 %all-to-all-start = ((f32[16,104,128]{2,1,0:T(8,128)}), f32[16,104,128]{2,1,0:T(8,128)}, u32[]{:S(2)}, u32[]{:S(2)}) async-start(f32[16,104,128]{2,1,0:T(8,128)} %shard_map.137), calls=%async_computation | async-start | bytes 1703936 | tf_op jit(solution)/shard_map/all_to_all | solution.py:145
  13.2 1.7 %copy-done.5 = f32[1,1,1,768,768]{4,3,2,1,0:T(8,128)S(1)} copy-done((f32[1,1,1,768,768]{4,3,2,1,0:T(8,128)S(1)}, f32[1,1,1,768,768]{4,3,2,1,0:T(8,128)}, u32[]{:S(2)}) %copy-start.5) | copy-done | bytes 2359320
  14.9 1.7 %copy-done.6 = f32[1,1,1,768,768]{4,3,2,1,0:T(8,128)S(1)} copy-done((f32[1,1,1,768,768]{4,3,2,1,0:T(8,128)S(1)}, f32[1,1,1,768,768]{4,3,2,1,0:T(8,128)}, u32[]{:S(2)}) %copy-start.6) | copy-done | bytes 2359320
  16.5 3.5 %shard_map.138 = (f32[768,512]{1,0:T(8,128)S(1)}, f32[1,512]{1,0:T(1,128)S(1)}, f32[1,512]{1,0:T(1,128)S(1)}, bf16[256,384]{1,0:T(8,128)(2,1)S(1)}, bf16[768,256...) custom-call(s32[6]{0:T(128)S(1)} %bitcast.26, ...), custom_call_target="tpu_custom_call" | custom-call | flops 1811939328 | bytes 10223616 | tf_op jit(solution)/shard_map/pallas_call | solution.py:37
  21.1 1.1 %copy-done.7 = f32[768,512]{1,0:T(8,128)} copy-done((f32[768,512]{1,0:T(8,128)}, f32[768,512]{1,0:T(8,128)S(1)}, u32[]{:S(2)}) %copy-start.7) | copy-done | bytes 1572888
  24.4 9.0 %all-to-all-done.incoming_any = f32[16,104,128]{2,1,0:T(8,128)} async-done(((f32[16,104,128]{2,1,0:T(8,128)}), f32[16,104,128]{2,1,0:T(8,128)}, u32[]{:S(2)}, u32[]{:S(2)}) %all-to-all-start) | async-done | bytes 852000 | tf_op jit(solution)/shard_map/all_to_all | solution.py:145
  33.4 2.7 %shard_map.139 = f32[16,104,128]{2,1,0:T(8,128)S(1)} custom-call(f32[16,104,128]{2,1,0:T(8,128)} %all-to-all-done.incoming_any, f32[256,256]{1,0:T(8,128)} %bitcast.39, f32[1,512]{1,0:T(1,128)S(1)} %get-tuple-element.38.local_part_ref, f32[1,512]{1,0:T(1,128)S(1)} %get-tuple-element.39.square_ref), custom_call_target="tpu_custom_call" | custom-call | flops 603979776 | bytes 1572864 | tf_op jit(solution)/shard_map/pallas_call | solution.py:37
  36.1 26.5 %all_to_all.15.returned_ref = f32[16,104,128]{2,1,0:T(8,128)S(1)} all-to-all(f32[16,104,128]{2,1,0:T(8,128)S(1)} %shard_map.139), channel_id=1, replica_groups={{0,2,6,4,8,10,14,12,16,18,22,20,24,26,30,28},{1,3,7,5,9,11,15,13,17,19,..., dimensions={0} | all-to-all | bytes 1703936 | tf_op jit(solution)/shard_map/all_to_all | solution.py:145
  62.6 1.3 %shard_map.140 = (f32[768,512]{1,0:T(8,128)S(1)}, f32[8,128]{1,0:T(8,128)S(1)}, f32[128,512]{1,0:T(8,128)S(1)}, f32[128,512]{1,0:T(8,128)S(1)}, f32[128,512]{1,0...) custom-call(f32[16,104,128]{2,1,0:T(8,128)S(1)} %all_to_all.15.returned_ref, ...), custom_call_target="tpu_custom_call" | custom-call | flops 805306368 | bytes 6291456 | tf_op jit(solution)/shard_map/pallas_call | solution.py:37
  63.9 1.2 %collective-permute-start = (f32[128,512]{1,0:T(8,128)S(1)}, f32[128,512]{1,0:T(8,128)S(1)}, u32[]{:S(2)}, u32[]{:S(2)}) collective-permute-start(f32[128,512]{1,0:T(8,128)S(1)} %get-tuple-element.48), channel_id=1, source_target_pairs={{0,8},{8,16},{16,24},{24,0},{1,9},{9,17},{17,25},{25,1},{2,10},{10... | collective-permute-start | bytes 786440 | tf_op jit(solution)/shard_map/ppermute | solution.py:335
  65.1 1.2 %collective-permute-start.1 = (f32[128,512]{1,0:T(8,128)S(1)}, f32[128,512]{1,0:T(8,128)S(1)}, u32[]{:S(2)}, u32[]{:S(2)}) collective-permute-start(f32[128,512]{1,0:T(8,128)S(1)} %get-tuple-element.49), channel_id=1, source_target_pairs={{0,2},{2,0},{4,6},{6,4},{1,3},{3,1},{5,7},{7,5},{8,10},{10,8},{12,... | collective-permute-start | bytes 786440 | tf_op jit(solution)/shard_map/ppermute | solution.py:335
  66.8 2.8 %collective-permute-start.4 = (f32[128,512]{1,0:T(8,128)S(1)}, f32[128,512]{1,0:T(8,128)S(1)}, u32[]{:S(2)}, u32[]{:S(2)}) collective-permute-start(f32[128,512]{1,0:T(8,128)S(1)} %get-tuple-element.54), channel_id=1, source_target_pairs={{0,24},{8,0},{16,8},{24,16},{1,25},{9,1},{17,9},{25,17},{2,26},{10... | collective-permute-start | bytes 786440 | tf_op jit(solution)/shard_map/ppermute | solution.py:335
  70.3 3.3 %collective-permute-done.refs_0_ = f32[128,512]{1,0:T(8,128)S(1)} collective-permute-done((f32[128,512]{1,0:T(8,128)S(1)}, f32[128,512]{1,0:T(8,128)S(1)}, u32[]{:S(2)}, u32[]{:S(2)}) %collective-permute-start) | collective-permute-done | bytes 262176 | tf_op jit(solution)/shard_map/ppermute | solution.py:335
  73.7 2.5 %shard_map.141 = (f32[1,512]{1,0:T(1,128)}, f32[1,512]{1,0:T(1,128)S(1)}, f32[1,512]{1,0:T(1,128)S(1)}, f32[512,512]{1,0:T(8,128)S(1)}, f32[768,512]{1,0:T(8,128)S(1)}) custom-call(s32[6]{0:T(128)S(1)} %bitcast.27, f32[8,128]{1,0:T(8,128)S(1)} %get-tuple-element.44.sums_ref, f32[1,512]{1,0:T(1,128)S(1)} %bitcast.34, ...), custom_call_target="tpu_custom_call" | custom-call | flops 1207959552 | bytes 8650752 | tf_op jit(solution)/shard_map/pallas_call | solution.py:37
  76.2 1.5 %collective-permute-done.4.refs_0_ = f32[128,512]{1,0:T(8,128)S(1)} collective-permute-done((f32[128,512]{1,0:T(8,128)S(1)}, f32[128,512]{1,0:T(8,128)S(1)}, u32[]{:S(2)}, u32[]{:S(2)}) %collective-permute-start.4) | collective-permute-done | bytes 262176 | tf_op jit(solution)/shard_map/ppermute | solution.py:335
  80.0 3.0 %collective-permute-start.7 = (f32[128,512]{1,0:T(8,128)S(1)}, f32[128,512]{1,0:T(8,128)S(1)}, u32[]{:S(2)}, u32[]{:S(2)}) collective-permute-start(f32[128,512]{1,0:T(8,128)S(1)} %get-tuple-element.60), channel_id=1, source_target_pairs={{0,2},{2,0},{4,6},{6,4},{1,3},{3,1},{5,7},{7,5},{8,10},{10,8},{12,... | collective-permute-start | bytes 786440 | tf_op jit(solution)/shard_map/ppermute | solution.py:335
  83.0 3.6 %collective-permute-start.8 = (f32[128,512]{1,0:T(8,128)S(1)}, f32[128,512]{1,0:T(8,128)S(1)}, u32[]{:S(2)}, u32[]{:S(2)}) collective-permute-start(f32[128,512]{1,0:T(8,128)S(1)} %get-tuple-element.61), channel_id=1, source_target_pairs={{0,24},{8,0},{16,8},{24,16},{1,25},{9,1},{17,9},{25,17},{2,26},{10... | collective-permute-start | bytes 786440 | tf_op jit(solution)/shard_map/ppermute | solution.py:335
  87.4 2.4 %collective-permute-done.6.arrived.refs_0_ = f32[128,512]{1,0:T(8,128)S(1)} collective-permute-done((f32[128,512]{1,0:T(8,128)S(1)}, f32[128,512]{1,0:T(8,128)S(1)}, u32[]{:S(2)}, u32[]{:S(2)}) %collective-permute-start.6) | collective-permute-done | bytes 262176 | tf_op jit(solution)/shard_map/ppermute | solution.py:335
  89.8 1.3 %shard_map.145.refs_5_ = f32[8,128]{1,0:T(8,128)S(1)} custom-call(s32[6]{0:T(128)S(1)} %bitcast.29, f32[512,512]{1,0:T(8,128)S(1)} %get-tuple-element.51.near_ref, f32[256,512]{1,0:T(8,128)S(1)} %get-tuple-element.56.far_ref, f32[768,512]{1,0:T(8,128)S(1)} %get-tuple-element.58.schur_ref, f32[768,512]{1,0:T(8,128)S(1)} %bitcast.17, ...), custom_call_target="tpu_custom_call" | custom-call | flops 1572864 | bytes 4718592 | tf_op jit(solution)/shard_map/pallas_call | solution.py:37
  91.2 1.2 %shard_map.143.stored = f32[768,512]{1,0:T(8,128)} custom-call(f32[512,512]{1,0:T(8,128)S(1)} %get-tuple-element.51.near_ref, f32[256,512]{1,0:T(8,128)S(1)} %get-tuple-element.56.far_ref), custom_call_target="tpu_custom_call" | custom-call | bytes 3145728 | tf_op jit(solution)/shard_map/pallas_call | solution.py:37
  92.4 2.0 %collective-permute-done.8.refs_2_ = f32[128,512]{1,0:T(8,128)S(1)} collective-permute-done((f32[128,512]{1,0:T(8,128)S(1)}, f32[128,512]{1,0:T(8,128)S(1)}, u32[]{:S(2)}, u32[]{:S(2)}) %collective-permute-start.8) | collective-permute-done | bytes 262176 | tf_op jit(solution)/shard_map/ppermute | solution.py:335
  95.3 12.0 %all_to_all.16.sums_ref = f32[32,8,128]{2,1,0:T(8,128)S(1)} all-to-all(f32[32,8,128]{2,1,0:T(8,128)S(1)} %get-tuple-element.64), channel_id=1, replica_groups=mesh['blk'=4,'lat'=4,'depth'=2] {'depth','blk','lat'}, dimensions={0} | all-to-all | bytes 262144 | tf_op jit(solution)/shard_map/all_to_all | solution.py:505
  107.3 2.4 %shard_map.147 = (f32[768,512]{1,0:T(8,128)}, f32[1,512]{1,0:T(1,128)}, f32[1,512]{1,0:T(1,128)}) custom-call(s32[6]{0:T(128)S(1)} %bitcast.31, f32[32,8,128]{2,1,0:T(8,128)S(1)} %all_to_all.16.sums_ref, f32[1,512]{1,0:T(1,128)S(1)} %copy-done.18, f32[1,512]{1,0:T(1,128)S(1)} %get-tuple-element.66.square_ref, f32[768,512]{1,0:T(8,128)S(1)} %bitcast.18, ...), custom_call_target="tpu_custom_call" | custom-call | flops 1572864 | bytes 4718592 | tf_op jit(solution)/shard_map/pallas_call | solution.py:37
  (53 shorter events, 8.4 us)
Async XLA Ops:
  0.6 12.5 %copy-start.4 = (f32[1,1,1,768,256]{4,3,2,1,0:T(8,128)S(1)}, f32[1,1,1,768,256]{4,3,2,1,0:T(8,128)}, u32[]{:S(2)}) copy-start(f32[1,1,1,768,256]{4,3,2,1,0:T(8,128)} %param.16) | copy-start | bytes 2359300
  4.6 8.6 %copy-start = (f32[1,1,1,768,512]{4,3,2,1,0:T(8,128)S(1)}, f32[1,1,1,768,512]{4,3,2,1,0:T(8,128)}, u32[]{:S(2)}) copy-start(f32[1,1,1,768,512]{4,3,2,1,0:T(8,128)} %param.11) | copy-start | bytes 4718596
  4.6 8.6 %copy-start.15 = (s32[1,1,1,6]{3,2,1,0:T(1,128)S(1)}, s32[1,1,1,6]{3,2,1,0:T(1,128)}, u32[]{:S(2)}) copy-start(s32[1,1,1,6]{3,2,1,0:T(1,128)} %param.10) | copy-start | bytes 76
  4.7 28.7 %all-to-all-start = ((f32[16,104,128]{2,1,0:T(8,128)}), f32[16,104,128]{2,1,0:T(8,128)}, u32[]{:S(2)}, u32[]{:S(2)}) async-start(f32[16,104,128]{2,1,0:T(8,128)} %shard_map.137), calls=%async_computation | async-start | bytes 1703936 | tf_op jit(solution)/shard_map/all_to_all | solution.py:145
  33.4 29.2 %copy-start.8 = (f32[768,512]{1,0:T(8,128)S(1)}, f32[768,512]{1,0:T(8,128)}, u32[]{:S(2)}) copy-start(f32[768,512]{1,0:T(8,128)} %copy-done.7) | copy-start | bytes 4718596
  33.4 29.2 %copy-start.10 = (bf16[768,256]{1,0:T(8,128)(2,1)S(1)}, bf16[768,256]{1,0:T(8,128)(2,1)}, u32[]{:S(2)}) copy-start(bf16[768,256]{1,0:T(8,128)(2,1)} %copy-done.9) | copy-start | bytes 1179652
  33.4 29.2 %copy-start.12 = (bf16[768,256]{1,0:T(8,128)(2,1)S(1)}, bf16[768,256]{1,0:T(8,128)(2,1)}, u32[]{:S(2)}) copy-start(bf16[768,256]{1,0:T(8,128)(2,1)} %copy-done.11) | copy-start | bytes 1179652
  33.4 29.2 %copy-start.14 = (bf16[256,384]{1,0:T(8,128)(2,1)S(1)}, bf16[256,384]{1,0:T(8,128)(2,1)}, u32[]{:S(2)}) copy-start(bf16[256,384]{1,0:T(8,128)(2,1)} %copy-done.13) | copy-start | bytes 589828
  62.5 11.1 %copy-start.2 = (bf16[768,768]{1,0:T(8,128)(2,1)S(1)}, bf16[768,768]{1,0:T(8,128)(2,1)}, u32[]{:S(2)}) copy-start(bf16[768,768]{1,0:T(8,128)(2,1)} %copy-done.1) | copy-start | bytes 3538948
  62.6 11.1 %copy-start.3 = (f32[1,1,1,768,512]{4,3,2,1,0:T(8,128)S(1)}, f32[1,1,1,768,512]{4,3,2,1,0:T(8,128)}, u32[]{:S(2)}) copy-start(f32[1,1,1,768,512]{4,3,2,1,0:T(8,128)} %param.12) | copy-start | bytes 4718596
  62.6 11.1 %copy-start.17 = (f32[512]{0:T(512)S(1)}, f32[512]{0:T(512)}, u32[]{:S(2)}) copy-start(f32[512]{0:T(512)} %param.13) | copy-start | bytes 6148
  63.9 9.8 %collective-permute-start = (f32[128,512]{1,0:T(8,128)S(1)}, f32[128,512]{1,0:T(8,128)S(1)}, u32[]{:S(2)}, u32[]{:S(2)}) collective-permute-start(f32[128,512]{1,0:T(8,128)S(1)} %get-tuple-element.48), channel_id=1, source_target_pairs={{0,8},{8,16},{16,24},{24,0},{1,9},{9,17},{17,25},{25,1},{2,10},{10... | collective-permute-start | bytes 786440 | tf_op jit(solution)/shard_map/ppermute | solution.py:335
  65.1 8.6 %collective-permute-start.1 = (f32[128,512]{1,0:T(8,128)S(1)}, f32[128,512]{1,0:T(8,128)S(1)}, u32[]{:S(2)}, u32[]{:S(2)}) collective-permute-start(f32[128,512]{1,0:T(8,128)S(1)} %get-tuple-element.49), channel_id=1, source_target_pairs={{0,2},{2,0},{4,6},{6,4},{1,3},{3,1},{5,7},{7,5},{8,10},{10,8},{12,... | collective-permute-start | bytes 786440 | tf_op jit(solution)/shard_map/ppermute | solution.py:335
  66.3 7.3 %collective-permute-start.2 = (f32[128,512]{1,0:T(8,128)S(1)}, f32[128,512]{1,0:T(8,128)S(1)}, u32[]{:S(2)}, u32[]{:S(2)}) collective-permute-start(f32[128,512]{1,0:T(8,128)S(1)} %get-tuple-element.50), channel_id=1, source_target_pairs={{0,1},{1,0},{2,3},{3,2},{4,5},{5,4},{6,7},{7,6},{8,9},{9,8},{10,11... | collective-permute-start | bytes 786440 | tf_op jit(solution)/shard_map/ppermute | solution.py:335
  66.3 3.3 %collective-permute-start.3 = (f32[8,128]{1,0:T(8,128)S(1)}, f32[8,128]{1,0:T(8,128)S(1)}, u32[]{:S(2)}, u32[]{:S(2)}) collective-permute-start(f32[8,128]{1,0:T(8,128)S(1)} %get-tuple-element.44.sums_ref), channel_id=1, source_target_pairs={{0,1},{1,0},{2,3},{3,2},{4,5},{5,4},{6,7},{7,6},{8,9},{9,8},{10,11... | collective-permute-start | bytes 12296 | tf_op jit(solution)/shard_map/ppermute | solution.py:602
  66.8 10.9 %collective-permute-start.4 = (f32[128,512]{1,0:T(8,128)S(1)}, f32[128,512]{1,0:T(8,128)S(1)}, u32[]{:S(2)}, u32[]{:S(2)}) collective-permute-start(f32[128,512]{1,0:T(8,128)S(1)} %get-tuple-element.54), channel_id=1, source_target_pairs={{0,24},{8,0},{16,8},{24,16},{1,25},{9,1},{17,9},{25,17},{2,26},{10... | collective-permute-start | bytes 786440 | tf_op jit(solution)/shard_map/ppermute | solution.py:335
  69.7 8.1 %collective-permute-start.5 = (f32[128,512]{1,0:T(8,128)S(1)}, f32[128,512]{1,0:T(8,128)S(1)}, u32[]{:S(2)}, u32[]{:S(2)}) collective-permute-start(f32[128,512]{1,0:T(8,128)S(1)} %get-tuple-element.55), channel_id=1, source_target_pairs={{2,4},{4,2},{3,5},{5,3},{10,12},{12,10},{11,13},{13,11},{18,20},{2... | collective-permute-start | bytes 786440 | tf_op jit(solution)/shard_map/ppermute | solution.py:335
  78.7 11.1 %collective-permute-start.6 = (f32[128,512]{1,0:T(8,128)S(1)}, f32[128,512]{1,0:T(8,128)S(1)}, u32[]{:S(2)}, u32[]{:S(2)}) collective-permute-start(f32[128,512]{1,0:T(8,128)S(1)} %get-tuple-element.59), channel_id=1, source_target_pairs={{0,8},{8,16},{16,24},{24,0},{1,9},{9,17},{17,25},{25,1},{2,10},{10... | collective-permute-start | bytes 786440 | tf_op jit(solution)/shard_map/ppermute | solution.py:335
  80.0 12.4 %collective-permute-start.7 = (f32[128,512]{1,0:T(8,128)S(1)}, f32[128,512]{1,0:T(8,128)S(1)}, u32[]{:S(2)}, u32[]{:S(2)}) collective-permute-start(f32[128,512]{1,0:T(8,128)S(1)} %get-tuple-element.60), channel_id=1, source_target_pairs={{0,2},{2,0},{4,6},{6,4},{1,3},{3,1},{5,7},{7,5},{8,10},{10,8},{12,... | collective-permute-start | bytes 786440 | tf_op jit(solution)/shard_map/ppermute | solution.py:335
  83.0 11.4 %collective-permute-start.8 = (f32[128,512]{1,0:T(8,128)S(1)}, f32[128,512]{1,0:T(8,128)S(1)}, u32[]{:S(2)}, u32[]{:S(2)}) collective-permute-start(f32[128,512]{1,0:T(8,128)S(1)} %get-tuple-element.61), channel_id=1, source_target_pairs={{0,24},{8,0},{16,8},{24,16},{1,25},{9,1},{17,9},{25,17},{2,26},{10... | collective-permute-start | bytes 786440 | tf_op jit(solution)/shard_map/ppermute | solution.py:335
  86.6 7.8 %collective-permute-start.9 = (f32[128,512]{1,0:T(8,128)S(1)}, f32[128,512]{1,0:T(8,128)S(1)}, u32[]{:S(2)}, u32[]{:S(2)}) collective-permute-start(f32[128,512]{1,0:T(8,128)S(1)} %get-tuple-element.62), channel_id=1, source_target_pairs={{2,4},{4,2},{3,5},{5,3},{10,12},{12,10},{11,13},{13,11},{18,20},{2... | collective-permute-start | bytes 786440 | tf_op jit(solution)/shard_map/ppermute | solution.py:335
  87.3 7.1 %collective-permute-start.10 = (f32[128,512]{1,0:T(8,128)S(1)}, f32[128,512]{1,0:T(8,128)S(1)}, u32[]{:S(2)}, u32[]{:S(2)}) collective-permute-start(f32[128,512]{1,0:T(8,128)S(1)} %get-tuple-element.63), channel_id=1, source_target_pairs={{0,1},{1,0},{2,3},{3,2},{4,5},{5,4},{6,7},{7,6},{8,9},{9,8},{10,11... | collective-permute-start | bytes 786440 | tf_op jit(solution)/shard_map/ppermute | solution.py:335
  91.1 3.3 %collective-permute-start.11 = (f32[8,128]{1,0:T(8,128)S(1)}, f32[8,128]{1,0:T(8,128)S(1)}, u32[]{:S(2)}, u32[]{:S(2)}) collective-permute-start(f32[8,128]{1,0:T(8,128)S(1)} %shard_map.145.refs_5_), channel_id=1, source_target_pairs={{0,1},{1,0},{2,3},{3,2},{4,5},{5,4},{6,7},{7,6},{8,9},{9,8},{10,11... | collective-permute-start | bytes 12296 | tf_op jit(solution)/shard_map/ppermute | solution.py:647
  92.4 14.9 %copy-start.18 = (f32[1,512]{1,0:T(1,128)S(1)}, f32[1,512]{1,0:T(1,128)}, u32[]{:S(2)}) copy-start(f32[1,512]{1,0:T(1,128)} %get-tuple-element.65.rho_ref) | copy-start | bytes 6148
  (8 other events, 16.2 us)

commit v20 on v19

--- a/solution.py
+++ b/solution.py
@@ -435,7 +435,7 @@
         copy.wait()
 
 
-def products_kernel(len_ref, near_ref, far_ref, schur_ref, residual_ref, arrived, out_ref):
+def products_kernel(len_ref, near_ref, far_ref, schur_ref, residual_ref, arrived, stored, out_ref):
     rows = schur_ref.shape[0] // 6
     curve = cross = jnp.zeros((1, schur_ref.shape[1]), f32)
     for ref, served_moves in ((near_ref, NEAR), (far_ref, FAR)):
@@ -451,7 +451,7 @@
         out_ref[j : j + 1, :] = piece
 
 
-def applied_kernel(pair_depth, len_ref, stored, schur_ref, *refs):
+def applied_kernel(pair_depth, len_ref, schur_ref, *refs):
     keys = moves(SECOND)
     got, refs = dict(zip(keys, refs)), refs[len(keys) :]
     products, (applied_ref, spread_ref) = refs[:-2], refs[-2:]
@@ -633,18 +633,6 @@
     outward["blk", "up"] = plus
     outward = [outward[move] for move in moves(SECOND)]
     got = exchange(outward, SECOND)
-    (products,) = call(
-        products_kernel,
-        [shape_of(2 * folds, LANES)],
-        [lengths, near, far, schur_image, residual, got[0]],
-        smem=(0,),
-        loose=(5,),
-        flops=4 * height * width,
-        moved=12 * height * width,
-    )
-    products = [products]
-    if pair_depth:
-        products.append(lax.ppermute(products[0], "depth", route("depth", 0)))
     (direction,) = call(
         store_kernel,
         [whole],
@@ -653,12 +641,24 @@
         moved=8 * height * width,
         scratch=[pltpu.SemaphoreType.DMA((6,))],
     )
+    (products,) = call(
+        products_kernel,
+        [shape_of(2 * folds, LANES)],
+        [lengths, near, far, schur_image, residual, got[0], direction],
+        smem=(0,),
+        loose=(5,),
+        far=(6,),
+        flops=4 * height * width,
+        moved=12 * height * width,
+    )
+    products = [products]
+    if pair_depth:
+        products.append(lax.ppermute(products[0], "depth", route("depth", 0)))
     applied, spread_sums = call(
         functools.partial(applied_kernel, pair_depth),
         [whole, shape_of(devices, (2 if pair_depth else 3) * folds, LANES)],
-        [lengths, direction, schur_image, *got, *products],
+        [lengths, schur_image, *got, *products],
         smem=(0,),
-        far=(1,),
         flops=4 * height * width,
         moved=12 * height * width,
     )

time: 110 us -> 110 us (level)
  no operation moved by 1% of the time
where the time goes in v20:
time: 110 us
  blocking collectives  38.5 us (35%)
  starting transfers between devices  23 us (21%)
  Pallas kernels  21.4 us (19%)
  waiting for transfers between devices  18.2 us (17%)
  local copies, waits for them, and re-layouts  7.72 us (7%)
    all_to_all x1, blocking collectives, to_layer(): return lax.all_to_all(x, LAYER, 0, 0, axis_index_groups=[order], tiled=True)  26.5 us
    pallas_call x11, Pallas kernels, call(): pl.pallas_call(body, out_shape=list(outs), in_specs=in_specs, out_specs=o...  21.4 us
    ppermute x10, starting transfers between devices, exchange(): lax.ppermute(block, axis, route(axis, way))  13.9 us
    all_to_all x1, blocking collectives, to_all(): return lax.all_to_all(x, axes, split_axis=0, concat_axis=0, tiled=True)  12 us
    ppermute x10, waiting for transfers between devices, exchange(): lax.ppermute(block, axis, route(axis, way))  9.23 us
    all_to_all x1, waiting for transfers between devices, to_layer(): return lax.all_to_all(x, LAYER, 0, 0, axis_index_groups=[order], tiled=True)  8.98 us
    all_to_all x1, starting transfers between devices, to_layer(): return lax.all_to_all(x, LAYER, 0, 0, axis_index_groups=[order], tiled=True)  8.5 us
    unnamed x38, local copies, waits for them, and re-layouts  7.72 us
  transfers between devices with their start and end apart: 13, of which 5 were waited for; matrix products, arithmetic and copies ran while one was open for 0% of the time, Pallas kernels for 8%

profile of v20, /device:TPU:0, one launch (start us, length us, event | category | flops | bytes accessed | tf_op | source)
XLA Modules:
  0.0 109.7 jit_solution(9885135893959980331)
XLA Ops:
  0.6 4.0 %shard_map.138 = f32[16,104,128]{2,1,0:T(8,128)} custom-call(s32[6]{0:T(128)} %bitcast.25, s32[1,256]{1,0:T(1,128)} %bitcast.32, s32[1,256]{1,0:T(1,128)} %bitcast.37, f32[768,512]{1,0:T(8,128)} %bitcast.15, f32[768,256]{1,0:T(8,128)} %bitcast.21), custom_call_target="tpu_custom_call" | custom-call | flops 603979776 | bytes 3145728 | tf_op jit(solution)/shard_map/pallas_call | solution.py:37
  4.7 8.5 %all-to-all-start = ((f32[16,104,128]{2,1,0:T(8,128)}), f32[16,104,128]{2,1,0:T(8,128)}, u32[]{:S(2)}, u32[]{:S(2)}) async-start(f32[16,104,128]{2,1,0:T(8,128)} %shard_map.138), calls=%async_computation | async-start | bytes 1703936 | tf_op jit(solution)/shard_map/all_to_all | solution.py:145
  13.2 1.7 %copy-done.5 = f32[1,1,1,768,768]{4,3,2,1,0:T(8,128)S(1)} copy-done((f32[1,1,1,768,768]{4,3,2,1,0:T(8,128)S(1)}, f32[1,1,1,768,768]{4,3,2,1,0:T(8,128)}, u32[]{:S(2)}) %copy-start.5) | copy-done | bytes 2359320
  14.9 1.7 %copy-done.6 = f32[1,1,1,768,768]{4,3,2,1,0:T(8,128)S(1)} copy-done((f32[1,1,1,768,768]{4,3,2,1,0:T(8,128)S(1)}, f32[1,1,1,768,768]{4,3,2,1,0:T(8,128)}, u32[]{:S(2)}) %copy-start.6) | copy-done | bytes 2359320
  16.5 3.5 %shard_map.137 = (f32[768,512]{1,0:T(8,128)S(1)}, f32[1,512]{1,0:T(1,128)S(1)}, f32[1,512]{1,0:T(1,128)S(1)}, bf16[256,384]{1,0:T(8,128)(2,1)S(1)}, bf16[768,256...) custom-call(s32[6]{0:T(128)S(1)} %bitcast.26, ...), custom_call_target="tpu_custom_call" | custom-call | flops 1811939328 | bytes 10223616 | tf_op jit(solution)/shard_map/pallas_call | solution.py:37
  21.1 1.1 %copy-done.7 = f32[768,512]{1,0:T(8,128)} copy-done((f32[768,512]{1,0:T(8,128)}, f32[768,512]{1,0:T(8,128)S(1)}, u32[]{:S(2)}) %copy-start.7) | copy-done | bytes 1572888
  24.4 9.0 %all-to-all-done.incoming_any = f32[16,104,128]{2,1,0:T(8,128)} async-done(((f32[16,104,128]{2,1,0:T(8,128)}), f32[16,104,128]{2,1,0:T(8,128)}, u32[]{:S(2)}, u32[]{:S(2)}) %all-to-all-start) | async-done | bytes 852000 | tf_op jit(solution)/shard_map/all_to_all | solution.py:145
  33.4 2.7 %shard_map.139 = f32[16,104,128]{2,1,0:T(8,128)S(1)} custom-call(f32[16,104,128]{2,1,0:T(8,128)} %all-to-all-done.incoming_any, f32[256,256]{1,0:T(8,128)} %bitcast.39, f32[1,512]{1,0:T(1,128)S(1)} %get-tuple-element.40.local_part_ref, f32[1,512]{1,0:T(1,128)S(1)} %get-tuple-element.41.square_ref), custom_call_target="tpu_custom_call" | custom-call | flops 603979776 | bytes 1572864 | tf_op jit(solution)/shard_map/pallas_call | solution.py:37
  36.1 26.5 %all_to_all.15.returned_ref = f32[16,104,128]{2,1,0:T(8,128)S(1)} all-to-all(f32[16,104,128]{2,1,0:T(8,128)S(1)} %shard_map.139), channel_id=1, replica_groups={{0,2,6,4,8,10,14,12,16,18,22,20,24,26,30,28},{1,3,7,5,9,11,15,13,17,19,..., dimensions={0} | all-to-all | bytes 1703936 | tf_op jit(solution)/shard_map/all_to_all | solution.py:145
  62.6 1.3 %shard_map.140 = (f32[768,512]{1,0:T(8,128)S(1)}, f32[8,128]{1,0:T(8,128)S(1)}, f32[128,512]{1,0:T(8,128)S(1)}, f32[128,512]{1,0:T(8,128)S(1)}, f32[128,512]{1,0...) custom-call(f32[16,104,128]{2,1,0:T(8,128)S(1)} %all_to_all.15.returned_ref, ...), custom_call_target="tpu_custom_call" | custom-call | flops 805306368 | bytes 6291456 | tf_op jit(solution)/shard_map/pallas_call | solution.py:37
  63.9 1.2 %collective-permute-start = (f32[128,512]{1,0:T(8,128)S(1)}, f32[128,512]{1,0:T(8,128)S(1)}, u32[]{:S(2)}, u32[]{:S(2)}) collective-permute-start(f32[128,512]{1,0:T(8,128)S(1)} %get-tuple-element.48), channel_id=1, source_target_pairs={{0,8},{8,16},{16,24},{24,0},{1,9},{9,17},{17,25},{25,1},{2,10},{10... | collective-permute-start | bytes 786440 | tf_op jit(solution)/shard_map/ppermute | solution.py:335
  65.1 1.2 %collective-permute-start.1 = (f32[128,512]{1,0:T(8,128)S(1)}, f32[128,512]{1,0:T(8,128)S(1)}, u32[]{:S(2)}, u32[]{:S(2)}) collective-permute-start(f32[128,512]{1,0:T(8,128)S(1)} %get-tuple-element.49), channel_id=1, source_target_pairs={{0,2},{2,0},{4,6},{6,4},{1,3},{3,1},{5,7},{7,5},{8,10},{10,8},{12,... | collective-permute-start | bytes 786440 | tf_op jit(solution)/shard_map/ppermute | solution.py:335
  66.8 2.8 %collective-permute-start.4 = (f32[128,512]{1,0:T(8,128)S(1)}, f32[128,512]{1,0:T(8,128)S(1)}, u32[]{:S(2)}, u32[]{:S(2)}) collective-permute-start(f32[128,512]{1,0:T(8,128)S(1)} %get-tuple-element.53), channel_id=1, source_target_pairs={{0,24},{8,0},{16,8},{24,16},{1,25},{9,1},{17,9},{25,17},{2,26},{10... | collective-permute-start | bytes 786440 | tf_op jit(solution)/shard_map/ppermute | solution.py:335
  70.3 3.3 %collective-permute-done.refs_0_ = f32[128,512]{1,0:T(8,128)S(1)} collective-permute-done((f32[128,512]{1,0:T(8,128)S(1)}, f32[128,512]{1,0:T(8,128)S(1)}, u32[]{:S(2)}, u32[]{:S(2)}) %collective-permute-start) | collective-permute-done | bytes 262176 | tf_op jit(solution)/shard_map/ppermute | solution.py:335
  73.7 2.5 %shard_map.141 = (f32[1,512]{1,0:T(1,128)}, f32[1,512]{1,0:T(1,128)S(1)}, f32[1,512]{1,0:T(1,128)S(1)}, f32[512,512]{1,0:T(8,128)S(1)}, f32[768,512]{1,0:T(8,128)S(1)}) custom-call(s32[6]{0:T(128)S(1)} %bitcast.27, f32[8,128]{1,0:T(8,128)S(1)} %get-tuple-element.46.sums_ref, f32[1,512]{1,0:T(1,128)S(1)} %bitcast.34, ...), custom_call_target="tpu_custom_call" | custom-call | flops 1207959552 | bytes 8650752 | tf_op jit(solution)/shard_map/pallas_call | solution.py:37
  76.2 1.5 %collective-permute-done.4.refs_0_ = f32[128,512]{1,0:T(8,128)S(1)} collective-permute-done((f32[128,512]{1,0:T(8,128)S(1)}, f32[128,512]{1,0:T(8,128)S(1)}, u32[]{:S(2)}, u32[]{:S(2)}) %collective-permute-start.4) | collective-permute-done | bytes 262176 | tf_op jit(solution)/shard_map/ppermute | solution.py:335
  80.0 3.0 %collective-permute-start.7 = (f32[128,512]{1,0:T(8,128)S(1)}, f32[128,512]{1,0:T(8,128)S(1)}, u32[]{:S(2)}, u32[]{:S(2)}) collective-permute-start(f32[128,512]{1,0:T(8,128)S(1)} %get-tuple-element.59), channel_id=1, source_target_pairs={{0,2},{2,0},{4,6},{6,4},{1,3},{3,1},{5,7},{7,5},{8,10},{10,8},{12,... | collective-permute-start | bytes 786440 | tf_op jit(solution)/shard_map/ppermute | solution.py:335
  83.1 3.6 %collective-permute-start.8 = (f32[128,512]{1,0:T(8,128)S(1)}, f32[128,512]{1,0:T(8,128)S(1)}, u32[]{:S(2)}, u32[]{:S(2)}) collective-permute-start(f32[128,512]{1,0:T(8,128)S(1)} %get-tuple-element.60), channel_id=1, source_target_pairs={{0,24},{8,0},{16,8},{24,16},{1,25},{9,1},{17,9},{25,17},{2,26},{10... | collective-permute-start | bytes 786440 | tf_op jit(solution)/shard_map/ppermute | solution.py:335
  87.4 1.2 %shard_map.144.stored = f32[768,512]{1,0:T(8,128)} custom-call(f32[512,512]{1,0:T(8,128)S(1)} %get-tuple-element.63.near_ref, f32[256,512]{1,0:T(8,128)S(1)} %get-tuple-element.55.far_ref), custom_call_target="tpu_custom_call" | custom-call | bytes 3145728 | tf_op jit(solution)/shard_map/pallas_call | solution.py:37
  88.6 1.2 %collective-permute-done.6.arrived.refs_0_ = f32[128,512]{1,0:T(8,128)S(1)} collective-permute-done((f32[128,512]{1,0:T(8,128)S(1)}, f32[128,512]{1,0:T(8,128)S(1)}, u32[]{:S(2)}, u32[]{:S(2)}) %collective-permute-start.6) | collective-permute-done | bytes 262176 | tf_op jit(solution)/shard_map/ppermute | solution.py:335
  89.8 1.3 %shard_map.145.refs_5_ = f32[8,128]{1,0:T(8,128)S(1)} custom-call(s32[6]{0:T(128)S(1)} %bitcast.29, f32[512,512]{1,0:T(8,128)S(1)} %get-tuple-element.63.near_ref, f32[256,512]{1,0:T(8,128)S(1)} %get-tuple-element.55.far_ref, f32[768,512]{1,0:T(8,128)S(1)} %get-tuple-element.57.schur_ref, f32[768,512]{1,0:T(8,128)S(1)} %bitcast.17, ...), custom_call_target="tpu_custom_call" | custom-call | flops 1572864 | bytes 4718592 | tf_op jit(solution)/shard_map/pallas_call | solution.py:37
  91.2 3.2 %collective-permute-done.8.refs_2_ = f32[128,512]{1,0:T(8,128)S(1)} collective-permute-done((f32[128,512]{1,0:T(8,128)S(1)}, f32[128,512]{1,0:T(8,128)S(1)}, u32[]{:S(2)}, u32[]{:S(2)}) %collective-permute-start.8) | collective-permute-done | bytes 262176 | tf_op jit(solution)/shard_map/ppermute | solution.py:335
  95.3 12.0 %all_to_all.16.sums_ref = f32[32,8,128]{2,1,0:T(8,128)S(1)} all-to-all(f32[32,8,128]{2,1,0:T(8,128)S(1)} %get-tuple-element.64), channel_id=1, replica_groups=mesh['blk'=4,'lat'=4,'depth'=2] {'depth','blk','lat'}, dimensions={0} | all-to-all | bytes 262144 | tf_op jit(solution)/shard_map/all_to_all | solution.py:505
  107.3 2.4 %shard_map.147 = (f32[768,512]{1,0:T(8,128)}, f32[1,512]{1,0:T(1,128)}, f32[1,512]{1,0:T(1,128)}) custom-call(s32[6]{0:T(128)S(1)} %bitcast.31, f32[32,8,128]{2,1,0:T(8,128)S(1)} %all_to_all.16.sums_ref, f32[1,512]{1,0:T(1,128)S(1)} %copy-done.18, f32[1,512]{1,0:T(1,128)S(1)} %get-tuple-element.66.square_ref, f32[768,512]{1,0:T(8,128)S(1)} %bitcast.18, ...), custom_call_target="tpu_custom_call" | custom-call | flops 1572864 | bytes 4718592 | tf_op jit(solution)/shard_map/pallas_call | solution.py:37
  (53 shorter events, 8.4 us)
Async XLA Ops:
  0.6 12.5 %copy-start.4 = (f32[1,1,1,768,256]{4,3,2,1,0:T(8,128)S(1)}, f32[1,1,1,768,256]{4,3,2,1,0:T(8,128)}, u32[]{:S(2)}) copy-start(f32[1,1,1,768,256]{4,3,2,1,0:T(8,128)} %param.16) | copy-start | bytes 2359300
  4.6 8.6 %copy-start = (f32[1,1,1,768,512]{4,3,2,1,0:T(8,128)S(1)}, f32[1,1,1,768,512]{4,3,2,1,0:T(8,128)}, u32[]{:S(2)}) copy-start(f32[1,1,1,768,512]{4,3,2,1,0:T(8,128)} %param.11) | copy-start | bytes 4718596
  4.6 8.6 %copy-start.15 = (s32[1,1,1,6]{3,2,1,0:T(1,128)S(1)}, s32[1,1,1,6]{3,2,1,0:T(1,128)}, u32[]{:S(2)}) copy-start(s32[1,1,1,6]{3,2,1,0:T(1,128)} %param.10) | copy-start | bytes 76
  4.7 28.7 %all-to-all-start = ((f32[16,104,128]{2,1,0:T(8,128)}), f32[16,104,128]{2,1,0:T(8,128)}, u32[]{:S(2)}, u32[]{:S(2)}) async-start(f32[16,104,128]{2,1,0:T(8,128)} %shard_map.138), calls=%async_computation | async-start | bytes 1703936 | tf_op jit(solution)/shard_map/all_to_all | solution.py:145
  33.4 29.2 %copy-start.8 = (f32[768,512]{1,0:T(8,128)S(1)}, f32[768,512]{1,0:T(8,128)}, u32[]{:S(2)}) copy-start(f32[768,512]{1,0:T(8,128)} %copy-done.7) | copy-start | bytes 4718596
  33.4 29.2 %copy-start.10 = (bf16[768,256]{1,0:T(8,128)(2,1)S(1)}, bf16[768,256]{1,0:T(8,128)(2,1)}, u32[]{:S(2)}) copy-start(bf16[768,256]{1,0:T(8,128)(2,1)} %copy-done.9) | copy-start | bytes 1179652
  33.4 29.2 %copy-start.12 = (bf16[768,256]{1,0:T(8,128)(2,1)S(1)}, bf16[768,256]{1,0:T(8,128)(2,1)}, u32[]{:S(2)}) copy-start(bf16[768,256]{1,0:T(8,128)(2,1)} %copy-done.11) | copy-start | bytes 1179652
  33.4 29.2 %copy-start.14 = (bf16[256,384]{1,0:T(8,128)(2,1)S(1)}, bf16[256,384]{1,0:T(8,128)(2,1)}, u32[]{:S(2)}) copy-start(bf16[256,384]{1,0:T(8,128)(2,1)} %copy-done.13) | copy-start | bytes 589828
  62.5 11.1 %copy-start.2 = (bf16[768,768]{1,0:T(8,128)(2,1)S(1)}, bf16[768,768]{1,0:T(8,128)(2,1)}, u32[]{:S(2)}) copy-start(bf16[768,768]{1,0:T(8,128)(2,1)} %copy-done.1) | copy-start | bytes 3538948
  62.6 11.1 %copy-start.3 = (f32[1,1,1,768,512]{4,3,2,1,0:T(8,128)S(1)}, f32[1,1,1,768,512]{4,3,2,1,0:T(8,128)}, u32[]{:S(2)}) copy-start(f32[1,1,1,768,512]{4,3,2,1,0:T(8,128)} %param.12) | copy-start | bytes 4718596
  62.6 11.1 %copy-start.17 = (f32[512]{0:T(512)S(1)}, f32[512]{0:T(512)}, u32[]{:S(2)}) copy-start(f32[512]{0:T(512)} %param.13) | copy-start | bytes 6148
  63.9 9.8 %collective-permute-start = (f32[128,512]{1,0:T(8,128)S(1)}, f32[128,512]{1,0:T(8,128)S(1)}, u32[]{:S(2)}, u32[]{:S(2)}) collective-permute-start(f32[128,512]{1,0:T(8,128)S(1)} %get-tuple-element.48), channel_id=1, source_target_pairs={{0,8},{8,16},{16,24},{24,0},{1,9},{9,17},{17,25},{25,1},{2,10},{10... | collective-permute-start | bytes 786440 | tf_op jit(solution)/shard_map/ppermute | solution.py:335
  65.1 8.6 %collective-permute-start.1 = (f32[128,512]{1,0:T(8,128)S(1)}, f32[128,512]{1,0:T(8,128)S(1)}, u32[]{:S(2)}, u32[]{:S(2)}) collective-permute-start(f32[128,512]{1,0:T(8,128)S(1)} %get-tuple-element.49), channel_id=1, source_target_pairs={{0,2},{2,0},{4,6},{6,4},{1,3},{3,1},{5,7},{7,5},{8,10},{10,8},{12,... | collective-permute-start | bytes 786440 | tf_op jit(solution)/shard_map/ppermute | solution.py:335
  66.3 7.3 %collective-permute-start.2 = (f32[128,512]{1,0:T(8,128)S(1)}, f32[128,512]{1,0:T(8,128)S(1)}, u32[]{:S(2)}, u32[]{:S(2)}) collective-permute-start(f32[128,512]{1,0:T(8,128)S(1)} %get-tuple-element.50), channel_id=1, source_target_pairs={{0,1},{1,0},{2,3},{3,2},{4,5},{5,4},{6,7},{7,6},{8,9},{9,8},{10,11... | collective-permute-start | bytes 786440 | tf_op jit(solution)/shard_map/ppermute | solution.py:335
  66.3 3.3 %collective-permute-start.3 = (f32[8,128]{1,0:T(8,128)S(1)}, f32[8,128]{1,0:T(8,128)S(1)}, u32[]{:S(2)}, u32[]{:S(2)}) collective-permute-start(f32[8,128]{1,0:T(8,128)S(1)} %get-tuple-element.46.sums_ref), channel_id=1, source_target_pairs={{0,1},{1,0},{2,3},{3,2},{4,5},{5,4},{6,7},{7,6},{8,9},{9,8},{10,11... | collective-permute-start | bytes 12296 | tf_op jit(solution)/shard_map/ppermute | solution.py:602
  66.8 10.9 %collective-permute-start.4 = (f32[128,512]{1,0:T(8,128)S(1)}, f32[128,512]{1,0:T(8,128)S(1)}, u32[]{:S(2)}, u32[]{:S(2)}) collective-permute-start(f32[128,512]{1,0:T(8,128)S(1)} %get-tuple-element.53), channel_id=1, source_target_pairs={{0,24},{8,0},{16,8},{24,16},{1,25},{9,1},{17,9},{25,17},{2,26},{10... | collective-permute-start | bytes 786440 | tf_op jit(solution)/shard_map/ppermute | solution.py:335
  69.7 8.1 %collective-permute-start.5 = (f32[128,512]{1,0:T(8,128)S(1)}, f32[128,512]{1,0:T(8,128)S(1)}, u32[]{:S(2)}, u32[]{:S(2)}) collective-permute-start(f32[128,512]{1,0:T(8,128)S(1)} %get-tuple-element.54), channel_id=1, source_target_pairs={{2,4},{4,2},{3,5},{5,3},{10,12},{12,10},{11,13},{13,11},{18,20},{2... | collective-permute-start | bytes 786440 | tf_op jit(solution)/shard_map/ppermute | solution.py:335
  78.7 11.1 %collective-permute-start.6 = (f32[128,512]{1,0:T(8,128)S(1)}, f32[128,512]{1,0:T(8,128)S(1)}, u32[]{:S(2)}, u32[]{:S(2)}) collective-permute-start(f32[128,512]{1,0:T(8,128)S(1)} %get-tuple-element.58), channel_id=1, source_target_pairs={{0,8},{8,16},{16,24},{24,0},{1,9},{9,17},{17,25},{25,1},{2,10},{10... | collective-permute-start | bytes 786440 | tf_op jit(solution)/shard_map/ppermute | solution.py:335
  80.0 11.2 %collective-permute-start.7 = (f32[128,512]{1,0:T(8,128)S(1)}, f32[128,512]{1,0:T(8,128)S(1)}, u32[]{:S(2)}, u32[]{:S(2)}) collective-permute-start(f32[128,512]{1,0:T(8,128)S(1)} %get-tuple-element.59), channel_id=1, source_target_pairs={{0,2},{2,0},{4,6},{6,4},{1,3},{3,1},{5,7},{7,5},{8,10},{10,8},{12,... | collective-permute-start | bytes 786440 | tf_op jit(solution)/shard_map/ppermute | solution.py:335
  83.1 11.4 %collective-permute-start.8 = (f32[128,512]{1,0:T(8,128)S(1)}, f32[128,512]{1,0:T(8,128)S(1)}, u32[]{:S(2)}, u32[]{:S(2)}) collective-permute-start(f32[128,512]{1,0:T(8,128)S(1)} %get-tuple-element.60), channel_id=1, source_target_pairs={{0,24},{8,0},{16,8},{24,16},{1,25},{9,1},{17,9},{25,17},{2,26},{10... | collective-permute-start | bytes 786440 | tf_op jit(solution)/shard_map/ppermute | solution.py:335
  86.7 7.8 %collective-permute-start.9 = (f32[128,512]{1,0:T(8,128)S(1)}, f32[128,512]{1,0:T(8,128)S(1)}, u32[]{:S(2)}, u32[]{:S(2)}) collective-permute-start(f32[128,512]{1,0:T(8,128)S(1)} %get-tuple-element.61), channel_id=1, source_target_pairs={{2,4},{4,2},{3,5},{5,3},{10,12},{12,10},{11,13},{13,11},{18,20},{2... | collective-permute-start | bytes 786440 | tf_op jit(solution)/shard_map/ppermute | solution.py:335
  87.3 7.1 %collective-permute-start.10 = (f32[128,512]{1,0:T(8,128)S(1)}, f32[128,512]{1,0:T(8,128)S(1)}, u32[]{:S(2)}, u32[]{:S(2)}) collective-permute-start(f32[128,512]{1,0:T(8,128)S(1)} %get-tuple-element.62), channel_id=1, source_target_pairs={{0,1},{1,0},{2,3},{3,2},{4,5},{5,4},{6,7},{7,6},{8,9},{9,8},{10,11... | collective-permute-start | bytes 786440 | tf_op jit(solution)/shard_map/ppermute | solution.py:335
  91.1 16.2 %copy-start.18 = (f32[1,512]{1,0:T(1,128)S(1)}, f32[1,512]{1,0:T(1,128)}, u32[]{:S(2)}) copy-start(f32[1,512]{1,0:T(1,128)} %get-tuple-element.65.rho_ref) | copy-start | bytes 6148
  91.1 3.3 %collective-permute-start.11 = (f32[8,128]{1,0:T(8,128)S(1)}, f32[8,128]{1,0:T(8,128)S(1)}, u32[]{:S(2)}, u32[]{:S(2)}) collective-permute-start(f32[8,128]{1,0:T(8,128)S(1)} %shard_map.145.refs_5_), channel_id=1, source_target_pairs={{0,1},{1,0},{2,3},{3,2},{4,5},{5,4},{6,7},{7,6},{8,9},{9,8},{10,11... | collective-permute-start | bytes 12296 | tf_op jit(solution)/shard_map/ppermute | solution.py:656
  (8 other events, 16.2 us)
